TPU v7x, 32 devices: a whole 2x2x4 slice. The times are simulated.
32 devices in a mesh: wide: 8 (over z, x), narrow: 4 (over y, core).
Axes of the slice: x: 2, y: 2, z: 4, core: 2. Of those that a mesh axis runs over, the one named last changes fastest.
Arguments:
- target_in: bfloat16 [12288, 1024], P(('wide', 'narrow')), may hold values from -6 to 6
- memory: bfloat16 [32768, 1024], P(('wide', 'narrow')), may hold values from -6 to 6
- block_rows: int32 [32, 3], P(('wide', 'narrow')), may hold values from 1 to 640, 1024 in all within a row
- pad_rows: int32 [32, 3], P(('wide', 'narrow')), may hold values from 0 to 340
- seq_lengths: int32 [32, 3], P(('wide', 'narrow')), may hold values from 32 to 128
- self_qkv: bfloat16 [1024, 3072], P(('wide', 'narrow')), may hold values from -0.1875 to 0.1875
- self_out: bfloat16 [1024, 1024], P(('wide', 'narrow')), may hold values from -0.75 to 0.75
- cross_query: bfloat16 [1024, 1024], P(('wide', 'narrow')), may hold values from -0.1875 to 0.1875
- cross_kv: bfloat16 [1024, 2048], P(('wide', 'narrow')), may hold values from -0.1875 to 0.1875
- cross_out: bfloat16 [1024, 1024], P(('wide', 'narrow')), may hold values from -0.75 to 0.75
- ffn_in: bfloat16 [1024, 4096], P(('wide', 'narrow')), may hold values from -0.1875 to 0.1875
- ffn_out: bfloat16 [4096, 1024], P(('wide', 'narrow')), may hold values from -0.09375 to 0.09375
- norm_scale: bfloat16 [3, 1024], P(None, ('wide', 'narrow')), may hold values from 0.5 to 1.5
- small_bias: bfloat16 [10, 1024], P(None, ('wide', 'narrow')), may hold values from -2 to 2
- ffn_bias: bfloat16 [4096], P(('wide', 'narrow')), may hold values from -2 to 2
- cotangent: bfloat16 [12288, 1024], P(('wide', 'narrow')), may hold values from -6 to 6
Outputs:
- block_out: bfloat16 [12288, 1024], P(('wide', 'narrow'))
- target_grad: float32 [12288, 1024], P(('wide', 'narrow'))
- memory_grad: float32 [32768, 1024], P(('wide', 'narrow'))
- self_qkv_grad: float32 [1024, 3072], P(('wide', 'narrow'))
- self_out_grad: float32 [1024, 1024], P(('wide', 'narrow'))
- cross_query_grad: float32 [1024, 1024], P(('wide', 'narrow'))
- cross_kv_grad: float32 [1024, 2048], P(('wide', 'narrow'))
- cross_out_grad: float32 [1024, 1024], P(('wide', 'narrow'))
- ffn_in_grad: float32 [1024, 4096], P(('wide', 'narrow'))
- ffn_out_grad: float32 [4096, 1024], P(('wide', 'narrow'))
- norm_scale_grad: float32 [3, 1024], P(None, ('wide', 'narrow'))
- small_bias_grad: float32 [10, 1024], P(None, ('wide', 'narrow'))
- ffn_bias_grad: float32 [4096], P(('wide', 'narrow'))
Inputs may be any that keep to these rules, and one draw needn't show every extreme that they name: `block_rows`: each row's 3 blocks together hold its 1024 memory rows.
All inputs are finite; a program needn't handle non-finite values.
Results may differ from a plain program's by a relative error of at most 0.018.
Values may be sent and summed in bfloat16 or wider, within the bound.
No kernel may reach another device: no remote copies, remote signals or barrier semaphores. Data moves between devices by JAX's collectives and lax.ppermute only.
A program may use at most 256 MiB of HBM per device.

v0:
```python
import jax
import jax.numpy as jnp
from jax import lax
from jax.sharding import PartitionSpec as P

HEADS = 16
HEAD_DIM = 64
SEQ_LEN = 128


norm_eps = 1e-05
neg_fill = -1e30


def matmul(first, second):
    return jnp.dot(first, second, preferred_element_type=jnp.float32)


def inner_rows(first, second):
    return lax.dot_general(
        first, second, (((0,), (0,)), ((), ())), preferred_element_type=jnp.float32
    )


def inner_cols(first, second):
    return lax.dot_general(
        first, second, (((1,), (1,)), ((), ())), preferred_element_type=jnp.float32
    )


def column_sums(values):
    return jnp.sum(values.astype(jnp.float32), axis=0)


def exact_gelu(values):
    return jax.nn.gelu(values, approximate=False)


def build_masks(block_rows, pad_rows, seq_lengths, seq_len, mem_rows):
    starts = jnp.cumsum(block_rows) - block_rows
    valid = jnp.maximum(block_rows - pad_rows, (block_rows + 1) // 2)
    places = jnp.arange(mem_rows, dtype=jnp.int32)
    memory_ok = (places[None, :] >= starts[:, None]) & (places[None, :] < (starts + valid)[:, None])
    cross_mask = jnp.repeat(memory_ok, seq_len, axis=0)
    slots = jnp.arange(seq_len, dtype=jnp.int32)
    causal = slots[None, :] <= slots[:, None]
    self_mask = causal[None] & (slots[None, None, :] < seq_lengths[:, None, None])
    return (self_mask, cross_mask)


def normalize(values, gain, shift):
    centered = values - jnp.mean(values, axis=-1, keepdims=True)
    inverse = lax.rsqrt(jnp.mean(centered * centered, axis=-1, keepdims=True) + norm_eps)
    unit = centered * inverse
    return (unit * gain + shift, unit, inverse)


def normalize_back(grad, unit, inverse, gain):
    scaled = grad * gain
    inner = (
        scaled
        - jnp.mean(scaled, axis=-1, keepdims=True)
        - unit * jnp.mean(scaled * unit, axis=-1, keepdims=True)
    )
    return (inverse * inner, jnp.sum(grad * unit, axis=0), jnp.sum(grad, axis=0))


def softmax_rows(scores):
    top = jnp.max(scores, axis=-1, keepdims=True)
    shifted = jnp.exp(scores - top)
    total = jnp.sum(shifted, axis=-1, keepdims=True)
    return (shifted / total, top + jnp.log(total))


def self_split(qkv):
    tokens = qkv.shape[0]
    parts = qkv.reshape(tokens // SEQ_LEN, SEQ_LEN, 3, HEADS, HEAD_DIM)
    return (parts[:, :, 0], parts[:, :, 1], parts[:, :, 2])


def self_scores(queries, keys, mask):
    raw = jnp.einsum(
        "sqhe,skhe->shqk", queries, keys, preferred_element_type=jnp.float32
    ) * HEAD_DIM ** (-0.5)
    return jnp.where(mask[:, None], raw, neg_fill)


def self_forward(qkv, mask):
    queries, keys, values = self_split(qkv)
    probs, summary = softmax_rows(self_scores(queries, keys, mask))
    context = jnp.einsum(
        "shqk,skhe->sqhe", probs.astype(jnp.bfloat16), values, preferred_element_type=jnp.float32
    )
    return (context.reshape(qkv.shape[0], -1).astype(jnp.bfloat16), summary)


def self_backward(qkv, context_grad, summary, mask):
    queries, keys, values = self_split(qkv)
    scale = HEAD_DIM ** (-0.5)
    tokens = qkv.shape[0]
    probs = jnp.exp(self_scores(queries, keys, mask) - summary)
    grad_heads = context_grad.reshape(queries.shape)
    value_grad = jnp.einsum(
        "shqk,sqhe->skhe",
        probs.astype(jnp.bfloat16),
        grad_heads,
        preferred_element_type=jnp.float32,
    )
    prob_grad = jnp.einsum(
        "sqhe,skhe->shqk", grad_heads, values, preferred_element_type=jnp.float32
    )
    score_grad = (probs * (prob_grad - jnp.sum(probs * prob_grad, axis=-1, keepdims=True))).astype(
        jnp.bfloat16
    )
    query_grad = (
        jnp.einsum("shqk,skhe->sqhe", score_grad, keys, preferred_element_type=jnp.float32) * scale
    )
    key_grad = (
        jnp.einsum("shqk,sqhe->skhe", score_grad, queries, preferred_element_type=jnp.float32)
        * scale
    )
    joined = [
        query_grad.reshape(tokens, -1),
        key_grad.reshape(tokens, -1),
        value_grad.reshape(tokens, -1),
    ]
    return jnp.concatenate(joined, axis=1).astype(jnp.bfloat16)


def head_groups(matrix, parts):
    rows = matrix.shape[0]
    groups = HEADS // min(HEADS, 4)
    shaped = matrix.reshape(rows, parts, groups, HEADS // groups, HEAD_DIM)
    return jnp.transpose(shaped, (1, 2, 0, 3, 4))


def from_groups(stacked):
    rows = stacked.shape[1]
    return jnp.transpose(stacked, (1, 0, 2, 3)).reshape(rows, -1)


def cross_scores(queries, keys, mask):
    raw = jnp.einsum(
        "qhe,khe->hqk", queries, keys, preferred_element_type=jnp.float32
    ) * HEAD_DIM ** (-0.5)
    return jnp.where(mask[None], raw, neg_fill)


def cross_forward(cross_q, cross_pairs, mask):
    queries = head_groups(cross_q, 1)[0]
    pairs = head_groups(cross_pairs, 2)

    def one_group(item):
        group_q, group_k, group_v = item
        probs, summary = softmax_rows(cross_scores(group_q, group_k, mask))
        context = jnp.einsum(
            "hqk,khe->qhe", probs.astype(jnp.bfloat16), group_v, preferred_element_type=jnp.float32
        )
        return (context.astype(jnp.bfloat16), summary)

    context, summary = lax.map(one_group, (queries, pairs[0], pairs[1]))
    return (from_groups(context), summary)


def cross_backward(cross_q, cross_pairs, context_grad, summary, mask):
    queries = head_groups(cross_q, 1)[0]
    pairs = head_groups(cross_pairs, 2)
    grads = head_groups(context_grad, 1)[0]
    scale = HEAD_DIM ** (-0.5)

    def one_group(item):
        group_q, group_k, group_v, grad_heads, group_summary = item
        probs = jnp.exp(cross_scores(group_q, group_k, mask) - group_summary)
        value_grad = jnp.einsum(
            "hqk,qhe->khe",
            probs.astype(jnp.bfloat16),
            grad_heads,
            preferred_element_type=jnp.float32,
        )
        prob_grad = jnp.einsum(
            "qhe,khe->hqk", grad_heads, group_v, preferred_element_type=jnp.float32
        )
        score_grad = (
            probs * (prob_grad - jnp.sum(probs * prob_grad, axis=-1, keepdims=True))
        ).astype(jnp.bfloat16)
        query_grad = (
            jnp.einsum("hqk,khe->qhe", score_grad, group_k, preferred_element_type=jnp.float32)
            * scale
        )
        key_grad = (
            jnp.einsum("hqk,qhe->khe", score_grad, group_q, preferred_element_type=jnp.float32)
            * scale
        )
        return (
            query_grad.astype(jnp.bfloat16),
            key_grad.astype(jnp.bfloat16),
            value_grad.astype(jnp.bfloat16),
        )

    query_grad, key_grad, value_grad = lax.map(
        one_group, (queries, pairs[0], pairs[1], grads, summary)
    )
    return (
        from_groups(query_grad),
        jnp.concatenate([from_groups(key_grad), from_groups(value_grad)], axis=1),
    )


def attention_back(saved, weights, second_total, third_norm):
    (
        target_in,
        memory,
        qkv,
        self_context,
        self_summary,
        self_mask,
        first_low,
        first_unit,
        first_inverse,
        cross_q,
        cross_pairs,
        cross_context,
        cross_summary,
        cross_mask,
        second_unit,
        second_inverse,
    ) = saved
    w_qkv, w_self, w_query, w_pairs, w_cross, gains, biases = weights
    width = target_in.shape[1]
    second_grad, scale_two, shift_two = normalize_back(
        second_total, second_unit, second_inverse, gains[1]
    )
    cross_branch = second_grad.astype(jnp.bfloat16)
    cross_out_grad = inner_rows(cross_context, cross_branch)
    context_grad = inner_cols(cross_branch, w_cross).astype(jnp.bfloat16)
    query_delta, pair_delta = cross_backward(
        cross_q, cross_pairs, context_grad, cross_summary, cross_mask
    )
    cross_query_grad = inner_rows(first_low, query_delta)
    cross_kv_grad = inner_rows(memory, pair_delta)
    memory_grad = inner_cols(pair_delta, w_pairs)
    first_total = second_grad + inner_cols(query_delta, w_query)
    first_grad, scale_one, shift_one = normalize_back(
        first_total, first_unit, first_inverse, gains[0]
    )
    self_branch = first_grad.astype(jnp.bfloat16)
    self_out_grad = inner_rows(self_context, self_branch)
    self_context_grad = inner_cols(self_branch, w_self).astype(jnp.bfloat16)
    qkv_delta = self_backward(qkv, self_context_grad, self_summary, self_mask)
    self_qkv_grad = inner_rows(target_in, qkv_delta)
    target_grad = first_grad + inner_cols(qkv_delta, w_qkv)
    scale_three, shift_three, out_bias = third_norm
    norm_grad = jnp.stack([scale_one, scale_two, scale_three])
    bias_grad = jnp.stack(
        [
            column_sums(qkv_delta[:, :width]),
            column_sums(qkv_delta[:, 2 * width :]),
            column_sums(self_branch),
            column_sums(query_delta),
            column_sums(pair_delta[:, width:]),
            column_sums(cross_branch),
            out_bias,
            shift_one,
            shift_two,
            shift_three,
        ]
    )
    return (
        target_grad,
        memory_grad,
        (
            self_qkv_grad,
            self_out_grad,
            cross_query_grad,
            cross_kv_grad,
            cross_out_grad,
            norm_grad,
            bias_grad,
        ),
    )


def body(
    target_in,
    memory,
    block_rows,
    pad_rows,
    seq_lengths,
    self_qkv,
    self_out,
    cross_query,
    cross_kv,
    cross_out,
    ffn_in,
    ffn_out,
    norm_scale,
    small_bias,
    ffn_bias,
    cotangent,
):
    attn_full = (
        lax.all_gather(self_qkv, ("wide", "narrow"), axis=0, tiled=True),
        lax.all_gather(self_out, ("wide", "narrow"), axis=0, tiled=True),
        lax.all_gather(cross_query, ("wide", "narrow"), axis=0, tiled=True),
        lax.all_gather(cross_kv, ("wide", "narrow"), axis=0, tiled=True),
        lax.all_gather(cross_out, ("wide", "narrow"), axis=0, tiled=True),
        lax.all_gather(norm_scale, ("wide", "narrow"), axis=1, tiled=True),
        lax.all_gather(small_bias, ("wide", "narrow"), axis=1, tiled=True),
    )
    ffn_full = (
        lax.all_gather(ffn_in, ("wide", "narrow"), axis=0, tiled=True),
        lax.all_gather(ffn_out, ("wide", "narrow"), axis=0, tiled=True),
        lax.all_gather(ffn_bias, ("wide", "narrow"), axis=0, tiled=True),
    )
    self_mask, cross_mask = build_masks(
        block_rows[0], pad_rows[0], seq_lengths[0], SEQ_LEN, memory.shape[0]
    )
    width = target_in.shape[1]
    zeros = jnp.zeros((width,), jnp.float32)
    w_qkv, w_self, w_query, w_pairs, w_cross, gains, biases = attn_full
    w_in, w_out, in_bias = ffn_full
    gains = gains.astype(jnp.float32)
    biases = biases.astype(jnp.float32)
    in_bias = in_bias.astype(jnp.float32)
    qkv = (matmul(target_in, w_qkv) + jnp.concatenate([biases[0], zeros, biases[1]])).astype(
        jnp.bfloat16
    )
    self_context, self_summary = self_forward(qkv, self_mask)
    first, first_unit, first_inverse = normalize(
        target_in.astype(jnp.float32) + matmul(self_context, w_self) + biases[2],
        gains[0],
        biases[7],
    )
    first_low = first.astype(jnp.bfloat16)
    cross_q = (matmul(first_low, w_query) + biases[3]).astype(jnp.bfloat16)
    cross_pairs = (matmul(memory, w_pairs) + jnp.concatenate([zeros, biases[4]])).astype(
        jnp.bfloat16
    )
    cross_context, cross_summary = cross_forward(cross_q, cross_pairs, cross_mask)
    second, second_unit, second_inverse = normalize(
        first + matmul(cross_context, w_cross) + biases[5], gains[1], biases[8]
    )
    second_low = second.astype(jnp.bfloat16)
    hidden = exact_gelu(matmul(second_low, w_in) + in_bias).astype(jnp.bfloat16)
    third, third_unit, third_inverse = normalize(
        second + matmul(hidden, w_out) + biases[6], gains[2], biases[9]
    )
    block_out = third.astype(jnp.bfloat16)
    back_attn = (
        lax.all_gather(self_qkv, ("wide", "narrow"), axis=0, tiled=True),
        lax.all_gather(self_out, ("wide", "narrow"), axis=0, tiled=True),
        lax.all_gather(cross_query, ("wide", "narrow"), axis=0, tiled=True),
        lax.all_gather(cross_kv, ("wide", "narrow"), axis=0, tiled=True),
        lax.all_gather(cross_out, ("wide", "narrow"), axis=0, tiled=True),
        lax.all_gather(norm_scale, ("wide", "narrow"), axis=1, tiled=True),
        lax.all_gather(small_bias, ("wide", "narrow"), axis=1, tiled=True),
    )
    back_ffn = (
        lax.all_gather(ffn_in, ("wide", "narrow"), axis=0, tiled=True),
        lax.all_gather(ffn_out, ("wide", "narrow"), axis=0, tiled=True),
        lax.all_gather(ffn_bias, ("wide", "narrow"), axis=0, tiled=True),
    )
    back_weights = back_attn[:5] + (
        back_attn[5].astype(jnp.float32),
        back_attn[6].astype(jnp.float32),
    )
    back_in, back_out, back_bias = back_ffn
    back_gains = back_weights[5]
    third_grad, scale_three, shift_three = normalize_back(
        cotangent.astype(jnp.float32), third_unit, third_inverse, back_gains[2]
    )
    out_grad = third_grad.astype(jnp.bfloat16)
    pre = matmul(second_low, back_in) + back_bias.astype(jnp.float32)
    activation, gelu_back = jax.vjp(exact_gelu, pre)
    hidden_again = activation.astype(jnp.bfloat16)
    ffn_out_grad = inner_rows(hidden_again, out_grad)
    pre_grad = gelu_back(inner_cols(out_grad, back_out))[0].astype(jnp.bfloat16)
    ffn_in_grad = inner_rows(second_low, pre_grad)
    ffn_bias_grad = column_sums(pre_grad)
    second_total = third_grad + inner_cols(pre_grad, back_in)
    third_norm = (scale_three, shift_three, column_sums(out_grad))
    saved = (
        target_in,
        memory,
        qkv,
        self_context,
        self_summary,
        self_mask,
        first_low,
        first_unit,
        first_inverse,
        cross_q,
        cross_pairs,
        cross_context,
        cross_summary,
        cross_mask,
        second_unit,
        second_inverse,
    )
    target_grad, memory_grad, attn_grads = attention_back(
        saved, back_weights, second_total, third_norm
    )
    shards = (
        lax.psum_scatter(attn_grads[0], ("wide", "narrow"), scatter_dimension=0, tiled=True),
        lax.psum_scatter(attn_grads[1], ("wide", "narrow"), scatter_dimension=0, tiled=True),
        lax.psum_scatter(attn_grads[2], ("wide", "narrow"), scatter_dimension=0, tiled=True),
        lax.psum_scatter(attn_grads[3], ("wide", "narrow"), scatter_dimension=0, tiled=True),
        lax.psum_scatter(attn_grads[4], ("wide", "narrow"), scatter_dimension=0, tiled=True),
        lax.psum_scatter(attn_grads[5], ("wide", "narrow"), scatter_dimension=1, tiled=True),
        lax.psum_scatter(attn_grads[6], ("wide", "narrow"), scatter_dimension=1, tiled=True),
        lax.psum_scatter(ffn_in_grad, ("wide", "narrow"), scatter_dimension=0, tiled=True),
        lax.psum_scatter(ffn_out_grad, ("wide", "narrow"), scatter_dimension=0, tiled=True),
        lax.psum_scatter(ffn_bias_grad, ("wide", "narrow"), scatter_dimension=0, tiled=True),
    )
    return (
        block_out,
        target_grad,
        memory_grad,
        shards[0],
        shards[1],
        shards[2],
        shards[3],
        shards[4],
        shards[7],
        shards[8],
        shards[5],
        shards[6],
        shards[9],
    )


def solution(mesh):
    in_specs = (
        P(("wide", "narrow"), None),
        P(("wide", "narrow"), None),
        P(("wide", "narrow"), None),
        P(("wide", "narrow"), None),
        P(("wide", "narrow"), None),
        P(("wide", "narrow"), None),
        P(("wide", "narrow"), None),
        P(("wide", "narrow"), None),
        P(("wide", "narrow"), None),
        P(("wide", "narrow"), None),
        P(("wide", "narrow"), None),
        P(("wide", "narrow"), None),
        P(None, ("wide", "narrow")),
        P(None, ("wide", "narrow")),
        P(("wide", "narrow")),
        P(("wide", "narrow"), None),
    )
    out_specs = (
        P(("wide", "narrow"), None),
        P(("wide", "narrow"), None),
        P(("wide", "narrow"), None),
        P(("wide", "narrow"), None),
        P(("wide", "narrow"), None),
        P(("wide", "narrow"), None),
        P(("wide", "narrow"), None),
        P(("wide", "narrow"), None),
        P(("wide", "narrow"), None),
        P(("wide", "narrow"), None),
        P(None, ("wide", "narrow")),
        P(None, ("wide", "narrow")),
        P(("wide", "narrow")),
    )
    return jax.shard_map(body, mesh=mesh, in_specs=in_specs, out_specs=out_specs, check_vma=False)
```

profile of v0, /device:TPU:0, one launch (start us, length us, event | category | flops | bytes accessed | tf_op | source)
XLA Modules:
  0.0 1966.8 jit_solution(15004765118023975650)
XLA Ops:
  12.0 43.8 %all-gather = bf16[32,32,10]{1,2,0:T(8,128)(2,1)S(1)} all-gather(bf16[1,32,10]{1,2,0:T(8,128)(2,1)} %bitcast.358), channel_id=1, replica_groups=mesh['wide'=8,'narrow'=4] {'wide','narrow'}, dimensions={0}, use_global_device_ids=true | all-gather | bytes 21120 | tf_op jit(solution)/shard_map/all_gather | solution.py:308
  57.4 37.0 %all-gather.1 = bf16[32,32,3]{1,2,0:T(4,128)(2,1)S(1)} all-gather(bf16[1,32,3]{1,2,0:T(4,128)(2,1)} %bitcast.365), channel_id=1, replica_groups=mesh['wide'=8,'narrow'=4] {'wide','narrow'}, dimensions={0}, use_global_device_ids=true | all-gather | bytes 6336 | tf_op jit(solution)/shard_map/all_gather | solution.py:307
  95.9 37.9 %all-gather.2 = bf16[32,1,128]{2,1,0:T(2,128)(2,1)S(1)} all-gather(bf16[1,1,128]{2,1,0:T(2,128)(2,1)} %bitcast.366), channel_id=1, replica_groups=mesh['wide'=8,'narrow'=4] {'wide','narrow'}, dimensions={0}, use_global_device_ids=true | all-gather | bytes 8448 | tf_op jit(solution)/shard_map/all_gather | solution.py:313
  134.8 8.2 add_convert_fusion
  143.1 6.4 copy.95
  149.5 5.0 slice_bitcast_fusion
  154.5 6.7 add_convert_fusion.2
  161.1 6.7 reshape.302
  167.8 4.9 fusion.132
  185.3 19.4 all-gather.13.cloned.1.call-done
  209.0 53.7 %all-gather.17.cloned.1.call-done = bf16[1024,1024]{1,0:T(8,128)(2,1)} async-done(((bf16[32,1024]{1,0:T(8,128)(2,1)}), bf16[1024,1024]{1,0:T(8,128)(2,1)}) %all-gather.17.cloned.1.call-update) | async-done | bytes 2097168 | tf_op jit(solution)/shard_map/all_gather | solution.py:304
  262.7 4.0 add_convert_fusion.4
  269.2 32.9 %while.28 = (s32[]{:T(128)}, bf16[4,384,4,64]{1,3,2,0:T(8,128)(2,1)}, f32[4,4,384,1]{2,1,3,0:T(4,128)S(1)}, bf16[4,1024,4,64]{1,3,2,0:T(8,128)(2,1)}, bf16[4,384...) while((s32[]{:T(128)}, ...), condition=%wide.region_8.9_spmd.clone, body=%wide.region_5.8_spmd.clone.sunk | while | flops 421624320 | bytes 21943384 | solution.py:161
  273.8 3.9 fusion.192
  281.9 3.9 fusion.192
  290.1 3.9 fusion.192
  298.2 3.9 fusion.192
  302.0 18.6 all-gather.19.cloned.1.call-done
  326.3 73.5 %all-gather.21.cloned.1.call-done = bf16[1024,4096]{1,0:T(8,128)(2,1)} async-done(((bf16[32,4096]{1,0:T(8,128)(2,1)}), bf16[1024,4096]{1,0:T(8,128)(2,1)}) %all-gather.21.cloned.1.call-update) | async-done | bytes 8388624 | tf_op jit(solution)/shard_map/all_gather | solution.py:311
  399.9 20.9 %multiply_convert_fusion.1 = (bf16[384,4096]{1,0:T(8,128)(2,1)}, f32[384,4096]{1,0:T(8,128)}, f32[384,4096]{1,0:T(8,128)}) fusion(f32[4096]{0:T(1024)S(1)} %bitcast.353, bf16[1024,4096]{1,0:T(8,128)(2,1)} %all-gather.21.cloned.1.call-done, f32[384,1024]{1,0:T(8,128)} %copy-done.5, f32[1024]{0:T(1024)S(1)} %bitcast.327, f32[1024]{0:T(1024)S(1)} %bitcast.322, ...), kind=kOutput, calls=%fused_computation.70 | convolution fusion | flops 3327000576 | bytes 25717760 | tf_op jit(solution)/shard_map/dot_general | solution.py:16
  420.8 58.1 %all-gather.23.cloned.1.call-done = bf16[4096,1024]{1,0:T(8,128)(2,1)} async-done(((bf16[128,1024]{1,0:T(8,128)(2,1)}), bf16[4096,1024]{1,0:T(8,128)(2,1)}) %all-gather.23.cloned.1.call-update) | async-done | bytes 8388624 | tf_op jit(solution)/shard_map/all_gather | solution.py:312
  478.9 8.3 fusion.138
  489.9 14.2 convert_reduce_fusion
  504.2 4.0 multiply_reduce_fusion.2
  515.2 59.1 %while.29 = (s32[]{:T(128)}, bf16[4,384,4,64]{1,3,2,0:T(8,128)(2,1)}, bf16[4,1024,4,64]{1,3,2,0:T(8,128)(2,1)}, bf16[4,1024,4,64]{1,3,2,0:T(8,128)(2,1)}, bf16[4...) while((s32[]{:T(128)}, ...), condition=%wide.region_19.20_spmd.clone, body=%wide.region_17.19_spmd.clone.sunk | while | flops 1031207424 | bytes 55560332 | solution.py:200
  517.5 3.5 multiply_reduce_fusion.12
  546.9 3.5 multiply_reduce_fusion.12
  574.4 4.4 multiply_reduce_fusion.3
  600.1 5.1 fusion.127
  605.6 5.0 fusion.95
  610.7 4.9 fusion.115
  615.7 9.1 convolution_bitcast_fusion.1
  624.8 9.2 copy.115
  639.6 6.4 convolution_bitcast_fusion
  646.0 12.6 copy.113
  659.3 12.8 fusion.124
  672.1 12.7 fusion.118
  685.5 39.6 %all-reduce.1 = f32[4096]{0:T(1024)S(1)} all-reduce(f32[4096]{0:T(1024)S(1)} %copy-done.38), channel_id=11, replica_groups=mesh['wide'=8,'narrow'=4] {'wide','narrow'}, use_global_device_ids=true, to_apply=%region_46.47.clone | all-reduce | flops 4096 | bytes 32768
  725.7 7.8 convolution_add_fusion.3
  733.5 7.7 fusion.70
  742.6 119.8 %reduce-scatter.34.cloned.1.call-done = f32[32,10]{1,0:T(8,128)} async-done(((f32[1024,10]{1,0:T(8,128)}), f32[32,10]{1,0:T(8,128)}) %reduce-scatter.34.cloned.1.call-update) | async-done | bytes 1296
  863.8 138.4 %reduce-scatter.20.cloned.1.call-done = f32[32,1024]{1,0:T(8,128)} async-done(((f32[1024,1024]{1,0:T(8,128)}), f32[32,1024]{1,0:T(8,128)}) %reduce-scatter.20.cloned.1.call-update) | async-done | bytes 131088 | tf_op jit(solution)/shard_map/reduce_scatter | solution.py:406
  1002.3 140.1 %reduce-scatter.18.cloned.1.call-done = f32[32,1024]{1,0:T(8,128)} async-done(((f32[1024,1024]{1,0:T(8,128)}), f32[32,1024]{1,0:T(8,128)}) %reduce-scatter.18.cloned.1.call-update) | async-done | bytes 131088 | tf_op jit(solution)/shard_map/reduce_scatter | solution.py:405
  1142.3 139.8 %reduce-scatter.22.cloned.1.call-done = f32[32,1024]{1,0:T(8,128)} async-done(((f32[1024,1024]{1,0:T(8,128)}), f32[32,1024]{1,0:T(8,128)}) %reduce-scatter.22.cloned.1.call-update) | async-done | bytes 131088 | tf_op jit(solution)/shard_map/reduce_scatter | solution.py:408
  1282.2 147.7 %reduce-scatter.30.cloned.1.call-done = f32[32,2048]{1,0:T(8,128)} async-done(((f32[1024,2048]{1,0:T(8,128)}), f32[32,2048]{1,0:T(8,128)}) %reduce-scatter.30.cloned.1.call-update) | async-done | bytes 262160
  1429.9 157.8 %reduce-scatter.28.cloned.1.call-done = f32[32,3072]{1,0:T(8,128)} async-done(((f32[1024,3072]{1,0:T(8,128)}), f32[32,3072]{1,0:T(8,128)}) %reduce-scatter.28.cloned.1.call-update) | async-done | bytes 393232
  1587.6 185.0 %reduce-scatter.24.cloned.1.call-done = f32[32,4096]{1,0:T(8,128)} async-done(((f32[1024,4096]{1,0:T(8,128)}), f32[32,4096]{1,0:T(8,128)}) %reduce-scatter.24.cloned.1.call-update) | async-done | bytes 524304 | tf_op jit(solution)/shard_map/reduce_scatter | solution.py:411
  1772.6 187.4 %reduce-scatter.26.cloned.1.call-done = f32[128,1024]{1,0:T(8,128)} async-done(((f32[4096,1024]{1,0:T(8,128)}), f32[128,1024]{1,0:T(8,128)}) %reduce-scatter.26.cloned.1.call-update) | async-done | bytes 524304 | tf_op jit(solution)/shard_map/reduce_scatter | solution.py:412
  (255 shorter events, 144.0 us)
Async XLA Ops:
  7.2 127.7 %copy-start = (bf16[1024,1024]{1,0:T(8,128)(2,1)S(1)}, bf16[1024,1024]{1,0:T(8,128)(2,1)}, u32[]{:S(2)}) copy-start(bf16[1024,1024]{1,0:T(8,128)(2,1)} %param.21) | copy-start | bytes 6291460
  7.2 127.6 %all-gather.15.cloned.1.call-start = ((), (), s32[]{:S(2)}) async-start(), calls=%async_computation.11 | async-start | bytes 4325376 | tf_op jit(solution)/shard_map/all_gather | solution.py:305
  7.9 146.5 %all-gather.11.cloned.1.call-start = ((), (), s32[]{:S(2)}) async-start(), calls=%async_computation.9 | async-start | bytes 6488064 | tf_op jit(solution)/shard_map/all_gather | solution.py:302
  8.7 196.0 %all-gather.13.cloned.1.call-start = ((), (), s32[]{:S(2)}) async-start(), calls=%async_computation.10 | async-start | bytes 2162688 | tf_op jit(solution)/shard_map/all_gather | solution.py:303
  9.4 253.3 %all-gather.17.cloned.1.call-start = ((), (), s32[]{:S(2)}) async-start(), calls=%async_computation.12 | async-start | bytes 2162688 | tf_op jit(solution)/shard_map/all_gather | solution.py:304
  10.0 310.7 %all-gather.19.cloned.1.call-start = ((), (), s32[]{:S(2)}) async-start(), calls=%async_computation.13 | async-start | bytes 2162688 | tf_op jit(solution)/shard_map/all_gather | solution.py:306
  10.6 389.3 %all-gather.21.cloned.1.call-start = ((), (), s32[]{:S(2)}) async-start(), calls=%async_computation.14 | async-start | bytes 8650752 | tf_op jit(solution)/shard_map/all_gather | solution.py:311
  11.2 467.7 %all-gather.23.cloned.1.call-start = ((), (), s32[]{:S(2)}) async-start(), calls=%async_computation.15 | async-start | bytes 8650752 | tf_op jit(solution)/shard_map/all_gather | solution.py:312
  11.9 729.4 %reduce-scatter.32.cloned.1.call-start = ((), (), s32[]{:S(2)}) async-start(), calls=%async_computation.23 | async-start | bytes 540672
  56.6 264.1 %copy-start.31 = (f32[1,1024]{1,0:T(1,128)}, f32[1,1024]{1,0:T(1,128)S(1)}, u32[]{:S(2)}) copy-start(f32[1,1024]{1,0:T(1,128)S(1)} %get-tuple-element.272) | copy-start | bytes 12292
  56.6 422.3 %copy-start.27 = (f32[1,1024]{1,0:T(1,128)}, f32[1,1024]{1,0:T(1,128)S(1)}, u32[]{:S(2)}) copy-start(f32[1,1024]{1,0:T(1,128)S(1)} %get-tuple-element.268) | copy-start | bytes 12292
  95.1 225.6 %copy-start.29 = (f32[1,1024]{1,0:T(1,128)}, f32[1,1024]{1,0:T(1,128)S(1)}, u32[]{:S(2)}) copy-start(f32[1,1024]{1,0:T(1,128)S(1)} %get-tuple-element.278) | copy-start | bytes 12292
  149.5 5.0 copy-start.22
  174.7 5.6 copy-start.10
  182.2 2.4 copy-start.1
  185.3 22.3 %copy-start.12 = (bf16[3,128,16,64]{1,0,3,2:T(4,128)(2,1)}, bf16[3,128,16,64]{1,0,3,2:T(4,128)(2,1)S(1)}, u32[]{:S(2)}) copy-start(bf16[3,128,16,64]{1,0,3,2:T(4,128)(2,1)S(1)} %copy.93) | copy-start | bytes 2359300
  207.6 113.1 %copy-start.33 = (f32[384]{0:T(512)}, f32[384]{0:T(512)S(1)}, u32[]{:S(2)}) copy-start(f32[384]{0:T(512)S(1)} %broadcast_multiply_fusion.8) | copy-start | bytes 4612
  209.0 111.7 %copy-start.35 = (f32[384]{0:T(512)}, f32[384]{0:T(512)S(1)}, u32[]{:S(2)}) copy-start(f32[384]{0:T(512)S(1)} %add_rsqrt_fusion.2) | copy-start | bytes 4612
  478.9 8.7 copy-start.19
  478.9 8.7 copy-start.37
  488.4 15.8 slice-start
  489.9 14.2 copy-start.13
  489.9 14.2 copy-start.6
  489.9 14.2 slice-start.1
  504.1 4.0 copy-start.18
  515.2 59.1 %copy-start.30 = (f32[1,1024]{1,0:T(1,128)S(1)}, f32[1,1024]{1,0:T(1,128)}, u32[]{:S(2)}) copy-start(f32[1,1024]{1,0:T(1,128)} %copy-done.29) | copy-start | bytes 12292
  515.2 59.1 %copy-start.34 = (f32[384]{0:T(512)S(1)}, f32[384]{0:T(512)}, u32[]{:S(2)}) copy-start(f32[384]{0:T(512)} %copy-done.33) | copy-start | bytes 4612
  515.2 59.1 %copy-start.36 = (f32[384]{0:T(512)S(1)}, f32[384]{0:T(512)}, u32[]{:S(2)}) copy-start(f32[384]{0:T(512)} %copy-done.35) | copy-start | bytes 4612
  515.2 2.3 copy-start.17
  530.0 2.3 copy-start.17
  544.7 2.3 copy-start.17
  559.4 2.3 copy-start.17
  574.3 4.4 copy-start.4
  581.6 3.9 copy-start.26
  585.5 3.3 copy-start.2
  585.5 3.3 copy-start.21
  594.2 5.8 copy-start.32
  597.2 265.2 %reduce-scatter.34.cloned.1.call-start = ((), (), s32[]{:S(2)}) async-start(), calls=%async_computation.24 | async-start | bytes 540672
  600.0 402.3 %reduce-scatter.20.cloned.1.call-start = ((), (), s32[]{:S(2)}) async-start(), calls=%async_computation.17 | async-start | bytes 4325376 | tf_op jit(solution)/shard_map/reduce_scatter | solution.py:406
  605.2 537.2 %reduce-scatter.18.cloned.1.call-start = ((), (), s32[]{:S(2)}) async-start(), calls=%async_computation.16 | async-start | bytes 4325376 | tf_op jit(solution)/shard_map/reduce_scatter | solution.py:405
  610.7 671.5 %reduce-scatter.22.cloned.1.call-start = ((), (), s32[]{:S(2)}) async-start(), calls=%async_computation.18 | async-start | bytes 4325376 | tf_op jit(solution)/shard_map/reduce_scatter | solution.py:408
  615.7 814.2 %reduce-scatter.30.cloned.1.call-start = ((), (), s32[]{:S(2)}) async-start(), calls=%async_computation.22 | async-start | bytes 8650752
  634.0 953.7 %reduce-scatter.28.cloned.1.call-start = ((), (), s32[]{:S(2)}) async-start(), calls=%async_computation.21 | async-start | bytes 12976128
  634.0 3.6 copy-start.9
  658.6 1114.0 %reduce-scatter.24.cloned.1.call-start = ((), (), s32[]{:S(2)}) async-start(), calls=%async_computation.19 | async-start | bytes 17301504 | tf_op jit(solution)/shard_map/reduce_scatter | solution.py:411
  672.1 1287.9 %reduce-scatter.26.cloned.1.call-start = ((), (), s32[]{:S(2)}) async-start(), calls=%async_computation.20 | async-start | bytes 17301504 | tf_op jit(solution)/shard_map/reduce_scatter | solution.py:412
  725.7 7.9 copy-start.40
  725.7 7.9 copy-start.41
  (15 other events, 19.4 us)
Sparse Core Ops, SparseCore 0:
  10.9 64.7 all-gather.14
  78.6 68.2 all-gather.10
  149.8 54.8 all-gather.12
  207.4 55.2 all-gather.16
  265.4 55.2 all-gather.18
  323.4 76.4 all-gather.20
  402.7 76.1 all-gather.22
  597.4 132.5 reduce-scatter.31
  732.2 130.1 reduce-scatter.33
  865.1 137.0 reduce-scatter.19
  1005.1 137.1 reduce-scatter.17
  1145.0 137.0 reduce-scatter.21
  1285.0 144.8 reduce-scatter.29
  1436.3 151.2 reduce-scatter.27
  1590.5 182.0 reduce-scatter.23
  1775.4 184.5 reduce-scatter.25
where the time goes:
time: 1980 us; the launch traced here: 1970 us
  waiting for transfers between devices  1440 us (73%)
  matrix products  237 us (12%)
  blocking collectives  158 us (8%)
  local copies, waits for them, and re-layouts  82.9 us (4%)
  other arithmetic  27.4 us (1%)
    unnamed x20, waiting for transfers between devices  430 us
    reduce_scatter x1, waiting for transfers between devices, body(): lax.psum_scatter(ffn_out_grad, ('wide', 'narrow'), scatter_dimension=0, t...  187 us
    reduce_scatter x1, waiting for transfers between devices, body(): lax.psum_scatter(ffn_in_grad, ('wide', 'narrow'), scatter_dimension=0, ti...  185 us
    reduce_scatter x1, waiting for transfers between devices, body(): lax.psum_scatter(attn_grads[1], ('wide', 'narrow'), scatter_dimension=0,...  140 us
    reduce_scatter x1, waiting for transfers between devices, body(): lax.psum_scatter(attn_grads[4], ('wide', 'narrow'), scatter_dimension=0,...  140 us
    reduce_scatter x1, waiting for transfers between devices, body(): lax.psum_scatter(attn_grads[2], ('wide', 'narrow'), scatter_dimension=0,...  138 us
    all_gather x1, waiting for transfers between devices, body(): lax.all_gather(ffn_in, ('wide', 'narrow'), axis=0, tiled=True)  73.5 us
    all_gather x1, waiting for transfers between devices, body(): lax.all_gather(ffn_out, ('wide', 'narrow'), axis=0, tiled=True)  58.1 us
  transfers between devices with their start and end apart: 16, of which 13 were waited for; matrix products, arithmetic and copies ran while one was open for 11% of the time, Pallas kernels for 0%

commit v1 on v0

--- a/solution.py
+++ b/solution.py
@@ -37,7 +37,9 @@
 
 
 def build_masks(block_rows, pad_rows, seq_lengths, seq_len, mem_rows):
-    starts = jnp.cumsum(block_rows) - block_rows
+    count = block_rows.shape[0]
+    before = jnp.arange(count)[None, :] < jnp.arange(count)[:, None]
+    starts = jnp.sum(jnp.where(before, block_rows[None, :], 0), axis=1)
     valid = jnp.maximum(block_rows - pad_rows, (block_rows + 1) // 2)
     places = jnp.arange(mem_rows, dtype=jnp.int32)
     memory_ok = (places[None, :] >= starts[:, None]) & (places[None, :] < (starts + valid)[:, None])
@@ -280,6 +282,50 @@
     )
 
 
+def exchange(values, bit):
+    count = lax.axis_size(("wide", "narrow"))
+    return lax.ppermute(
+        values, ("wide", "narrow"), [(i, i ^ (1 << bit)) for i in range(count)]
+    )
+
+
+class Scatter:
+    def __init__(self, values, bits):
+        self.values = values
+        self.bits = bits
+
+    def pick(self, bit, other):
+        me = lax.axis_index(("wide", "narrow"))
+        mine = (me >> bit) & 1
+        axis = self.bits.index(bit)
+        return lax.dynamic_index_in_dim(
+            self.values, 1 - mine if other else mine, axis, keepdims=False
+        )
+
+    def step(self, bit):
+        arrived = exchange(self.pick(bit, True), bit)
+        kept = self.pick(bit, False)
+        total = kept.astype(jnp.float32) + arrived.astype(jnp.float32)
+        return Scatter(total.astype(jnp.bfloat16), [b for b in self.bits if b != bit])
+
+
+def scatter_sum(parts):
+    count = lax.axis_size(("wide", "narrow"))
+    bits = list(range(count.bit_length() - 1))[::-1]
+    split = (2,) * len(bits)
+    joined = jnp.concatenate([p.astype(jnp.bfloat16) for p in parts], axis=-1)
+    first = Scatter(joined.reshape(split + joined.shape[1:]), bits).step(0)
+    half = joined.shape[-1] // 256 * 128
+    left = Scatter(first.values[..., :half], first.bits)
+    right = Scatter(first.values[..., half:], first.bits)
+    left = left.step(2).step(1)
+    right = right.step(1).step(2)
+    rest = Scatter(jnp.concatenate([left.values, right.values], axis=-1), left.bits)
+    for bit in rest.bits[::-1]:
+        rest = rest.step(bit)
+    return rest.values.astype(jnp.float32)
+
+
 def body(
     target_in,
     memory,
@@ -298,30 +344,36 @@
     ffn_bias,
     cotangent,
 ):
+    axes = ("wide", "narrow")
+    width = target_in.shape[1]
+    owned = self_qkv.shape[0]
+    pack = jnp.concatenate([norm_scale.T, small_bias.T, ffn_bias.reshape(owned, -1)], axis=1)
+    small_cols = pack.shape[1]
+    pack = jnp.pad(pack, ((0, 0), (0, -small_cols % 128)))
+    attn = lax.all_gather(
+        jnp.concatenate([self_qkv, self_out, cross_query, cross_kv, cross_out, pack], axis=1),
+        axes,
+        axis=0,
+        tiled=True,
+    )
     attn_full = (
-        lax.all_gather(self_qkv, ("wide", "narrow"), axis=0, tiled=True),
-        lax.all_gather(self_out, ("wide", "narrow"), axis=0, tiled=True),
-        lax.all_gather(cross_query, ("wide", "narrow"), axis=0, tiled=True),
-        lax.all_gather(cross_kv, ("wide", "narrow"), axis=0, tiled=True),
-        lax.all_gather(cross_out, ("wide", "narrow"), axis=0, tiled=True),
-        lax.all_gather(norm_scale, ("wide", "narrow"), axis=1, tiled=True),
-        lax.all_gather(small_bias, ("wide", "narrow"), axis=1, tiled=True),
-    )
-    ffn_full = (
-        lax.all_gather(ffn_in, ("wide", "narrow"), axis=0, tiled=True),
-        lax.all_gather(ffn_out, ("wide", "narrow"), axis=0, tiled=True),
-        lax.all_gather(ffn_bias, ("wide", "narrow"), axis=0, tiled=True),
-    )
+        attn[:, : 3 * width],
+        attn[:, 3 * width : 4 * width],
+        attn[:, 4 * width : 5 * width],
+        attn[:, 5 * width : 7 * width],
+        attn[:, 7 * width : 8 * width],
+    )
+    small = attn[:, 8 * width : 8 * width + small_cols].astype(jnp.float32)
+    gains = small[:, :3].T
+    biases = small[:, 3:13].T
+    in_bias = small[:, 13:].reshape(-1)
+    w_in = lax.all_gather(ffn_in, axes, axis=0, tiled=True)
+    w_out = lax.all_gather(ffn_out, axes, axis=0, tiled=True)
     self_mask, cross_mask = build_masks(
         block_rows[0], pad_rows[0], seq_lengths[0], SEQ_LEN, memory.shape[0]
     )
-    width = target_in.shape[1]
     zeros = jnp.zeros((width,), jnp.float32)
-    w_qkv, w_self, w_query, w_pairs, w_cross, gains, biases = attn_full
-    w_in, w_out, in_bias = ffn_full
-    gains = gains.astype(jnp.float32)
-    biases = biases.astype(jnp.float32)
-    in_bias = in_bias.astype(jnp.float32)
+    w_qkv, w_self, w_query, w_pairs, w_cross = attn_full
     qkv = (matmul(target_in, w_qkv) + jnp.concatenate([biases[0], zeros, biases[1]])).astype(
         jnp.bfloat16
     )
@@ -341,43 +393,22 @@
         first + matmul(cross_context, w_cross) + biases[5], gains[1], biases[8]
     )
     second_low = second.astype(jnp.bfloat16)
-    hidden = exact_gelu(matmul(second_low, w_in) + in_bias).astype(jnp.bfloat16)
+    activation, gelu_back = jax.vjp(exact_gelu, matmul(second_low, w_in) + in_bias)
+    hidden = activation.astype(jnp.bfloat16)
     third, third_unit, third_inverse = normalize(
         second + matmul(hidden, w_out) + biases[6], gains[2], biases[9]
     )
     block_out = third.astype(jnp.bfloat16)
-    back_attn = (
-        lax.all_gather(self_qkv, ("wide", "narrow"), axis=0, tiled=True),
-        lax.all_gather(self_out, ("wide", "narrow"), axis=0, tiled=True),
-        lax.all_gather(cross_query, ("wide", "narrow"), axis=0, tiled=True),
-        lax.all_gather(cross_kv, ("wide", "narrow"), axis=0, tiled=True),
-        lax.all_gather(cross_out, ("wide", "narrow"), axis=0, tiled=True),
-        lax.all_gather(norm_scale, ("wide", "narrow"), axis=1, tiled=True),
-        lax.all_gather(small_bias, ("wide", "narrow"), axis=1, tiled=True),
-    )
-    back_ffn = (
-        lax.all_gather(ffn_in, ("wide", "narrow"), axis=0, tiled=True),
-        lax.all_gather(ffn_out, ("wide", "narrow"), axis=0, tiled=True),
-        lax.all_gather(ffn_bias, ("wide", "narrow"), axis=0, tiled=True),
-    )
-    back_weights = back_attn[:5] + (
-        back_attn[5].astype(jnp.float32),
-        back_attn[6].astype(jnp.float32),
-    )
-    back_in, back_out, back_bias = back_ffn
-    back_gains = back_weights[5]
+    back_weights = attn_full + (gains, biases)
     third_grad, scale_three, shift_three = normalize_back(
-        cotangent.astype(jnp.float32), third_unit, third_inverse, back_gains[2]
+        cotangent.astype(jnp.float32), third_unit, third_inverse, gains[2]
     )
     out_grad = third_grad.astype(jnp.bfloat16)
-    pre = matmul(second_low, back_in) + back_bias.astype(jnp.float32)
-    activation, gelu_back = jax.vjp(exact_gelu, pre)
-    hidden_again = activation.astype(jnp.bfloat16)
-    ffn_out_grad = inner_rows(hidden_again, out_grad)
-    pre_grad = gelu_back(inner_cols(out_grad, back_out))[0].astype(jnp.bfloat16)
+    ffn_out_grad = inner_rows(hidden, out_grad)
+    pre_grad = gelu_back(inner_cols(out_grad, w_out))[0].astype(jnp.bfloat16)
     ffn_in_grad = inner_rows(second_low, pre_grad)
     ffn_bias_grad = column_sums(pre_grad)
-    second_total = third_grad + inner_cols(pre_grad, back_in)
+    second_total = third_grad + inner_cols(pre_grad, w_in)
     third_norm = (scale_three, shift_three, column_sums(out_grad))
     saved = (
         target_in,
@@ -400,32 +431,43 @@
     target_grad, memory_grad, attn_grads = attention_back(
         saved, back_weights, second_total, third_norm
     )
-    shards = (
-        lax.psum_scatter(attn_grads[0], ("wide", "narrow"), scatter_dimension=0, tiled=True),
-        lax.psum_scatter(attn_grads[1], ("wide", "narrow"), scatter_dimension=0, tiled=True),
-        lax.psum_scatter(attn_grads[2], ("wide", "narrow"), scatter_dimension=0, tiled=True),
-        lax.psum_scatter(attn_grads[3], ("wide", "narrow"), scatter_dimension=0, tiled=True),
-        lax.psum_scatter(attn_grads[4], ("wide", "narrow"), scatter_dimension=0, tiled=True),
-        lax.psum_scatter(attn_grads[5], ("wide", "narrow"), scatter_dimension=1, tiled=True),
-        lax.psum_scatter(attn_grads[6], ("wide", "narrow"), scatter_dimension=1, tiled=True),
-        lax.psum_scatter(ffn_in_grad, ("wide", "narrow"), scatter_dimension=0, tiled=True),
-        lax.psum_scatter(ffn_out_grad, ("wide", "narrow"), scatter_dimension=0, tiled=True),
-        lax.psum_scatter(ffn_bias_grad, ("wide", "narrow"), scatter_dimension=0, tiled=True),
-    )
+    (
+        self_qkv_grad,
+        self_out_grad,
+        cross_query_grad,
+        cross_kv_grad,
+        cross_out_grad,
+        norm_grad,
+        bias_grad,
+    ) = attn_grads
+    small_grad = jnp.concatenate(
+        [norm_grad.T, bias_grad.T, ffn_bias_grad.reshape(width, -1)], axis=1
+    )
+    small_grad = jnp.pad(small_grad, ((0, 0), (0, -small_cols % 128)))
+    n = lax.axis_size(axes)
+    ffn_shard = scatter_sum([ffn_in_grad.reshape(n, owned, -1), ffn_out_grad.reshape(n, owned, -1)])
+    cross_shard = scatter_sum(
+        [x.reshape(n, owned, -1) for x in (cross_query_grad, cross_kv_grad, cross_out_grad)]
+    )
+    self_shard = scatter_sum(
+        [x.reshape(n, owned, -1) for x in (self_qkv_grad, self_out_grad, small_grad)]
+    )
+    hidden_cols = ffn_in.shape[1]
+    small_shard = self_shard[:, 4 * width : 4 * width + small_cols]
     return (
         block_out,
         target_grad,
         memory_grad,
-        shards[0],
-        shards[1],
-        shards[2],
-        shards[3],
-        shards[4],
-        shards[7],
-        shards[8],
-        shards[5],
-        shards[6],
-        shards[9],
+        self_shard[:, : 3 * width],
+        self_shard[:, 3 * width : 4 * width],
+        cross_shard[:, :width],
+        cross_shard[:, width : 3 * width],
+        cross_shard[:, 3 * width :],
+        ffn_shard[:, :hidden_cols],
+        ffn_shard[:, hidden_cols:].reshape(ffn_out.shape),
+        small_shard[:, :3].T,
+        small_shard[:, 3:13].T,
+        small_shard[:, 13:].reshape(-1),
     )
 
 

time: 1980 us -> 732 us (0.37)
  waiting for transfers between devices: 1440 us -> 313 us
  blocking collectives: 158 us -> 0 us
  other arithmetic: 27.4 us -> 55.6 us
  starting transfers between devices: 1.22 us -> 27 us
  matrix products: 237 us -> 214 us
    reduce_scatter x5 -> x0, waiting for transfers between devices: 791 us -> none  [the longest x1 187 us: body(): lax.psum_scatter(ffn_out_grad, ('wide', 'narrow'), scatter_dimension=0, t...]
    unnamed x20 -> x3, waiting for transfers between devices: 430 us -> 1.39 us
    ppermute x0 -> x21, waiting for transfers between devices: none -> 149 us  [exchange(): lax.ppermute(values, ('wide', 'narrow'), [(i, i ^ 1 << bit) for i in rang...]
    all_gather x3 -> x0, blocking collectives: 119 us -> none  [the longest x1 43.8 us: body(): lax.all_gather(small_bias, ('wide', 'narrow'), axis=1, tiled=True)]
    all_gather x7 -> x3, waiting for transfers between devices: 223 us -> 163 us  [the longest x1 115 us: body(): lax.all_gather(jnp.concatenate([self_qkv, self_out, cross_query, cross_kv...]
    unnamed x1 -> x0, blocking collectives: 39.6 us -> none
    ppermute x0 -> x21, starting transfers between devices: none -> 26.9 us  [exchange(): lax.ppermute(values, ('wide', 'narrow'), [(i, i ^ 1 << bit) for i in rang...]
    dot_general x7, matrix products: 55.9 us -> 31.8 us  [inner_rows(): lax.dot_general(first, second, (((0,), (0,)), ((), ())), preferred_elemen...]
  transfers between devices with their start and end apart: 16 -> 24, of which waited for: 13 -> 14; matrix products, arithmetic and copies ran while one was open for 11% -> 29% of each run, Pallas kernels for 0% -> 0%
where the time goes in v1:
time: 732 us; the launch traced here: 723 us
  waiting for transfers between devices  313 us (43%)
  matrix products  214 us (29%)
  local copies, waits for them, and re-layouts  97.5 us (13%)
  other arithmetic  55.6 us (8%)
  starting transfers between devices  27 us (4%)
  between operations  15.6 us (2%)
    ppermute x21, waiting for transfers between devices, exchange(): lax.ppermute(values, ('wide', 'narrow'), [(i, i ^ 1 << bit) for i in rang...  149 us
    all_gather x1, waiting for transfers between devices, body(): lax.all_gather(jnp.concatenate([self_qkv, self_out, cross_query, cross_kv...  115 us
    dot_general x7, matrix products, matmul(): return jnp.dot(first, second, preferred_element_type=jnp.float32)  55.2 us
    all_gather x1, waiting for transfers between devices, body(): w_out = lax.all_gather(ffn_out, axes, axis=0, tiled=True)  48.1 us
    dot_general x7, matrix products, inner_cols(): lax.dot_general(first, second, (((1,), (1,)), ((), ())), preferred_elemen...  42.9 us
    dot_general x7, matrix products, inner_rows(): lax.dot_general(first, second, (((0,), (0,)), ((), ())), preferred_elemen...  31.8 us
    unnamed x145, local copies, waits for them, and re-layouts  29.1 us
    ppermute x21, starting transfers between devices, exchange(): lax.ppermute(values, ('wide', 'narrow'), [(i, i ^ 1 << bit) for i in rang...  26.9 us
  transfers between devices with their start and end apart: 24, of which 14 were waited for; matrix products, arithmetic and copies ran while one was open for 29% of the time, Pallas kernels for 0%

profile of v1, /device:TPU:0, one launch (start us, length us, event | category | flops | bytes accessed | tf_op | source)
XLA Modules:
  0.0 723.5 jit_solution(7169742489718911294)
XLA Ops:
  18.2 115.0 %all-gather.4.cloned.1.call-done = bf16[1024,8320]{1,0:T(8,128)(2,1)} async-done(((bf16[32,8320]{1,0:T(8,128)(2,1)}), bf16[1024,8320]{1,0:T(8,128)(2,1)}) %all-gather.4.cloned.1.call-update) | async-done | bytes 17039376 | tf_op jit(solution)/shard_map/all_gather | solution.py:353
  136.7 3.9 slice_reduce_fusion
  140.7 8.2 %fusion.82 = bf16[384,3072]{0,1:T(8,128)(2,1)} fusion(bf16[384,1024]{1,0:T(8,128)(2,1)S(1)} %copy-done.35, bf16[1024,8320]{1,0:T(8,128)(2,1)} %all-gather.4.cloned.1.call-done, f32[3072]{0:T(1024)S(1)} %pad_maximum_fusion.6), kind=kOutput, calls=%fused_computation.114 | convolution fusion | flops 2418278400 | bytes 9449472 | tf_op jit(solution)/shard_map/dot_general | solution.py:16
  148.9 7.2 reshape.327
  166.9 3.6 add_convert_fusion.4
  172.0 7.5 %add_convert_fusion = bf16[2048,1024]{1,0:T(8,128)(2,1)S(1)} fusion(f32[2048]{0:T(1024)S(1)} %concatenate.45, bf16[1024,1024]{1,0:T(8,128)(2,1)S(1)} %copy-done, bf16[1024,8320]{1,0:T(8,128)(2,1)} %all-gather.4.cloned.1.call-done), kind=kOutput, calls=%fused_computation.81 | convolution fusion | flops 4299161600 | bytes 10493952 | tf_op jit(solution)/shard_map/dot_general | solution.py:16
  182.9 32.8 %while.28 = (s32[]{:T(128)}, bf16[4,384,4,64]{1,3,2,0:T(8,128)(2,1)}, f32[4,4,384,1]{2,1,3,0:T(4,128)S(1)}, bf16[4,1024,4,64]{1,3,2,0:T(8,128)(2,1)}, bf16[4,384...) while((s32[]{:T(128)}, ...), condition=%wide.region_8.9_spmd.clone, body=%wide.region_5.8_spmd.clone.sunk | while | flops 421624320 | bytes 21943392 | solution.py:163
  187.4 3.9 fusion.255
  195.5 3.9 fusion.255
  203.7 3.9 fusion.255
  211.8 3.9 fusion.255
  215.7 3.5 fusion.204
  221.3 21.4 %multiply_convert_fusion.1 = (bf16[384,4096]{1,0:T(8,128)(2,1)}, f32[384,4096]{1,0:T(8,128)}, f32[384,4096]{1,0:T(8,128)}) fusion(f32[4096]{0:T(1024)S(1)} %add.410, bf16[1024,4096]{1,0:T(8,128)(2,1)} %all-gather.6.cloned.1.call-done, f32[384,1024]{1,0:T(8,128)} %copy-done.15, f32[1024]{0:T(1024)S(1)} %get-tuple-element.218, ...), kind=kOutput, calls=%fused_computation.86 | convolution fusion | flops 3327000576 | bytes 25717760 | tf_op jit(solution)/shard_map/dot_general | solution.py:16
  242.8 48.1 %all-gather.8.cloned.1.call-done = bf16[4096,1024]{1,0:T(8,128)(2,1)} async-done(((bf16[128,1024]{1,0:T(8,128)(2,1)}), bf16[4096,1024]{1,0:T(8,128)(2,1)}) %all-gather.8.cloned.1.call-update) | async-done | bytes 8388624 | tf_op jit(solution)/shard_map/all_gather | solution.py:371
  290.9 8.3 %fusion.205 = (f32[384]{0:T(512)S(1)}, f32[384,1024]{1,0:T(8,128)S(1)}) fusion(f32[1024]{0:T(1024)S(1)} %get-tuple-element.217, bf16[384,4096]{1,0:T(8,128)(2,1)} %get-tuple-element.266, bf16[4096,1024]{1,0:T(8,128)(2,1)} %all-gather.8.cloned.1.call-done, f32[1024]{0:T(1024)S(1)} %get-tuple-element.218, f32[1024]{0:T(1024)S(1)} %get-tuple-element.313, ...), kind=kOutput, calls=%fused_computation.362 | convolution fusion | flops 3223977472 | bytes 14696960 | tf_op jit(solution)/shard_map/dot_general | solution.py:16
  301.8 13.9 %fusion.206 = (bf16[4096]{0:T(1024)(128)(2,1)S(1)}, bf16[384,4096]{1,0:T(8,128)(2,1)S(1)}) fusion(f32[384,4096]{1,0:T(8,128)} %get-tuple-element.267, f32[384,4096]{1,0:T(8,128)} %get-tuple-element.300, bf16[4096,1024]{1,0:T(8,128)(2,1)} %all-gather.8.cloned.1.call-done, f32[384,1024]{1,0:T(8,128)S(1)} %get-tuple-element.261), kind=kOutput, calls=%fused_computation.363 | convolution fusion | flops 3245207552 | bytes 25698304 | tf_op jit(solution)/shard_map/dot_general | solution.py:26
  315.8 3.9 multiply_reduce_fusion.2
  321.5 3.5 fusion.139
  328.3 59.1 %while.29 = (s32[]{:T(128)}, bf16[4,384,4,64]{1,3,2,0:T(8,128)(2,1)}, bf16[4,1024,4,64]{1,3,2,0:T(8,128)(2,1)}, bf16[4,1024,4,64]{1,3,2,0:T(8,128)(2,1)}, bf16[4...) while((s32[]{:T(128)}, ...), condition=%wide.region_19.20_spmd.clone, body=%wide.region_17.19_spmd.clone.sunk | while | flops 1031207424 | bytes 55560340 | solution.py:202
  330.6 3.5 multiply_reduce_fusion.12
  345.3 3.5 multiply_reduce_fusion.12
  360.0 3.5 multiply_reduce_fusion.12
  374.7 3.5 multiply_reduce_fusion.12
  387.5 3.4 fusion.124
  400.9 3.5 multiply_reduce_fusion.1
  421.7 3.7 convolution_convert_fusion.2
  436.8 7.1 convolution_convert_fusion.3
  448.6 3.5 copy-done.5
  452.3 6.8 convolution_convert_fusion
  459.1 14.1 %convert_element_type.545 = bf16[2,2,2,2,2,32,4096]{6,5,4,3,2,1,0:T(8,128)(2,1)} reshape(bf16[4096,1024]{1,0:T(8,128)(2,1)} %convolution_convert_fusion) | data formatting | bytes 16777216 | tf_op jit(solution)/shard_map/convert_element_type | solution.py:316
  473.2 7.2 convolution_convert_fusion.1
  480.4 6.6 fusion.66
  487.0 7.7 %copy.192 = bf16[2,2,2,2,1,32,8192]{6,5,0,1,2,3,4:T(8,128)(2,1)} copy(bf16[2,2,2,2,1,32,8192]{6,5,4,3,2,1,0:T(8,128)(2,1)} %get-tuple-element.273) | data formatting | bytes 16777216
  495.0 6.8 fusion.129
  501.9 8.7 %fusion.85 = f32[1024,1024]{1,0:T(8,128)} fusion(bf16[1024,8320]{1,0:T(8,128)(2,1)} %all-gather.4.cloned.1.call-done, bf16[1024,1024]{0,1:T(8,128)(2,1)S(1)} %bitcast.426, bf16[1024,1024]{0,1:T(8,128)(2,1)S(1)} %bitcast.438), kind=kOutput, calls=%fused_computation.116 | convolution fusion | flops 4303355904 | bytes 12582912 | tf_op jit(solution)/shard_map/dot_general | solution.py:26
  510.6 3.7 fusion.67
  517.9 3.3 fusion.64
  524.3 16.9 %collective-permute-done.8 = bf16[2,2,2,32,2048]{4,3,1,0,2:T(8,128)(2,1)S(1)} collective-permute-done((bf16[2,2,2,32,2048]{4,3,1,0,2:T(8,128)(2,1)S(1)}, bf16[2,2,2,32,2048]{4,3,1,0,2:T(8,128)(2,1)S(1)}, u32[]{:S(2)}, u32[]{:S(2)}) %collective-permute-start.8) | collective-permute-done | bytes 1048608 | tf_op jit(solution)/shard_map/ppermute | solution.py:287
  544.3 19.3 %collective-permute-done.1 = bf16[2,2,2,32,2048]{4,3,1,0,2:T(8,128)(2,1)S(1)} collective-permute-done((bf16[2,2,2,32,2048]{4,3,1,0,2:T(8,128)(2,1)S(1)}, bf16[2,2,2,32,2048]{4,3,1,0,2:T(8,128)(2,1)S(1)}, u32[]{:S(2)}, u32[]{:S(2)}) %collective-permute-start.1) | collective-permute-done | bytes 1048608 | tf_op jit(solution)/shard_map/ppermute | solution.py:287
  567.7 10.2 %collective-permute-done.9 = bf16[2,2,32,2048]{3,2,1,0:T(8,128)(2,1)S(1)} collective-permute-done((bf16[2,2,32,2048]{3,2,1,0:T(8,128)(2,1)S(1)}, bf16[2,2,32,2048]{3,2,1,0:T(8,128)(2,1)S(1)}, u32[]{:S(2)}, u32[]{:S(2)}) %collective-permute-start.9) | collective-permute-done | bytes 524320 | tf_op jit(solution)/shard_map/ppermute | solution.py:287
  579.8 8.3 %collective-permute-done.2 = bf16[2,2,32,2048]{3,2,1,0:T(8,128)(2,1)S(1)} collective-permute-done((bf16[2,2,32,2048]{3,2,1,0:T(8,128)(2,1)S(1)}, bf16[2,2,32,2048]{3,2,1,0:T(8,128)(2,1)S(1)}, u32[]{:S(2)}, u32[]{:S(2)}) %collective-permute-start.2) | collective-permute-done | bytes 524320 | tf_op jit(solution)/shard_map/ppermute | solution.py:287
  590.4 5.0 fusion.63
  601.2 4.4 collective-permute-done.5
  605.7 37.3 %collective-permute-done.15 = bf16[2,2,2,32,4096]{4,3,0,1,2:T(8,128)(2,1)S(1)} collective-permute-done((bf16[2,2,2,32,4096]{4,3,0,1,2:T(8,128)(2,1)S(1)}, bf16[2,2,2,32,4096]{4,3,0,1,2:T(8,128)(2,1)S(1)}, u32[]{:S(2)}, u32[]{:S(2)}) %collective-permute-start.15) | collective-permute-done | bytes 2097184 | tf_op jit(solution)/shard_map/ppermute | solution.py:287
  647.7 4.0 collective-permute-start.6
  651.7 15.2 %collective-permute-done.16 = bf16[2,2,32,4096]{3,2,0,1:T(8,128)(2,1)S(1)} collective-permute-done((bf16[2,2,32,4096]{3,2,0,1:T(8,128)(2,1)S(1)}, bf16[2,2,32,4096]{3,2,0,1:T(8,128)(2,1)S(1)}, u32[]{:S(2)}, u32[]{:S(2)}) %collective-permute-start.16) | collective-permute-done | bytes 1048608 | tf_op jit(solution)/shard_map/ppermute | solution.py:287
  671.0 19.2 %collective-permute-done.19 = bf16[2,32,8192]{2,1,0:T(8,128)(2,1)S(1)} collective-permute-done((bf16[2,32,8192]{2,1,0:T(8,128)(2,1)S(1)}, bf16[2,32,8192]{2,1,0:T(8,128)(2,1)S(1)}, u32[]{:S(2)}, u32[]{:S(2)}) %collective-permute-start.19) | collective-permute-done | bytes 1048608 | tf_op jit(solution)/shard_map/ppermute | solution.py:287
  698.0 15.8 %collective-permute-done.20 = bf16[32,8192]{1,0:T(8,128)(2,1)} collective-permute-done((bf16[32,8192]{1,0:T(8,128)(2,1)}, bf16[32,8192]{1,0:T(8,128)(2,1)}, u32[]{:S(2)}, u32[]{:S(2)}) %collective-permute-start.20) | collective-permute-done | bytes 524320 | tf_op jit(solution)/shard_map/ppermute | solution.py:287
  (381 shorter events, 188.0 us)
Async XLA Ops:
  7.2 164.8 %copy-start = (bf16[1024,1024]{1,0:T(8,128)(2,1)S(1)}, bf16[1024,1024]{1,0:T(8,128)(2,1)}, u32[]{:S(2)}) copy-start(bf16[1024,1024]{1,0:T(8,128)(2,1)} %param.21) | copy-start | bytes 6291460
  7.2 126.0 %all-gather.4.cloned.1.call-start = ((), (), s32[]{:S(2)}) async-start(), calls=%async_computation | async-start | bytes 17571840 | tf_op jit(solution)/shard_map/all_gather | solution.py:353
  14.3 207.0 %all-gather.6.cloned.1.call-start = ((), (), s32[]{:S(2)}) async-start(), calls=%async_computation.1 | async-start | bytes 8650752 | tf_op jit(solution)/shard_map/all_gather | solution.py:370
  15.0 275.8 %all-gather.8.cloned.1.call-start = ((), (), s32[]{:S(2)}) async-start(), calls=%async_computation.2 | async-start | bytes 8650752 | tf_op jit(solution)/shard_map/all_gather | solution.py:371
  140.7 75.0 %copy-start.42 = (f32[1024]{0:T(1024)}, f32[1024]{0:T(1024)S(1)}, u32[]{:S(2)}) copy-start(f32[1024]{0:T(1024)S(1)} %get-tuple-element.312) | copy-start | bytes 12292
  140.7 75.0 %copy-start.49 = (f32[1024]{0:T(1024)}, f32[1024]{0:T(1024)S(1)}, u32[]{:S(2)}) copy-start(f32[1024]{0:T(1024)S(1)} %get-tuple-element.222) | copy-start | bytes 12292
  140.7 150.2 %copy-start.52 = (f32[1024]{0:T(1024)}, f32[1024]{0:T(1024)S(1)}, u32[]{:S(2)}) copy-start(f32[1024]{0:T(1024)S(1)} %get-tuple-element.218) | copy-start | bytes 12292
  165.8 49.9 %copy-start.45 = (f32[384]{0:T(512)}, f32[384]{0:T(512)S(1)}, u32[]{:S(2)}) copy-start(f32[384]{0:T(512)S(1)} %broadcast_multiply_fusion.8) | copy-start | bytes 4612
  166.1 49.6 %copy-start.47 = (f32[384]{0:T(512)}, f32[384]{0:T(512)S(1)}, u32[]{:S(2)}) copy-start(f32[384]{0:T(512)S(1)} %add_rsqrt_fusion.2) | copy-start | bytes 4612
  290.9 8.6 %copy-start.27 = (bf16[384,1024]{1,0:T(8,128)(2,1)S(1)}, bf16[384,1024]{1,0:T(8,128)(2,1)}, u32[]{:S(2)}) copy-start(bf16[384,1024]{1,0:T(8,128)(2,1)} %param.35) | copy-start | bytes 2359300
  290.9 8.7 %copy-start.44 = (f32[1024]{0:T(1024)S(1)}, f32[1024]{0:T(1024)}, u32[]{:S(2)}) copy-start(f32[1024]{0:T(1024)} %get-tuple-element.314) | copy-start | bytes 12292
  290.9 8.7 %copy-start.51 = (f32[1024]{0:T(1024)S(1)}, f32[1024]{0:T(1024)}, u32[]{:S(2)}) copy-start(f32[1024]{0:T(1024)} %get-tuple-element.216) | copy-start | bytes 12292
  301.1 14.7 %slice-start.7 = ((s8[8388608]{0:T(1024)(128)(4,1)}), s8[4194304]{0:T(1024)(128)(4,1)S(1)}, s32[]{:S(2)}) async-start(s8[8388608]{0:T(1024)(128)(4,1)} %bitcast.435), calls=%async_computation.10 | async-start | bytes 8388608
  301.8 14.0 %copy-start.31 = (f32[384,1024]{1,0:T(8,128)}, f32[384,1024]{1,0:T(8,128)S(1)}, u32[]{:S(2)}) copy-start(f32[384,1024]{1,0:T(8,128)S(1)} %get-tuple-element.261) | copy-start | bytes 4718596
  301.8 14.0 %copy-start.16 = (f32[384,1024]{1,0:T(8,128)S(1)}, f32[384,1024]{1,0:T(8,128)}, u32[]{:S(2)}) copy-start(f32[384,1024]{1,0:T(8,128)} %copy-done.15) | copy-start | bytes 4718596
  301.8 14.0 %slice-start.8 = ((s8[8388608]{0:T(1024)(128)(4,1)}), s8[4194304]{0:T(1024)(128)(4,1)S(1)}, s32[]{:S(2)}) async-start(s8[8388608]{0:T(1024)(128)(4,1)} %bitcast.435), calls=%async_computation.11 | async-start | bytes 8388608
  431.6 85.8 %collective-permute-start = (bf16[2,2,2,2,32,4224]{5,4,3,2,1,0:T(8,128)(2,1)}, bf16[2,2,2,2,32,4224]{5,4,3,2,1,0:T(8,128)(2,1)}, u32[]{:S(2)}, u32[]{:S(2)}) collective-permute-start(bf16[2,2,2,2,32,4224]{5,4,3,2,1,0:T(8,128)(2,1)} %dynamic-slice_bitcast_fusion.1), channel_id=1, source_target_pairs={{0,1},{1,0},{2,3},{3,2},{4,5},{5,4},{6,7},{7,6},{8,9},{9,8},{10,11... | collective-permute-start | bytes 12976136 | tf_op jit(solution)/shard_map/ppermute | solution.py:287
  436.8 7.1 copy-start.34
  452.0 58.6 %collective-permute-start.7 = (bf16[2,2,2,2,32,4096]{5,4,3,2,1,0:T(8,128)(2,1)}, bf16[2,2,2,2,32,4096]{5,4,3,2,1,0:T(8,128)(2,1)}, u32[]{:S(2)}, u32[]{:S(2)}) collective-permute-start(bf16[2,2,2,2,32,4096]{5,4,3,2,1,0:T(8,128)(2,1)} %dynamic-slice_bitcast_fusion.2), channel_id=1, source_target_pairs={{0,1},{1,0},{2,3},{3,2},{4,5},{5,4},{6,7},{7,6},{8,9},{9,8},{10,11... | collective-permute-start | bytes 12582920 | tf_op jit(solution)/shard_map/ppermute | solution.py:287
  459.1 14.1 %copy-start.53 = (f32[1024]{0:T(1024)S(1)}, f32[1024]{0:T(1024)}, u32[]{:S(2)}) copy-start(f32[1024]{0:T(1024)} %copy-done.52) | copy-start | bytes 12292
  473.2 7.2 copy-start.4
  487.0 8.0 %copy-start.18 = (f32[384,1024]{1,0:T(8,128)S(1)}, f32[384,1024]{1,0:T(8,128)}, u32[]{:S(2)}) copy-start(f32[384,1024]{1,0:T(8,128)} %copy-done.17) | copy-start | bytes 4718596
  487.0 8.0 %copy-start.41 = (bf16[384,3072]{0,1:T(8,128)(2,1)S(1)}, bf16[384,3072]{0,1:T(8,128)(2,1)}, u32[]{:S(2)}) copy-start(bf16[384,3072]{0,1:T(8,128)(2,1)} %copy-done.40) | copy-start | bytes 7077892
  494.7 7.1 copy-start.30
  494.7 7.1 copy-start.54
  494.7 95.6 %collective-permute-start.14 = (bf16[2,2,2,2,32,8192]{5,4,0,1,2,3:T(8,128)(2,1)}, bf16[2,2,2,2,32,8192]{5,4,0,1,2,3:T(8,128)(2,1)}, u32[]{:S(2)}, u32[]{:S(2)}) collective-permute-start(bf16[2,2,2,2,32,8192]{5,4,0,1,2,3:T(8,128)(2,1)} %bitcast.410), channel_id=1, source_target_pairs={{0,1},{1,0},{2,3},{3,2},{4,5},{5,4},{6,7},{7,6},{8,9},{9,8},{10,11... | collective-permute-start | bytes 25165832 | tf_op jit(solution)/shard_map/ppermute | solution.py:287
  495.0 15.6 %slice-start.5 = ((s8[8388608]{0:T(1024)(128)(4,1)}), s8[4194304]{0:T(1024)(128)(4,1)S(1)}, s32[]{:S(2)}) async-start(s8[8388608]{0:T(1024)(128)(4,1)} %bitcast.405), calls=%async_computation.8 | async-start | bytes 8388608
  501.9 8.7 %slice-start.6 = ((s8[8388608]{0:T(1024)(128)(4,1)}), s8[4194304]{0:T(1024)(128)(4,1)S(1)}, s32[]{:S(2)}) async-start(s8[8388608]{0:T(1024)(128)(4,1)} %bitcast.405), calls=%async_computation.9 | async-start | bytes 8388608
  515.1 26.1 %collective-permute-start.8 = (bf16[2,2,2,32,2048]{4,3,1,0,2:T(8,128)(2,1)S(1)}, bf16[2,2,2,32,2048]{4,3,1,0,2:T(8,128)(2,1)S(1)}, u32[]{:S(2)}, u32[]{:S(2)}) collective-permute-start(bf16[2,2,2,32,2048]{4,3,1,0,2:T(8,128)(2,1)S(1)} %bitcast.428), channel_id=1, source_target_pairs={{0,4},{1,5},{2,6},{3,7},{4,0},{5,1},{6,2},{7,3},{8,12},{9,13},{10,... | collective-permute-start | bytes 3145736 | tf_op jit(solution)/shard_map/ppermute | solution.py:287
  516.7 26.4 %collective-permute-start.10 = (bf16[2,2,2,32,2048]{4,3,2,1,0:T(8,128)(2,1)S(1)}, bf16[2,2,2,32,2048]{4,3,2,1,0:T(8,128)(2,1)S(1)}, u32[]{:S(2)}, u32[]{:S(2)}) collective-permute-start(bf16[2,2,2,32,2048]{4,3,2,1,0:T(8,128)(2,1)S(1)} %dynamic-slice_bitcast_fusion.8), channel_id=1, source_target_pairs={{0,2},{1,3},{2,0},{3,1},{4,6},{5,7},{6,4},{7,5},{8,10},{9,11},{10,... | collective-permute-start | bytes 3145736 | tf_op jit(solution)/shard_map/ppermute | solution.py:287
  521.8 44.9 %collective-permute-start.3 = (bf16[2,2,2,32,2176]{4,3,2,1,0:T(8,128)(2,1)S(1)}, bf16[2,2,2,32,2176]{4,3,2,1,0:T(8,128)(2,1)S(1)}, u32[]{:S(2)}, u32[]{:S(2)}) collective-permute-start(bf16[2,2,2,32,2176]{4,3,2,1,0:T(8,128)(2,1)S(1)} %dynamic-slice_bitcast_fusion.5), channel_id=1, source_target_pairs={{0,2},{1,3},{2,0},{3,1},{4,6},{5,7},{6,4},{7,5},{8,10},{9,11},{10,... | collective-permute-start | bytes 3342344 | tf_op jit(solution)/shard_map/ppermute | solution.py:287
  523.7 40.0 %collective-permute-start.1 = (bf16[2,2,2,32,2048]{4,3,1,0,2:T(8,128)(2,1)S(1)}, bf16[2,2,2,32,2048]{4,3,1,0,2:T(8,128)(2,1)S(1)}, u32[]{:S(2)}, u32[]{:S(2)}) collective-permute-start(bf16[2,2,2,32,2048]{4,3,1,0,2:T(8,128)(2,1)S(1)} %bitcast.429), channel_id=1, source_target_pairs={{0,4},{1,5},{2,6},{3,7},{4,0},{5,1},{6,2},{7,3},{8,12},{9,13},{10,... | collective-permute-start | bytes 3145736 | tf_op jit(solution)/shard_map/ppermute | solution.py:287
  541.6 36.3 %collective-permute-start.9 = (bf16[2,2,32,2048]{3,2,1,0:T(8,128)(2,1)S(1)}, bf16[2,2,32,2048]{3,2,1,0:T(8,128)(2,1)S(1)}, u32[]{:S(2)}, u32[]{:S(2)}) collective-permute-start(bf16[2,2,32,2048]{3,2,1,0:T(8,128)(2,1)S(1)} %dynamic-slice_bitcast_fusion.12), channel_id=1, source_target_pairs={{0,2},{1,3},{2,0},{3,1},{4,6},{5,7},{6,4},{7,5},{8,10},{9,11},{10,... | collective-permute-start | bytes 1572872 | tf_op jit(solution)/shard_map/ppermute | solution.py:287
  543.7 34.4 %collective-permute-start.11 = (bf16[2,2,32,2048]{3,2,1,0:T(8,128)(2,1)S(1)}, bf16[2,2,32,2048]{3,2,1,0:T(8,128)(2,1)S(1)}, u32[]{:S(2)}, u32[]{:S(2)}) collective-permute-start(bf16[2,2,32,2048]{3,2,1,0:T(8,128)(2,1)S(1)} %dynamic-slice_bitcast_fusion.11), channel_id=1, source_target_pairs={{0,4},{1,5},{2,6},{3,7},{4,0},{5,1},{6,2},{7,3},{8,12},{9,13},{10,... | collective-permute-start | bytes 1572872 | tf_op jit(solution)/shard_map/ppermute | solution.py:287
  564.1 24.0 %collective-permute-start.2 = (bf16[2,2,32,2048]{3,2,1,0:T(8,128)(2,1)S(1)}, bf16[2,2,32,2048]{3,2,1,0:T(8,128)(2,1)S(1)}, u32[]{:S(2)}, u32[]{:S(2)}) collective-permute-start(bf16[2,2,32,2048]{3,2,1,0:T(8,128)(2,1)S(1)} %dynamic-slice_bitcast_fusion.13), channel_id=1, source_target_pairs={{0,2},{1,3},{2,0},{3,1},{4,6},{5,7},{6,4},{7,5},{8,10},{9,11},{10,... | collective-permute-start | bytes 1572872 | tf_op jit(solution)/shard_map/ppermute | solution.py:287
  566.7 23.7 %slice-start.3 = ((s8[8388608]{0:T(1024)(128)(4,1)}), s8[4194304]{0:T(1024)(128)(4,1)S(1)}, s32[]{:S(2)}) async-start(s8[8388608]{0:T(1024)(128)(4,1)} %bitcast.402), calls=%async_computation.6 | async-start | bytes 8388608
  567.1 21.2 %collective-permute-start.4 = (bf16[2,2,32,2176]{3,2,1,0:T(8,128)(2,1)S(1)}, bf16[2,2,32,2176]{3,2,1,0:T(8,128)(2,1)S(1)}, u32[]{:S(2)}, u32[]{:S(2)}) collective-permute-start(bf16[2,2,32,2176]{3,2,1,0:T(8,128)(2,1)S(1)} %dynamic-slice_bitcast_fusion.9), channel_id=1, source_target_pairs={{0,4},{1,5},{2,6},{3,7},{4,0},{5,1},{6,2},{7,3},{8,12},{9,13},{10,... | collective-permute-start | bytes 1671176 | tf_op jit(solution)/shard_map/ppermute | solution.py:287
  578.2 12.2 %slice-start.4 = ((s8[8388608]{0:T(1024)(128)(4,1)}), s8[4194304]{0:T(1024)(128)(4,1)S(1)}, s32[]{:S(2)}) async-start(s8[8388608]{0:T(1024)(128)(4,1)} %bitcast.402), calls=%async_computation.7 | async-start | bytes 8388608
  578.3 12.0 %collective-permute-start.12 = (bf16[2,32,4096]{2,1,0:T(8,128)(2,1)S(1)}, bf16[2,32,4096]{2,1,0:T(8,128)(2,1)S(1)}, u32[]{:S(2)}, u32[]{:S(2)}) collective-permute-start(bf16[2,32,4096]{2,1,0:T(8,128)(2,1)S(1)} %fusion.171), channel_id=1, source_target_pairs={{0,8},{1,9},{2,10},{3,11},{4,12},{5,13},{6,14},{7,15},{8,0},{9,1},... | collective-permute-start | bytes 1572872 | tf_op jit(solution)/shard_map/ppermute | solution.py:287
  588.5 17.1 %collective-permute-start.5 = (bf16[2,32,4224]{2,1,0:T(8,128)(2,1)S(1)}, bf16[2,32,4224]{2,1,0:T(8,128)(2,1)S(1)}, u32[]{:S(2)}, u32[]{:S(2)}) collective-permute-start(bf16[2,32,4224]{2,1,0:T(8,128)(2,1)S(1)} %fusion.165), channel_id=1, source_target_pairs={{0,8},{1,9},{2,10},{3,11},{4,12},{5,13},{6,14},{7,15},{8,0},{9,1},... | collective-permute-start | bytes 1622024 | tf_op jit(solution)/shard_map/ppermute | solution.py:287
  596.8 46.2 %collective-permute-start.15 = (bf16[2,2,2,32,4096]{4,3,0,1,2:T(8,128)(2,1)S(1)}, bf16[2,2,2,32,4096]{4,3,0,1,2:T(8,128)(2,1)S(1)}, u32[]{:S(2)}, u32[]{:S(2)}) collective-permute-start(bf16[2,2,2,32,4096]{4,3,0,1,2:T(8,128)(2,1)S(1)} %dynamic-slice_bitcast_fusion.4), channel_id=1, source_target_pairs={{0,4},{1,5},{2,6},{3,7},{4,0},{5,1},{6,2},{7,3},{8,12},{9,13},{10,... | collective-permute-start | bytes 6291464 | tf_op jit(solution)/shard_map/ppermute | solution.py:287
  597.5 72.0 %collective-permute-start.13 = (bf16[32,4096]{1,0:T(8,128)(2,1)S(1)}, bf16[32,4096]{1,0:T(8,128)(2,1)S(1)}, u32[]{:S(2)}, u32[]{:S(2)}) collective-permute-start(bf16[32,4096]{1,0:T(8,128)(2,1)S(1)} %dynamic-slice_bitcast_fusion.15), channel_id=1, source_target_pairs={{0,16},{1,17},{2,18},{3,19},{4,20},{5,21},{6,22},{7,23},{8,24},{9,... | collective-permute-start | bytes 786440 | tf_op jit(solution)/shard_map/ppermute | solution.py:287
  599.7 44.9 %collective-permute-start.17 = (bf16[2,2,2,32,4096]{4,3,0,1,2:T(8,128)(2,1)S(1)}, bf16[2,2,2,32,4096]{4,3,0,1,2:T(8,128)(2,1)S(1)}, u32[]{:S(2)}, u32[]{:S(2)}) collective-permute-start(bf16[2,2,2,32,4096]{4,3,0,1,2:T(8,128)(2,1)S(1)} %dynamic-slice_bitcast_fusion.3), channel_id=1, source_target_pairs={{0,2},{1,3},{2,0},{3,1},{4,6},{5,7},{6,4},{7,5},{8,10},{9,11},{10,... | collective-permute-start | bytes 6291464 | tf_op jit(solution)/shard_map/ppermute | solution.py:287
  644.0 22.9 %collective-permute-start.16 = (bf16[2,2,32,4096]{3,2,0,1:T(8,128)(2,1)S(1)}, bf16[2,2,32,4096]{3,2,0,1:T(8,128)(2,1)S(1)}, u32[]{:S(2)}, u32[]{:S(2)}) collective-permute-start(bf16[2,2,32,4096]{3,2,0,1:T(8,128)(2,1)S(1)} %dynamic-slice_bitcast_fusion.7), channel_id=1, source_target_pairs={{0,2},{1,3},{2,0},{3,1},{4,6},{5,7},{6,4},{7,5},{8,10},{9,11},{10,... | collective-permute-start | bytes 3145736 | tf_op jit(solution)/shard_map/ppermute | solution.py:287
  645.5 22.6 %collective-permute-start.18 = (bf16[2,2,32,4096]{3,2,0,1:T(8,128)(2,1)S(1)}, bf16[2,2,32,4096]{3,2,0,1:T(8,128)(2,1)S(1)}, u32[]{:S(2)}, u32[]{:S(2)}) collective-permute-start(bf16[2,2,32,4096]{3,2,0,1:T(8,128)(2,1)S(1)} %dynamic-slice_bitcast_fusion.6), channel_id=1, source_target_pairs={{0,4},{1,5},{2,6},{3,7},{4,0},{5,1},{6,2},{7,3},{8,12},{9,13},{10,... | collective-permute-start | bytes 3145736 | tf_op jit(solution)/shard_map/ppermute | solution.py:287
  647.7 45.9 %collective-permute-start.6 = (bf16[32,4224]{1,0:T(8,128)(2,1)S(1)}, bf16[32,4224]{1,0:T(8,128)(2,1)S(1)}, u32[]{:S(2)}, u32[]{:S(2)}) collective-permute-start(bf16[32,4224]{1,0:T(8,128)(2,1)S(1)} %dynamic-slice_bitcast_fusion.14), channel_id=1, source_target_pairs={{0,16},{1,17},{2,18},{3,19},{4,20},{5,21},{6,22},{7,23},{8,24},{9,... | collective-permute-start | bytes 811016 | tf_op jit(solution)/shard_map/ppermute | solution.py:287
  668.4 21.8 %collective-permute-start.19 = (bf16[2,32,8192]{2,1,0:T(8,128)(2,1)S(1)}, bf16[2,32,8192]{2,1,0:T(8,128)(2,1)S(1)}, u32[]{:S(2)}, u32[]{:S(2)}) collective-permute-start(bf16[2,32,8192]{2,1,0:T(8,128)(2,1)S(1)} %fusion.153), channel_id=1, source_target_pairs={{0,8},{1,9},{2,10},{3,11},{4,12},{5,13},{6,14},{7,15},{8,0},{9,1},... | collective-permute-start | bytes 3145736 | tf_op jit(solution)/shard_map/ppermute | solution.py:287
  691.3 22.4 %collective-permute-start.20 = (bf16[32,8192]{1,0:T(8,128)(2,1)}, bf16[32,8192]{1,0:T(8,128)(2,1)}, u32[]{:S(2)}, u32[]{:S(2)}) collective-permute-start(bf16[32,8192]{1,0:T(8,128)(2,1)} %dynamic-slice_bitcast_fusion.10), channel_id=1, source_target_pairs={{0,16},{1,17},{2,18},{3,19},{4,20},{5,21},{6,22},{7,23},{8,24},{9,... | collective-permute-start | bytes 1572872 | tf_op jit(solution)/shard_map/ppermute | solution.py:287
  (45 other events, 130.9 us)
Sparse Core Ops, SparseCore 0:
  14.4 118.7 all-gather.3
  136.1 75.7 all-gather.5
  214.7 76.1 all-gather.7

commit v2 on v1

v2 whole, which is shorter than its diff:
```python
import functools

import jax
import jax.numpy as jnp
from jax import lax
from jax.experimental import pallas as pl
from jax.experimental.pallas import tpu as pltpu
from jax.sharding import PartitionSpec as P

HEADS = 16
HEAD_DIM = 64
SEQ_LEN = 128
PAIRS = HEADS // 2
neg_fill = -1e30
AXES = ("wide", "narrow")
vmem = pl.BlockSpec(memory_space=pltpu.VMEM)
smem = pl.BlockSpec(memory_space=pltpu.SMEM)
anywhere = pl.BlockSpec(memory_space=pl.ANY)
norm_eps = 1e-05


def kernel_params(megabytes):
    return pltpu.CompilerParams(vmem_limit_bytes=megabytes << 20)


def cost(flops, megabytes, transcendentals=0):
    return pl.CostEstimate(
        flops=int(flops), bytes_accessed=int(megabytes * 2**20), transcendentals=int(transcendentals)
    )


def matmul(first, second):
    return jnp.dot(first, second, preferred_element_type=jnp.float32)


def inner_cols(first, second):
    return lax.dot_general(
        first, second, (((1,), (1,)), ((), ())), preferred_element_type=jnp.float32
    )


def column_sums(values):
    return jnp.sum(values.astype(jnp.float32), axis=0)


def memory_bounds(block_rows, pad_rows):
    count = block_rows.shape[0]
    before = jnp.arange(count)[None, :] < jnp.arange(count)[:, None]
    starts = jnp.sum(jnp.where(before, block_rows[None, :], 0), axis=1)
    valid = jnp.maximum(block_rows - pad_rows, (block_rows + 1) // 2)
    return jnp.stack([starts, starts + valid])


def dot(first, second, contract):
    return lax.dot_general(
        first, second, ((contract[:1], contract[1:]), ((), ())), preferred_element_type=jnp.float32
    )


def cols(pair, base=0):
    return slice((base + pair) * 128, (base + pair + 1) * 128)


def split_heads(block):
    low = lax.broadcasted_iota(jnp.int32, block.shape, 1) < HEAD_DIM
    zero = jnp.zeros_like(block)
    return jnp.concatenate([jnp.where(low, block, zero), jnp.where(low, zero, block)], axis=0)


def join_heads(stacked):
    low = lax.broadcasted_iota(jnp.int32, (SEQ_LEN, 128), 1) < HEAD_DIM
    return jnp.where(low, stacked[:SEQ_LEN], stacked[SEQ_LEN:])


def join_heads_t(stacked):
    both = jnp.concatenate([stacked[:HEAD_DIM, :SEQ_LEN], stacked[HEAD_DIM:, SEQ_LEN:]], axis=0)
    return both.T


def cross_mask(tile, low, high):
    rows = tile * 128 + lax.broadcasted_iota(jnp.int32, (128, 2 * SEQ_LEN), 0)
    return (rows >= low) & (rows < high)


def cross_forward_kernel(bound, q, pairs, *rest, extra):
    context, summary, stack, scores, top, total, acc = rest[extra:]

    def sequence(s, carry):
        low, high = bound[0, s], bound[1, s]
        first, last = low // 128, (high + 127) // 128
        rows = pl.ds(pl.multiple_of(s * SEQ_LEN, SEQ_LEN), SEQ_LEN)
        for p in range(PAIRS):
            stack[p] = split_heads(q[rows, cols(p)] * jnp.bfloat16(HEAD_DIM**-0.5))
        top[...] = jnp.full_like(top, neg_fill)
        total[...] = jnp.zeros_like(total)
        acc[...] = jnp.zeros_like(acc)

        def one(t, carry):
            keys = pl.ds(pl.multiple_of(t * 128, 128), 128)
            ok = cross_mask(t, low, high)
            for p in range(PAIRS):
                raw = jnp.where(ok, dot(pairs[keys, cols(p)], stack[p], (1, 1)), neg_fill)
                scores[t, p] = raw
                top[p] = jnp.maximum(top[p], jnp.max(raw, axis=0, keepdims=True))
            return carry

        lax.fori_loop(first, last, one, 0)

        def two(t, carry):
            keys = pl.ds(pl.multiple_of(t * 128, 128), 128)
            for p in range(PAIRS):
                weights = jnp.exp(scores[t, p] - top[p])
                total[p] += jnp.sum(weights, axis=0, keepdims=True)
                acc[p] += dot(pairs[keys, cols(p, PAIRS)], weights.astype(jnp.bfloat16), (0, 0))
            return carry

        lax.fori_loop(first, last, two, 0)
        for p in range(PAIRS):
            context[rows, cols(p)] = join_heads_t(acc[p] / total[p]).astype(jnp.bfloat16)
            summary[s, p] = top[p] + jnp.log(total[p])
        return carry

    lax.fori_loop(0, bound.shape[1], sequence, 0)


def cross_backward_kernel(bound, q, pairs, grad, summary, *rest, extra):
    q_grad, pair_grad, stack, grads, probs, prob_grads, delta, acc, pair_acc = rest[extra:]
    pair_acc[...] = jnp.zeros_like(pair_acc)
    scale = HEAD_DIM**-0.5

    def sequence(s, carry):
        low, high = bound[0, s], bound[1, s]
        first, last = low // 128, (high + 127) // 128
        rows = pl.ds(pl.multiple_of(s * SEQ_LEN, SEQ_LEN), SEQ_LEN)
        for p in range(PAIRS):
            stack[p] = split_heads(q[rows, cols(p)] * jnp.bfloat16(scale))
            grads[p] = split_heads(grad[rows, cols(p)])
        delta[...] = jnp.zeros_like(delta)
        acc[...] = jnp.zeros_like(acc)

        def one(t, carry):
            keys = pl.ds(pl.multiple_of(t * 128, 128), 128)
            ok = cross_mask(t, low, high)
            for p in range(PAIRS):
                raw = dot(pairs[keys, cols(p)], stack[p], (1, 1))
                weights = jnp.where(ok, jnp.exp(raw - summary[s, p]), 0.0)
                back = dot(pairs[keys, cols(p, PAIRS)], grads[p], (1, 1))
                delta[p] += jnp.sum(weights * back, axis=0, keepdims=True)
                probs[t, p] = weights
                prob_grads[t, p] = back
                pair_acc[keys, cols(p, PAIRS)] += dot(weights.astype(jnp.bfloat16), grads[p], (1, 0))
            return carry

        lax.fori_loop(first, last, one, 0)

        def two(t, carry):
            keys = pl.ds(pl.multiple_of(t * 128, 128), 128)
            for p in range(PAIRS):
                score = (probs[t, p] * (prob_grads[t, p] - delta[p])).astype(jnp.bfloat16)
                pair_acc[keys, cols(p)] += dot(score, stack[p], (1, 0))
                acc[p] += dot(pairs[keys, cols(p)], score, (0, 0))
            return carry

        lax.fori_loop(first, last, two, 0)
        for p in range(PAIRS):
            q_grad[rows, cols(p)] = (join_heads_t(acc[p]) * scale).astype(jnp.bfloat16)
        return carry

    lax.fori_loop(0, bound.shape[1], sequence, 0)
    pair_grad[...] = pair_acc[...].astype(jnp.bfloat16)


def cross_forward(bound, q, pairs, after=()):
    seqs, tiles = bound.shape[1], pairs.shape[0] // 128
    wide = 2 * SEQ_LEN
    return pl.pallas_call(
        functools.partial(cross_forward_kernel, extra=len(after)),
        out_shape=(
            jax.ShapeDtypeStruct(q.shape, jnp.bfloat16),
            jax.ShapeDtypeStruct((seqs, PAIRS, 1, wide), jnp.float32),
        ),
        in_specs=[smem, vmem, vmem] + [anywhere] * len(after),
        out_specs=(vmem, vmem),
        scratch_shapes=[
            pltpu.VMEM((PAIRS, wide, 128), jnp.bfloat16),
            pltpu.VMEM((tiles, PAIRS, 128, wide), jnp.float32),
            pltpu.VMEM((PAIRS, 1, wide), jnp.float32),
            pltpu.VMEM((PAIRS, 1, wide), jnp.float32),
            pltpu.VMEM((PAIRS, 128, wide), jnp.float32),
        ],
        compiler_params=kernel_params(40),
        cost_estimate=pl.CostEstimate(flops=8 * 10**9, bytes_accessed=8 * 2**20, transcendentals=2 * 10**6),
    )(bound, q, pairs, *after)


def cross_backward(bound, q, pairs, grad, summary, after=()):
    seqs, tiles = bound.shape[1], pairs.shape[0] // 128
    wide = 2 * SEQ_LEN
    return pl.pallas_call(
        functools.partial(cross_backward_kernel, extra=len(after)),
        out_shape=(
            jax.ShapeDtypeStruct(q.shape, jnp.bfloat16),
            jax.ShapeDtypeStruct(pairs.shape, jnp.bfloat16),
        ),
        in_specs=[smem, vmem, vmem, vmem, vmem] + [anywhere] * len(after),
        out_specs=(vmem, vmem),
        scratch_shapes=[
            pltpu.VMEM((PAIRS, wide, 128), jnp.bfloat16),
            pltpu.VMEM((PAIRS, wide, 128), jnp.bfloat16),
            pltpu.VMEM((tiles, PAIRS, 128, wide), jnp.float32),
            pltpu.VMEM((tiles, PAIRS, 128, wide), jnp.float32),
            pltpu.VMEM((PAIRS, 1, wide), jnp.float32),
            pltpu.VMEM((PAIRS, 128, wide), jnp.float32),
            pltpu.VMEM(pairs.shape, jnp.float32),
        ],
        compiler_params=kernel_params(56),
        cost_estimate=pl.CostEstimate(flops=16 * 10**9, bytes_accessed=12 * 2**20, transcendentals=2 * 10**6),
    )(bound, q, pairs, grad, summary, *after)


def self_mask(length):
    keys = lax.broadcasted_iota(jnp.int32, (SEQ_LEN, 2 * SEQ_LEN), 0)
    tokens = lax.broadcasted_iota(jnp.int32, (SEQ_LEN, 2 * SEQ_LEN), 1) & (SEQ_LEN - 1)
    return (keys <= tokens) & (keys < length)


def self_forward_kernel(lengths, qkv, *rest, extra):
    context, summary = rest[extra:]

    def sequence(s, carry):
        ok = self_mask(lengths[s])
        rows = pl.ds(pl.multiple_of(s * SEQ_LEN, SEQ_LEN), SEQ_LEN)
        for p in range(PAIRS):
            stack = split_heads(qkv[rows, cols(p)] * jnp.bfloat16(HEAD_DIM**-0.5))
            raw = jnp.where(ok, dot(qkv[rows, cols(p, PAIRS)], stack, (1, 1)), neg_fill)
            top = jnp.max(raw, axis=0, keepdims=True)
            weights = jnp.exp(raw - top)
            total = jnp.sum(weights, axis=0, keepdims=True)
            weights = (weights / total).astype(jnp.bfloat16)
            acc = dot(qkv[rows, cols(p, 2 * PAIRS)], weights, (0, 0))
            context[rows, cols(p)] = join_heads_t(acc).astype(jnp.bfloat16)
            summary[s, p] = top + jnp.log(total)
        return carry

    lax.fori_loop(0, lengths.shape[0], sequence, 0)


def self_backward_kernel(lengths, qkv, grad, summary, *rest, extra):
    [delta_out] = rest[extra:]
    scale = HEAD_DIM**-0.5

    def sequence(s, carry):
        ok = self_mask(lengths[s])
        rows = pl.ds(pl.multiple_of(s * SEQ_LEN, SEQ_LEN), SEQ_LEN)
        for p in range(PAIRS):
            stack = split_heads(qkv[rows, cols(p)] * jnp.bfloat16(scale))
            grads = split_heads(grad[rows, cols(p)])
            keys = qkv[rows, cols(p, PAIRS)]
            raw = dot(keys, stack, (1, 1))
            weights = jnp.where(ok, jnp.exp(raw - summary[s, p]), 0.0)
            back = dot(qkv[rows, cols(p, 2 * PAIRS)], grads, (1, 1))
            delta = jnp.sum(weights * back, axis=0, keepdims=True)
            score = (weights * (back - delta)).astype(jnp.bfloat16)
            value_grad = dot(weights.astype(jnp.bfloat16), grads, (1, 0))
            key_grad = dot(score, stack, (1, 0))
            query_grad = join_heads_t(dot(keys, score, (0, 0))) * scale
            delta_out[rows, cols(p)] = query_grad.astype(jnp.bfloat16)
            delta_out[rows, cols(p, PAIRS)] = key_grad.astype(jnp.bfloat16)
            delta_out[rows, cols(p, 2 * PAIRS)] = value_grad.astype(jnp.bfloat16)
        return carry

    lax.fori_loop(0, lengths.shape[0], sequence, 0)


def self_forward(lengths, qkv, after=()):
    tokens, width = qkv.shape[0], qkv.shape[1] // 3
    return pl.pallas_call(
        functools.partial(self_forward_kernel, extra=len(after)),
        out_shape=(
            jax.ShapeDtypeStruct((tokens, width), jnp.bfloat16),
            jax.ShapeDtypeStruct((lengths.shape[0], PAIRS, 1, 2 * SEQ_LEN), jnp.float32),
        ),
        in_specs=[smem, vmem] + [anywhere] * len(after),
        out_specs=(vmem, vmem),
        compiler_params=kernel_params(24),
        cost_estimate=pl.CostEstimate(flops=2 * 10**9, bytes_accessed=4 * 2**20, transcendentals=10**6),
    )(lengths, qkv, *after)


def self_backward(lengths, qkv, grad, summary, after=()):
    return pl.pallas_call(
        functools.partial(self_backward_kernel, extra=len(after)),
        out_shape=jax.ShapeDtypeStruct(qkv.shape, jnp.bfloat16),
        in_specs=[smem, vmem, vmem, vmem] + [anywhere] * len(after),
        out_specs=vmem,
        compiler_params=kernel_params(24),
        cost_estimate=pl.CostEstimate(flops=4 * 10**9, bytes_accessed=6 * 2**20, transcendentals=10**6),
    )(lengths, qkv, grad, summary, *after)


def normalize(values, gain, shift):
    centered = values - jnp.mean(values, axis=-1, keepdims=True)
    inverse = lax.rsqrt(jnp.mean(centered * centered, axis=-1, keepdims=True) + norm_eps)
    unit = centered * inverse
    return (unit * gain + shift, unit, inverse)


def normalize_back(grad, unit, inverse, gain):
    scaled = grad * gain
    inner = (
        scaled
        - jnp.mean(scaled, axis=-1, keepdims=True)
        - unit * jnp.mean(scaled * unit, axis=-1, keepdims=True)
    )
    return inverse * inner


def sum_rows(*rows):
    stacked = [jnp.sum(r, axis=0, keepdims=True) for r in rows]
    return jnp.concatenate(stacked + [jnp.zeros_like(stacked[0])] * (8 - len(rows)), axis=0)


def deal(core, product, rows, keep, send):
    for i in range(product.shape[0] // (2 * rows)):
        even = product[2 * i * rows : (2 * i + 1) * rows]
        odd = product[(2 * i + 1) * rows : (2 * i + 2) * rows]
        here = slice(i * rows, (i + 1) * rows)
        keep[here, :] = jnp.where(core == 0, even, odd).astype(jnp.bfloat16)
        send[here, :] = jnp.where(core == 0, odd, even).astype(jnp.bfloat16)


def ffn_forward_kernel(
    second, w_in, bias, w_out, cot, vectors, hidden, slope, block_out, third_grad, out_grad, sums, acc, low
):
    step = pl.program_id(0)

    @pl.when(step == 0)
    def _():
        low[...] = second[...].astype(jnp.bfloat16)
        acc[...] = second[...] + vectors[0:1]

    pre = dot(low[...], w_in[...], (1, 0)) + bias[...]
    part = 0.5 + 0.5 * lax.erf(pre * 0.5**0.5)
    active = (pre * part).astype(jnp.bfloat16)
    hidden[...] = active
    slope[...] = (part + pre * jnp.exp(-0.5 * pre * pre) * 0.3989422804014327).astype(jnp.bfloat16)
    acc[...] += dot(active, w_out[...], (1, 0))

    @pl.when(step == pl.num_programs(0) - 1)
    def _():
        gain = vectors[1:2]
        third, unit, inverse = normalize(acc[...], gain, vectors[2:3])
        block_out[...] = third.astype(jnp.bfloat16)
        grad = cot[...].astype(jnp.float32)
        third = normalize_back(grad, unit, inverse, gain)
        third_grad[...] = third
        lower = third.astype(jnp.bfloat16)
        out_grad[...] = lower
        sums[...] = sum_rows(grad * unit, grad, lower.astype(jnp.float32))


def ffn_forward(second, w_in, bias, w_out, cot, vectors):
    tokens, width = second.shape
    hidden = w_in.shape[1]
    chunk = 512
    whole = lambda shape: pl.BlockSpec(shape, lambda j: (0, 0))
    full = whole((tokens, width))
    strip = pl.BlockSpec((tokens, chunk), lambda j: (0, j))
    return pl.pallas_call(
        ffn_forward_kernel,
        grid=(hidden // chunk,),
        out_shape=(
            jax.ShapeDtypeStruct((tokens, hidden), jnp.bfloat16),
            jax.ShapeDtypeStruct((tokens, hidden), jnp.bfloat16),
            jax.ShapeDtypeStruct((tokens, width), jnp.bfloat16),
            jax.ShapeDtypeStruct((tokens, width), jnp.float32),
            jax.ShapeDtypeStruct((tokens, width), jnp.bfloat16),
            jax.ShapeDtypeStruct((8, width), jnp.float32),
        ),
        in_specs=[
            full,
            pl.BlockSpec((width, chunk), lambda j: (0, j)),
            pl.BlockSpec((1, chunk), lambda j: (0, j)),
            pl.BlockSpec((chunk, width), lambda j: (j, 0)),
            full,
            whole((8, width)),
        ],
        out_specs=(strip, strip, full, full, full, whole((8, width))),
        scratch_shapes=[
            pltpu.VMEM((tokens, width), jnp.float32),
            pltpu.VMEM((tokens, width), jnp.bfloat16),
        ],
        compiler_params=kernel_params(40),
        cost_estimate=cost(16e9, 26, 4e6),
    )(second, w_in, bias, w_out, cot, vectors)


def ffn_out_kernel(core, hidden, out_grad, keep, send, *, rows):
    deal(core[0], dot(hidden[...], out_grad[...], (0, 0)), rows, keep, send)


def ffn_out_grads(core, hidden, out_grad, rows):
    tokens, width = out_grad.shape
    size = hidden.shape[1]
    chunk = 1024
    half = jax.ShapeDtypeStruct((size // 2, width), jnp.bfloat16)
    block = pl.BlockSpec((chunk // 2, width), lambda j: (j, 0))
    return pl.pallas_call(
        functools.partial(ffn_out_kernel, rows=rows),
        grid=(size // chunk,),
        out_shape=(half, half),
        in_specs=[
            smem,
            pl.BlockSpec((tokens, chunk), lambda j: (0, j)),
            pl.BlockSpec((tokens, width), lambda j: (0, 0)),
        ],
        out_specs=(block, block),
        compiler_params=kernel_params(40),
        cost_estimate=cost(8e9, 12),
    )(core, hidden, out_grad)


def ffn_backward_kernel(
    core, second, w_in, w_out, slope, third_grad, out_grad, unit, inverse, gain, *rest, extra, rows
):
    keep, send, bias_grad, second_grad, branch, sums, acc, turned = rest[extra:]
    step = pl.program_id(0)

    @pl.when(step == 0)
    def _():
        turned[...] = second[...].astype(jnp.bfloat16).T
        acc[...] = third_grad[...]

    grad = dot(out_grad[...], w_out[...], (1, 1)) * slope[...].astype(jnp.float32)
    lower = grad.astype(jnp.bfloat16)
    bias_grad[...] = jnp.sum(lower.astype(jnp.float32), axis=0, keepdims=True)
    deal(core[0], dot(turned[...], lower, (1, 0)), rows, keep, send)
    acc[...] += dot(lower, w_in[...], (1, 1))

    @pl.when(step == pl.num_programs(0) - 1)
    def _():
        total = acc[...]
        grad = normalize_back(total, unit[...], inverse[...], gain[...])
        second_grad[...] = grad
        lower = grad.astype(jnp.bfloat16)
        branch[...] = lower
        sums[...] = sum_rows(total * unit[...], total, lower.astype(jnp.float32))


def ffn_backward(core, second, w_in, w_out, slope, third_grad, out_grad, unit, inverse, gain, rows, after):
    tokens, width = second.shape
    hidden = w_in.shape[1]
    chunk = 512
    whole = lambda shape: pl.BlockSpec(shape, lambda j: (0, 0))
    full = whole((tokens, width))
    half = jax.ShapeDtypeStruct((width // 2, hidden), jnp.bfloat16)
    block = pl.BlockSpec((width // 2, chunk), lambda j: (0, j))
    return pl.pallas_call(
        functools.partial(ffn_backward_kernel, extra=len(after), rows=rows),
        grid=(hidden // chunk,),
        out_shape=(
            half,
            half,
            jax.ShapeDtypeStruct((1, hidden), jnp.float32),
            jax.ShapeDtypeStruct((tokens, width), jnp.float32),
            jax.ShapeDtypeStruct((tokens, width), jnp.bfloat16),
            jax.ShapeDtypeStruct((8, width), jnp.float32),
        ),
        in_specs=[
            smem,
            full,
            pl.BlockSpec((width, chunk), lambda j: (0, j)),
            pl.BlockSpec((chunk, width), lambda j: (j, 0)),
            pl.BlockSpec((tokens, chunk), lambda j: (0, j)),
            full,
            full,
            full,
            whole((tokens, 1)),
            whole((1, width)),
        ]
        + [anywhere] * len(after),
        out_specs=(block, block, pl.BlockSpec((1, chunk), lambda j: (0, j)), full, full, whole((8, width))),
        scratch_shapes=[
            pltpu.VMEM((tokens, width), jnp.float32),
            pltpu.VMEM((width, tokens), jnp.bfloat16),
        ],
        compiler_params=kernel_params(44),
        cost_estimate=cost(24e9, 32),
    )(core, second, w_in, w_out, slope, third_grad, out_grad, unit, inverse, gain, *after)


def product_grads_kernel(core, *rest, spans, extra, rows, chunk):
    n_left = 1 + max(s[0] for s in spans)
    lefts, rights = rest[:n_left], rest[n_left : n_left + len(spans)]
    small = rest[n_left + len(spans)] if extra[0] else None
    keep, send, *turned = rest[n_left + len(spans) + extra[0] + extra[1] :]
    step = pl.program_id(0)

    @pl.when(step == 0)
    def _():
        for left, out in zip(lefts, turned):
            out[...] = left[...].T

    for left, right, first, count in spans:

        @pl.when((step >= first) & (step < first + count))
        def _(left=left, right=right, first=first):
            columns = pl.ds(pl.multiple_of((step - first) * chunk, chunk), chunk)
            deal(core[0], dot(turned[left][...], rights[right][:, columns], (1, 0)), rows, keep, send)

    if small is not None:

        @pl.when(step == pl.num_programs(0) - 1)
        def _():
            deal(core[0], small[...], rows, keep, send)


def product_grads(core, lefts, rights, rows, chunk, small=None, after=()):
    width = lefts[0].shape[1]
    spans, first = [], 0
    for i, right in enumerate(rights):
        spans.append((i, i, first, right.shape[1] // chunk))
        first += right.shape[1] // chunk
    steps = first + (small is not None)
    half = jax.ShapeDtypeStruct((width // 2, steps * chunk), jnp.bfloat16)
    block = pl.BlockSpec((width // 2, chunk), lambda j: (0, j))
    whole = lambda array: pl.BlockSpec(array.shape, lambda j: (0, 0))
    smalls = [] if small is None else [small]
    return pl.pallas_call(
        functools.partial(
            product_grads_kernel, spans=spans, extra=(len(smalls), len(after)), rows=rows, chunk=chunk
        ),
        grid=(steps,),
        out_shape=(half, half),
        in_specs=[smem] + [whole(x) for x in (*lefts, *rights, *smalls)] + [anywhere] * len(after),
        out_specs=(block, block),
        scratch_shapes=[pltpu.VMEM(x.shape[::-1], jnp.bfloat16) for x in lefts],
        compiler_params=kernel_params(44),
        cost_estimate=cost(sum(2.5 * x.shape[0] * width * y.shape[1] for x, y in zip(lefts, rights)), 20),
    )(core, *lefts, *rights, *smalls, *after)


def exchange(values, bit):
    count = lax.axis_size(AXES)
    return lax.ppermute(values, AXES, [(i, i ^ (1 << bit)) for i in range(count)])


class Chain:
    def __init__(self, parts, rows, order):
        bits = lax.axis_size(AXES).bit_length() - 1
        self.bits = list(range(1, bits))[::-1]
        self.order = [b for b in order if b < bits] + [b for b in range(3, bits)]
        self.parts = []
        for keep, send in parts:
            shape = (2,) * len(self.bits) + (rows, keep.shape[-1])
            self.parts.append((keep.reshape(shape), exchange(send, 0).reshape(shape)))

    def pick(self, bit, other):
        mine = (lax.axis_index(AXES) >> bit) & 1
        take = functools.partial(
            lax.dynamic_index_in_dim,
            index=1 - mine if other else mine,
            axis=self.bits.index(bit),
            keepdims=False,
        )
        sums = [take(a).astype(jnp.float32) + take(b).astype(jnp.float32) for a, b in self.parts]
        return jnp.concatenate(sums, axis=-1).astype(jnp.bfloat16)

    def step(self):
        bit = self.order.pop(0)
        self.send = self.pick(bit, True)
        keep = self.pick(bit, False)
        self.bits = [b for b in self.bits if b != bit]
        self.parts = [(keep, exchange(self.send, bit))]
        return self.send

    def finish(self):
        while self.order:
            self.step()
        [(keep, arrived)] = self.parts
        return keep.astype(jnp.float32) + arrived.astype(jnp.float32)


def body(
    target_in,
    memory,
    block_rows,
    pad_rows,
    seq_lengths,
    self_qkv,
    self_out,
    cross_query,
    cross_kv,
    cross_out,
    ffn_in,
    ffn_out,
    norm_scale,
    small_bias,
    ffn_bias,
    cotangent,
):
    width = target_in.shape[1]
    owned = self_qkv.shape[0]
    core = (lax.axis_index(AXES) & 1).reshape(1)
    pack = jnp.concatenate([norm_scale.T, small_bias.T, ffn_bias.reshape(owned, -1)], axis=1)
    small_cols = pack.shape[1]
    pack = jnp.pad(pack, ((0, 0), (0, -small_cols % 128)))
    attn = lax.all_gather(
        jnp.concatenate([self_qkv, self_out, cross_query, cross_kv, cross_out, pack], axis=1),
        AXES,
        axis=0,
        tiled=True,
    )
    w_qkv = attn[:, : 3 * width]
    w_self = attn[:, 3 * width : 4 * width]
    w_query = attn[:, 4 * width : 5 * width]
    w_pairs = attn[:, 5 * width : 7 * width]
    w_cross = attn[:, 7 * width : 8 * width]
    small = attn[:, 8 * width : 8 * width + small_cols].astype(jnp.float32)
    gains = small[:, :3].T
    biases = small[:, 3:13].T
    in_bias = small[:, 13:].reshape(1, -1)
    w_in = lax.all_gather(ffn_in, AXES, axis=0, tiled=True)
    w_out = lax.all_gather(ffn_out, AXES, axis=0, tiled=True)

    bound = memory_bounds(block_rows[0], pad_rows[0])
    lengths = seq_lengths[0]
    zeros = jnp.zeros((width,), jnp.float32)
    qkv = (matmul(target_in, w_qkv) + jnp.concatenate([biases[0], zeros, biases[1]])).astype(
        jnp.bfloat16
    )
    self_context, self_summary = self_forward(lengths, qkv)
    first, first_unit, first_inverse = normalize(
        target_in.astype(jnp.float32) + matmul(self_context, w_self) + biases[2],
        gains[0],
        biases[7],
    )
    first_low = first.astype(jnp.bfloat16)
    cross_q = (matmul(first_low, w_query) + biases[3]).astype(jnp.bfloat16)
    cross_pairs = (matmul(memory, w_pairs) + jnp.concatenate([zeros, biases[4]])).astype(
        jnp.bfloat16
    )
    cross_context, cross_summary = cross_forward(bound, cross_q, cross_pairs)
    second, second_unit, second_inverse = normalize(
        first + matmul(cross_context, w_cross) + biases[5], gains[1], biases[8]
    )

    vectors = jnp.concatenate([biases[6:7], gains[2:3], biases[9:10], jnp.zeros((5, width), jnp.float32)])
    hidden, slope, block_out, third_grad, out_grad, third_sums = ffn_forward(
        second, w_in, in_bias, w_out, cotangent, vectors
    )
    keep, send = ffn_out_grads(core, hidden, out_grad, ffn_out.shape[0])
    out_chain = Chain([(keep, send)], ffn_out.shape[0], [2, 1])
    keep, send, ffn_bias_grad, second_grad, cross_branch, second_sums = ffn_backward(
        core,
        second,
        w_in,
        w_out,
        slope,
        third_grad,
        out_grad,
        second_unit,
        second_inverse,
        gains[1:2],
        owned,
        after=(send,),
    )
    in_chain = Chain([(keep, send)], owned, [1, 2])

    context_grad = inner_cols(cross_branch, w_cross).astype(jnp.bfloat16)
    query_delta, pair_delta = cross_backward(
        bound,
        cross_q,
        cross_pairs,
        context_grad,
        cross_summary,
        after=(out_chain.step(), in_chain.step()),
    )
    keep, send = product_grads(
        core,
        [first_low, memory, cross_context],
        [query_delta, pair_delta, cross_branch],
        owned,
        512,
    )
    cross_chain = Chain([(keep, send)], owned, [2, 1])

    first_total = second_grad + inner_cols(query_delta, w_query)
    first_grad = normalize_back(first_total, first_unit, first_inverse, gains[0])
    self_branch = first_grad.astype(jnp.bfloat16)
    self_context_grad = inner_cols(self_branch, w_self).astype(jnp.bfloat16)
    qkv_delta = self_backward(lengths, qkv, self_context_grad, self_summary, after=(send,))
    keep, send = product_grads(core, [target_in, self_context], [qkv_delta, self_branch], owned, 512)

    norm_grad = jnp.stack([jnp.sum(first_total * first_unit, axis=0), second_sums[0], third_sums[0]])
    bias_grad = jnp.stack(
        [
            column_sums(qkv_delta[:, :width]),
            column_sums(qkv_delta[:, 2 * width :]),
            column_sums(self_branch),
            column_sums(query_delta),
            column_sums(pair_delta[:, width:]),
            second_sums[2],
            third_sums[2],
            jnp.sum(first_total, axis=0),
            second_sums[1],
            third_sums[1],
        ]
    )
    small_grad = jnp.concatenate(
        [norm_grad.T, bias_grad.T, ffn_bias_grad.reshape(width, -1)], axis=1
    )
    small_grad = jnp.pad(small_grad, ((0, 0), (0, -small_cols % 128))).astype(jnp.bfloat16)
    small_grad = small_grad.reshape(-1, 2, owned, small_grad.shape[1])
    small_keep, small_send = [
        lax.dynamic_index_in_dim(small_grad, i, 1, keepdims=False).reshape(width // 2, -1)
        for i in (core[0], 1 - core[0])
    ]
    self_chain = Chain([(keep, send), (small_keep, small_send)], owned, [1, 2])
    memory_grad = inner_cols(pair_delta, w_pairs)
    target_grad = first_grad + inner_cols(qkv_delta, w_qkv)
    ffn_out_shard = out_chain.finish()
    ffn_in_shard = in_chain.finish()
    cross_shard = cross_chain.finish()
    self_shard = self_chain.finish()
    small_shard = self_shard[:, 4 * width : 4 * width + small_cols]
    return (
        block_out,
        target_grad,
        memory_grad,
        self_shard[:, : 3 * width],
        self_shard[:, 3 * width : 4 * width],
        cross_shard[:, :width],
        cross_shard[:, width : 3 * width],
        cross_shard[:, 3 * width :],
        ffn_in_shard,
        ffn_out_shard,
        small_shard[:, :3].T,
        small_shard[:, 3:13].T,
        small_shard[:, 13:].reshape(-1),
    )


def solution(mesh):
    in_specs = (
        P(("wide", "narrow"), None),
        P(("wide", "narrow"), None),
        P(("wide", "narrow"), None),
        P(("wide", "narrow"), None),
        P(("wide", "narrow"), None),
        P(("wide", "narrow"), None),
        P(("wide", "narrow"), None),
        P(("wide", "narrow"), None),
        P(("wide", "narrow"), None),
        P(("wide", "narrow"), None),
        P(("wide", "narrow"), None),
        P(("wide", "narrow"), None),
        P(None, ("wide", "narrow")),
        P(None, ("wide", "narrow")),
        P(("wide", "narrow")),
        P(("wide", "narrow"), None),
    )
    out_specs = (
        P(("wide", "narrow"), None),
        P(("wide", "narrow"), None),
        P(("wide", "narrow"), None),
        P(("wide", "narrow"), None),
        P(("wide", "narrow"), None),
        P(("wide", "narrow"), None),
        P(("wide", "narrow"), None),
        P(("wide", "narrow"), None),
        P(("wide", "narrow"), None),
        P(("wide", "narrow"), None),
        P(None, ("wide", "narrow")),
        P(None, ("wide", "narrow")),
        P(("wide", "narrow")),
    )
    return jax.shard_map(body, mesh=mesh, in_specs=in_specs, out_specs=out_specs, check_vma=False)
```

time: 732 us -> 600 us (0.82)
  matrix products: 214 us -> 46.9 us
  Pallas kernels: 0 us -> 93.5 us
  local copies, waits for them, and re-layouts: 97.5 us -> 29.6 us
  waiting for transfers between devices: 313 us -> 350 us
  other arithmetic: 55.6 us -> 33.3 us
    dot_general x41 -> x0, matrix products: 116 us -> none  [the longest x7 31.8 us: inner_rows(): lax.dot_general(first, second, (((0,), (0,)), ((), ())), preferred_elemen...]
    pallas_call x0 -> x9, Pallas kernels: none -> 93.5 us  [the longest x2 20.9 us: product_grads(): pl.pallas_call(functools.partial(product_grads_kernel, spans=spans, extra...]
    all_gather x2, waiting for transfers between devices: 48.1 us -> 122 us  [the longest x1 79.1 us: body(): w_out = lax.all_gather(ffn_out, AXES, axis=0, tiled=True)]
    ppermute x21, waiting for transfers between devices: 149 us -> 109 us  [exchange(): return lax.ppermute(values, AXES, [(i, i ^ 1 << bit) for i in range(count)])]
    dot_general x7 -> x5, matrix products: 55.2 us -> 21.6 us  [matmul(): return jnp.dot(first, second, preferred_element_type=jnp.float32)]
    convert_element_type x4 -> x1, local copies, waits for them, and re-layouts: 18.5 us -> 0.07 us  [pick(): return jnp.concatenate(sums, axis=-1).astype(jnp.bfloat16)]
    dot_general x7 -> x5, matrix products: 42.9 us -> 25.3 us  [inner_cols(): lax.dot_general(first, second, (((1,), (1,)), ((), ())), preferred_elemen...]
    reduce_sum x8 -> x1, other arithmetic: 11.8 us -> 0.12 us  [memory_bounds(): starts = jnp.sum(jnp.where(before, block_rows[None, :], 0), axis=1)]
  transfers between devices with their start and end apart: 24 -> 24, of which waited for: 14 -> 13; matrix products, arithmetic and copies ran while one was open for 29% -> 15% of each run, Pallas kernels for 0% -> 12%
where the time goes in v2:
time: 600 us; the launch traced here: 590 us
  waiting for transfers between devices  350 us (58%)
  Pallas kernels  93.5 us (16%)
  matrix products  46.9 us (8%)
  other arithmetic  33.3 us (6%)
  local copies, waits for them, and re-layouts  29.6 us (5%)
  starting transfers between devices  22.3 us (4%)
  between operations  14.8 us (2%)
    all_gather x1, waiting for transfers between devices, body(): lax.all_gather(jnp.concatenate([self_qkv, self_out, cross_query, cross_kv...  117 us
    ppermute x21, waiting for transfers between devices, exchange(): return lax.ppermute(values, AXES, [(i, i ^ 1 << bit) for i in range(count)])  109 us
    all_gather x1, waiting for transfers between devices, body(): w_out = lax.all_gather(ffn_out, AXES, axis=0, tiled=True)  79.1 us
    all_gather x1, waiting for transfers between devices, body(): w_in = lax.all_gather(ffn_in, AXES, axis=0, tiled=True)  43.4 us
    dot_general x5, matrix products, inner_cols(): lax.dot_general(first, second, (((1,), (1,)), ((), ())), preferred_elemen...  25.3 us
    convert_element_type x20, other arithmetic, pick(): return jnp.concatenate(sums, axis=-1).astype(jnp.bfloat16)  23.7 us
    ppermute x21, starting transfers between devices, exchange(): return lax.ppermute(values, AXES, [(i, i ^ 1 << bit) for i in range(count)])  22.1 us
    dot_general x5, matrix products, matmul(): return jnp.dot(first, second, preferred_element_type=jnp.float32)  21.6 us
  transfers between devices with their start and end apart: 24, of which 13 were waited for; matrix products, arithmetic and copies ran while one was open for 15% of the time, Pallas kernels for 12%

profile of v2, /device:TPU:0, one launch (start us, length us, event | category | flops | bytes accessed | tf_op | source)
XLA Modules:
  0.0 590.3 jit_solution(13908468365275496789)
XLA Ops:
  16.7 117.1 %all-gather.4.cloned.1.call-done = bf16[1024,8320]{1,0:T(8,128)(2,1)} async-done(((bf16[32,8320]{1,0:T(8,128)(2,1)}), bf16[1024,8320]{1,0:T(8,128)(2,1)}) %all-gather.4.cloned.1.call-update) | async-done | bytes 17039376 | tf_op jit(solution)/shard_map/all_gather | solution.py:608
  135.7 5.6 fusion.7.qkv
  141.3 3.5 shard_map.255
  144.9 3.0 fusion.102
  148.6 2.7 add_convert_fusion.12.q
  152.2 7.2 %fusion.6.pairs = bf16[1024,2048]{1,0:T(8,128)(2,1)S(1)} fusion(f32[2048]{0:T(1024)S(1)} %concatenate.30, bf16[1024,1024]{1,0:T(8,128)(2,1)S(1)} %copy-done.12, bf16[1024,8320]{1,0:T(8,128)(2,1)} %all-gather.4.cloned.1.call-done), kind=kOutput, calls=%fused_computation.6 | convolution fusion | flops 4299161600 | bytes 10493952 | tf_op jit(solution)/shard_map/dot_general | solution.py:33
  159.5 5.7 shard_map.256
  165.2 3.0 fusion.103
  169.1 43.4 %all-gather.6.cloned.1.call-done.w_in = bf16[1024,4096]{1,0:T(8,128)(2,1)} async-done(((bf16[32,4096]{1,0:T(8,128)(2,1)}), bf16[1024,4096]{1,0:T(8,128)(2,1)}) %all-gather.6.cloned.1.call-update) | async-done | bytes 8388624 | tf_op jit(solution)/shard_map/all_gather | solution.py:623
  212.5 79.1 %all-gather.8.cloned.1.call-done.w_out = bf16[4096,1024]{1,0:T(8,128)(2,1)} async-done(((bf16[128,1024]{1,0:T(8,128)(2,1)}), bf16[4096,1024]{1,0:T(8,128)(2,1)}) %all-gather.8.cloned.1.call-update) | async-done | bytes 8388624 | tf_op jit(solution)/shard_map/all_gather | solution.py:624
  292.6 15.4 %shard_map.257 = (bf16[384,4096]{1,0:T(8,128)(2,1)S(1)}, bf16[384,4096]{1,0:T(8,128)(2,1)S(1)}, bf16[384,1024]{1,0:T(8,128)(2,1)}, f32[384,1024]{1,0:T(8,128)S(1...) custom-call(f32[384,1024]{1,0:T(8,128)S(1)} %get-tuple-element.122.second, ...), custom_call_target="tpu_custom_call" | custom-call | flops 16000000000 | bytes 27262976 | tf_op jit(solution)/shard_map/pallas_call | solution.py:369
  308.1 6.6 %shard_map.258 = (bf16[2048,1024]{1,0:T(8,128)(2,1)S(1)}, bf16[2048,1024]{1,0:T(8,128)(2,1)}) custom-call(s32[1]{0:T(128)} %bitcast.19.core, bf16[384,4096]{1,0:T(8,128)(2,1)S(1)} %get-tuple-element.43.hidden, bf16[384,1024]{1,0:T(8,128)(2,1)S(1)} %get-tuple-element.42.out_grad), custom_call_target="tpu_custom_call" | custom-call | flops 8000000000 | bytes 12582912 | tf_op jit(solution)/shard_map/pallas_call | solution.py:408
  314.7 2.0 copy-done
  317.0 18.8 %shard_map.259 = (bf16[512,4096]{1,0:T(8,128)(2,1)}, bf16[512,4096]{1,0:T(8,128)(2,1)}, f32[1,4096]{1,0:T(1,128)S(1)}, f32[384,1024]{1,0:T(8,128)S(1)}, bf16[384...) custom-call(s32[1]{0:T(128)} %bitcast.19.core, f32[384,1024]{1,0:T(8,128)S(1)} %get-tuple-element.122.second, ...), custom_call_target="tpu_custom_call" | custom-call | flops 24000000000 | bytes 33554432 | tf_op jit(solution)/shard_map/pallas_call | solution.py:458
  338.8 3.9 fusion.51.grad
  342.7 4.0 fusion.13.rest_0_
  348.2 3.7 fusion.14.rest_1_
  352.6 16.0 %shard_map.260 = (bf16[384,1024]{1,0:T(8,128)(2,1)}, bf16[1024,2048]{1,0:T(8,128)(2,1)}) custom-call(s32[2,3]{1,0:T(2,128)} %copy-done.10, bf16[384,1024]{1,0:T(8,128)(2,1)} %copy-done.28, bf16[1024,2048]{1,0:T(8,128)(2,1)} %copy-done.29, bf16[384,1024]{1,0:T(8,128)(2,1)} %fusion.51.grad, f32[3,8,1,256]{3,2,1,0:T(1,128)} %copy-done.31, ...), custom_call_target="tpu_custom_call" | custom-call | flops 16000000000 | bytes 12582912 | tf_op jit(solution)/shard_map/pallas_call | solution.py:199
  368.6 2.1 slice_reduce_fusion
  370.7 13.2 %shard_map.261 = (bf16[512,4096]{1,0:T(8,128)(2,1)S(1)}, bf16[512,4096]{1,0:T(8,128)(2,1)}) custom-call(s32[1]{0:T(128)} %bitcast.19.core, bf16[384,1024]{1,0:T(8,128)(2,1)S(1)} %copy-done.7, bf16[1024,1024]{1,0:T(8,128)(2,1)S(1)} %copy-done.13, bf16[384,1024]{1,0:T(8,128)(2,1)S(1)} %copy-done.23, bf16[384,1024]{1,0:T(8,128)(2,1)S(1)} %copy-done.5, ...), custom_call_target="tpu_custom_call" | custom-call | flops 7381975040 | bytes 20971520 | tf_op jit(solution)/shard_map/pallas_call | solution.py:529
  385.1 3.3 multiply_reduce_fusion
  388.5 1.7 fusion.96
  390.2 2.9 fusion.48.grad
  393.4 6.6 %shard_map.262.rest_2_ = bf16[384,3072]{1,0:T(8,128)(2,1)S(1)} custom-call(s32[3]{0:T(128)S(1)} %bitcast.218, bf16[384,3072]{1,0:T(8,128)(2,1)S(1)} %copy-done.27, bf16[384,1024]{1,0:T(8,128)(2,1)S(1)} %fusion.48.grad, f32[3,8,1,256]{3,2,1,0:T(1,128)S(1)} %get-tuple-element.52.summary, bf16[512,4096]{1,0:T(8,128)(2,1)S(1)} %copy-done.11), custom_call_target="tpu_custom_call" | custom-call | flops 4000000000 | bytes 6291456 | tf_op jit(solution)/shard_map/pallas_call | solution.py:291
  405.7 7.7 %shard_map.263 = (bf16[512,4096]{1,0:T(8,128)(2,1)S(1)}, bf16[512,4096]{1,0:T(8,128)(2,1)}) custom-call(s32[1]{0:T(128)} %bitcast.19.core, bf16[384,1024]{1,0:T(8,128)(2,1)S(1)} %copy-done.16, bf16[384,1024]{1,0:T(8,128)(2,1)S(1)} %copy-done.25, bf16[384,3072]{1,0:T(8,128)(2,1)S(1)} %shard_map.262.rest_2_, bf16[384,1024]{1,0:T(8,128)(2,1)S(1)} %copy-done.9), custom_call_target="tpu_custom_call" | custom-call | flops 4026531840 | bytes 20971520 | tf_op jit(solution)/shard_map/pallas_call | solution.py:529
  413.4 2.6 add_convert_fusion.3
  416.2 8.5 %fusion.10 = f32[1024,1024]{1,0:T(8,128)} fusion(bf16[1024,2048]{1,0:T(8,128)(2,1)S(1)} %copy-done.37, bf16[1024,8320]{1,0:T(8,128)(2,1)} %all-gather.4.cloned.1.call-done), kind=kOutput, calls=%fused_computation.16 | convolution fusion | flops 4294967296 | bytes 12582912 | tf_op jit(solution)/shard_map/dot_general | solution.py:37
  424.8 2.6 add_convert_fusion.2
  427.4 1.8 fusion.61
  429.2 3.0 collective-permute-start.18
  433.6 1.6 collective-permute-start.14
  435.6 1.6 fusion.18
  437.2 1.5 fusion.19
  438.7 17.1 %collective-permute-done.18 = bf16[2,2,128,1024]{3,2,1,0:T(8,128)(2,1)S(1)} collective-permute-done((bf16[2,2,128,1024]{3,2,1,0:T(8,128)(2,1)S(1)}, bf16[2,2,128,1024]{3,2,1,0:T(8,128)(2,1)S(1)}, u32[]{:S(2)}, u32[]{:S(2)}) %collective-permute-start.18) | collective-permute-done | bytes 1048608 | tf_op jit(solution)/shard_map/ppermute | solution.py:545
  456.3 3.0 collective-permute-start.19
  459.6 2.6 collective-permute-start.15
  462.2 2.7 constant_dynamic-slice_fusion.7
  466.7 1.6 fusion.16
  469.7 6.6 %fusion.45 = f32[384,1024]{1,0:T(8,128)} fusion(f32[384,1024]{1,0:T(8,128)S(1)} %copy-done.36, bf16[384,3072]{1,0:T(8,128)(2,1)S(1)} %shard_map.262.rest_2_, bf16[1024,8320]{1,0:T(8,128)(2,1)} %all-gather.4.cloned.1.call-done), kind=kOutput, calls=%fused_computation.69 | convolution fusion | flops 2416312320 | bytes 11796480 | tf_op jit(solution)/shard_map/dot_general | solution.py:37
  477.5 10.5 %collective-permute-done.15 = bf16[2,32,4096]{2,1,0:T(8,128)(2,1)S(1)} collective-permute-done((bf16[2,32,4096]{2,1,0:T(8,128)(2,1)S(1)}, bf16[2,32,4096]{2,1,0:T(8,128)(2,1)S(1)}, u32[]{:S(2)}, u32[]{:S(2)}) %collective-permute-start.15) | collective-permute-done | bytes 524320 | tf_op jit(solution)/shard_map/ppermute | solution.py:545
  489.1 23.1 %collective-permute-done.9 = bf16[2,2,2,32,4096]{4,3,0,2,1:T(8,128)(2,1)S(1)} collective-permute-done((bf16[2,2,2,32,4096]{4,3,0,2,1:T(8,128)(2,1)S(1)}, bf16[2,2,2,32,4096]{4,3,0,2,1:T(8,128)(2,1)S(1)}, u32[]{:S(2)}, u32[]{:S(2)}) %collective-permute-start.9) | collective-permute-done | bytes 2097184 | tf_op jit(solution)/shard_map/ppermute | solution.py:545
  513.7 4.3 collective-permute-done.4
  518.7 1.6 collective-permute-start.5
  521.2 17.2 %collective-permute-done.10 = bf16[2,2,32,4096]{3,2,1,0:T(8,128)(2,1)S(1)} collective-permute-done((bf16[2,2,32,4096]{3,2,1,0:T(8,128)(2,1)S(1)}, bf16[2,2,32,4096]{3,2,1,0:T(8,128)(2,1)S(1)}, u32[]{:S(2)}, u32[]{:S(2)}) %collective-permute-start.10) | collective-permute-done | bytes 1048608 | tf_op jit(solution)/shard_map/ppermute | solution.py:545
  542.1 14.3 %collective-permute-done.11 = bf16[2,32,4096]{2,1,0:T(8,128)(2,1)S(1)} collective-permute-done((bf16[2,32,4096]{2,1,0:T(8,128)(2,1)S(1)}, bf16[2,32,4096]{2,1,0:T(8,128)(2,1)S(1)}, u32[]{:S(2)}, u32[]{:S(2)}) %collective-permute-start.11) | collective-permute-done | bytes 524320 | tf_op jit(solution)/shard_map/ppermute | solution.py:545
  556.5 10.9 %collective-permute-done.6 = bf16[2,32,4224]{2,1,0:T(8,128)(2,1)S(1)} collective-permute-done((bf16[2,32,4224]{2,1,0:T(8,128)(2,1)S(1)}, bf16[2,32,4224]{2,1,0:T(8,128)(2,1)S(1)}, u32[]{:S(2)}, u32[]{:S(2)}) %collective-permute-start.6) | collective-permute-done | bytes 540704 | tf_op jit(solution)/shard_map/ppermute | solution.py:545
  567.5 7.0 %collective-permute-done.12 = bf16[32,4096]{1,0:T(8,128)(2,1)S(1)} collective-permute-done((bf16[32,4096]{1,0:T(8,128)(2,1)S(1)}, bf16[32,4096]{1,0:T(8,128)(2,1)S(1)}, u32[]{:S(2)}, u32[]{:S(2)}) %collective-permute-start.12) | collective-permute-done | bytes 262176 | tf_op jit(solution)/shard_map/ppermute | solution.py:545
  576.0 4.0 collective-permute-done.7
  (205 shorter events, 47.7 us)
Async XLA Ops:
  7.2 9.4 %copy-start.39 = (s32[1,3]{1,0:T(1,128)S(1)}, s32[1,3]{1,0:T(1,128)}, u32[]{:S(2)}) copy-start(s32[1,3]{1,0:T(1,128)} %param.18) | copy-start | bytes 40
  7.2 9.5 %copy-start.40 = (s32[1,3]{1,0:T(1,128)S(1)}, s32[1,3]{1,0:T(1,128)}, u32[]{:S(2)}) copy-start(s32[1,3]{1,0:T(1,128)} %param.19) | copy-start | bytes 40
  7.2 126.6 %all-gather.4.cloned.1.call-start = ((), (), s32[]{:S(2)}) async-start(), calls=%async_computation | async-start | bytes 17571840 | tf_op jit(solution)/shard_map/all_gather | solution.py:608
  8.2 127.5 %copy-start.15 = (bf16[384,1024]{1,0:T(8,128)(2,1)S(1)}, bf16[384,1024]{1,0:T(8,128)(2,1)}, u32[]{:S(2)}) copy-start(bf16[384,1024]{1,0:T(8,128)(2,1)} %rest_0_.1) | copy-start | bytes 2359300
  15.0 197.5 %all-gather.6.cloned.1.call-start = ((), (), s32[]{:S(2)}) async-start(), calls=%async_computation.1 | async-start | bytes 8650752 | tf_op jit(solution)/shard_map/all_gather | solution.py:623
  15.7 275.8 %all-gather.8.cloned.1.call-start = ((), (), s32[]{:S(2)}) async-start(), calls=%async_computation.2 | async-start | bytes 8650752 | tf_op jit(solution)/shard_map/all_gather | solution.py:624
  16.7 142.7 %copy-start.10 = (s32[2,3]{1,0:T(2,128)}, s32[2,3]{1,0:T(2,128)S(1)}, u32[]{:S(2)}) copy-start(s32[2,3]{1,0:T(2,128)S(1)} %pad_add_fusion.bound) | copy-start | bytes 76
  135.7 5.7 copy-start.17
  141.3 3.6 copy-start.26
  147.9 17.3 %copy-start.32 = (f32[384,1024]{1,0:T(8,128)}, f32[384,1024]{1,0:T(8,128)S(1)}, u32[]{:S(2)}) copy-start(f32[384,1024]{1,0:T(8,128)S(1)} %get-tuple-element.168) | copy-start | bytes 4718596
  148.6 3.7 copy-start.12
  152.2 7.2 %copy-start.28 = (bf16[384,1024]{1,0:T(8,128)(2,1)}, bf16[384,1024]{1,0:T(8,128)(2,1)S(1)}, u32[]{:S(2)}) copy-start(bf16[384,1024]{1,0:T(8,128)(2,1)S(1)} %add_convert_fusion.12.q) | copy-start | bytes 2359300
  159.4 5.7 copy-start.29
  308.1 6.7 %copy-start.30 = (bf16[384,4096]{1,0:T(8,128)(2,1)}, bf16[384,4096]{1,0:T(8,128)(2,1)S(1)}, u32[]{:S(2)}) copy-start(bf16[384,4096]{1,0:T(8,128)(2,1)S(1)} %get-tuple-element.40.slope) | copy-start | bytes 9437188
  316.7 26.1 %collective-permute-start = (bf16[2048,1024]{1,0:T(8,128)(2,1)}, bf16[2048,1024]{1,0:T(8,128)(2,1)}, u32[]{:S(2)}, u32[]{:S(2)}) collective-permute-start(bf16[2048,1024]{1,0:T(8,128)(2,1)} %get-tuple-element.44.rest_0_), channel_id=1, source_target_pairs={{0,1},{1,0},{2,3},{3,2},{4,5},{5,4},{6,7},{7,6},{8,9},{9,8},{10,11... | collective-permute-start | bytes 12582920 | tf_op jit(solution)/shard_map/ppermute | solution.py:545
  337.8 10.5 %collective-permute-start.1 = (bf16[512,4096]{1,0:T(8,128)(2,1)}, bf16[512,4096]{1,0:T(8,128)(2,1)}, u32[]{:S(2)}, u32[]{:S(2)}) collective-permute-start(bf16[512,4096]{1,0:T(8,128)(2,1)} %get-tuple-element.50), channel_id=1, source_target_pairs={{0,1},{1,0},{2,3},{3,2},{4,5},{5,4},{6,7},{7,6},{8,9},{9,8},{10,11... | collective-permute-start | bytes 12582920 | tf_op jit(solution)/shard_map/ppermute | solution.py:545
  338.8 3.9 copy-start.1
  342.7 5.5 copy-start.34
  346.8 80.6 %collective-permute-start.17 = (bf16[2,2,2,128,1024]{4,3,2,1,0:T(8,128)(2,1)}, bf16[2,2,2,128,1024]{4,3,2,1,0:T(8,128)(2,1)}, u32[]{:S(2)}, u32[]{:S(2)}) collective-permute-start(bf16[2,2,2,128,1024]{4,3,2,1,0:T(8,128)(2,1)} %fusion.13.rest_0_), channel_id=1, source_target_pairs={{0,4},{1,5},{2,6},{3,7},{4,0},{5,1},{6,2},{7,3},{8,12},{9,13},{10,... | collective-permute-start | bytes 6291464 | tf_op jit(solution)/shard_map/ppermute | solution.py:545
  352.0 80.2 %collective-permute-start.13 = (bf16[2,2,2,32,4096]{4,3,2,1,0:T(8,128)(2,1)}, bf16[2,2,2,32,4096]{4,3,2,1,0:T(8,128)(2,1)}, u32[]{:S(2)}, u32[]{:S(2)}) collective-permute-start(bf16[2,2,2,32,4096]{4,3,2,1,0:T(8,128)(2,1)} %fusion.14.rest_1_), channel_id=1, source_target_pairs={{0,2},{1,3},{2,0},{3,1},{4,6},{5,7},{6,4},{7,5},{8,10},{9,11},{10,... | collective-permute-start | bytes 6291464 | tf_op jit(solution)/shard_map/ppermute | solution.py:545
  352.6 18.1 %copy-start.13 = (bf16[1024,1024]{1,0:T(8,128)(2,1)S(1)}, bf16[1024,1024]{1,0:T(8,128)(2,1)}, u32[]{:S(2)}) copy-start(bf16[1024,1024]{1,0:T(8,128)(2,1)} %rest_1_.1) | copy-start | bytes 6291460
  352.6 18.1 %copy-start.21 = (bf16[384,1024]{1,0:T(8,128)(2,1)S(1)}, bf16[384,1024]{1,0:T(8,128)(2,1)}, u32[]{:S(2)}) copy-start(bf16[384,1024]{1,0:T(8,128)(2,1)} %copy-done.20) | copy-start | bytes 2359300
  352.6 18.1 %copy-start.23 = (bf16[384,1024]{1,0:T(8,128)(2,1)S(1)}, bf16[384,1024]{1,0:T(8,128)(2,1)}, u32[]{:S(2)}) copy-start(bf16[384,1024]{1,0:T(8,128)(2,1)} %copy-done.22) | copy-start | bytes 2359300
  370.7 14.4 %copy-start.19 = (f32[384,1024]{1,0:T(8,128)S(1)}, f32[384,1024]{1,0:T(8,128)}, u32[]{:S(2)}) copy-start(f32[384,1024]{1,0:T(8,128)} %copy-done.18) | copy-start | bytes 4718596
  370.7 14.4 %copy-start.33 = (f32[384,1024]{1,0:T(8,128)S(1)}, f32[384,1024]{1,0:T(8,128)}, u32[]{:S(2)}) copy-start(f32[384,1024]{1,0:T(8,128)} %copy-done.32) | copy-start | bytes 4718596
  383.9 4.5 copy-start.3
  383.9 78.2 %collective-permute-start.8 = (bf16[512,4096]{1,0:T(8,128)(2,1)}, bf16[512,4096]{1,0:T(8,128)(2,1)}, u32[]{:S(2)}, u32[]{:S(2)}) collective-permute-start(bf16[512,4096]{1,0:T(8,128)(2,1)} %get-tuple-element.54.rest_0_), channel_id=1, source_target_pairs={{0,1},{1,0},{2,3},{3,2},{4,5},{5,4},{6,7},{7,6},{8,9},{9,8},{10,11... | collective-permute-start | bytes 12582920 | tf_op jit(solution)/shard_map/ppermute | solution.py:545
  388.5 4.6 copy-start.27
  390.2 3.2 copy-start.11
  401.0 34.6 %collective-permute-start.3 = (bf16[512,128]{1,0:T(8,128)(2,1)S(1)}, bf16[512,128]{1,0:T(8,128)(2,1)S(1)}, u32[]{:S(2)}, u32[]{:S(2)}) collective-permute-start(bf16[512,128]{1,0:T(8,128)(2,1)S(1)} %bitcast.226), channel_id=1, source_target_pairs={{0,1},{1,0},{2,3},{3,2},{4,5},{5,4},{6,7},{7,6},{8,9},{9,8},{10,11... | collective-permute-start | bytes 393224 | tf_op jit(solution)/shard_map/ppermute | solution.py:545
  405.7 7.7 %copy-start.35 = (bf16[512,4096]{1,0:T(8,128)(2,1)S(1)}, bf16[512,4096]{1,0:T(8,128)(2,1)}, u32[]{:S(2)}) copy-start(bf16[512,4096]{1,0:T(8,128)(2,1)} %get-tuple-element.49) | copy-start | bytes 12582916
  413.4 53.3 %collective-permute-start.2 = (bf16[512,4096]{1,0:T(8,128)(2,1)}, bf16[512,4096]{1,0:T(8,128)(2,1)S(1)}, u32[]{:S(2)}, u32[]{:S(2)}) collective-permute-start(bf16[512,4096]{1,0:T(8,128)(2,1)} %get-tuple-element.56), channel_id=1, source_target_pairs={{0,1},{1,0},{2,3},{3,2},{4,5},{5,4},{6,7},{7,6},{8,9},{9,8},{10,11... | collective-permute-start | bytes 12582920 | tf_op jit(solution)/shard_map/ppermute | solution.py:545
  416.2 8.6 %copy-start.2 = (bf16[2048,1024]{1,0:T(8,128)(2,1)S(1)}, bf16[2048,1024]{1,0:T(8,128)(2,1)}, u32[]{:S(2)}) copy-start(bf16[2048,1024]{1,0:T(8,128)(2,1)} %copy-done) | copy-start | bytes 12582916
  427.4 7.9 %copy-start.4 = (bf16[512,4096]{1,0:T(8,128)(2,1)S(1)}, bf16[512,4096]{1,0:T(8,128)(2,1)}, u32[]{:S(2)}) copy-start(bf16[512,4096]{1,0:T(8,128)(2,1)} %copy-done.3) | copy-start | bytes 12582916
  429.2 26.7 %collective-permute-start.18 = (bf16[2,2,128,1024]{3,2,1,0:T(8,128)(2,1)S(1)}, bf16[2,2,128,1024]{3,2,1,0:T(8,128)(2,1)S(1)}, u32[]{:S(2)}, u32[]{:S(2)}) collective-permute-start(bf16[2,2,128,1024]{3,2,1,0:T(8,128)(2,1)S(1)} %fusion.61), channel_id=1, source_target_pairs={{0,2},{1,3},{2,0},{3,1},{4,6},{5,7},{6,4},{7,5},{8,10},{9,11},{10,... | collective-permute-start | bytes 3145736 | tf_op jit(solution)/shard_map/ppermute | solution.py:545
  433.6 25.7 %collective-permute-start.14 = (bf16[2,2,32,4096]{3,2,1,0:T(8,128)(2,1)S(1)}, bf16[2,2,32,4096]{3,2,1,0:T(8,128)(2,1)S(1)}, u32[]{:S(2)}, u32[]{:S(2)}) collective-permute-start(bf16[2,2,32,4096]{3,2,1,0:T(8,128)(2,1)S(1)} %fusion.60), channel_id=1, source_target_pairs={{0,4},{1,5},{2,6},{3,7},{4,0},{5,1},{6,2},{7,3},{8,12},{9,13},{10,... | collective-permute-start | bytes 3145736 | tf_op jit(solution)/shard_map/ppermute | solution.py:545
  456.3 20.0 %collective-permute-start.19 = (bf16[2,128,1024]{2,1,0:T(8,128)(2,1)S(1)}, bf16[2,128,1024]{2,1,0:T(8,128)(2,1)S(1)}, u32[]{:S(2)}, u32[]{:S(2)}) collective-permute-start(bf16[2,128,1024]{2,1,0:T(8,128)(2,1)S(1)} %get-tuple-element.137), channel_id=1, source_target_pairs={{0,8},{1,9},{2,10},{3,11},{4,12},{5,13},{6,14},{7,15},{8,0},{9,1},... | collective-permute-start | bytes 1572872 | tf_op jit(solution)/shard_map/ppermute | solution.py:545
  459.6 28.5 %collective-permute-start.15 = (bf16[2,32,4096]{2,1,0:T(8,128)(2,1)S(1)}, bf16[2,32,4096]{2,1,0:T(8,128)(2,1)S(1)}, u32[]{:S(2)}, u32[]{:S(2)}) collective-permute-start(bf16[2,32,4096]{2,1,0:T(8,128)(2,1)S(1)} %get-tuple-element.139), channel_id=1, source_target_pairs={{0,8},{1,9},{2,10},{3,11},{4,12},{5,13},{6,14},{7,15},{8,0},{9,1},... | collective-permute-start | bytes 1572872 | tf_op jit(solution)/shard_map/ppermute | solution.py:545
  465.7 46.6 %collective-permute-start.9 = (bf16[2,2,2,32,4096]{4,3,0,2,1:T(8,128)(2,1)S(1)}, bf16[2,2,2,32,4096]{4,3,0,2,1:T(8,128)(2,1)S(1)}, u32[]{:S(2)}, u32[]{:S(2)}) collective-permute-start(bf16[2,2,2,32,4096]{4,3,0,2,1:T(8,128)(2,1)S(1)} %fusion.17), channel_id=1, source_target_pairs={{0,4},{1,5},{2,6},{3,7},{4,0},{5,1},{6,2},{7,3},{8,12},{9,13},{10,... | collective-permute-start | bytes 6291464 | tf_op jit(solution)/shard_map/ppermute | solution.py:545
  468.5 49.5 %collective-permute-start.4 = (bf16[2,2,2,32,4224]{4,3,2,1,0:T(8,128)(2,1)S(1)}, bf16[2,2,2,32,4224]{4,3,2,1,0:T(8,128)(2,1)S(1)}, u32[]{:S(2)}, u32[]{:S(2)}) collective-permute-start(bf16[2,2,2,32,4224]{4,3,2,1,0:T(8,128)(2,1)S(1)} %pad_maximum_fusion), channel_id=1, source_target_pairs={{0,2},{1,3},{2,0},{3,1},{4,6},{5,7},{6,4},{7,5},{8,10},{9,11},{10,... | collective-permute-start | bytes 6488072 | tf_op jit(solution)/shard_map/ppermute | solution.py:545
  476.4 64.8 %collective-permute-start.20 = (bf16[128,1024]{1,0:T(8,128)(2,1)S(1)}, bf16[128,1024]{1,0:T(8,128)(2,1)S(1)}, u32[]{:S(2)}, u32[]{:S(2)}) collective-permute-start(bf16[128,1024]{1,0:T(8,128)(2,1)S(1)} %fusion.88), channel_id=1, source_target_pairs={{0,16},{1,17},{2,18},{3,19},{4,20},{5,21},{6,22},{7,23},{8,24},{9,... | collective-permute-start | bytes 786440 | tf_op jit(solution)/shard_map/ppermute | solution.py:545
  488.1 32.2 %collective-permute-start.16 = (bf16[32,4096]{1,0:T(8,128)(2,1)S(1)}, bf16[32,4096]{1,0:T(8,128)(2,1)S(1)}, u32[]{:S(2)}, u32[]{:S(2)}) collective-permute-start(bf16[32,4096]{1,0:T(8,128)(2,1)S(1)} %fusion.86), channel_id=1, source_target_pairs={{0,16},{1,17},{2,18},{3,19},{4,20},{5,21},{6,22},{7,23},{8,24},{9,... | collective-permute-start | bytes 786440 | tf_op jit(solution)/shard_map/ppermute | solution.py:545
  513.0 25.4 %collective-permute-start.10 = (bf16[2,2,32,4096]{3,2,1,0:T(8,128)(2,1)S(1)}, bf16[2,2,32,4096]{3,2,1,0:T(8,128)(2,1)S(1)}, u32[]{:S(2)}, u32[]{:S(2)}) collective-permute-start(bf16[2,2,32,4096]{3,2,1,0:T(8,128)(2,1)S(1)} %copy.167), channel_id=1, source_target_pairs={{0,2},{1,3},{2,0},{3,1},{4,6},{5,7},{6,4},{7,5},{8,10},{9,11},{10,... | collective-permute-start | bytes 3145736 | tf_op jit(solution)/shard_map/ppermute | solution.py:545
  518.7 21.2 %collective-permute-start.5 = (bf16[2,2,32,4224]{3,2,1,0:T(8,128)(2,1)S(1)}, bf16[2,2,32,4224]{3,2,1,0:T(8,128)(2,1)S(1)}, u32[]{:S(2)}, u32[]{:S(2)}) collective-permute-start(bf16[2,2,32,4224]{3,2,1,0:T(8,128)(2,1)S(1)} %get-tuple-element.127), channel_id=1, source_target_pairs={{0,4},{1,5},{2,6},{3,7},{4,0},{5,1},{6,2},{7,3},{8,12},{9,13},{10,... | collective-permute-start | bytes 3244040 | tf_op jit(solution)/shard_map/ppermute | solution.py:545
  538.6 17.7 %collective-permute-start.11 = (bf16[2,32,4096]{2,1,0:T(8,128)(2,1)S(1)}, bf16[2,32,4096]{2,1,0:T(8,128)(2,1)S(1)}, u32[]{:S(2)}, u32[]{:S(2)}) collective-permute-start(bf16[2,32,4096]{2,1,0:T(8,128)(2,1)S(1)} %get-tuple-element.141), channel_id=1, source_target_pairs={{0,8},{1,9},{2,10},{3,11},{4,12},{5,13},{6,14},{7,15},{8,0},{9,1},... | collective-permute-start | bytes 1572872 | tf_op jit(solution)/shard_map/ppermute | solution.py:545
  540.2 27.2 %collective-permute-start.6 = (bf16[2,32,4224]{2,1,0:T(8,128)(2,1)S(1)}, bf16[2,32,4224]{2,1,0:T(8,128)(2,1)S(1)}, u32[]{:S(2)}, u32[]{:S(2)}) collective-permute-start(bf16[2,32,4224]{2,1,0:T(8,128)(2,1)S(1)} %get-tuple-element.135), channel_id=1, source_target_pairs={{0,8},{1,9},{2,10},{3,11},{4,12},{5,13},{6,14},{7,15},{8,0},{9,1},... | collective-permute-start | bytes 1622024 | tf_op jit(solution)/shard_map/ppermute | solution.py:545
  556.4 18.1 %collective-permute-start.12 = (bf16[32,4096]{1,0:T(8,128)(2,1)S(1)}, bf16[32,4096]{1,0:T(8,128)(2,1)S(1)}, u32[]{:S(2)}, u32[]{:S(2)}) collective-permute-start(bf16[32,4096]{1,0:T(8,128)(2,1)S(1)} %fusion.84), channel_id=1, source_target_pairs={{0,16},{1,17},{2,18},{3,19},{4,20},{5,21},{6,22},{7,23},{8,24},{9,... | collective-permute-start | bytes 786440 | tf_op jit(solution)/shard_map/ppermute | solution.py:545
  567.4 12.6 %collective-permute-start.7 = (bf16[32,4224]{1,0:T(8,128)(2,1)S(1)}, bf16[32,4224]{1,0:T(8,128)(2,1)S(1)}, u32[]{:S(2)}, u32[]{:S(2)}) collective-permute-start(bf16[32,4224]{1,0:T(8,128)(2,1)S(1)} %fusion.82), channel_id=1, source_target_pairs={{0,16},{1,17},{2,18},{3,19},{4,20},{5,21},{6,22},{7,23},{8,24},{9,... | collective-permute-start | bytes 811016 | tf_op jit(solution)/shard_map/ppermute | solution.py:545
  (17 other events, 30.8 us)
Sparse Core Ops, SparseCore 0:
  15.1 118.7 all-gather.3
  136.7 75.7 all-gather.5
  215.3 76.1 all-gather.7

commit v3 on v2

v3 whole, which is shorter than its diff:
```python
import functools

import jax
import jax.numpy as jnp
from jax import lax
from jax.experimental import pallas as pl
from jax.experimental.pallas import tpu as pltpu
from jax.sharding import PartitionSpec as P

HEADS = 16
HEAD_DIM = 64
SEQ_LEN = 128
PAIRS = HEADS // 2
neg_fill = -1e30
AXES = ("wide", "narrow")
vmem = pl.BlockSpec(memory_space=pltpu.VMEM)
smem = pl.BlockSpec(memory_space=pltpu.SMEM)
anywhere = pl.BlockSpec(memory_space=pl.ANY)
norm_eps = 1e-05


def kernel_params(megabytes):
    return pltpu.CompilerParams(vmem_limit_bytes=megabytes << 20)


def cost(flops, megabytes, transcendentals=0):
    return pl.CostEstimate(
        flops=int(10 * flops), bytes_accessed=int(10 * megabytes * 2**20), transcendentals=int(10 * transcendentals)
    )


def matmul(first, second):
    return jnp.dot(first, second, preferred_element_type=jnp.float32)


def inner_cols(first, second):
    return lax.dot_general(
        first, second, (((1,), (1,)), ((), ())), preferred_element_type=jnp.float32
    )


def column_sums(values):
    return jnp.sum(values.astype(jnp.float32), axis=0)


def memory_bounds(block_rows, pad_rows):
    count = block_rows.shape[0]
    before = jnp.arange(count)[None, :] < jnp.arange(count)[:, None]
    starts = jnp.sum(jnp.where(before, block_rows[None, :], 0), axis=1)
    valid = jnp.maximum(block_rows - pad_rows, (block_rows + 1) // 2)
    return jnp.stack([starts, starts + valid])


def dot(first, second, contract):
    return lax.dot_general(
        first, second, ((contract[:1], contract[1:]), ((), ())), preferred_element_type=jnp.float32
    )


def cols(pair, base=0):
    return slice((base + pair) * 128, (base + pair + 1) * 128)


def split_heads(block):
    low = lax.broadcasted_iota(jnp.int32, block.shape, 1) < HEAD_DIM
    zero = jnp.zeros_like(block)
    return jnp.concatenate([jnp.where(low, block, zero), jnp.where(low, zero, block)], axis=0)


def join_heads(stacked):
    low = lax.broadcasted_iota(jnp.int32, (SEQ_LEN, 128), 1) < HEAD_DIM
    return jnp.where(low, stacked[:SEQ_LEN], stacked[SEQ_LEN:])


def join_heads_t(stacked):
    both = jnp.concatenate([stacked[:HEAD_DIM, :SEQ_LEN], stacked[HEAD_DIM:, SEQ_LEN:]], axis=0)
    return both.T


def cross_mask(tile, low, high):
    rows = tile * 128 + lax.broadcasted_iota(jnp.int32, (128, 2 * SEQ_LEN), 0)
    return (rows >= low) & (rows < high)


def cross_forward_kernel(bound, q, pairs, *rest, extra):
    context, summary, stack, scores, top, total, acc = rest[extra:]

    def sequence(s, carry):
        low, high = bound[0, s], bound[1, s]
        first, last = low // 128, (high + 127) // 128
        rows = pl.ds(pl.multiple_of(s * SEQ_LEN, SEQ_LEN), SEQ_LEN)
        for p in range(PAIRS):
            stack[p] = split_heads(q[rows, cols(p)] * jnp.bfloat16(HEAD_DIM**-0.5))
        top[...] = jnp.full_like(top, neg_fill)
        total[...] = jnp.zeros_like(total)
        acc[...] = jnp.zeros_like(acc)

        def one(t, carry):
            keys = pl.ds(pl.multiple_of(t * 128, 128), 128)
            ok = cross_mask(t, low, high)
            for p in range(PAIRS):
                raw = jnp.where(ok, dot(pairs[keys, cols(p)], stack[p], (1, 1)), neg_fill)
                scores[t, p] = raw
                top[p] = jnp.maximum(top[p], jnp.max(raw, axis=0, keepdims=True))
            return carry

        lax.fori_loop(first, last, one, 0)

        def two(t, carry):
            keys = pl.ds(pl.multiple_of(t * 128, 128), 128)
            for p in range(PAIRS):
                weights = jnp.exp(scores[t, p] - top[p])
                total[p] += jnp.sum(weights, axis=0, keepdims=True)
                acc[p] += dot(pairs[keys, cols(p, PAIRS)], weights.astype(jnp.bfloat16), (0, 0))
            return carry

        lax.fori_loop(first, last, two, 0)
        for p in range(PAIRS):
            context[rows, cols(p)] = join_heads_t(acc[p] / total[p]).astype(jnp.bfloat16)
            summary[s, p] = top[p] + jnp.log(total[p])
        return carry

    lax.fori_loop(0, bound.shape[1], sequence, 0)


def cross_backward_kernel(bound, q, pairs, summary, branch, weight, *rest, extra):
    out, sums, grad, stack, grads, probs, prob_grads, delta, acc, pair_acc = rest[extra:]
    pair_acc[...] = jnp.zeros_like(pair_acc)
    scale = HEAD_DIM**-0.5
    (tokens, width), mems = q.shape, pairs.shape[0]
    grad[...] = dot(branch[...], weight[...], (1, 1)).astype(jnp.bfloat16)
    keys_at, values_at = 2 * tokens, 2 * tokens + mems

    def sequence(s, carry):
        low, high = bound[0, s], bound[1, s]
        first, last = low // 128, (high + 127) // 128
        rows = pl.ds(pl.multiple_of(s * SEQ_LEN, SEQ_LEN), SEQ_LEN)
        for p in range(PAIRS):
            stack[p] = split_heads(q[rows, cols(p)] * jnp.bfloat16(scale))
            grads[p] = split_heads(grad[rows, cols(p)])
        delta[...] = jnp.zeros_like(delta)
        acc[...] = jnp.zeros_like(acc)

        def one(t, carry):
            keys = pl.ds(pl.multiple_of(t * 128, 128), 128)
            ok = cross_mask(t, low, high)
            for p in range(PAIRS):
                raw = dot(pairs[keys, cols(p)], stack[p], (1, 1))
                weights = jnp.where(ok, jnp.exp(raw - summary[s, p]), 0.0)
                back = dot(pairs[keys, cols(p, PAIRS)], grads[p], (1, 1))
                delta[p] += jnp.sum(weights * back, axis=0, keepdims=True)
                probs[t, p] = weights
                prob_grads[t, p] = back
                pair_acc[keys, cols(p, PAIRS)] += dot(weights.astype(jnp.bfloat16), grads[p], (1, 0))
            return carry

        lax.fori_loop(first, last, one, 0)

        def two(t, carry):
            keys = pl.ds(pl.multiple_of(t * 128, 128), 128)
            for p in range(PAIRS):
                score = (probs[t, p] * (prob_grads[t, p] - delta[p])).astype(jnp.bfloat16)
                pair_acc[keys, cols(p)] += dot(score, stack[p], (1, 0))
                acc[p] += dot(pairs[keys, cols(p)], score, (0, 0))
            return carry

        lax.fori_loop(first, last, two, 0)
        for p in range(PAIRS):
            out[rows, cols(p)] = (join_heads_t(acc[p]) * scale).astype(jnp.bfloat16)
        return carry

    lax.fori_loop(0, bound.shape[1], sequence, 0)
    out[keys_at:values_at, :] = pair_acc[:, :width].astype(jnp.bfloat16)
    out[values_at:, :] = pair_acc[:, width:].astype(jnp.bfloat16)
    out[tokens:keys_at, :] = branch[...]
    sums[...] = sum_rows(out[:tokens, :].astype(jnp.float32), out[values_at:, :].astype(jnp.float32))


def cross_forward(bound, q, pairs, after=()):
    seqs, tiles = bound.shape[1], pairs.shape[0] // 128
    wide = 2 * SEQ_LEN
    return pl.pallas_call(
        functools.partial(cross_forward_kernel, extra=len(after)),
        out_shape=(
            jax.ShapeDtypeStruct(q.shape, jnp.bfloat16),
            jax.ShapeDtypeStruct((seqs, PAIRS, 1, wide), jnp.float32),
        ),
        in_specs=[smem, vmem, vmem] + [anywhere] * len(after),
        out_specs=(vmem, vmem),
        scratch_shapes=[
            pltpu.VMEM((PAIRS, wide, 128), jnp.bfloat16),
            pltpu.VMEM((tiles, PAIRS, 128, wide), jnp.float32),
            pltpu.VMEM((PAIRS, 1, wide), jnp.float32),
            pltpu.VMEM((PAIRS, 1, wide), jnp.float32),
            pltpu.VMEM((PAIRS, 128, wide), jnp.float32),
        ],
        compiler_params=kernel_params(40),
        cost_estimate=cost(8e9, 8),
    )(bound, q, pairs, *after)


def cross_backward(bound, q, pairs, summary, branch, weights, column, after=()):
    seqs, tiles = bound.shape[1], pairs.shape[0] // 128
    wide = 2 * SEQ_LEN
    width = q.shape[1]
    whole = lambda shape: pl.BlockSpec(shape, lambda i: (0,) * len(shape))
    rows = 2 * pairs.shape[0] + 2 * q.shape[0]
    return pl.pallas_call(
        functools.partial(cross_backward_kernel, extra=len(after)),
        grid=(1,),
        out_shape=(
            jax.ShapeDtypeStruct((rows, width), jnp.bfloat16),
            jax.ShapeDtypeStruct((8, width), jnp.float32),
        ),
        in_specs=[smem]
        + [whole(x.shape) for x in (q, pairs, summary, branch)]
        + [pl.BlockSpec((width, width), lambda i: (0, column))]
        + [anywhere] * len(after),
        out_specs=(whole((rows, width)), whole((8, width))),
        scratch_shapes=[
            pltpu.VMEM(q.shape, jnp.bfloat16),
            pltpu.VMEM((PAIRS, wide, 128), jnp.bfloat16),
            pltpu.VMEM((PAIRS, wide, 128), jnp.bfloat16),
            pltpu.VMEM((tiles, PAIRS, 128, wide), jnp.float32),
            pltpu.VMEM((tiles, PAIRS, 128, wide), jnp.float32),
            pltpu.VMEM((PAIRS, 1, wide), jnp.float32),
            pltpu.VMEM((PAIRS, 128, wide), jnp.float32),
            pltpu.VMEM(pairs.shape, jnp.float32),
        ],
        compiler_params=kernel_params(58),
        cost_estimate=cost(16e9, 12),
    )(bound, q, pairs, summary, branch, weights, *after)


def self_mask(length):
    keys = lax.broadcasted_iota(jnp.int32, (SEQ_LEN, 2 * SEQ_LEN), 0)
    tokens = lax.broadcasted_iota(jnp.int32, (SEQ_LEN, 2 * SEQ_LEN), 1) & (SEQ_LEN - 1)
    return (keys <= tokens) & (keys < length)


def self_forward_kernel(lengths, qkv, *rest, extra):
    context, summary = rest[extra:]

    def sequence(s, carry):
        ok = self_mask(lengths[s])
        rows = pl.ds(pl.multiple_of(s * SEQ_LEN, SEQ_LEN), SEQ_LEN)
        for p in range(PAIRS):
            stack = split_heads(qkv[rows, cols(p)] * jnp.bfloat16(HEAD_DIM**-0.5))
            raw = jnp.where(ok, dot(qkv[rows, cols(p, PAIRS)], stack, (1, 1)), neg_fill)
            top = jnp.max(raw, axis=0, keepdims=True)
            weights = jnp.exp(raw - top)
            total = jnp.sum(weights, axis=0, keepdims=True)
            weights = (weights / total).astype(jnp.bfloat16)
            acc = dot(qkv[rows, cols(p, 2 * PAIRS)], weights, (0, 0))
            context[rows, cols(p)] = join_heads_t(acc).astype(jnp.bfloat16)
            summary[s, p] = top + jnp.log(total)
        return carry

    lax.fori_loop(0, lengths.shape[0], sequence, 0)


def self_backward_kernel(
    lengths, qkv, summary, second_grad, query_delta, w_query, w_self, unit, inverse, gain, *rest, extra
):
    out, sums, first_grad, grad = rest[extra:]
    scale = HEAD_DIM**-0.5
    tokens = qkv.shape[0]
    total = second_grad[...] + dot(query_delta[...], w_query[...], (1, 1))
    first = normalize_back(total, unit[...], inverse[...], gain[...])
    first_grad[...] = first
    branch = first.astype(jnp.bfloat16)
    out[3 * tokens :, :] = branch
    grad[...] = dot(branch, w_self[...], (1, 1)).astype(jnp.bfloat16)

    def sequence(s, carry):
        ok = self_mask(lengths[s])
        rows = pl.ds(pl.multiple_of(s * SEQ_LEN, SEQ_LEN), SEQ_LEN)
        for p in range(PAIRS):
            stack = split_heads(qkv[rows, cols(p)] * jnp.bfloat16(scale))
            grads = split_heads(grad[rows, cols(p)])
            keys = qkv[rows, cols(p, PAIRS)]
            raw = dot(keys, stack, (1, 1))
            weights = jnp.where(ok, jnp.exp(raw - summary[s, p]), 0.0)
            back = dot(qkv[rows, cols(p, 2 * PAIRS)], grads, (1, 1))
            delta = jnp.sum(weights * back, axis=0, keepdims=True)
            score = (weights * (back - delta)).astype(jnp.bfloat16)
            value_grad = dot(weights.astype(jnp.bfloat16), grads, (1, 0))
            key_grad = dot(score, stack, (1, 0))
            query_grad = join_heads_t(dot(keys, score, (0, 0))) * scale
            for i, part in enumerate((query_grad, key_grad, value_grad)):
                place = pl.ds(pl.multiple_of(i * tokens + s * SEQ_LEN, SEQ_LEN), SEQ_LEN)
                out[place, cols(p)] = part.astype(jnp.bfloat16)
        return carry

    lax.fori_loop(0, lengths.shape[0], sequence, 0)
    sums[...] = sum_rows(
        *[out[i * tokens : (i + 1) * tokens, :].astype(jnp.float32) for i in (0, 2, 3)],
        total * unit[...],
        total,
    )


def self_forward(lengths, qkv, after=()):
    tokens, width = qkv.shape[0], qkv.shape[1] // 3
    return pl.pallas_call(
        functools.partial(self_forward_kernel, extra=len(after)),
        out_shape=(
            jax.ShapeDtypeStruct((tokens, width), jnp.bfloat16),
            jax.ShapeDtypeStruct((lengths.shape[0], PAIRS, 1, 2 * SEQ_LEN), jnp.float32),
        ),
        in_specs=[smem, vmem] + [anywhere] * len(after),
        out_specs=(vmem, vmem),
        compiler_params=kernel_params(24),
        cost_estimate=cost(2e9, 4),
    )(lengths, qkv, *after)


def self_backward(
    lengths, qkv, summary, second_grad, cross_delta, late, early, unit, inverse, gain, after=()
):
    tokens, width = second_grad.shape
    whole = lambda shape: pl.BlockSpec(shape, lambda i: (0,) * len(shape))
    full = whole((tokens, width))
    return pl.pallas_call(
        functools.partial(self_backward_kernel, extra=len(after)),
        grid=(1,),
        out_shape=(
            jax.ShapeDtypeStruct((4 * tokens, width), jnp.bfloat16),
            jax.ShapeDtypeStruct((8, width), jnp.float32),
            jax.ShapeDtypeStruct((tokens, width), jnp.float32),
        ),
        in_specs=[
            smem,
            whole(qkv.shape),
            whole(summary.shape),
            full,
            full,
            pl.BlockSpec((width, width), lambda i: (0, 0)),
            pl.BlockSpec((width, width), lambda i: (0, 3)),
            full,
            whole((tokens, 1)),
            whole((1, width)),
        ]
        + [anywhere] * len(after),
        out_specs=(whole((4 * tokens, width)), whole((8, width)), full),
        scratch_shapes=[pltpu.VMEM((tokens, width), jnp.bfloat16)],
        compiler_params=kernel_params(48),
        cost_estimate=cost(6e9, 12),
    )(lengths, qkv, summary, second_grad, cross_delta, late, early, unit, inverse, gain, *after)


def normalize(values, gain, shift):
    centered = values - jnp.mean(values, axis=-1, keepdims=True)
    inverse = lax.rsqrt(jnp.mean(centered * centered, axis=-1, keepdims=True) + norm_eps)
    unit = centered * inverse
    return (unit * gain + shift, unit, inverse)


def normalize_back(grad, unit, inverse, gain):
    scaled = grad * gain
    inner = (
        scaled
        - jnp.mean(scaled, axis=-1, keepdims=True)
        - unit * jnp.mean(scaled * unit, axis=-1, keepdims=True)
    )
    return inverse * inner


def sum_rows(*rows):
    stacked = [jnp.sum(r, axis=0, keepdims=True) for r in rows]
    return jnp.concatenate(stacked + [jnp.zeros_like(stacked[0])] * (8 - len(rows)), axis=0)


def deal(core, turned, rows, keep, send):
    for i in range(turned.shape[0] // (2 * rows)):
        even = turned[2 * i * rows : (2 * i + 1) * rows]
        odd = turned[(2 * i + 1) * rows : (2 * i + 2) * rows]
        here = slice(i * rows, (i + 1) * rows)
        keep(here, jnp.where(core == 0, even, odd).astype(jnp.bfloat16))
        send(here, jnp.where(core == 0, odd, even).astype(jnp.bfloat16))


def into(ref, columns):
    def store(rows, values):
        ref[rows, columns] = values

    return store


def turn_kernel(core, *refs, rows, count):
    arrays, (keep, send) = refs[:count], refs[-2:]
    start = 0
    for array in arrays:
        tokens = array.shape[0]
        columns = slice(start, start + tokens)
        turned = array[...].astype(jnp.float32).T
        deal(core[0], turned, rows, into(keep, columns), into(send, columns))
        start += tokens


def turn(core, arrays, rows, after=()):
    width = arrays[0].shape[1]
    half = jax.ShapeDtypeStruct((width // 2, sum(x.shape[0] for x in arrays)), jnp.bfloat16)
    return pl.pallas_call(
        functools.partial(turn_kernel, rows=rows, count=len(arrays)),
        out_shape=(half, half),
        in_specs=[smem] + [vmem] * len(arrays) + [anywhere] * len(after),
        out_specs=(vmem, vmem),
        compiler_params=kernel_params(32),
        cost_estimate=cost(0, 8),
    )(core, *arrays, *after)


def flat(block):
    values = block[...]
    if values.shape[1] % 16:
        values = values.astype(jnp.float32)
    return values.reshape(-1, values.shape[-1]).astype(jnp.bfloat16)


def weight_blocks(packed, chunk):
    devices, rows, width = packed.shape
    hidden = devices * rows // 2
    strips, owned = width // chunk, rows * width // (2 * hidden)
    return [
        pl.BlockSpec((devices, owned, chunk), lambda j: (0, j // strips, j % strips)),
        pl.BlockSpec((devices * chunk // hidden, rows // 2, width), lambda j: (j, 1, 0)),
    ]


def ffn_forward_kernel(
    core, second, w_in, w_out, bias, cot, vectors, *rest, rows, extra
):
    keep, send, slope, block_out, third_grad, out_grad, sums, acc, low = rest[extra:]

    step = pl.program_id(0)

    @pl.when(step == 0)
    def _():
        low[...] = second[...].astype(jnp.bfloat16)
        acc[...] = second[...] + vectors[0:1]

    pre = dot(low[...], flat(w_in), (1, 0)) + bias[...]
    part = 0.5 + 0.5 * lax.erf(pre * 0.5**0.5)
    active = pre * part
    everything = slice(None)
    deal(core[0], active.T, rows, into(keep, everything), into(send, everything))
    active = active.astype(jnp.bfloat16)
    slope[...] = (part + pre * jnp.exp(-0.5 * pre * pre) * 0.3989422804014327).astype(jnp.bfloat16)
    acc[...] += dot(active, flat(w_out), (1, 0))

    @pl.when(step == pl.num_programs(0) - 1)
    def _():
        gain = vectors[1:2]
        third, unit, inverse = normalize(acc[...], gain, vectors[2:3])
        block_out[...] = third.astype(jnp.bfloat16)
        grad = cot[...].astype(jnp.float32)
        third = normalize_back(grad, unit, inverse, gain)
        third_grad[...] = third
        lower = third.astype(jnp.bfloat16)
        out_grad[...] = lower
        sums[...] = sum_rows(grad * unit, grad, lower.astype(jnp.float32))


def ffn_forward(core, second, packed, bias, cot, vectors, rows, after):
    tokens, width = second.shape
    hidden = packed.shape[0] * packed.shape[1] // 2
    chunk = 512
    whole = lambda shape: pl.BlockSpec(shape, lambda j: (0, 0))
    full = whole((tokens, width))
    strip = pl.BlockSpec((tokens, chunk), lambda j: (0, j))
    turned = pl.BlockSpec((chunk // 2, tokens), lambda j: (j, 0))
    return pl.pallas_call(
        functools.partial(ffn_forward_kernel, rows=rows, extra=len(after)),
        grid=(hidden // chunk,),
        out_shape=(
            jax.ShapeDtypeStruct((hidden // 2, tokens), jnp.bfloat16),
            jax.ShapeDtypeStruct((hidden // 2, tokens), jnp.bfloat16),
            jax.ShapeDtypeStruct((tokens, hidden), jnp.bfloat16),
            jax.ShapeDtypeStruct((tokens, width), jnp.bfloat16),
            jax.ShapeDtypeStruct((tokens, width), jnp.float32),
            jax.ShapeDtypeStruct((tokens, width), jnp.bfloat16),
            jax.ShapeDtypeStruct((8, width), jnp.float32),
        ),
        in_specs=[
            smem,
            full,
            *weight_blocks(packed, chunk),
            pl.BlockSpec((1, chunk), lambda j: (0, j)),
            full,
            whole((8, width)),
        ]
        + [anywhere] * len(after),
        out_specs=(turned, turned, strip, full, full, full, whole((8, width))),
        scratch_shapes=[
            pltpu.VMEM((tokens, width), jnp.float32),
            pltpu.VMEM((tokens, width), jnp.bfloat16),
        ],
        compiler_params=kernel_params(40),
        cost_estimate=cost(16e9, 26, 4e6),
    )(core, second, packed, packed, bias, cot, vectors, *after)


def ffn_backward_kernel(
    w_in, w_out, slope, third_grad, out_grad, unit, inverse, gain, *rest, extra
):
    pre_grad, bias_grad, second_grad, branch, sums, acc = rest[extra:]
    step = pl.program_id(0)

    @pl.when(step == 0)
    def _():
        acc[...] = third_grad[...]

    grad = dot(out_grad[...], flat(w_out), (1, 1)) * slope[...].astype(jnp.float32)
    lower = grad.astype(jnp.bfloat16)
    pre_grad[...] = lower
    bias_grad[...] = jnp.sum(lower.astype(jnp.float32), axis=0, keepdims=True)
    acc[...] += dot(lower, flat(w_in), (1, 1))

    @pl.when(step == pl.num_programs(0) - 1)
    def _():
        total = acc[...]
        grad = normalize_back(total, unit[...], inverse[...], gain[...])
        second_grad[...] = grad
        lower = grad.astype(jnp.bfloat16)
        branch[...] = lower
        sums[...] = sum_rows(total * unit[...], total, lower.astype(jnp.float32))


def ffn_backward(packed, slope, third_grad, out_grad, unit, inverse, gain, after):
    tokens, width = third_grad.shape
    hidden = packed.shape[0] * packed.shape[1] // 2
    chunk = 512
    whole = lambda shape: pl.BlockSpec(shape, lambda j: (0, 0))
    full = whole((tokens, width))
    strip = pl.BlockSpec((tokens, chunk), lambda j: (0, j))
    return pl.pallas_call(
        functools.partial(ffn_backward_kernel, extra=len(after)),
        grid=(hidden // chunk,),
        out_shape=(
            jax.ShapeDtypeStruct((tokens, hidden), jnp.bfloat16),
            jax.ShapeDtypeStruct((1, hidden), jnp.float32),
            jax.ShapeDtypeStruct((tokens, width), jnp.float32),
            jax.ShapeDtypeStruct((tokens, width), jnp.bfloat16),
            jax.ShapeDtypeStruct((8, width), jnp.float32),
        ),
        in_specs=[
            *weight_blocks(packed, chunk),
            strip,
            full,
            full,
            full,
            whole((tokens, 1)),
            whole((1, width)),
        ]
        + [anywhere] * len(after),
        out_specs=(strip, pl.BlockSpec((1, chunk), lambda j: (0, j)), full, full, whole((8, width))),
        scratch_shapes=[pltpu.VMEM((tokens, width), jnp.float32)],
        compiler_params=kernel_params(40),
        cost_estimate=cost(14e9, 26),
    )(packed, packed, slope, third_grad, out_grad, unit, inverse, gain, *after)


def product_kernel(ids, *refs, spans, n_left, rows, chunk, extra):
    lefts, rights = refs[:n_left], refs[n_left : n_left + 2]
    keep_a, send_a, keep_b, send_b, ordered, *wide = refs[n_left + 2 + extra :]
    step = pl.program_id(0)
    blocks = lefts[0].shape[0] // rows
    half = blocks // 2 * rows

    @pl.when(step == 0)
    def _():
        start = 0
        for left in lefts:
            source, size = left, left.shape[1]
            if wide:
                source = wide[0].at[:, pl.ds(0, size)]
                source[...] = left[...].astype(jnp.float32)
            for order, bit in ((0, 1), (1, 0)):
                for i in range(blocks):
                    low, high = i % (1 << bit), (i % (blocks // 2)) >> bit
                    mine = ids[2 - order] if i < blocks // 2 else 1 - ids[2 - order]
                    place = (high << (bit + 1)) + (mine << bit) + low
                    taken = source[pl.ds(pl.multiple_of(place * rows, rows), rows), :]
                    ordered[order, i * rows : (i + 1) * rows, start : start + size] = taken.astype(jnp.bfloat16)
            start += size

    steps = sum(s[-1] for s in spans)
    first = 0
    for mine, other, tokens, row, count in spans:
        a, b = max(first, 0), min(first + count, steps)
        for order, keep, send in ((0, keep_a, send_a), (1, keep_b, send_b)):
            low, high = max(a, order * steps // 2), min(b, (order + 1) * steps // 2)
            if low >= high:
                continue

            @pl.when((step >= low) & (step < high))
            def _(mine=mine, other=other, tokens=tokens, row=row, order=order, keep=keep, send=send, first=first):
                columns = pl.ds(pl.multiple_of((step - first) * chunk, chunk), chunk)
                total = jnp.zeros((2 * half, chunk), jnp.float32)
                for start, right in ((mine, rights[0]), (other, rights[1])):
                    total += dot(
                        ordered[order, :, start : start + tokens], right[row : row + tokens, columns], (1, 0)
                    )
                keep[...] = total[:half].astype(jnp.bfloat16)
                send[...] = total[half:].astype(jnp.bfloat16)

        first += count


def products(ids, lefts, right, spans, rows, chunk, after=()):
    height = lefts[0][0].shape[0]
    columns = sum(s[-1] for s in spans)
    steps = columns // chunk
    spans = [(*s[:-1], s[-1] // chunk) for s in spans]
    part = jax.ShapeDtypeStruct((height // 2, columns // 2), jnp.bfloat16)
    block_a = pl.BlockSpec((height // 2, chunk), lambda j: (0, jnp.minimum(j, steps // 2 - 1)))
    block_b = pl.BlockSpec((height // 2, chunk), lambda j: (0, jnp.maximum(j - steps // 2, 0)))
    whole = lambda array: pl.BlockSpec(array.shape, lambda j: (0, 0))
    tokens = sum(x[1] for x in lefts)
    wide = [pltpu.VMEM((height, max(x[1] for x in lefts)), jnp.float32)] if rows % 16 else []
    taken = [pl.BlockSpec((height, size), lambda j, place=place: (0, place)) for _, size, place in lefts]
    return pl.pallas_call(
        functools.partial(
            product_kernel, spans=spans, n_left=len(lefts), rows=rows, chunk=chunk, extra=len(after)
        ),
        grid=(steps,),
        out_shape=(part,) * 4,
        in_specs=[smem] + taken + [whole(x) for x in right] + [anywhere] * len(after),
        out_specs=(block_a, block_a, block_b, block_b),
        scratch_shapes=[pltpu.VMEM((2, height, tokens), jnp.bfloat16)] + wide,
        compiler_params=kernel_params(48),
        cost_estimate=cost(2.5 * height * tokens * columns / len(lefts), 20),
    )(ids, *[x[0] for x in lefts], *right, *after)


def exchange(values, bit):
    count = lax.axis_size(AXES)
    return lax.ppermute(values, AXES, [(i, i ^ (1 << bit)) for i in range(count)])


def pack_kernel(*refs, places, extra):
    parts, out, sems = refs[: len(places)], refs[-2], refs[-1]
    copies = [
        pltpu.make_async_copy(
            part.at[:, pl.ds(begin, size)],
            out.at[pl.ds(row, part.shape[0]), pl.ds(column, size)],
            sems.at[i],
        )
        for i, (part, (begin, size, row, column)) in enumerate(zip(parts, places))
    ]
    for copy in copies:
        copy.start()
    for copy in copies:
        copy.wait()


def pack_rows(parts, places, shape, after):
    return pl.pallas_call(
        functools.partial(pack_kernel, places=places, extra=len(after)),
        out_shape=jax.ShapeDtypeStruct(shape, jnp.bfloat16),
        in_specs=[anywhere] * (len(parts) + len(after)),
        out_specs=anywhere,
        scratch_shapes=[pltpu.SemaphoreType.DMA((len(parts),))],
        compiler_params=kernel_params(16),
        cost_estimate=cost(0, 4 * shape[0] * shape[1] / 2**20),
    )(*parts, *after)


def place_kernel(*refs, slots, rows):
    me = lax.axis_index(AXES)
    pieces, out, sems = refs[:-2], refs[-2], refs[-1]
    copies = []
    for piece, (start, order) in zip(pieces, slots):
        columns = pl.ds(start, piece.shape[-1])
        for i, slot in enumerate(order):
            place = pl.ds(pl.multiple_of((me ^ slot) * rows, rows), rows)
            copies.append(
                pltpu.make_async_copy(piece.at[i], out.at[place, columns], sems.at[len(copies)])
            )
    for copy in copies:
        copy.start()
    for copy in copies:
        copy.wait()


def join_kernel(mine, arrived, *refs):
    out = refs[-1]
    out[: mine.shape[0]] = mine[...]
    out[mine.shape[0] :] = arrived[...]


def join(mine, arrived, after):
    return pl.pallas_call(
        join_kernel,
        out_shape=jax.ShapeDtypeStruct((2 * mine.shape[0], *mine.shape[1:]), mine.dtype),
        in_specs=[vmem] * 2 + [anywhere] * len(after),
        out_specs=vmem,
        compiler_params=kernel_params(16),
        cost_estimate=cost(0, 8 * mine.size / 2**20),
    )(mine, arrived, *after)


def gather_rows(local, after=()):
    rows, width = local.shape
    count = lax.axis_size(AXES)
    values, order, stages = local[None], [0], []
    for bit in range(count.bit_length() - 2, 2, -1):
        stages.append(exchange(values, bit))
        values = jnp.concatenate([values, stages[-1]], axis=0)
        order = order + [i ^ (1 << bit) for i in order]
    half = width // 256 * 128
    pieces, slots = [], []
    for start, stop, bits in ((0, half, (2, 1)), (half, width, (1, 2))):
        part, listed = values[:, :, start:stop], order
        for bit in bits:
            if bit == bits[-1] and len(after):
                part = join(part, exchange(part, bit), after)
            else:
                part = jnp.concatenate([part, exchange(part, bit)], axis=0)
            listed = listed + [i ^ (1 << bit) for i in listed]
        pieces += [part, exchange(part, 0)]
        slots += [(start, listed), (start, [i ^ 1 for i in listed])]
    placed = pl.pallas_call(
        functools.partial(place_kernel, slots=slots, rows=rows),
        out_shape=jax.ShapeDtypeStruct((count * rows, width), local.dtype),
        in_specs=[anywhere] * len(pieces),
        out_specs=pl.BlockSpec(memory_space=pltpu.HBM),
        scratch_shapes=[pltpu.SemaphoreType.DMA((2 * count,))],
        compiler_params=kernel_params(16),
        cost_estimate=cost(0, 4 * count * rows * width / 2**20),
    )(*pieces)
    return placed, stages


def stage_kernel(ids, *refs, groups, extra):
    inputs = refs[: 2 * sum(count for _, count in groups)]
    outputs = refs[len(inputs) + extra :]
    for g, (bit, count) in enumerate(groups):
        send, keep = outputs[2 * g : 2 * g + 2]
        mine = ids[bit]
        start = 0
        for _ in range(count):
            left, right, *inputs = inputs
            columns = slice(start, start + left.shape[-1])
            for i in range(left.shape[0]):
                for out, b in ((send, 1 - mine), (keep, mine)):
                    total = left[i, b].astype(jnp.float32) + right[i, b].astype(jnp.float32)
                    out[i, :, columns] = total.astype(jnp.bfloat16)
            start += left.shape[-1]


class Chain:
    def __init__(self, ids, parts, rows):
        self.ids, self.rows = ids, rows
        self.rest = list(range(3, ids.shape[0]))
        keep_a, send_a, keep_b, send_b = parts
        self.sends = [send_a, send_b]
        self.groups = [
            [(keep_a, exchange(send_a, 2))],
            [(keep_b, exchange(send_b, 1))],
        ]

    def advance(self, groups, bits, after):
        rows = self.rows
        shaped = [
            a.reshape(-1, 2, rows, a.shape[-1]) for group in groups for part in group for a in part
        ]
        shapes = [
            jax.ShapeDtypeStruct(
                (g[0][0].size // (2 * rows * g[0][0].shape[-1]), rows, sum(p[0].shape[-1] for p in g)),
                jnp.bfloat16,
            )
            for g in groups
            for _ in range(2)
        ]
        outs = pl.pallas_call(
            functools.partial(
                stage_kernel, groups=[(b, len(g)) for b, g in zip(bits, groups)], extra=len(after)
            ),
            out_shape=shapes,
            in_specs=[smem] + [vmem] * len(shaped) + [anywhere] * len(after),
            out_specs=[vmem] * len(shapes),
            compiler_params=kernel_params(24),
            cost_estimate=cost(0, sum(3 * x.size for x in shaped) / 2**20),
        )(self.ids, *shaped, *after)
        self.sends = outs[::2]
        self.groups = [
            [(keep, exchange(send, b))] for send, keep, b in zip(outs[::2], outs[1::2], bits)
        ]
        return outs[1::2]

    def second(self, after=()):
        return self.advance(self.groups, [1, 2], after)

    def third(self, after=()):
        if len(self.groups) == 2:
            self.groups = [self.groups[0] + self.groups[1]]
        return self.advance(self.groups, [self.rest.pop(0)], after)

    def finish(self):
        [[(keep, arrived)]] = self.groups
        return (keep.astype(jnp.float32) + arrived.astype(jnp.float32))[0]


def small_kernel(*refs, rows, count, owned):
    sums, bias, out = refs[:count], refs[count], refs[-1]
    lines = [sums[i][row : row + 1] for i, row in rows]
    lines += [jnp.zeros_like(lines[0])] * (128 - len(lines))
    out[:, :128] = jnp.concatenate(lines, axis=0).T
    out[:, 128:] = jnp.zeros((out.shape[0], 128), jnp.float32)
    for i in range(bias.shape[0]):
        out[i * owned : i * owned + 1, 128:] = bias[i : i + 1]


def small_block(lines, sums, bias, owned, after):
    width = sums[0].shape[1]
    devices = width // owned
    bias = bias.reshape(devices, -1)
    bias = jnp.pad(bias, ((0, 0), (0, 128 - bias.shape[1])))
    places = [([i for i, x in enumerate(sums) if x is s][0], row) for s, row in lines]
    block = pl.pallas_call(
        functools.partial(small_kernel, rows=places, count=len(sums), owned=owned),
        out_shape=jax.ShapeDtypeStruct((width, 256), jnp.float32),
        in_specs=[vmem] * (len(sums) + 1) + [anywhere] * len(after),
        out_specs=vmem,
        compiler_params=kernel_params(16),
        cost_estimate=cost(0, 2),
    )(*sums, bias, *after)
    return block.astype(jnp.bfloat16)


def add_product_kernel(*refs, count, base, extra):
    out = refs[-1]
    total = refs[2 * count][...] if base else jnp.zeros(out.shape, jnp.float32)
    for left, right in zip(refs[:count], refs[count : 2 * count]):
        total += dot(left[...], right[...], (1, 1))
    out[...] = total


def add_product(stack, places, weights, columns, rows, chunk, base=None, after=()):
    width = stack.shape[1]
    count = len(places)
    bases = [] if base is None else [base]
    block = pl.BlockSpec((chunk, width), lambda i: (i, 0))
    return pl.pallas_call(
        functools.partial(add_product_kernel, count=count, base=len(bases), extra=len(after)),
        grid=(rows // chunk,),
        out_shape=jax.ShapeDtypeStruct((rows, width), jnp.float32),
        in_specs=[pl.BlockSpec((chunk, width), lambda i, p=p: (p // chunk + i, 0)) for p in places]
        + [pl.BlockSpec((width, width), lambda i, c=c: (0, c)) for c in columns]
        + [block] * len(bases)
        + [anywhere] * len(after),
        out_specs=block,
        compiler_params=kernel_params(40),
        cost_estimate=cost(3 * rows * count * width * width, 12),
    )(*[stack] * count, *[weights] * count, *bases, *after)


def body(
    target_in,
    memory,
    block_rows,
    pad_rows,
    seq_lengths,
    self_qkv,
    self_out,
    cross_query,
    cross_kv,
    cross_out,
    ffn_in,
    ffn_out,
    norm_scale,
    small_bias,
    ffn_bias,
    cotangent,
):
    width = target_in.shape[1]
    owned = self_qkv.shape[0]
    me = lax.axis_index(AXES)
    core = (me & 1).reshape(1)
    ids = (me >> jnp.arange(lax.axis_size(AXES).bit_length() - 1)) & 1
    tokens, mems = target_in.shape[0], memory.shape[0]

    def turned(*arrays, after=()):
        keep, send = turn(core, arrays, owned, after)
        return keep, exchange(send, 0)

    memory_turned = turned(memory)
    target_turned = turned(target_in)
    pack = jnp.concatenate([norm_scale.T, small_bias.T, ffn_bias.reshape(owned, -1)], axis=1)
    small_cols = pack.shape[1]
    pack = jnp.pad(pack, ((0, 0), (0, -small_cols % 128)))
    early, stages = gather_rows(jnp.concatenate([self_qkv, self_out, pack], axis=1))
    late = pack_rows(
        [cross_query, cross_kv, cross_out],
        [(0, width, 0, 0), (0, 2 * width, 0, width), (0, width, 0, 3 * width)],
        (owned, 4 * width),
        stages[:1],
    )
    blocks = ffn_in.shape[1] // width
    packed = pack_rows(
        [ffn_in] * blocks + [ffn_out],
        [(i * width, width, i * owned, 0) for i in range(blocks)] + [(0, width, blocks * owned, 0)],
        (blocks * owned + ffn_out.shape[0], width),
        stages[:1],
    )
    packed = lax.all_gather(packed, AXES)
    w_qkv, w_self = early[:, : 3 * width], early[:, 3 * width : 4 * width]
    small = early[:, 4 * width : 4 * width + small_cols].astype(jnp.float32)
    gains = small[:, :3].T
    biases = small[:, 3:13].T
    in_bias = small[:, 13:].reshape(1, -1)

    bound = memory_bounds(block_rows[0], pad_rows[0])
    lengths = seq_lengths[0]
    zeros = jnp.zeros((width,), jnp.float32)
    qkv = (matmul(target_in, w_qkv) + jnp.concatenate([biases[0], zeros, biases[1]])).astype(
        jnp.bfloat16
    )
    self_context, self_summary = self_forward(lengths, qkv)
    first, first_unit, first_inverse = normalize(
        target_in.astype(jnp.float32) + matmul(self_context, w_self) + biases[2],
        gains[0],
        biases[7],
    )
    first_low = first.astype(jnp.bfloat16)
    self_turned = turned(self_context, first_low)
    late, _ = gather_rows(late, after=self_turned[:1])
    w_query, w_pairs, w_cross = late[:, :width], late[:, width : 3 * width], late[:, 3 * width :]
    cross_q = (matmul(first_low, w_query) + biases[3]).astype(jnp.bfloat16)
    cross_pairs = (matmul(memory, w_pairs) + jnp.concatenate([zeros, biases[4]])).astype(
        jnp.bfloat16
    )
    cross_context, cross_summary = cross_forward(bound, cross_q, cross_pairs)
    second, second_unit, second_inverse = normalize(
        first + matmul(cross_context, w_cross) + biases[5], gains[1], biases[8]
    )

    cross_turned = turned(cross_context, second)
    vectors = jnp.concatenate([biases[6:7], gains[2:3], biases[9:10], jnp.zeros((5, width), jnp.float32)])
    hidden, hidden_send, slope, block_out, third_grad, out_grad, third_sums = ffn_forward(
        core,
        second,
        packed,
        in_bias,
        cotangent,
        vectors,
        ffn_out.shape[0],
        after=(memory_turned[1], target_turned[1], self_turned[1]),
    )
    hidden_other, out_grad_other = exchange(hidden_send, 0), exchange(out_grad, 0)
    pre_grad, ffn_bias_grad, second_grad, cross_branch, second_sums = ffn_backward(
        packed, slope, third_grad, out_grad, second_unit, second_inverse, gains[1:2], cross_turned[1:]
    )
    pre_grad_other = exchange(pre_grad, 0)
    parts = products(
        ids,
        [(hidden, tokens, 0), (hidden_other, tokens, 0)],
        (out_grad, out_grad_other),
        [(0, tokens, tokens, 0, width)],
        ffn_out.shape[0],
        256,
        after=(pre_grad,),
    )
    out_chain = Chain(ids, parts, ffn_out.shape[0])
    parts = products(
        ids,
        [(x, tokens, 1) for x in cross_turned],
        (pre_grad, pre_grad_other),
        [(0, tokens, tokens, 0, ffn_in.shape[1])],
        owned,
        512,
        after=out_chain.sends,
    )
    in_chain = Chain(ids, parts, owned)

    cross_delta, cross_sums = cross_backward(
        bound, cross_q, cross_pairs, cross_summary, cross_branch, late, 3, after=in_chain.sends
    )
    cross_other = exchange(cross_delta, 0)
    self_delta, self_sums, first_grad = self_backward(
        lengths,
        qkv,
        self_summary,
        second_grad,
        cross_delta,
        late,
        early,
        first_unit,
        first_inverse,
        gains[0:1],
        after=out_chain.second(after=(cross_sums,)),
    )
    self_other = exchange(self_delta, 0)
    beyond = mems + 2 * tokens
    parts = products(
        ids,
        [
            part
            for i in range(2)
            for part in (
                (memory_turned[i], mems, 0),
                (self_turned[i], tokens, 1),
                (cross_turned[i], tokens, 0),
            )
        ],
        (cross_delta, cross_other),
        [
            (mems, beyond + mems, tokens, 0, width),
            (0, beyond, mems, 2 * tokens, width),
            (0, beyond, mems, 2 * tokens + mems, width),
            (mems + tokens, beyond + mems + tokens, tokens, tokens, width),
        ],
        owned,
        512,
        after=in_chain.second(after=(self_sums,)),
    )
    cross_chain = Chain(ids, parts, owned)
    parts = products(
        ids,
        [part for i in range(2) for part in ((target_turned[i], tokens, 0), (self_turned[i], tokens, 0))],
        (self_delta, self_other),
        [(0, 2 * tokens, tokens, i * tokens, width) for i in range(3)]
        + [(tokens, 3 * tokens, tokens, 3 * tokens, width)],
        owned,
        512,
        after=out_chain.third(after=parts[:1]),
    )
    self_chain = Chain(ids, parts, owned)
    last = in_chain.third(after=parts[:1])

    small_grad = small_block(
        [
            (self_sums, 3),
            (second_sums, 0),
            (third_sums, 0),
            (self_sums, 0),
            (self_sums, 1),
            (self_sums, 2),
            (cross_sums, 0),
            (cross_sums, 1),
            (second_sums, 2),
            (third_sums, 2),
            (self_sums, 4),
            (second_sums, 1),
            (third_sums, 1),
        ],
        [self_sums, cross_sums, second_sums, third_sums],
        ffn_bias_grad,
        owned,
        last,
    )
    bits = list(range(lax.axis_size(AXES).bit_length() - 1))[::-1]
    small_part = small_grad.reshape((2,) * len(bits) + (owned, -1))
    for bit in (0, 1):
        mine = (me >> bit) & 1
        keep, send = [
            lax.dynamic_index_in_dim(small_part, i, bits.index(bit), keepdims=False)
            for i in (mine, 1 - mine)
        ]
        arrived = exchange(send, bit)
        small_part = (keep.astype(jnp.float32) + arrived.astype(jnp.float32)).astype(jnp.bfloat16)
        bits.remove(bit)
    self_chain.groups[1].append((keep, arrived))

    memory_grad = add_product(
        cross_delta, [2 * tokens, 2 * tokens + mems], late, [1, 2], mems, 256, after=(small_grad,)
    )
    last = cross_chain.second(after=(memory_grad,))
    last = out_chain.third(after=last)
    target_grad = add_product(
        self_delta, [0, tokens, 2 * tokens], early, [0, 1, 2], tokens, tokens, first_grad, after=last
    )
    last = in_chain.third(after=(target_grad,))
    last = self_chain.second(after=last)
    last = cross_chain.third(after=last)
    last = cross_chain.third(after=last)
    last = self_chain.third(after=last)
    while self_chain.rest:
        last = self_chain.third(after=last)
    for chain in (out_chain, in_chain, cross_chain):
        while chain.rest:
            last = chain.third(after=last)
    ffn_out_shard = out_chain.finish()
    ffn_in_shard = in_chain.finish()
    cross_shard = cross_chain.finish()
    self_shard = self_chain.finish()
    small_shard = self_shard[:, 4 * width :]
    return (
        block_out,
        target_grad,
        memory_grad,
        self_shard[:, : 3 * width],
        self_shard[:, 3 * width : 4 * width],
        cross_shard[:, :width],
        cross_shard[:, width : 3 * width],
        cross_shard[:, 3 * width :],
        ffn_in_shard,
        ffn_out_shard,
        small_shard[:, :3].T,
        small_shard[:, 3:13].T,
        small_shard[0, 128 : 128 + ffn_bias.shape[0]],
    )


def solution(mesh):
    in_specs = (
        P(("wide", "narrow"), None),
        P(("wide", "narrow"), None),
        P(("wide", "narrow"), None),
        P(("wide", "narrow"), None),
        P(("wide", "narrow"), None),
        P(("wide", "narrow"), None),
        P(("wide", "narrow"), None),
        P(("wide", "narrow"), None),
        P(("wide", "narrow"), None),
        P(("wide", "narrow"), None),
        P(("wide", "narrow"), None),
        P(("wide", "narrow"), None),
        P(None, ("wide", "narrow")),
        P(None, ("wide", "narrow")),
        P(("wide", "narrow")),
        P(("wide", "narrow"), None),
    )
    out_specs = (
        P(("wide", "narrow"), None),
        P(("wide", "narrow"), None),
        P(("wide", "narrow"), None),
        P(("wide", "narrow"), None),
        P(("wide", "narrow"), None),
        P(("wide", "narrow"), None),
        P(("wide", "narrow"), None),
        P(("wide", "narrow"), None),
        P(("wide", "narrow"), None),
        P(("wide", "narrow"), None),
        P(None, ("wide", "narrow")),
        P(None, ("wide", "narrow")),
        P(("wide", "narrow")),
    )
    return jax.shard_map(body, mesh=mesh, in_specs=in_specs, out_specs=out_specs, check_vma=False)
```

time: 600 us -> 484 us (0.81)
  waiting for transfers between devices: 350 us -> 172 us
  Pallas kernels: 93.5 us -> 166 us
  starting transfers between devices: 22.3 us -> 53.9 us
  matrix products: 46.9 us -> 15.6 us
  other arithmetic: 33.3 us -> 11.6 us
  local copies, waits for them, and re-layouts: 29.6 us -> 40.7 us
    all_gather x3 -> x1, waiting for transfers between devices: 240 us -> 0.01 us  [body(): packed = lax.all_gather(packed, AXES)]
    ppermute x21 -> x51, waiting for transfers between devices: 109 us -> 172 us  [exchange(): return lax.ppermute(values, AXES, [(i, i ^ 1 << bit) for i in range(count)])]
    pallas_call x5 -> x31, Pallas kernels: 61.7 us -> 120 us  [the longest x4 45.2 us: products(): pl.pallas_call(functools.partial(product_kernel, spans=spans, n_left=len(...]
    ppermute x21 -> x51, starting transfers between devices: 22.1 us -> 53.9 us  [exchange(): return lax.ppermute(values, AXES, [(i, i ^ 1 << bit) for i in range(count)])]
    dot_general x5 -> x0, matrix products: 25.3 us -> none  [inner_cols(): lax.dot_general(first, second, (((1,), (1,)), ((), ())), preferred_elemen...]
    convert_element_type x21 -> x3, other arithmetic: 23.7 us -> 0.14 us  [the longest x1 0.08 us: body(): (keep.astype(jnp.float32) + arrived.astype(jnp.float32)).astype(jnp.bfloa...]
    unnamed x93 -> x133, local copies, waits for them, and re-layouts: 19.4 us -> 34.5 us
    pallas_call x1, Pallas kernels: 6.61 us -> 13.6 us  [self_backward(): pl.pallas_call(functools.partial(self_backward_kernel, extra=len(after)),...]
  transfers between devices with their start and end apart: 24 -> 52, of which waited for: 13 -> 16; matrix products, arithmetic and copies ran while one was open for 15% -> 6% of each run, Pallas kernels for 12% -> 35%
where the time goes in v3:
time: 484 us; the launch traced here: 475 us
  waiting for transfers between devices  172 us (36%)
  Pallas kernels  166 us (34%)
  starting transfers between devices  53.9 us (11%)
  local copies, waits for them, and re-layouts  40.7 us (8%)
  matrix products  15.6 us (3%)
  between operations  15.5 us (3%)
  other arithmetic  11.6 us (2%)
    ppermute x51, waiting for transfers between devices, exchange(): return lax.ppermute(values, AXES, [(i, i ^ 1 << bit) for i in range(count)])  172 us
    ppermute x51, starting transfers between devices, exchange(): return lax.ppermute(values, AXES, [(i, i ^ 1 << bit) for i in range(count)])  53.9 us
    pallas_call x4, Pallas kernels, products(): pl.pallas_call(functools.partial(product_kernel, spans=spans, n_left=len(...  45.2 us
    unnamed x133, local copies, waits for them, and re-layouts  34.5 us
    pallas_call x1, Pallas kernels, cross_backward(): pl.pallas_call(functools.partial(cross_backward_kernel, extra=len(after))...  21.1 us
    dot_general x5, matrix products, matmul(): return jnp.dot(first, second, preferred_element_type=jnp.float32)  15.6 us
    pallas_call x1, Pallas kernels, ffn_forward(): pl.pallas_call(functools.partial(ffn_forward_kernel, rows=rows, extra=len...  15.5 us
    pallas_call x12, Pallas kernels, advance(): pl.pallas_call(functools.partial(stage_kernel, groups=[(b, len(g)) for b,...  14.4 us
  transfers between devices with their start and end apart: 52, of which 16 were waited for; matrix products, arithmetic and copies ran while one was open for 6% of the time, Pallas kernels for 35%

profile of v3, /device:TPU:0, one launch (start us, length us, event | category | flops | bytes accessed | tf_op | source)
XLA Modules:
  0.0 475.4 jit_solution(1304138576197408734)
XLA Ops:
  10.6 4.1 collective-permute-start
  14.7 12.3 %collective-permute-done.refs_3_.refs_5_ = bf16[1,32,4224]{2,1,0:T(8,128)(2,1)S(1)} collective-permute-done((bf16[1,32,4224]{2,1,0:T(8,128)(2,1)S(1)}, bf16[1,32,4224]{2,1,0:T(8,128)(2,1)S(1)}, u32[]{:S(2)}, u32[]{:S(2)}) %collective-permute-start) | collective-permute-done | bytes 270368 | tf_op jit(solution)/shard_map/ppermute | solution.py:639
  30.6 15.6 %collective-permute-done.1 = bf16[2,32,4224]{2,1,0:T(8,128)(2,1)S(1)} collective-permute-done((bf16[2,32,4224]{2,1,0:T(8,128)(2,1)S(1)}, bf16[2,32,4224]{2,1,0:T(8,128)(2,1)S(1)}, u32[]{:S(2)}, u32[]{:S(2)}) %collective-permute-start.1) | collective-permute-done | bytes 540704 | tf_op jit(solution)/shard_map/ppermute | solution.py:639
  48.0 10.3 %collective-permute-done.5 = bf16[4,32,2176]{2,1,0:T(8,128)(2,1)S(1)} collective-permute-done((bf16[4,32,2176]{2,1,0:T(8,128)(2,1)S(1)}, bf16[4,32,2176]{2,1,0:T(8,128)(2,1)S(1)}, u32[]{:S(2)}, u32[]{:S(2)}) %collective-permute-start.5) | collective-permute-done | bytes 557088 | tf_op jit(solution)/shard_map/ppermute | solution.py:639
  60.1 5.2 %collective-permute-start.8 = (bf16[1,32,4096]{2,1,0:T(8,128)(2,1)S(1)}, bf16[1,32,4096]{2,1,0:T(8,128)(2,1)S(1)}, u32[]{:S(2)}, u32[]{:S(2)}) collective-permute-start(bf16[1,32,4096]{2,1,0:T(8,128)(2,1)S(1)} %bitcast.107), channel_id=1, source_target_pairs={{0,16},{1,17},{2,18},{3,19},{4,20},{5,21},{6,22},{7,23},{8,24},{9,... | collective-permute-start | bytes 786440 | tf_op jit(solution)/shard_map/ppermute | solution.py:639
  65.4 2.3 collective-permute-start.3
  67.7 16.8 %collective-permute-done.8 = bf16[1,32,4096]{2,1,0:T(8,128)(2,1)S(1)} collective-permute-done((bf16[1,32,4096]{2,1,0:T(8,128)(2,1)S(1)}, bf16[1,32,4096]{2,1,0:T(8,128)(2,1)S(1)}, u32[]{:S(2)}, u32[]{:S(2)}) %collective-permute-start.8) | collective-permute-done | bytes 262176 | tf_op jit(solution)/shard_map/ppermute | solution.py:639
  85.8 11.9 %collective-permute-done.6 = bf16[8,32,2176]{2,1,0:T(8,128)(2,1)S(1)} collective-permute-done((bf16[8,32,2176]{2,1,0:T(8,128)(2,1)S(1)}, bf16[8,32,2176]{2,1,0:T(8,128)(2,1)S(1)}, u32[]{:S(2)}, u32[]{:S(2)}) %collective-permute-start.6) | collective-permute-done | bytes 1114144 | tf_op jit(solution)/shard_map/ppermute | solution.py:639
  100.1 6.4 %collective-permute-done.9 = bf16[2,32,4096]{2,1,0:T(8,128)(2,1)S(1)} collective-permute-done((bf16[2,32,4096]{2,1,0:T(8,128)(2,1)S(1)}, bf16[2,32,4096]{2,1,0:T(8,128)(2,1)S(1)}, u32[]{:S(2)}, u32[]{:S(2)}) %collective-permute-start.9) | collective-permute-done | bytes 524320 | tf_op jit(solution)/shard_map/ppermute | solution.py:639
  108.3 16.8 %collective-permute-done.10 = bf16[4,32,2048]{2,1,0:T(8,128)(2,1)} collective-permute-done((bf16[4,32,2048]{2,1,0:T(8,128)(2,1)S(1)}, bf16[4,32,2048]{2,1,0:T(8,128)(2,1)}, u32[]{:S(2)}, u32[]{:S(2)}) %collective-permute-start.10) | collective-permute-done | bytes 524320 | tf_op jit(solution)/shard_map/ppermute | solution.py:639
  127.5 2.3 pad_maximum_fusion.6.mine
  129.8 3.2 collective-permute-start.14
  133.1 3.6 shard_map.255.w_self.refs_3_.refs_4_.refs_5_
  136.7 3.5 copy-done
  140.5 5.7 %fusion.7.qkv = bf16[384,3072]{1,0:T(8,128)(2,1)S(1)} fusion(bf16[384,1024]{1,0:T(8,128)(2,1)} %refs_0_.7, bf16[1024,4224]{1,0:T(8,128)(2,1)} %copy-done, f32[3072]{0:T(1024)S(1)} %pad_maximum_fusion.12), kind=kOutput, calls=%fused_computation.7 | convolution fusion | flops 2418278400 | bytes 9449472 | tf_op jit(solution)/shard_map/dot_general | solution.py:33
  146.2 3.5 shard_map.256
  149.7 2.7 fusion.35
  155.7 13.6 %collective-permute-done.11.arrived = bf16[8,32,2048]{2,1,0:T(8,128)(2,1)} collective-permute-done((bf16[8,32,2048]{2,1,0:T(8,128)(2,1)S(1)}, bf16[8,32,2048]{2,1,0:T(8,128)(2,1)}, u32[]{:S(2)}, u32[]{:S(2)}) %collective-permute-start.11) | collective-permute-done | bytes 1048608 | tf_op jit(solution)/shard_map/ppermute | solution.py:639
  171.1 3.1 shard_map.260.refs_2_
  180.8 4.4 shard_map.261.weight.w_query.refs_2_.refs_3_
  186.2 2.2 copy-done.9
  188.5 5.2 %fusion.4.pairs = bf16[1024,2048]{1,0:T(8,128)(2,1)S(1)} fusion(f32[2048]{0:T(1024)S(1)} %concatenate.62, bf16[1024,1024]{1,0:T(8,128)(2,1)S(1)} %copy-done.9, bf16[1024,4096]{1,0:T(8,128)(2,1)S(1)} %shard_map.261.weight.w_query.refs_2_.refs_3_), kind=kOutput, calls=%fused_computation.4 | convolution fusion | flops 4299161600 | bytes 10493952 | tf_op jit(solution)/shard_map/dot_general | solution.py:33
  193.7 7.0 %shard_map.262 = (bf16[384,1024]{1,0:T(8,128)(2,1)S(1)}, f32[3,8,1,256]{3,2,1,0:T(1,128)S(1)}) custom-call(s32[2,3]{1,0:T(2,128)S(1)} %pad_add_fusion.bound, bf16[384,1024]{1,0:T(8,128)(2,1)S(1)} %add_convert_fusion.2.q, bf16[1024,2048]{1,0:T(8,128)(2,1)S(1)} %fusion.4.pairs), custom_call_target="tpu_custom_call" | custom-call | flops 80000000000 | bytes 83886080 | tf_op jit(solution)/shard_map/pallas_call | solution.py:182
  208.2 15.5 %shard_map.266 = (bf16[2048,384]{1,0:T(8,128)(2,1)S(1)}, bf16[2048,384]{1,0:T(8,128)(2,1)S(1)}, bf16[384,4096]{1,0:T(8,128)(2,1)S(1)}, bf16[384,1024]{1,0:T(8,12...) custom-call(s32[1]{0:T(128)} %bitcast.core, ...), custom_call_target="tpu_custom_call" | custom-call | flops 160000000000 | bytes 272629760 | tf_op jit(solution)/shard_map/pallas_call | solution.py:473
  224.2 13.4 %shard_map.268 = (bf16[384,4096]{1,0:T(8,128)(2,1)S(1)}, f32[1,4096]{1,0:T(1,128)S(1)}, f32[384,1024]{1,0:T(8,128)S(1)}, bf16[384,1024]{1,0:T(8,128)(2,1)S(1)}, f32[8,1024]{1,0:T(8,128)S(1)}) custom-call(bf16[32,256,1024]{2,1,0:T(8,128)(2,1)} %bitcast.167, bf16[32,256,1024]{2,1,0:T(8,128)(2,1)} %bitcast.168, bf16[384,4096]{1,0:T(8,128)(2,1)S(1)} %get-tuple-element.98.slope, ...), custom_call_target="tpu_custom_call" | custom-call | flops 140000002048 | bytes 272629760 | tf_op jit(solution)/shard_map/pallas_call | solution.py:537
  240.3 6.1 %collective-permute-done.22.refs_3_ = bf16[384,1024]{1,0:T(8,128)(2,1)S(1)} collective-permute-done((bf16[384,1024]{1,0:T(8,128)(2,1)S(1)}, bf16[384,1024]{1,0:T(8,128)(2,1)S(1)}, u32[]{:S(2)}, u32[]{:S(2)}) %collective-permute-start.22) | collective-permute-done | bytes 786464 | tf_op jit(solution)/shard_map/ppermute | solution.py:639
  247.6 9.0 %shard_map.269 = (bf16[1024,512]{1,0:T(8,128)(2,1)S(1)}, bf16[1024,512]{1,0:T(8,128)(2,1)}, bf16[1024,512]{1,0:T(8,128)(2,1)S(1)}, bf16[1024,512]{1,0:T(8,128)(2,1)}) custom-call(s32[5]{0:T(128)S(1)} %shift-right-arithmetic_and_fusion.ids, bf16[2048,384]{1,0:T(8,128)(2,1)} %copy-done.48, bf16[2048,384]{1,0:T(8,128)(2,1)} %copy-done.60, ...), custom_call_target="tpu_custom_call" | custom-call | flops 20132659200 | bytes 209715200 | tf_op jit(solution)/shard_map/pallas_call | solution.py:623
  258.1 10.5 %shard_map.270 = (bf16[256,2048]{1,0:T(8,128)(2,1)S(1)}, bf16[256,2048]{1,0:T(8,128)(2,1)}, bf16[256,2048]{1,0:T(8,128)(2,1)S(1)}, bf16[256,2048]{1,0:T(8,128)(2,1)}) custom-call(s32[5]{0:T(128)S(1)} %shift-right-arithmetic_and_fusion.ids, bf16[512,768]{1,0:T(8,128)(2,1)S(1)} %copy-done.37, bf16[512,768]{1,0:T(8,128)(2,1)} %collective-permute-done.19.rest_0_.refs_1_.refs_5_, ...), custom_call_target="tpu_custom_call" | custom-call | flops 20132659200 | bytes 209715200 | tf_op jit(solution)/shard_map/pallas_call | solution.py:623
  271.2 21.1 %shard_map.271 = (bf16[2816,1024]{1,0:T(8,128)(2,1)}, f32[8,1024]{1,0:T(8,128)}) custom-call(s32[2,3]{1,0:T(2,128)} %copy-done.27, bf16[384,1024]{1,0:T(8,128)(2,1)} %copy-done.45, bf16[1024,2048]{1,0:T(8,128)(2,1)} %copy-done.47, f32[3,8,1,256]{3,2,1,0:T(1,128)} %copy-done.54, bf16[384,1024]{1,0:T(8,128)(2,1)} %copy-done.53, bf16[1024,4096]{1,0:T(8,128)(2,1)} %copy-done.1, ...), custom_call_target="tpu_custom_call" | custom-call | flops 160000000000 | bytes 125829120 | tf_op jit(solution)/shard_map/pallas_call | solution.py:208
  293.0 2.2 shard_map.272
  296.0 13.6 %shard_map.273 = (bf16[1536,1024]{1,0:T(8,128)(2,1)}, f32[8,1024]{1,0:T(8,128)S(1)}, f32[384,1024]{1,0:T(8,128)S(1)}) custom-call(s32[3]{0:T(128)S(1)} %bitcast.150, bf16[384,3072]{1,0:T(8,128)(2,1)} %copy-done.46, f32[3,8,1,256]{3,2,1,0:T(1,128)S(1)} %get-tuple-element.97.summary, f32[384,1024]{1,0:T(8,128)S(1)} %copy-done.52, ...), custom_call_target="tpu_custom_call" | custom-call | flops 60000002048 | bytes 125829120 | tf_op jit(solution)/shard_map/pallas_call | solution.py:324
  311.7 2.2 shard_map.274
  317.6 15.2 %shard_map.275 = (bf16[256,2048]{1,0:T(8,128)(2,1)S(1)}, bf16[256,2048]{1,0:T(8,128)(2,1)}, bf16[256,2048]{1,0:T(8,128)(2,1)}, bf16[256,2048]{1,0:T(8,128)(2,1)}) custom-call(s32[5]{0:T(128)S(1)} %copy-done.22, bf16[512,1024]{1,0:T(8,128)(2,1)} %copy-done.31, bf16[512,768]{1,0:T(8,128)(2,1)S(1)} %copy-done.5, bf16[512,768]{1,0:T(8,128)(2,1)S(1)} %copy-done.38, ...), custom_call_target="tpu_custom_call" | custom-call | flops 31317469184 | bytes 209715200 | tf_op jit(solution)/shard_map/pallas_call | solution.py:623
  334.8 10.5 %shard_map.277 = (bf16[256,2048]{1,0:T(8,128)(2,1)S(1)}, bf16[256,2048]{1,0:T(8,128)(2,1)S(1)}, bf16[256,2048]{1,0:T(8,128)(2,1)S(1)}, bf16[256,2048]{1,0:T(8,128)(2,1)}) custom-call(s32[5]{0:T(128)S(1)} %copy-done.22, bf16[512,384]{1,0:T(8,128)(2,1)S(1)} %copy-done.42, bf16[512,768]{1,0:T(8,128)(2,1)S(1)} %copy-done.5, ...), custom_call_target="tpu_custom_call" | custom-call | flops 20132659200 | bytes 209715200 | tf_op jit(solution)/shard_map/pallas_call | solution.py:623
  346.6 2.0 collective-permute-start.40
  348.6 2.7 copy-done.28
  351.3 8.6 %shard_map.280.refs_4_ = f32[1024,1024]{1,0:T(8,128)} custom-call(bf16[2816,1024]{1,0:T(8,128)(2,1)S(1)} %copy-done.28, bf16[2816,1024]{1,0:T(8,128)(2,1)S(1)} %copy-done.28, bf16[1024,4096]{1,0:T(8,128)(2,1)} %copy-done.1, bf16[1024,4096]{1,0:T(8,128)(2,1)} %copy-done.1, bf16[1024,256]{1,0:T(8,128)(2,1)S(1)} %convert_element_type.71.refs_4_), custom_call_target="tpu_custom_call" | custom-call | flops 64424509440 | bytes 125829120 | tf_op jit(solution)/shard_map/pallas_call | solution.py:846
  359.9 2.0 collective-permute-start.36
  365.1 2.2 copy-done.2
  368.5 2.4 shard_map.281
  376.7 3.8 shard_map.283.refs_2_
  382.5 9.6 %collective-permute-done.39 = bf16[2,2,2,32,256]{4,3,2,1,0:T(8,128)(2,1)S(1)} collective-permute-done((bf16[2,2,2,32,256]{4,3,2,1,0:T(8,128)(2,1)S(1)}, bf16[2,2,2,32,256]{4,3,2,1,0:T(8,128)(2,1)S(1)}, u32[]{:S(2)}, u32[]{:S(2)}) %collective-permute-start.39) | collective-permute-done | bytes 131104 | tf_op jit(solution)/shard_map/ppermute | solution.py:639
  393.3 9.0 %collective-permute-done.43 = bf16[4,32,2048]{2,1,0:T(8,128)(2,1)S(1)} collective-permute-done((bf16[4,32,2048]{2,1,0:T(8,128)(2,1)}, bf16[4,32,2048]{2,1,0:T(8,128)(2,1)S(1)}, u32[]{:S(2)}, u32[]{:S(2)}) %collective-permute-start.43) | collective-permute-done | bytes 524320 | tf_op jit(solution)/shard_map/ppermute | solution.py:639
  405.4 5.9 %collective-permute-start.49 = (bf16[1,32,4096]{2,1,0:T(8,128)(2,1)S(1)}, bf16[1,32,4096]{2,1,0:T(8,128)(2,1)S(1)}, u32[]{:S(2)}, u32[]{:S(2)}) collective-permute-start(bf16[1,32,4096]{2,1,0:T(8,128)(2,1)S(1)} %get-tuple-element.165), channel_id=1, source_target_pairs={{0,16},{1,17},{2,18},{3,19},{4,20},{5,21},{6,22},{7,23},{8,24},{9,... | collective-permute-start | bytes 786440 | tf_op jit(solution)/shard_map/ppermute | solution.py:639
  411.3 15.7 %collective-permute-done.45 = bf16[2,32,4096]{2,1,0:T(8,128)(2,1)S(1)} collective-permute-done((bf16[2,32,4096]{2,1,0:T(8,128)(2,1)S(1)}, bf16[2,32,4096]{2,1,0:T(8,128)(2,1)S(1)}, u32[]{:S(2)}, u32[]{:S(2)}) %collective-permute-start.45) | collective-permute-done | bytes 524320 | tf_op jit(solution)/shard_map/ppermute | solution.py:639
  431.9 15.1 %collective-permute-done.46 = bf16[2,32,4352]{2,1,0:T(8,128)(2,1)S(1)} collective-permute-done((bf16[2,32,4352]{2,1,0:T(8,128)(2,1)S(1)}, bf16[2,32,4352]{2,1,0:T(8,128)(2,1)S(1)}, u32[]{:S(2)}, u32[]{:S(2)}) %collective-permute-start.46) | collective-permute-done | bytes 557088 | tf_op jit(solution)/shard_map/ppermute | solution.py:639
  447.7 4.8 %collective-permute-start.47 = (bf16[1,32,4352]{2,1,0:T(8,128)(2,1)S(1)}, bf16[1,32,4352]{2,1,0:T(8,128)(2,1)S(1)}, u32[]{:S(2)}, u32[]{:S(2)}) collective-permute-start(bf16[1,32,4352]{2,1,0:T(8,128)(2,1)S(1)} %get-tuple-element.163), channel_id=1, source_target_pairs={{0,16},{1,17},{2,18},{3,19},{4,20},{5,21},{6,22},{7,23},{8,24},{9,... | collective-permute-start | bytes 835592 | tf_op jit(solution)/shard_map/ppermute | solution.py:639
  453.9 10.7 %collective-permute-done.47 = bf16[1,32,4352]{2,1,0:T(8,128)(2,1)S(1)} collective-permute-done((bf16[1,32,4352]{2,1,0:T(8,128)(2,1)S(1)}, bf16[1,32,4352]{2,1,0:T(8,128)(2,1)S(1)}, u32[]{:S(2)}, u32[]{:S(2)}) %collective-permute-start.47) | collective-permute-done | bytes 278560 | tf_op jit(solution)/shard_map/ppermute | solution.py:639
  (291 shorter events, 84.5 us)
Async XLA Ops:
  7.2 198.7 %all-gather.3.cloned.1.call-start = ((), (), s32[]{:S(2)}) async-start(), calls=%async_computation | async-start | bytes 17301504 | tf_op jit(solution)/shard_map/all_gather | solution.py:908
  10.6 16.4 %collective-permute-start = (bf16[1,32,4224]{2,1,0:T(8,128)(2,1)S(1)}, bf16[1,32,4224]{2,1,0:T(8,128)(2,1)S(1)}, u32[]{:S(2)}, u32[]{:S(2)}) collective-permute-start(bf16[1,32,4224]{2,1,0:T(8,128)(2,1)S(1)} %maximum_bitcast_fusion), channel_id=1, source_target_pairs={{0,16},{1,17},{2,18},{3,19},{4,20},{5,21},{6,22},{7,23},{8,24},{9,... | collective-permute-start | bytes 811016 | tf_op jit(solution)/shard_map/ppermute | solution.py:639
  29.8 16.4 %collective-permute-start.1 = (bf16[2,32,4224]{2,1,0:T(8,128)(2,1)S(1)}, bf16[2,32,4224]{2,1,0:T(8,128)(2,1)S(1)}, u32[]{:S(2)}, u32[]{:S(2)}) collective-permute-start(bf16[2,32,4224]{2,1,0:T(8,128)(2,1)S(1)} %pad_maximum_fusion.9), channel_id=1, source_target_pairs={{0,8},{1,9},{2,10},{3,11},{4,12},{5,13},{6,14},{7,15},{8,0},{9,1},... | collective-permute-start | bytes 1622024 | tf_op jit(solution)/shard_map/ppermute | solution.py:639
  46.5 18.8 %collective-permute-start.2 = (bf16[4,32,2048]{2,1,0:T(8,128)(2,1)S(1)}, bf16[4,32,2048]{2,1,0:T(8,128)(2,1)S(1)}, u32[]{:S(2)}, u32[]{:S(2)}) collective-permute-start(bf16[4,32,2048]{2,1,0:T(8,128)(2,1)S(1)} %pad_maximum_fusion.10), channel_id=1, source_target_pairs={{0,4},{1,5},{2,6},{3,7},{4,0},{5,1},{6,2},{7,3},{8,12},{9,13},{10,... | collective-permute-start | bytes 1572872 | tf_op jit(solution)/shard_map/ppermute | solution.py:639
  58.4 39.3 %collective-permute-start.6 = (bf16[8,32,2176]{2,1,0:T(8,128)(2,1)S(1)}, bf16[8,32,2176]{2,1,0:T(8,128)(2,1)S(1)}, u32[]{:S(2)}, u32[]{:S(2)}) collective-permute-start(bf16[8,32,2176]{2,1,0:T(8,128)(2,1)S(1)} %pad_maximum_fusion.2), channel_id=1, source_target_pairs={{0,4},{1,5},{2,6},{3,7},{4,0},{5,1},{6,2},{7,3},{8,12},{9,13},{10,... | collective-permute-start | bytes 3342344 | tf_op jit(solution)/shard_map/ppermute | solution.py:639
  60.1 24.4 %collective-permute-start.8 = (bf16[1,32,4096]{2,1,0:T(8,128)(2,1)S(1)}, bf16[1,32,4096]{2,1,0:T(8,128)(2,1)S(1)}, u32[]{:S(2)}, u32[]{:S(2)}) collective-permute-start(bf16[1,32,4096]{2,1,0:T(8,128)(2,1)S(1)} %bitcast.107), channel_id=1, source_target_pairs={{0,16},{1,17},{2,18},{3,19},{4,20},{5,21},{6,22},{7,23},{8,24},{9,... | collective-permute-start | bytes 786440 | tf_op jit(solution)/shard_map/ppermute | solution.py:639
  65.4 32.7 %collective-permute-start.3 = (bf16[8,32,2048]{2,1,0:T(8,128)(2,1)S(1)}, bf16[8,32,2048]{2,1,0:T(8,128)(2,1)S(1)}, u32[]{:S(2)}, u32[]{:S(2)}) collective-permute-start(bf16[8,32,2048]{2,1,0:T(8,128)(2,1)S(1)} %pad_maximum_fusion.3), channel_id=1, source_target_pairs={{0,2},{1,3},{2,0},{3,1},{4,6},{5,7},{6,4},{7,5},{8,10},{9,11},{10,... | collective-permute-start | bytes 3145736 | tf_op jit(solution)/shard_map/ppermute | solution.py:639
  84.5 22.0 %collective-permute-start.9 = (bf16[2,32,4096]{2,1,0:T(8,128)(2,1)S(1)}, bf16[2,32,4096]{2,1,0:T(8,128)(2,1)S(1)}, u32[]{:S(2)}, u32[]{:S(2)}) collective-permute-start(bf16[2,32,4096]{2,1,0:T(8,128)(2,1)S(1)} %pad_maximum_fusion.11), channel_id=1, source_target_pairs={{0,8},{1,9},{2,10},{3,11},{4,12},{5,13},{6,14},{7,15},{8,0},{9,1},... | collective-permute-start | bytes 1572872 | tf_op jit(solution)/shard_map/ppermute | solution.py:639
  98.0 35.1 %collective-permute-start.7 = (bf16[16,32,2176]{2,1,0:T(8,128)(2,1)S(1)}, bf16[16,32,2176]{2,1,0:T(8,128)(2,1)}, u32[]{:S(2)}, u32[]{:S(2)}) collective-permute-start(bf16[16,32,2176]{2,1,0:T(8,128)(2,1)S(1)} %pad_maximum_fusion.refs_2_), channel_id=1, source_target_pairs={{0,1},{1,0},{2,3},{3,2},{4,5},{5,4},{6,7},{7,6},{8,9},{9,8},{10,11... | collective-permute-start | bytes 6684680 | tf_op jit(solution)/shard_map/ppermute | solution.py:639
  99.6 33.5 %collective-permute-start.4 = (bf16[16,32,2048]{2,1,0:T(8,128)(2,1)}, bf16[16,32,2048]{2,1,0:T(8,128)(2,1)}, u32[]{:S(2)}, u32[]{:S(2)}) collective-permute-start(bf16[16,32,2048]{2,1,0:T(8,128)(2,1)} %pad_maximum_fusion.1.refs_0_), channel_id=1, source_target_pairs={{0,1},{1,0},{2,3},{3,2},{4,5},{5,4},{6,7},{7,6},{8,9},{9,8},{10,11... | collective-permute-start | bytes 6291464 | tf_op jit(solution)/shard_map/ppermute | solution.py:639
  107.5 17.6 %collective-permute-start.10 = (bf16[4,32,2048]{2,1,0:T(8,128)(2,1)S(1)}, bf16[4,32,2048]{2,1,0:T(8,128)(2,1)}, u32[]{:S(2)}, u32[]{:S(2)}) collective-permute-start(bf16[4,32,2048]{2,1,0:T(8,128)(2,1)S(1)} %get-tuple-element.211), channel_id=1, source_target_pairs={{0,4},{1,5},{2,6},{3,7},{4,0},{5,1},{6,2},{7,3},{8,12},{9,13},{10,... | collective-permute-start | bytes 1572872 | tf_op jit(solution)/shard_map/ppermute | solution.py:639
  107.5 20.0 %collective-permute-start.13 = (bf16[4,32,2048]{2,1,0:T(8,128)(2,1)}, bf16[4,32,2048]{2,1,0:T(8,128)(2,1)}, u32[]{:S(2)}, u32[]{:S(2)}) collective-permute-start(bf16[4,32,2048]{2,1,0:T(8,128)(2,1)} %get-tuple-element.210), channel_id=1, source_target_pairs={{0,2},{1,3},{2,0},{3,1},{4,6},{5,7},{6,4},{7,5},{8,10},{9,11},{10,... | collective-permute-start | bytes 1572872 | tf_op jit(solution)/shard_map/ppermute | solution.py:639
  126.4 42.9 %collective-permute-start.11 = (bf16[8,32,2048]{2,1,0:T(8,128)(2,1)S(1)}, bf16[8,32,2048]{2,1,0:T(8,128)(2,1)}, u32[]{:S(2)}, u32[]{:S(2)}) collective-permute-start(bf16[8,32,2048]{2,1,0:T(8,128)(2,1)S(1)} %pad_maximum_fusion.5.mine), channel_id=1, source_target_pairs={{0,2},{1,3},{2,0},{3,1},{4,6},{5,7},{6,4},{7,5},{8,10},{9,11},{10,... | collective-permute-start | bytes 3145736 | tf_op jit(solution)/shard_map/ppermute | solution.py:639
  129.8 41.2 %collective-permute-start.14 = (bf16[8,32,2048]{2,1,0:T(8,128)(2,1)}, bf16[8,32,2048]{2,1,0:T(8,128)(2,1)}, u32[]{:S(2)}, u32[]{:S(2)}) collective-permute-start(bf16[8,32,2048]{2,1,0:T(8,128)(2,1)} %pad_maximum_fusion.6.mine), channel_id=1, source_target_pairs={{0,4},{1,5},{2,6},{3,7},{4,0},{5,1},{6,2},{7,3},{8,12},{9,13},{10,... | collective-permute-start | bytes 3145736 | tf_op jit(solution)/shard_map/ppermute | solution.py:639
  177.3 27.7 %collective-permute-start.16 = (bf16[512,1024]{1,0:T(8,128)(2,1)}, bf16[512,1024]{1,0:T(8,128)(2,1)}, u32[]{:S(2)}, u32[]{:S(2)}) collective-permute-start(bf16[512,1024]{1,0:T(8,128)(2,1)} %get-tuple-element.93), channel_id=1, source_target_pairs={{0,1},{1,0},{2,3},{3,2},{4,5},{5,4},{6,7},{7,6},{8,9},{9,8},{10,11... | collective-permute-start | bytes 3145736 | tf_op jit(solution)/shard_map/ppermute | solution.py:639
  179.3 25.7 %collective-permute-start.17 = (bf16[512,384]{1,0:T(8,128)(2,1)}, bf16[512,384]{1,0:T(8,128)(2,1)}, u32[]{:S(2)}, u32[]{:S(2)}) collective-permute-start(bf16[512,384]{1,0:T(8,128)(2,1)} %get-tuple-element.94), channel_id=1, source_target_pairs={{0,1},{1,0},{2,3},{3,2},{4,5},{5,4},{6,7},{7,6},{8,9},{9,8},{10,11... | collective-permute-start | bytes 1179656 | tf_op jit(solution)/shard_map/ppermute | solution.py:639
  180.5 24.5 %collective-permute-start.18 = (bf16[512,768]{1,0:T(8,128)(2,1)}, bf16[512,768]{1,0:T(8,128)(2,1)S(1)}, u32[]{:S(2)}, u32[]{:S(2)}) collective-permute-start(bf16[512,768]{1,0:T(8,128)(2,1)} %get-tuple-element.95), channel_id=1, source_target_pairs={{0,1},{1,0},{2,3},{3,2},{4,5},{5,4},{6,7},{7,6},{8,9},{9,8},{10,11... | collective-permute-start | bytes 2359304 | tf_op jit(solution)/shard_map/ppermute | solution.py:639
  205.0 19.2 %collective-permute-start.19 = (bf16[512,768]{1,0:T(8,128)(2,1)}, bf16[512,768]{1,0:T(8,128)(2,1)}, u32[]{:S(2)}, u32[]{:S(2)}) collective-permute-start(bf16[512,768]{1,0:T(8,128)(2,1)} %get-tuple-element.101), channel_id=1, source_target_pairs={{0,1},{1,0},{2,3},{3,2},{4,5},{5,4},{6,7},{7,6},{8,9},{9,8},{10,11... | collective-permute-start | bytes 2359304 | tf_op jit(solution)/shard_map/ppermute | solution.py:639
  223.7 22.8 %collective-permute-start.21 = (bf16[2048,384]{1,0:T(8,128)(2,1)S(1)}, bf16[2048,384]{1,0:T(8,128)(2,1)S(1)}, u32[]{:S(2)}, u32[]{:S(2)}) collective-permute-start(bf16[2048,384]{1,0:T(8,128)(2,1)S(1)} %get-tuple-element.108), channel_id=1, source_target_pairs={{0,1},{1,0},{2,3},{3,2},{4,5},{5,4},{6,7},{7,6},{8,9},{9,8},{10,11... | collective-permute-start | bytes 4718600 | tf_op jit(solution)/shard_map/ppermute | solution.py:639
  239.7 18.4 %collective-permute-start.20 = (bf16[384,4096]{1,0:T(8,128)(2,1)S(1)}, bf16[384,4096]{1,0:T(8,128)(2,1)}, u32[]{:S(2)}, u32[]{:S(2)}) collective-permute-start(bf16[384,4096]{1,0:T(8,128)(2,1)S(1)} %get-tuple-element.106.refs_4_.refs_2_), channel_id=1, source_target_pairs={{0,1},{1,0},{2,3},{3,2},{4,5},{5,4},{6,7},{7,6},{8,9},{9,8},{10,11... | collective-permute-start | bytes 9437192 | tf_op jit(solution)/shard_map/ppermute | solution.py:639
  256.7 35.6 %collective-permute-start.23 = (bf16[1024,512]{1,0:T(8,128)(2,1)}, bf16[1024,512]{1,0:T(8,128)(2,1)}, u32[]{:S(2)}, u32[]{:S(2)}) collective-permute-start(bf16[1024,512]{1,0:T(8,128)(2,1)} %get-tuple-element.109.refs_4_), channel_id=1, source_target_pairs={{0,4},{1,5},{2,6},{3,7},{4,0},{5,1},{6,2},{7,3},{8,12},{9,13},{10,... | collective-permute-start | bytes 3145736 | tf_op jit(solution)/shard_map/ppermute | solution.py:639
  257.8 34.5 %collective-permute-start.24 = (bf16[1024,512]{1,0:T(8,128)(2,1)}, bf16[1024,512]{1,0:T(8,128)(2,1)}, u32[]{:S(2)}, u32[]{:S(2)}) collective-permute-start(bf16[1024,512]{1,0:T(8,128)(2,1)} %get-tuple-element.110.refs_5_), channel_id=1, source_target_pairs={{0,2},{1,3},{2,0},{3,1},{4,6},{5,7},{6,4},{7,5},{8,10},{9,11},{10,... | collective-permute-start | bytes 3145736 | tf_op jit(solution)/shard_map/ppermute | solution.py:639
  268.6 43.1 %collective-permute-start.28 = (bf16[256,2048]{1,0:T(8,128)(2,1)}, bf16[256,2048]{1,0:T(8,128)(2,1)}, u32[]{:S(2)}, u32[]{:S(2)}) collective-permute-start(bf16[256,2048]{1,0:T(8,128)(2,1)} %get-tuple-element.111.rest_0_), channel_id=1, source_target_pairs={{0,4},{1,5},{2,6},{3,7},{4,0},{5,1},{6,2},{7,3},{8,12},{9,13},{10,... | collective-permute-start | bytes 3145736 | tf_op jit(solution)/shard_map/ppermute | solution.py:639
  269.6 42.1 %collective-permute-start.29 = (bf16[256,2048]{1,0:T(8,128)(2,1)}, bf16[256,2048]{1,0:T(8,128)(2,1)}, u32[]{:S(2)}, u32[]{:S(2)}) collective-permute-start(bf16[256,2048]{1,0:T(8,128)(2,1)} %get-tuple-element.112.rest_1_), channel_id=1, source_target_pairs={{0,2},{1,3},{2,0},{3,1},{4,6},{5,7},{6,4},{7,5},{8,10},{9,11},{10,... | collective-permute-start | bytes 3145736 | tf_op jit(solution)/shard_map/ppermute | solution.py:639
  292.2 23.3 %collective-permute-start.27 = (bf16[2816,1024]{1,0:T(8,128)(2,1)}, bf16[2816,1024]{1,0:T(8,128)(2,1)}, u32[]{:S(2)}, u32[]{:S(2)}) collective-permute-start(bf16[2816,1024]{1,0:T(8,128)(2,1)} %get-tuple-element.113.query_delta.refs_6_.refs_0_.refs_1_), channel_id=1, source_target_pairs={{0,1},{1,0},{2,3},{3,2},{4,5},{5,4},{6,7},{7,6},{8,9},{9,8},{10,11... | collective-permute-start | bytes 17301512 | tf_op jit(solution)/shard_map/ppermute | solution.py:639
  310.7 23.5 %collective-permute-start.35 = (bf16[1536,1024]{1,0:T(8,128)(2,1)}, bf16[1536,1024]{1,0:T(8,128)(2,1)}, u32[]{:S(2)}, u32[]{:S(2)}) collective-permute-start(bf16[1536,1024]{1,0:T(8,128)(2,1)} %get-tuple-element.119.refs_4_.refs_0_.refs_1_.refs_2_), channel_id=1, source_target_pairs={{0,1},{1,0},{2,3},{3,2},{4,5},{5,4},{6,7},{7,6},{8,9},{9,8},{10,11... | collective-permute-start | bytes 9437192 | tf_op jit(solution)/shard_map/ppermute | solution.py:639
  311.2 21.5 %collective-permute-start.25 = (bf16[4,128,512]{2,1,0:T(8,128)(2,1)}, bf16[4,128,512]{2,1,0:T(8,128)(2,1)S(1)}, u32[]{:S(2)}, u32[]{:S(2)}) collective-permute-start(bf16[4,128,512]{2,1,0:T(8,128)(2,1)} %copy-done.40), channel_id=1, source_target_pairs={{0,2},{1,3},{2,0},{3,1},{4,6},{5,7},{6,4},{7,5},{8,10},{9,11},{10,... | collective-permute-start | bytes 1572872 | tf_op jit(solution)/shard_map/ppermute | solution.py:639
  311.7 21.1 %collective-permute-start.26 = (bf16[4,128,512]{2,1,0:T(8,128)(2,1)}, bf16[4,128,512]{2,1,0:T(8,128)(2,1)S(1)}, u32[]{:S(2)}, u32[]{:S(2)}) collective-permute-start(bf16[4,128,512]{2,1,0:T(8,128)(2,1)} %copy-done.39), channel_id=1, source_target_pairs={{0,4},{1,5},{2,6},{3,7},{4,0},{5,1},{6,2},{7,3},{8,12},{9,13},{10,... | collective-permute-start | bytes 1572872 | tf_op jit(solution)/shard_map/ppermute | solution.py:639
  313.9 31.4 %collective-permute-start.33 = (bf16[4,32,2048]{2,1,0:T(8,128)(2,1)S(1)}, bf16[4,32,2048]{2,1,0:T(8,128)(2,1)S(1)}, u32[]{:S(2)}, u32[]{:S(2)}) collective-permute-start(bf16[4,32,2048]{2,1,0:T(8,128)(2,1)S(1)} %get-tuple-element.138), channel_id=1, source_target_pairs={{0,2},{1,3},{2,0},{3,1},{4,6},{5,7},{6,4},{7,5},{8,10},{9,11},{10,... | collective-permute-start | bytes 1572872 | tf_op jit(solution)/shard_map/ppermute | solution.py:639
  315.6 29.7 %collective-permute-start.34 = (bf16[4,32,2048]{2,1,0:T(8,128)(2,1)S(1)}, bf16[4,32,2048]{2,1,0:T(8,128)(2,1)S(1)}, u32[]{:S(2)}, u32[]{:S(2)}) collective-permute-start(bf16[4,32,2048]{2,1,0:T(8,128)(2,1)S(1)} %get-tuple-element.139), channel_id=1, source_target_pairs={{0,4},{1,5},{2,6},{3,7},{4,0},{5,1},{6,2},{7,3},{8,12},{9,13},{10,... | collective-permute-start | bytes 1572872 | tf_op jit(solution)/shard_map/ppermute | solution.py:639
  334.3 36.7 %collective-permute-start.30 = (bf16[2,128,1024]{2,1,0:T(8,128)(2,1)}, bf16[2,128,1024]{2,1,0:T(8,128)(2,1)S(1)}, u32[]{:S(2)}, u32[]{:S(2)}) collective-permute-start(bf16[2,128,1024]{2,1,0:T(8,128)(2,1)} %get-tuple-element.131), channel_id=1, source_target_pairs={{0,8},{1,9},{2,10},{3,11},{4,12},{5,13},{6,14},{7,15},{8,0},{9,1},... | collective-permute-start | bytes 1572872 | tf_op jit(solution)/shard_map/ppermute | solution.py:639
  334.3 27.8 %collective-permute-start.31 = (bf16[256,2048]{1,0:T(8,128)(2,1)}, bf16[256,2048]{1,0:T(8,128)(2,1)S(1)}, u32[]{:S(2)}, u32[]{:S(2)}) collective-permute-start(bf16[256,2048]{1,0:T(8,128)(2,1)} %get-tuple-element.132), channel_id=1, source_target_pairs={{0,4},{1,5},{2,6},{3,7},{4,0},{5,1},{6,2},{7,3},{8,12},{9,13},{10,... | collective-permute-start | bytes 3145736 | tf_op jit(solution)/shard_map/ppermute | solution.py:639
  334.3 30.4 %collective-permute-start.32 = (bf16[256,2048]{1,0:T(8,128)(2,1)}, bf16[256,2048]{1,0:T(8,128)(2,1)}, u32[]{:S(2)}, u32[]{:S(2)}) collective-permute-start(bf16[256,2048]{1,0:T(8,128)(2,1)} %get-tuple-element.134), channel_id=1, source_target_pairs={{0,2},{1,3},{2,0},{3,1},{4,6},{5,7},{6,4},{7,5},{8,10},{9,11},{10,... | collective-permute-start | bytes 3145736 | tf_op jit(solution)/shard_map/ppermute | solution.py:639
  346.5 13.4 %collective-permute-start.38 = (bf16[2,2,2,2,32,256]{5,4,2,1,0,3:T(8,128)(2,1)S(1)}, bf16[2,2,2,2,32,256]{5,4,2,1,0,3:T(8,128)(2,1)S(1)}, u32[]{:S(2)}, u32[]{:S(2)}) collective-permute-start(bf16[2,2,2,2,32,256]{5,4,2,1,0,3:T(8,128)(2,1)S(1)} %bitcast.151), channel_id=1, source_target_pairs={{0,1},{1,0},{2,3},{3,2},{4,5},{5,4},{6,7},{7,6},{8,9},{9,8},{10,11... | collective-permute-start | bytes 786440 | tf_op jit(solution)/shard_map/ppermute | solution.py:639
  346.6 26.6 %collective-permute-start.40 = (bf16[2,32,4096]{2,1,0:T(8,128)(2,1)S(1)}, bf16[2,32,4096]{2,1,0:T(8,128)(2,1)S(1)}, u32[]{:S(2)}, u32[]{:S(2)}) collective-permute-start(bf16[2,32,4096]{2,1,0:T(8,128)(2,1)S(1)} %get-tuple-element.149), channel_id=1, source_target_pairs={{0,8},{1,9},{2,10},{3,11},{4,12},{5,13},{6,14},{7,15},{8,0},{9,1},... | collective-permute-start | bytes 1572872 | tf_op jit(solution)/shard_map/ppermute | solution.py:639
  359.9 32.2 %collective-permute-start.36 = (bf16[256,2048]{1,0:T(8,128)(2,1)S(1)}, bf16[256,2048]{1,0:T(8,128)(2,1)S(1)}, u32[]{:S(2)}, u32[]{:S(2)}) collective-permute-start(bf16[256,2048]{1,0:T(8,128)(2,1)S(1)} %get-tuple-element.146), channel_id=1, source_target_pairs={{0,4},{1,5},{2,6},{3,7},{4,0},{5,1},{6,2},{7,3},{8,12},{9,13},{10,... | collective-permute-start | bytes 3145736 | tf_op jit(solution)/shard_map/ppermute | solution.py:639
  363.1 29.1 %collective-permute-start.37 = (bf16[256,2048]{1,0:T(8,128)(2,1)}, bf16[256,2048]{1,0:T(8,128)(2,1)S(1)}, u32[]{:S(2)}, u32[]{:S(2)}) collective-permute-start(bf16[256,2048]{1,0:T(8,128)(2,1)} %get-tuple-element.148), channel_id=1, source_target_pairs={{0,2},{1,3},{2,0},{3,1},{4,6},{5,7},{6,4},{7,5},{8,10},{9,11},{10,... | collective-permute-start | bytes 3145736 | tf_op jit(solution)/shard_map/ppermute | solution.py:639
  364.7 27.4 %collective-permute-start.39 = (bf16[2,2,2,32,256]{4,3,2,1,0:T(8,128)(2,1)S(1)}, bf16[2,2,2,32,256]{4,3,2,1,0:T(8,128)(2,1)S(1)}, u32[]{:S(2)}, u32[]{:S(2)}) collective-permute-start(bf16[2,2,2,32,256]{4,3,2,1,0:T(8,128)(2,1)S(1)} %get-tuple-element.216), channel_id=1, source_target_pairs={{0,2},{1,3},{2,0},{3,1},{4,6},{5,7},{6,4},{7,5},{8,10},{9,11},{10,... | collective-permute-start | bytes 393224 | tf_op jit(solution)/shard_map/ppermute | solution.py:639
  370.9 31.3 %collective-permute-start.43 = (bf16[4,32,2048]{2,1,0:T(8,128)(2,1)}, bf16[4,32,2048]{2,1,0:T(8,128)(2,1)S(1)}, u32[]{:S(2)}, u32[]{:S(2)}) collective-permute-start(bf16[4,32,2048]{2,1,0:T(8,128)(2,1)} %get-tuple-element.155), channel_id=1, source_target_pairs={{0,2},{1,3},{2,0},{3,1},{4,6},{5,7},{6,4},{7,5},{8,10},{9,11},{10,... | collective-permute-start | bytes 1572872 | tf_op jit(solution)/shard_map/ppermute | solution.py:639
  373.2 29.0 %collective-permute-start.44 = (bf16[4,32,2048]{2,1,0:T(8,128)(2,1)S(1)}, bf16[4,32,2048]{2,1,0:T(8,128)(2,1)S(1)}, u32[]{:S(2)}, u32[]{:S(2)}) collective-permute-start(bf16[4,32,2048]{2,1,0:T(8,128)(2,1)S(1)} %get-tuple-element.156), channel_id=1, source_target_pairs={{0,4},{1,5},{2,6},{3,7},{4,0},{5,1},{6,2},{7,3},{8,12},{9,13},{10,... | collective-permute-start | bytes 1572872 | tf_op jit(solution)/shard_map/ppermute | solution.py:639
  393.2 34.5 %collective-permute-start.42 = (bf16[4,32,2304]{2,1,0:T(8,128)(2,1)S(1)}, bf16[4,32,2304]{2,1,0:T(8,128)(2,1)S(1)}, u32[]{:S(2)}, u32[]{:S(2)}) collective-permute-start(bf16[4,32,2304]{2,1,0:T(8,128)(2,1)S(1)} %get-tuple-element.154), channel_id=1, source_target_pairs={{0,4},{1,5},{2,6},{3,7},{4,0},{5,1},{6,2},{7,3},{8,12},{9,13},{10,... | collective-permute-start | bytes 1769480 | tf_op jit(solution)/shard_map/ppermute | solution.py:639
  403.0 24.0 %collective-permute-start.45 = (bf16[2,32,4096]{2,1,0:T(8,128)(2,1)S(1)}, bf16[2,32,4096]{2,1,0:T(8,128)(2,1)S(1)}, u32[]{:S(2)}, u32[]{:S(2)}) collective-permute-start(bf16[2,32,4096]{2,1,0:T(8,128)(2,1)S(1)} %get-tuple-element.158), channel_id=1, source_target_pairs={{0,8},{1,9},{2,10},{3,11},{4,12},{5,13},{6,14},{7,15},{8,0},{9,1},... | collective-permute-start | bytes 1572872 | tf_op jit(solution)/shard_map/ppermute | solution.py:639
  403.7 23.9 %collective-permute-start.41 = (bf16[4,32,2048]{2,1,0:T(8,128)(2,1)S(1)}, bf16[4,32,2048]{2,1,0:T(8,128)(2,1)S(1)}, u32[]{:S(2)}, u32[]{:S(2)}) collective-permute-start(bf16[4,32,2048]{2,1,0:T(8,128)(2,1)S(1)} %get-tuple-element.152), channel_id=1, source_target_pairs={{0,2},{1,3},{2,0},{3,1},{4,6},{5,7},{6,4},{7,5},{8,10},{9,11},{10,... | collective-permute-start | bytes 1572872 | tf_op jit(solution)/shard_map/ppermute | solution.py:639
  405.4 23.5 %collective-permute-start.49 = (bf16[1,32,4096]{2,1,0:T(8,128)(2,1)S(1)}, bf16[1,32,4096]{2,1,0:T(8,128)(2,1)S(1)}, u32[]{:S(2)}, u32[]{:S(2)}) collective-permute-start(bf16[1,32,4096]{2,1,0:T(8,128)(2,1)S(1)} %get-tuple-element.165), channel_id=1, source_target_pairs={{0,16},{1,17},{2,18},{3,19},{4,20},{5,21},{6,22},{7,23},{8,24},{9,... | collective-permute-start | bytes 786440 | tf_op jit(solution)/shard_map/ppermute | solution.py:639
  411.3 19.7 %collective-permute-start.50 = (bf16[1,128,1024]{2,1,0:T(8,128)(2,1)S(1)}, bf16[1,128,1024]{2,1,0:T(8,128)(2,1)S(1)}, u32[]{:S(2)}, u32[]{:S(2)}) collective-permute-start(bf16[1,128,1024]{2,1,0:T(8,128)(2,1)S(1)} %get-tuple-element.166), channel_id=1, source_target_pairs={{0,16},{1,17},{2,18},{3,19},{4,20},{5,21},{6,22},{7,23},{8,24},{9,... | collective-permute-start | bytes 786440 | tf_op jit(solution)/shard_map/ppermute | solution.py:639
  428.5 18.4 %collective-permute-start.46 = (bf16[2,32,4352]{2,1,0:T(8,128)(2,1)S(1)}, bf16[2,32,4352]{2,1,0:T(8,128)(2,1)S(1)}, u32[]{:S(2)}, u32[]{:S(2)}) collective-permute-start(bf16[2,32,4352]{2,1,0:T(8,128)(2,1)S(1)} %get-tuple-element.161), channel_id=1, source_target_pairs={{0,8},{1,9},{2,10},{3,11},{4,12},{5,13},{6,14},{7,15},{8,0},{9,1},... | collective-permute-start | bytes 1671176 | tf_op jit(solution)/shard_map/ppermute | solution.py:639
  428.6 23.8 %collective-permute-start.48 = (bf16[1,32,4096]{2,1,0:T(8,128)(2,1)S(1)}, bf16[1,32,4096]{2,1,0:T(8,128)(2,1)S(1)}, u32[]{:S(2)}, u32[]{:S(2)}) collective-permute-start(bf16[1,32,4096]{2,1,0:T(8,128)(2,1)S(1)} %get-tuple-element.164), channel_id=1, source_target_pairs={{0,16},{1,17},{2,18},{3,19},{4,20},{5,21},{6,22},{7,23},{8,24},{9,... | collective-permute-start | bytes 786440 | tf_op jit(solution)/shard_map/ppermute | solution.py:639
  447.7 17.0 %collective-permute-start.47 = (bf16[1,32,4352]{2,1,0:T(8,128)(2,1)S(1)}, bf16[1,32,4352]{2,1,0:T(8,128)(2,1)S(1)}, u32[]{:S(2)}, u32[]{:S(2)}) collective-permute-start(bf16[1,32,4352]{2,1,0:T(8,128)(2,1)S(1)} %get-tuple-element.163), channel_id=1, source_target_pairs={{0,16},{1,17},{2,18},{3,19},{4,20},{5,21},{6,22},{7,23},{8,24},{9,... | collective-permute-start | bytes 835592 | tf_op jit(solution)/shard_map/ppermute | solution.py:639
  (68 other events, 490.9 us)
Sparse Core Ops, SparseCore 0:
  29.9 162.0 all-gather.2

commit v4 on v3

--- a/solution.py
+++ b/solution.py
@@ -129,7 +129,8 @@
     scale = HEAD_DIM**-0.5
     (tokens, width), mems = q.shape, pairs.shape[0]
     grad[...] = dot(branch[...], weight[...], (1, 1)).astype(jnp.bfloat16)
-    keys_at, values_at = 2 * tokens, 2 * tokens + mems
+    pad = (out.shape[0] - 2 * mems) // 2
+    query_at, branch_at = 2 * mems, 2 * mems + pad
 
     def sequence(s, carry):
         low, high = bound[0, s], bound[1, s]
@@ -166,14 +167,19 @@
 
         lax.fori_loop(first, last, two, 0)
         for p in range(PAIRS):
-            out[rows, cols(p)] = (join_heads_t(acc[p]) * scale).astype(jnp.bfloat16)
+            place = pl.ds(pl.multiple_of(query_at + s * SEQ_LEN, SEQ_LEN), SEQ_LEN)
+            out[place, cols(p)] = (join_heads_t(acc[p]) * scale).astype(jnp.bfloat16)
         return carry
 
     lax.fori_loop(0, bound.shape[1], sequence, 0)
-    out[keys_at:values_at, :] = pair_acc[:, :width].astype(jnp.bfloat16)
-    out[values_at:, :] = pair_acc[:, width:].astype(jnp.bfloat16)
-    out[tokens:keys_at, :] = branch[...]
-    sums[...] = sum_rows(out[:tokens, :].astype(jnp.float32), out[values_at:, :].astype(jnp.float32))
+    out[:mems, :] = pair_acc[:, :width].astype(jnp.bfloat16)
+    out[mems:query_at, :] = pair_acc[:, width:].astype(jnp.bfloat16)
+    out[branch_at : branch_at + tokens, :] = branch[...]
+    for at in (query_at, branch_at):
+        out[at + tokens : at + pad, :] = jnp.zeros((pad - tokens, width), jnp.bfloat16)
+    sums[...] = sum_rows(
+        out[query_at : query_at + tokens, :].astype(jnp.float32), out[mems:query_at, :].astype(jnp.float32)
+    )
 
 
 def cross_forward(bound, q, pairs, after=()):
@@ -204,7 +210,7 @@
     wide = 2 * SEQ_LEN
     width = q.shape[1]
     whole = lambda shape: pl.BlockSpec(shape, lambda i: (0,) * len(shape))
-    rows = 2 * pairs.shape[0] + 2 * q.shape[0]
+    rows = 3 * pairs.shape[0]
     return pl.pallas_call(
         functools.partial(cross_backward_kernel, extra=len(after)),
         grid=(1,),
@@ -265,7 +271,7 @@
     out, sums, first_grad, grad = rest[extra:]
     scale = HEAD_DIM**-0.5
     tokens = qkv.shape[0]
-    total = second_grad[...] + dot(query_delta[...], w_query[...], (1, 1))
+    total = second_grad[...] + dot(query_delta[:tokens, :], w_query[...], (1, 1))
     first = normalize_back(total, unit[...], inverse[...], gain[...])
     first_grad[...] = first
     branch = first.astype(jnp.bfloat16)
@@ -316,7 +322,7 @@
 
 
 def self_backward(
-    lengths, qkv, summary, second_grad, cross_delta, late, early, unit, inverse, gain, after=()
+    lengths, qkv, summary, second_grad, cross_delta, weights, unit, inverse, gain, after=()
 ):
     tokens, width = second_grad.shape
     whole = lambda shape: pl.BlockSpec(shape, lambda i: (0,) * len(shape))
@@ -334,8 +340,8 @@
             whole(qkv.shape),
             whole(summary.shape),
             full,
-            full,
-            pl.BlockSpec((width, width), lambda i: (0, 0)),
+            pl.BlockSpec((cross_delta.shape[0] // 6, width), lambda i: (4, 0)),
+            pl.BlockSpec((width, width), lambda i: (0, 4)),
             pl.BlockSpec((width, width), lambda i: (0, 3)),
             full,
             whole((tokens, 1)),
@@ -346,7 +352,7 @@
         scratch_shapes=[pltpu.VMEM((tokens, width), jnp.bfloat16)],
         compiler_params=kernel_params(48),
         cost_estimate=cost(6e9, 12),
-    )(lengths, qkv, summary, second_grad, cross_delta, late, early, unit, inverse, gain, *after)
+    )(lengths, qkv, summary, second_grad, cross_delta, weights, weights, unit, inverse, gain, *after)
 
 
 def normalize(values, gain, shift):
@@ -561,9 +567,10 @@
     )(packed, packed, slope, third_grad, out_grad, unit, inverse, gain, *after)
 
 
-def product_kernel(ids, *refs, spans, n_left, rows, chunk, extra):
-    lefts, rights = refs[:n_left], refs[n_left : n_left + 2]
-    keep_a, send_a, keep_b, send_b, ordered, *wide = refs[n_left + 2 + extra :]
+def product_kernel(ids, *refs, spans, n_left, n_right, rows, chunk, extra, sides):
+    lefts, rights = refs[:n_left], refs[n_left : n_left + 2 * n_right]
+    rest = refs[n_left + 2 * n_right + extra :]
+    outs, (ordered, *wide) = rest[: 2 * len(sides)], rest[2 * len(sides) :]
     step = pl.program_id(0)
     blocks = lefts[0].shape[0] // rows
     half = blocks // 2 * rows
@@ -576,62 +583,96 @@
             if wide:
                 source = wide[0].at[:, pl.ds(0, size)]
                 source[...] = left[...].astype(jnp.float32)
-            for order, bit in ((0, 1), (1, 0)):
+            for side, order in enumerate(sides):
+                bit = 1 - order
                 for i in range(blocks):
                     low, high = i % (1 << bit), (i % (blocks // 2)) >> bit
                     mine = ids[2 - order] if i < blocks // 2 else 1 - ids[2 - order]
                     place = (high << (bit + 1)) + (mine << bit) + low
                     taken = source[pl.ds(pl.multiple_of(place * rows, rows), rows), :]
-                    ordered[order, i * rows : (i + 1) * rows, start : start + size] = taken.astype(jnp.bfloat16)
+                    ordered[side, i * rows : (i + 1) * rows, start : start + size] = taken.astype(jnp.bfloat16)
             start += size
 
     steps = sum(s[-1] for s in spans)
     first = 0
-    for mine, other, tokens, row, count in spans:
-        a, b = max(first, 0), min(first + count, steps)
-        for order, keep, send in ((0, keep_a, send_a), (1, keep_b, send_b)):
-            low, high = max(a, order * steps // 2), min(b, (order + 1) * steps // 2)
+    for mine, other, tokens, which, _, count in spans:
+        for side in range(len(sides)):
+            keep, send = outs[2 * side : 2 * side + 2]
+            low = max(first, side * steps // len(sides))
+            high = min(first + count, (side + 1) * steps // len(sides))
             if low >= high:
                 continue
 
             @pl.when((step >= low) & (step < high))
-            def _(mine=mine, other=other, tokens=tokens, row=row, order=order, keep=keep, send=send, first=first):
-                columns = pl.ds(pl.multiple_of((step - first) * chunk, chunk), chunk)
-                total = jnp.zeros((2 * half, chunk), jnp.float32)
-                for start, right in ((mine, rights[0]), (other, rights[1])):
-                    total += dot(
-                        ordered[order, :, start : start + tokens], right[row : row + tokens, columns], (1, 0)
-                    )
+            def _(mine=mine, other=other, tokens=tokens, which=which, side=side, keep=keep, send=send):
+                total = dot(
+                    ordered[side, :, mine : mine + tokens], rights[2 * which][:tokens, :], (1, 0)
+                ) + dot(
+                    ordered[side, :, other : other + tokens], rights[2 * which + 1][:tokens, :], (1, 0)
+                )
                 keep[...] = total[:half].astype(jnp.bfloat16)
                 send[...] = total[half:].astype(jnp.bfloat16)
 
         first += count
 
 
-def products(ids, lefts, right, spans, rows, chunk, after=()):
+def products(ids, lefts, rights, spans, rows, chunk, sides=(0, 1), after=()):
     height = lefts[0][0].shape[0]
     columns = sum(s[-1] for s in spans)
     steps = columns // chunk
     spans = [(*s[:-1], s[-1] // chunk) for s in spans]
-    part = jax.ShapeDtypeStruct((height // 2, columns // 2), jnp.bfloat16)
-    block_a = pl.BlockSpec((height // 2, chunk), lambda j: (0, jnp.minimum(j, steps // 2 - 1)))
-    block_b = pl.BlockSpec((height // 2, chunk), lambda j: (0, jnp.maximum(j - steps // 2, 0)))
-    whole = lambda array: pl.BlockSpec(array.shape, lambda j: (0, 0))
+    count = len(sides)
+    part = jax.ShapeDtypeStruct((height // 2, columns // count), jnp.bfloat16)
+    blocks = [
+        pl.BlockSpec(
+            (height // 2, chunk),
+            lambda j, side=side: (0, jnp.clip(j - side * steps // count, 0, steps // count - 1)),
+        )
+        for side in range(count)
+        for _ in range(2)
+    ]
     tokens = sum(x[1] for x in lefts)
     wide = [pltpu.VMEM((height, max(x[1] for x in lefts)), jnp.float32)] if rows % 16 else []
     taken = [pl.BlockSpec((height, size), lambda j, place=place: (0, place)) for _, size, place in lefts]
+
+    def place_of(which):
+        def index(j):
+            first, found = 0, []
+            for _, _, _, w, row, count in spans:
+                if w == which:
+                    found.append((first, first + count, row))
+                first += count
+            first, end, row = found[-1]
+            at_row, at_column = row, jnp.clip(j - first, 0, end - first - 1)
+            for first, end, row in found[-2::-1]:
+                at_row = jnp.where(j < end, row, at_row)
+                at_column = jnp.where(j < end, jnp.clip(j - first, 0, end - first - 1), at_column)
+            return at_row, at_column
+
+        return index
+
+    strips = [
+        pl.BlockSpec((block, chunk), place_of(i)) for i, (_, _, block) in enumerate(rights) for _ in range(2)
+    ]
     return pl.pallas_call(
         functools.partial(
-            product_kernel, spans=spans, n_left=len(lefts), rows=rows, chunk=chunk, extra=len(after)
+            product_kernel,
+            spans=spans,
+            n_left=len(lefts),
+            n_right=len(rights),
+            rows=rows,
+            chunk=chunk,
+            extra=len(after),
+            sides=sides,
         ),
         grid=(steps,),
-        out_shape=(part,) * 4,
-        in_specs=[smem] + taken + [whole(x) for x in right] + [anywhere] * len(after),
-        out_specs=(block_a, block_a, block_b, block_b),
-        scratch_shapes=[pltpu.VMEM((2, height, tokens), jnp.bfloat16)] + wide,
+        out_shape=(part,) * (2 * count),
+        in_specs=[smem] + taken + strips + [anywhere] * len(after),
+        out_specs=blocks,
+        scratch_shapes=[pltpu.VMEM((count, height, tokens), jnp.bfloat16)] + wide,
         compiler_params=kernel_params(48),
         cost_estimate=cost(2.5 * height * tokens * columns / len(lefts), 20),
-    )(ids, *[x[0] for x in lefts], *right, *after)
+    )(ids, *[x[0] for x in lefts], *[x for right in rights for x in right[:2]], *after)
 
 
 def exchange(values, bit):
@@ -639,37 +680,9 @@
     return lax.ppermute(values, AXES, [(i, i ^ (1 << bit)) for i in range(count)])
 
 
-def pack_kernel(*refs, places, extra):
-    parts, out, sems = refs[: len(places)], refs[-2], refs[-1]
-    copies = [
-        pltpu.make_async_copy(
-            part.at[:, pl.ds(begin, size)],
-            out.at[pl.ds(row, part.shape[0]), pl.ds(column, size)],
-            sems.at[i],
-        )
-        for i, (part, (begin, size, row, column)) in enumerate(zip(parts, places))
-    ]
-    for copy in copies:
-        copy.start()
-    for copy in copies:
-        copy.wait()
-
-
-def pack_rows(parts, places, shape, after):
-    return pl.pallas_call(
-        functools.partial(pack_kernel, places=places, extra=len(after)),
-        out_shape=jax.ShapeDtypeStruct(shape, jnp.bfloat16),
-        in_specs=[anywhere] * (len(parts) + len(after)),
-        out_specs=anywhere,
-        scratch_shapes=[pltpu.SemaphoreType.DMA((len(parts),))],
-        compiler_params=kernel_params(16),
-        cost_estimate=cost(0, 4 * shape[0] * shape[1] / 2**20),
-    )(*parts, *after)
-
-
 def place_kernel(*refs, slots, rows):
     me = lax.axis_index(AXES)
-    pieces, out, sems = refs[:-2], refs[-2], refs[-1]
+    pieces, out, sems = refs[: len(slots)], refs[-2], refs[-1]
     copies = []
     for piece, (start, order) in zip(pieces, slots):
         columns = pl.ds(start, piece.shape[-1])
@@ -684,53 +697,91 @@
         copy.wait()
 
 
-def join_kernel(mine, arrived, *refs):
+def join_kernel(*refs, count, split):
+    parts, outs = refs[: 2 * count], refs[-(2 if split else count) :]
+    for i in range(count):
+        first = 0
+        for part in parts[2 * i : 2 * i + 2]:
+            rows = slice(first, first + part.shape[0])
+            if split:
+                outs[0][rows] = part[:, :, :split]
+                outs[1][rows] = part[:, :, split:]
+            else:
+                outs[i][rows] = part[...]
+            first += part.shape[0]
+
+
+def pack_kernel(w_in, w_out, *refs):
     out = refs[-1]
-    out[: mine.shape[0]] = mine[...]
-    out[mine.shape[0] :] = arrived[...]
-
-
-def join(mine, arrived, after):
+    rows, width = w_in.shape[0], out.shape[1]
+    count = w_in.shape[1] // width
+    for i in range(count):
+        out[i * rows : (i + 1) * rows, :] = w_in[:, i * width : (i + 1) * width]
+    out[count * rows :, :] = w_out[...]
+
+
+def pack_ffn(w_in, w_out, after):
     return pl.pallas_call(
-        join_kernel,
-        out_shape=jax.ShapeDtypeStruct((2 * mine.shape[0], *mine.shape[1:]), mine.dtype),
+        pack_kernel,
+        out_shape=jax.ShapeDtypeStruct((2 * w_out.shape[0], w_out.shape[1]), jnp.bfloat16),
         in_specs=[vmem] * 2 + [anywhere] * len(after),
         out_specs=vmem,
         compiler_params=kernel_params(16),
-        cost_estimate=cost(0, 8 * mine.size / 2**20),
-    )(mine, arrived, *after)
-
-
-def gather_rows(local, after=()):
-    rows, width = local.shape
-    count = lax.axis_size(AXES)
-    values, order, stages = local[None], [0], []
-    for bit in range(count.bit_length() - 2, 2, -1):
-        stages.append(exchange(values, bit))
-        values = jnp.concatenate([values, stages[-1]], axis=0)
-        order = order + [i ^ (1 << bit) for i in order]
-    half = width // 256 * 128
-    pieces, slots = [], []
-    for start, stop, bits in ((0, half, (2, 1)), (half, width, (1, 2))):
-        part, listed = values[:, :, start:stop], order
-        for bit in bits:
-            if bit == bits[-1] and len(after):
-                part = join(part, exchange(part, bit), after)
-            else:
-                part = jnp.concatenate([part, exchange(part, bit)], axis=0)
-            listed = listed + [i ^ (1 << bit) for i in listed]
-        pieces += [part, exchange(part, 0)]
-        slots += [(start, listed), (start, [i ^ 1 for i in listed])]
-    placed = pl.pallas_call(
-        functools.partial(place_kernel, slots=slots, rows=rows),
-        out_shape=jax.ShapeDtypeStruct((count * rows, width), local.dtype),
-        in_specs=[anywhere] * len(pieces),
-        out_specs=pl.BlockSpec(memory_space=pltpu.HBM),
-        scratch_shapes=[pltpu.SemaphoreType.DMA((2 * count,))],
-        compiler_params=kernel_params(16),
-        cost_estimate=cost(0, 4 * count * rows * width / 2**20),
-    )(*pieces)
-    return placed, stages
+        cost_estimate=cost(0, 1),
+    )(w_in, w_out, *after)
+
+
+class Gather:
+    def __init__(self, local):
+        self.rows, self.width = local.shape
+        bits = lax.axis_size(AXES).bit_length() - 1
+        self.half = self.width // 256 * 128
+        high = [(b,) for b in range(bits - 1, 2, -1)]
+        self.bits = high + [(2, 1), (1, 2), (0, 0)]
+        self.count = len(high)
+        self.values, self.order, self.stage = [local[None]], [[0]], 0
+        self.send()
+
+    def send(self):
+        self.arrived = [exchange(v, b) for v, b in zip(self.values, self.bits[self.stage])]
+
+    def step(self, after=()):
+        self.order = [
+            order + [i ^ (1 << b) for i in order] for order, b in zip(self.order, self.bits[self.stage])
+        ]
+        self.stage += 1
+        split = self.half if self.stage == self.count else 0
+        slots, columns = 2 * self.values[0].shape[0], [v.shape[-1] for v in self.values]
+        if split:
+            self.order = self.order * 2
+            columns = [split, self.width - split]
+        parts = [x for pair in zip(self.values, self.arrived) for x in pair]
+        self.values = pl.pallas_call(
+            functools.partial(join_kernel, count=len(self.values), split=split),
+            out_shape=[jax.ShapeDtypeStruct((slots, self.rows, n), jnp.bfloat16) for n in columns],
+            in_specs=[vmem] * len(parts) + [anywhere] * len(after),
+            out_specs=[vmem] * len(columns),
+            compiler_params=kernel_params(32),
+            cost_estimate=cost(0, 4 * slots * self.rows * self.width / 2**20),
+        )(*parts, *after)
+        self.send()
+        return self.values[:1]
+
+    def place(self, after=()):
+        pieces = [x for pair in zip(self.values, self.arrived) for x in pair]
+        slots = []
+        for start, order in zip((0, self.half), self.order):
+            slots += [(start, order), (start, [i ^ 1 for i in order])]
+        count = lax.axis_size(AXES)
+        return pl.pallas_call(
+            functools.partial(place_kernel, slots=slots, rows=self.rows),
+            out_shape=jax.ShapeDtypeStruct((count * self.rows, self.width), jnp.bfloat16),
+            in_specs=[anywhere] * (len(pieces) + len(after)),
+            out_specs=anywhere,
+            scratch_shapes=[pltpu.SemaphoreType.DMA((2 * count,))],
+            compiler_params=kernel_params(16),
+            cost_estimate=cost(0, 4 * count * self.rows * self.width / 2**20),
+        )(*pieces, *after)
 
 
 def stage_kernel(ids, *refs, groups, extra):
@@ -738,42 +789,41 @@
     outputs = refs[len(inputs) + extra :]
     for g, (bit, count) in enumerate(groups):
         send, keep = outputs[2 * g : 2 * g + 2]
-        mine = ids[bit]
+        mine, rows = ids[bit], send.shape[1]
         start = 0
         for _ in range(count):
             left, right, *inputs = inputs
-            columns = slice(start, start + left.shape[-1])
-            for i in range(left.shape[0]):
-                for out, b in ((send, 1 - mine), (keep, mine)):
-                    total = left[i, b].astype(jnp.float32) + right[i, b].astype(jnp.float32)
-                    out[i, :, columns] = total.astype(jnp.bfloat16)
-            start += left.shape[-1]
+            for j in range(left.shape[2] // rows):
+                columns, block = slice(start, start + left.shape[-1]), slice(j * rows, (j + 1) * rows)
+                for i in range(left.shape[0]):
+                    for out, b in ((send, 1 - mine), (keep, mine)):
+                        total = left[i, b, block].astype(jnp.float32) + right[i, b, block].astype(jnp.float32)
+                        out[i, :, columns] = total.astype(jnp.bfloat16)
+                start += left.shape[-1]
 
 
 class Chain:
-    def __init__(self, ids, parts, rows):
+    def __init__(self, ids, parts, rows, sides=(0, 1)):
         self.ids, self.rows = ids, rows
         self.rest = list(range(3, ids.shape[0]))
-        keep_a, send_a, keep_b, send_b = parts
-        self.sends = [send_a, send_b]
+        self.sends = parts[1::2]
+        self.next = [(1, 2)[side] for side in sides]
         self.groups = [
-            [(keep_a, exchange(send_a, 2))],
-            [(keep_b, exchange(send_b, 1))],
+            [(keep, exchange(send, (2, 1)[side]), rows)]
+            for keep, send, side in zip(parts[::2], parts[1::2], sides)
         ]
 
+    def arrived(self):
+        return [part[1] for group in self.groups for part in group]
+
     def advance(self, groups, bits, after):
-        rows = self.rows
-        shaped = [
-            a.reshape(-1, 2, rows, a.shape[-1]) for group in groups for part in group for a in part
-        ]
-        shapes = [
-            jax.ShapeDtypeStruct(
-                (g[0][0].size // (2 * rows * g[0][0].shape[-1]), rows, sum(p[0].shape[-1] for p in g)),
-                jnp.bfloat16,
-            )
-            for g in groups
-            for _ in range(2)
-        ]
+        shaped, shapes = [], []
+        for group in groups:
+            columns = 0
+            for keep, arrived, rows in group:
+                shaped += [x.reshape(-1, 2, rows, x.shape[-1]) for x in (keep, arrived)]
+                columns += keep.shape[-1] * rows // self.rows
+            shapes += [jax.ShapeDtypeStruct((shaped[-1].shape[0], self.rows, columns), jnp.bfloat16)] * 2
         outs = pl.pallas_call(
             functools.partial(
                 stage_kernel, groups=[(b, len(g)) for b, g in zip(bits, groups)], extra=len(after)
@@ -781,25 +831,27 @@
             out_shape=shapes,
             in_specs=[smem] + [vmem] * len(shaped) + [anywhere] * len(after),
             out_specs=[vmem] * len(shapes),
-            compiler_params=kernel_params(24),
+            compiler_params=kernel_params(32),
             cost_estimate=cost(0, sum(3 * x.size for x in shaped) / 2**20),
         )(self.ids, *shaped, *after)
-        self.sends = outs[::2]
         self.groups = [
-            [(keep, exchange(send, b))] for send, keep, b in zip(outs[::2], outs[1::2], bits)
+            [(keep, exchange(send, b), self.rows)] for send, keep, b in zip(outs[::2], outs[1::2], bits)
         ]
         return outs[1::2]
 
+    def join(self, other):
+        self.rows = other.rows
+        self.groups = [[part for chain in (self, other) for group in chain.groups for part in group]]
+
     def second(self, after=()):
-        return self.advance(self.groups, [1, 2], after)
+        return self.advance(self.groups, self.next, after)
 
     def third(self, after=()):
-        if len(self.groups) == 2:
-            self.groups = [self.groups[0] + self.groups[1]]
+        self.groups = [[part for group in self.groups for part in group]]
         return self.advance(self.groups, [self.rest.pop(0)], after)
 
     def finish(self):
-        [[(keep, arrived)]] = self.groups
+        [[(keep, arrived, _)]] = self.groups
         return (keep.astype(jnp.float32) + arrived.astype(jnp.float32))[0]
 
 
@@ -886,28 +938,24 @@
         keep, send = turn(core, arrays, owned, after)
         return keep, exchange(send, 0)
 
-    memory_turned = turned(memory)
-    target_turned = turned(target_in)
     pack = jnp.concatenate([norm_scale.T, small_bias.T, ffn_bias.reshape(owned, -1)], axis=1)
     small_cols = pack.shape[1]
     pack = jnp.pad(pack, ((0, 0), (0, -small_cols % 128)))
-    early, stages = gather_rows(jnp.concatenate([self_qkv, self_out, pack], axis=1))
-    late = pack_rows(
-        [cross_query, cross_kv, cross_out],
-        [(0, width, 0, 0), (0, 2 * width, 0, width), (0, width, 0, 3 * width)],
-        (owned, 4 * width),
-        stages[:1],
-    )
-    blocks = ffn_in.shape[1] // width
-    packed = pack_rows(
-        [ffn_in] * blocks + [ffn_out],
-        [(i * width, width, i * owned, 0) for i in range(blocks)] + [(0, width, blocks * owned, 0)],
-        (blocks * owned + ffn_out.shape[0], width),
-        stages[:1],
-    )
-    packed = lax.all_gather(packed, AXES)
-    w_qkv, w_self = early[:, : 3 * width], early[:, 3 * width : 4 * width]
-    small = early[:, 4 * width : 4 * width + small_cols].astype(jnp.float32)
+    early = Gather(jnp.concatenate([self_qkv, self_out, cross_query, pack], axis=1))
+    late = Gather(jnp.concatenate([cross_kv, cross_out], axis=1))
+    memory_turned = turned(memory)
+    target_turned = turned(target_in, after=memory_turned[:1])
+    last = target_turned[:1]
+    for _ in range(early.count + 2):
+        last = early.step(last)
+        if early.stage == early.count:
+            packed = lax.all_gather(pack_ffn(ffn_in, ffn_out, last), AXES)
+        if early.stage < early.count + 2:
+            last = late.step(last)
+    early = early.place(last)
+
+    w_qkv, w_self, w_query = early[:, : 3 * width], early[:, 3 * width : 4 * width], early[:, 4 * width : 5 * width]
+    small = early[:, 5 * width : 5 * width + small_cols].astype(jnp.float32)
     gains = small[:, :3].T
     biases = small[:, 3:13].T
     in_bias = small[:, 13:].reshape(1, -1)
@@ -926,9 +974,10 @@
     )
     first_low = first.astype(jnp.bfloat16)
     self_turned = turned(self_context, first_low)
-    late, _ = gather_rows(late, after=self_turned[:1])
-    w_query, w_pairs, w_cross = late[:, :width], late[:, width : 3 * width], late[:, 3 * width :]
     cross_q = (matmul(first_low, w_query) + biases[3]).astype(jnp.bfloat16)
+    late.step((cross_q, self_turned[0]))
+    late = late.place()
+    w_pairs, w_cross = late[:, : 2 * width], late[:, 2 * width :]
     cross_pairs = (matmul(memory, w_pairs) + jnp.concatenate([zeros, biases[4]])).astype(
         jnp.bfloat16
     )
@@ -957,26 +1006,28 @@
     parts = products(
         ids,
         [(hidden, tokens, 0), (hidden_other, tokens, 0)],
-        (out_grad, out_grad_other),
-        [(0, tokens, tokens, 0, width)],
+        [(out_grad, out_grad_other, tokens)],
+        [(0, tokens, tokens, 0, 0, width)],
         ffn_out.shape[0],
-        256,
+        512,
+        sides=(0,),
         after=(pre_grad,),
     )
-    out_chain = Chain(ids, parts, ffn_out.shape[0])
+    out_chain = Chain(ids, parts, ffn_out.shape[0], sides=(0,))
     parts = products(
         ids,
         [(x, tokens, 1) for x in cross_turned],
-        (pre_grad, pre_grad_other),
-        [(0, tokens, tokens, 0, ffn_in.shape[1])],
+        [(pre_grad, pre_grad_other, tokens)],
+        [(0, tokens, tokens, 0, 0, ffn_in.shape[1])],
         owned,
-        512,
+        1024,
+        sides=(1,),
         after=out_chain.sends,
     )
-    in_chain = Chain(ids, parts, owned)
+    in_chain = Chain(ids, parts, owned, sides=(1,))
 
     cross_delta, cross_sums = cross_backward(
-        bound, cross_q, cross_pairs, cross_summary, cross_branch, late, 3, after=in_chain.sends
+        bound, cross_q, cross_pairs, cross_summary, cross_branch, late, 2, after=in_chain.sends
     )
     cross_other = exchange(cross_delta, 0)
     self_delta, self_sums, first_grad = self_backward(
@@ -985,51 +1036,12 @@
         self_summary,
         second_grad,
         cross_delta,
-        late,
         early,
         first_unit,
         first_inverse,
         gains[0:1],
-        after=out_chain.second(after=(cross_sums,)),
     )
     self_other = exchange(self_delta, 0)
-    beyond = mems + 2 * tokens
-    parts = products(
-        ids,
-        [
-            part
-            for i in range(2)
-            for part in (
-                (memory_turned[i], mems, 0),
-                (self_turned[i], tokens, 1),
-                (cross_turned[i], tokens, 0),
-            )
-        ],
-        (cross_delta, cross_other),
-        [
-            (mems, beyond + mems, tokens, 0, width),
-            (0, beyond, mems, 2 * tokens, width),
-            (0, beyond, mems, 2 * tokens + mems, width),
-            (mems + tokens, beyond + mems + tokens, tokens, tokens, width),
-        ],
-        owned,
-        512,
-        after=in_chain.second(after=(self_sums,)),
-    )
-    cross_chain = Chain(ids, parts, owned)
-    parts = products(
-        ids,
-        [part for i in range(2) for part in ((target_turned[i], tokens, 0), (self_turned[i], tokens, 0))],
-        (self_delta, self_other),
-        [(0, 2 * tokens, tokens, i * tokens, width) for i in range(3)]
-        + [(tokens, 3 * tokens, tokens, 3 * tokens, width)],
-        owned,
-        512,
-        after=out_chain.third(after=parts[:1]),
-    )
-    self_chain = Chain(ids, parts, owned)
-    last = in_chain.third(after=parts[:1])
-
     small_grad = small_block(
         [
             (self_sums, 3),
@@ -1049,41 +1061,81 @@
         [self_sums, cross_sums, second_sums, third_sums],
         ffn_bias_grad,
         owned,
-        last,
+        (self_sums,),
     )
     bits = list(range(lax.axis_size(AXES).bit_length() - 1))[::-1]
     small_part = small_grad.reshape((2,) * len(bits) + (owned, -1))
     for bit in (0, 1):
         mine = (me >> bit) & 1
-        keep, send = [
+        small_keep, small_send = [
             lax.dynamic_index_in_dim(small_part, i, bits.index(bit), keepdims=False)
             for i in (mine, 1 - mine)
         ]
-        arrived = exchange(send, bit)
-        small_part = (keep.astype(jnp.float32) + arrived.astype(jnp.float32)).astype(jnp.bfloat16)
+        small_other = exchange(small_send, bit)
+        small_part = (small_keep.astype(jnp.float32) + small_other.astype(jnp.float32)).astype(jnp.bfloat16)
         bits.remove(bit)
-    self_chain.groups[1].append((keep, arrived))
-
-    memory_grad = add_product(
-        cross_delta, [2 * tokens, 2 * tokens + mems], late, [1, 2], mems, 256, after=(small_grad,)
-    )
-    last = cross_chain.second(after=(memory_grad,))
-    last = out_chain.third(after=last)
+    beyond = mems + 2 * tokens
+    parts = products(
+        ids,
+        [
+            part
+            for i in range(2)
+            for part in (
+                (memory_turned[i], mems, 0),
+                (self_turned[i], tokens, 1),
+                (cross_turned[i], tokens, 0),
+            )
+        ],
+        [(cross_delta, cross_other, mems), (cross_delta, cross_other, mems // 2)],
+        [
+            (mems, beyond + mems, tokens, 1, 4, width),
+            (0, beyond, mems, 0, 0, width),
+            (0, beyond, mems, 0, 1, width),
+            (mems + tokens, beyond + mems + tokens, tokens, 1, 5, width),
+        ],
+        owned,
+        1024,
+        after=in_chain.second(after=out_chain.second(after=(small_grad,))),
+    )
+    cross_chain = Chain(ids, parts, owned)
+    out_chain.join(in_chain)
+    parts = products(
+        ids,
+        [part for i in range(2) for part in ((target_turned[i], tokens, 0), (self_turned[i], tokens, 0))],
+        [(self_delta, self_other, tokens)],
+        [(0, 2 * tokens, tokens, 0, i, width) for i in range(3)]
+        + [(tokens, 3 * tokens, tokens, 0, 3, width)],
+        owned,
+        1024,
+        after=(*out_chain.third(after=parts[:1]), small_other),
+    )
+    self_chain = Chain(ids, parts, owned)
+    self_chain.groups[1].append((small_keep, small_other, owned))
+    last = cross_chain.second(after=parts[:1])
+    memory_grad = add_product(cross_delta, [0, mems], late, [0, 1], mems, 512, after=last)
+    last = (memory_grad,)
+    while out_chain.rest:
+        last = out_chain.third(after=last)
     target_grad = add_product(
-        self_delta, [0, tokens, 2 * tokens], early, [0, 1, 2], tokens, tokens, first_grad, after=last
-    )
-    last = in_chain.third(after=(target_grad,))
-    last = self_chain.second(after=last)
-    last = cross_chain.third(after=last)
+        self_delta,
+        [0, tokens, 2 * tokens],
+        early,
+        [0, 1, 2],
+        tokens,
+        tokens,
+        first_grad,
+        after=last,
+    )
+    last = self_chain.second(after=(target_grad,))
     last = cross_chain.third(after=last)
     last = self_chain.third(after=last)
     while self_chain.rest:
+        last = cross_chain.third(after=last)
         last = self_chain.third(after=last)
-    for chain in (out_chain, in_chain, cross_chain):
-        while chain.rest:
-            last = chain.third(after=last)
-    ffn_out_shard = out_chain.finish()
-    ffn_in_shard = in_chain.finish()
+    ffn_shard = out_chain.finish()
+    size = ffn_in.shape[1]
+    ffn_out_shard = ffn_shard[:, :size].reshape(owned, -1, width).swapaxes(0, 1).reshape(ffn_out.shape)
+    ffn_in_shard = ffn_shard[:, size:]
     cross_shard = cross_chain.finish()
     self_shard = self_chain.finish()
     small_shard = self_shard[:, 4 * width :]

time: 484 us -> 461 us (0.952)
  Pallas kernels: 166 us -> 157 us
  other arithmetic: 11.6 us -> 4.16 us
  starting transfers between devices: 53.9 us -> 46.6 us
    pallas_call x4, Pallas kernels: 45.2 us -> 37.8 us  [products(): pl.pallas_call(functools.partial(product_kernel, spans=spans, n_left=len(...]
    ppermute x51 -> x45, starting transfers between devices: 53.9 us -> 46.6 us  [exchange(): return lax.ppermute(values, AXES, [(i, i ^ 1 << bit) for i in range(count)])]
    concatenate x10 -> x0, other arithmetic: 5.86 us -> none  [the longest x6 5.6 us: gather_rows(): part = jnp.concatenate([part, exchange(part, bit)], axis=0)]
    ppermute x51 -> x45, waiting for transfers between devices: 172 us -> 171 us  [exchange(): return lax.ppermute(values, AXES, [(i, i ^ 1 << bit) for i in range(count)])]
    unnamed x133 -> x141, local copies, waits for them, and re-layouts: 34.5 us -> 33.3 us
    pallas_call x6 -> x11, Pallas kernels: 13.8 us -> 12.8 us  [the longest x2 8.58 us: place(): pl.pallas_call(functools.partial(place_kernel, slots=slots, rows=self.row...]
    pallas_call x12 -> x10, Pallas kernels: 14.4 us -> 13.9 us  [advance(): pl.pallas_call(functools.partial(stage_kernel, groups=[(b, len(g)) for b,...]
  transfers between devices with their start and end apart: 52 -> 46, of which waited for: 16 -> 24; matrix products, arithmetic and copies ran while one was open for 6% -> 6% of each run, Pallas kernels for 35% -> 34%
where the time goes in v4:
time: 461 us; the launch traced here: 457 us
  waiting for transfers between devices  175 us (38%)
  Pallas kernels  157 us (34%)
  starting transfers between devices  46.6 us (10%)
  local copies, waits for them, and re-layouts  42.1 us (9%)
  matrix products  16.9 us (4%)
  between operations  15.2 us (3%)
    ppermute x45, waiting for transfers between devices, exchange(): return lax.ppermute(values, AXES, [(i, i ^ 1 << bit) for i in range(count)])  171 us
    ppermute x45, starting transfers between devices, exchange(): return lax.ppermute(values, AXES, [(i, i ^ 1 << bit) for i in range(count)])  46.6 us
    pallas_call x4, Pallas kernels, products(): pl.pallas_call(functools.partial(product_kernel, spans=spans, n_left=len(...  37.8 us
    unnamed x141, local copies, waits for them, and re-layouts  33.3 us
    pallas_call x1, Pallas kernels, cross_backward(): pl.pallas_call(functools.partial(cross_backward_kernel, extra=len(after))...  20.1 us
    dot_general x5, matrix products, matmul(): return jnp.dot(first, second, preferred_element_type=jnp.float32)  16.9 us
    pallas_call x1, Pallas kernels, ffn_forward(): pl.pallas_call(functools.partial(ffn_forward_kernel, rows=rows, extra=len...  15.9 us
    pallas_call x1, Pallas kernels, ffn_backward(): pl.pallas_call(functools.partial(ffn_backward_kernel, extra=len(after)),...  14.7 us
  transfers between devices with their start and end apart: 46, of which 24 were waited for; matrix products, arithmetic and copies ran while one was open for 6% of the time, Pallas kernels for 34%

profile of v4, /device:TPU:0, one launch (start us, length us, event | category | flops | bytes accessed | tf_op | source)
XLA Modules:
  0.0 456.6 jit_solution(10493533796610027028)
XLA Ops:
  10.7 4.1 collective-permute-start
  19.1 10.7 %collective-permute-done.refs_1_ = bf16[1,32,5248]{2,1,0:T(8,128)(2,1)S(1)} collective-permute-done((bf16[1,32,5248]{2,1,0:T(8,128)(2,1)S(1)}, bf16[1,32,5248]{2,1,0:T(8,128)(2,1)S(1)}, u32[]{:S(2)}, u32[]{:S(2)}) %collective-permute-start) | collective-permute-done | bytes 335904 | tf_op jit(solution)/shard_map/ppermute | solution.py:680
  30.7 3.4 collective-permute-start.2
  34.2 15.2 %collective-permute-done.2.refs_1_ = bf16[1,32,3072]{2,1,0:T(8,128)(2,1)S(1)} collective-permute-done((bf16[1,32,3072]{2,1,0:T(8,128)(2,1)S(1)}, bf16[1,32,3072]{2,1,0:T(8,128)(2,1)S(1)}, u32[]{:S(2)}, u32[]{:S(2)}) %collective-permute-start.2) | collective-permute-done | bytes 196640 | tf_op jit(solution)/shard_map/ppermute | solution.py:680
  54.3 3.4 collective-permute-start.5
  57.7 11.6 %collective-permute-done.5.refs_1_ = bf16[2,32,3072]{2,1,0:T(8,128)(2,1)S(1)} collective-permute-done((bf16[2,32,3072]{2,1,0:T(8,128)(2,1)S(1)}, bf16[2,32,3072]{2,1,0:T(8,128)(2,1)S(1)}, u32[]{:S(2)}, u32[]{:S(2)}) %collective-permute-start.5) | collective-permute-done | bytes 393248 | tf_op jit(solution)/shard_map/ppermute | solution.py:680
  69.3 3.6 collective-permute-done.3.refs_1_
  77.1 47.0 %collective-permute-done.8.refs_1_ = bf16[4,32,1536]{2,1,0:T(8,128)(2,1)S(1)} collective-permute-done((bf16[4,32,1536]{2,1,0:T(8,128)(2,1)S(1)}, bf16[4,32,1536]{2,1,0:T(8,128)(2,1)S(1)}, u32[]{:S(2)}, u32[]{:S(2)}) %collective-permute-start.8) | collective-permute-done | bytes 393248 | tf_op jit(solution)/shard_map/ppermute | solution.py:680
  127.2 6.3 %collective-permute-done.10.refs_1_ = bf16[16,32,2560]{2,1,0:T(8,128)(2,1)S(1)} collective-permute-done((bf16[16,32,2560]{2,1,0:T(8,128)(2,1)S(1)}, bf16[16,32,2560]{2,1,0:T(8,128)(2,1)S(1)}, u32[]{:S(2)}, u32[]{:S(2)}) %collective-permute-start.10) | collective-permute-done | bytes 2621472 | tf_op jit(solution)/shard_map/ppermute | solution.py:680
  133.6 5.1 %shard_map.264.w_query.w_self.refs_3_.refs_4_.refs_5_ = bf16[1024,5248]{1,0:T(8,128)(2,1)S(1)} custom-call(bf16[16,32,2560]{2,1,0:T(8,128)(2,1)S(1)} %get-tuple-element.99.refs_0_.refs_4_, bf16[16,32,2560]{2,1,0:T(8,128)(2,1)S(1)} %collective-permute-done.10.refs_1_, bf16[16,32,2688]{2,1,0:T(8,128)(2,1)S(1)} %get-tuple-element.100.refs_2_, ...), custom_call_target="tpu_custom_call" | custom-call | bytes 214958080 | tf_op jit(solution)/shard_map/pallas_call | solution.py:776
  138.7 3.9 copy-done
  142.9 5.6 %fusion.7.qkv = bf16[384,3072]{1,0:T(8,128)(2,1)S(1)} fusion(bf16[384,1024]{1,0:T(8,128)(2,1)S(1)} %copy-done.24, bf16[1024,5248]{1,0:T(8,128)(2,1)} %copy-done, f32[3072]{0:T(1024)S(1)} %pad_maximum_fusion), kind=kOutput, calls=%fused_computation.7 | convolution fusion | flops 2418278400 | bytes 9449472 | tf_op jit(solution)/shard_map/dot_general | solution.py:33
  148.6 3.5 shard_map.265
  152.1 2.7 fusion.35
  158.1 2.6 add_convert_fusion.2.refs_4_.q
  162.9 2.5 shard_map.267
  167.5 2.3 collective-permute-done.14.refs_1_
  169.8 2.9 collective-permute-done.15.refs_3_
  172.8 3.5 shard_map.268.weight.refs_2_.refs_3_
  176.3 4.8 %fusion.4.pairs = bf16[1024,2048]{1,0:T(8,128)(2,1)S(1)} fusion(f32[2048]{0:T(1024)S(1)} %concatenate.22, bf16[1024,1024]{1,0:T(8,128)(2,1)S(1)} %copy-done.5, bf16[1024,3072]{1,0:T(8,128)(2,1)S(1)} %shard_map.268.weight.refs_2_.refs_3_), kind=kOutput, calls=%fused_computation.4 | convolution fusion | flops 4299161600 | bytes 10493952 | tf_op jit(solution)/shard_map/dot_general | solution.py:33
  181.1 6.9 %shard_map.269 = (bf16[384,1024]{1,0:T(8,128)(2,1)S(1)}, f32[3,8,1,256]{3,2,1,0:T(1,128)S(1)}) custom-call(s32[2,3]{1,0:T(2,128)S(1)} %pad_add_fusion.bound, bf16[384,1024]{1,0:T(8,128)(2,1)S(1)} %add_convert_fusion.2.refs_4_.q, bf16[1024,2048]{1,0:T(8,128)(2,1)S(1)} %fusion.4.pairs), custom_call_target="tpu_custom_call" | custom-call | flops 80000000000 | bytes 83886080 | tf_op jit(solution)/shard_map/pallas_call | solution.py:188
  194.0 3.8 all-gather.3.cloned.1.call-done
  200.1 15.9 %shard_map.271 = (bf16[2048,384]{1,0:T(8,128)(2,1)S(1)}, bf16[2048,384]{1,0:T(8,128)(2,1)}, bf16[384,4096]{1,0:T(8,128)(2,1)S(1)}, bf16[384,1024]{1,0:T(8,128)(2...) custom-call(s32[1]{0:T(128)} %bitcast.core, ...), custom_call_target="tpu_custom_call" | custom-call | flops 160000000000 | bytes 272629760 | tf_op jit(solution)/shard_map/pallas_call | solution.py:479
  217.5 14.7 %shard_map.273 = (bf16[384,4096]{1,0:T(8,128)(2,1)}, f32[1,4096]{1,0:T(1,128)S(1)}, f32[384,1024]{1,0:T(8,128)S(1)}, bf16[384,1024]{1,0:T(8,128)(2,1)S(1)}, f32[8,1024]{1,0:T(8,128)S(1)}) custom-call(bf16[32,256,1024]{2,1,0:T(8,128)(2,1)} %bitcast.146, bf16[32,256,1024]{2,1,0:T(8,128)(2,1)} %bitcast.147, bf16[384,4096]{1,0:T(8,128)(2,1)S(1)} %get-tuple-element.112.slope, ...), custom_call_target="tpu_custom_call" | custom-call | flops 140000002048 | bytes 272629760 | tf_op jit(solution)/shard_map/pallas_call | solution.py:543
  234.8 5.5 %collective-permute-done.22.refs_3_ = bf16[384,1024]{1,0:T(8,128)(2,1)S(1)} collective-permute-done((bf16[384,1024]{1,0:T(8,128)(2,1)}, bf16[384,1024]{1,0:T(8,128)(2,1)S(1)}, u32[]{:S(2)}, u32[]{:S(2)}) %collective-permute-start.22) | collective-permute-done | bytes 786464 | tf_op jit(solution)/shard_map/ppermute | solution.py:680
  241.7 8.1 %shard_map.274 = (bf16[1024,1024]{1,0:T(8,128)(2,1)}, bf16[1024,1024]{1,0:T(8,128)(2,1)}) custom-call(s32[5]{0:T(128)S(1)} %shift-right-arithmetic_and_fusion.ids, bf16[2048,384]{1,0:T(8,128)(2,1)S(1)} %copy-done.53, bf16[2048,384]{1,0:T(8,128)(2,1)} %collective-permute-done.21.refs_1_, bf16[384,1024]{1,0:T(8,128)(2,1)} %get-tuple-element.114.out_grad.refs_2_, ...), custom_call_target="tpu_custom_call" | custom-call | flops 20132659200 | bytes 209715200 | tf_op jit(solution)/shard_map/pallas_call | solution.py:657
  251.4 8.0 %shard_map.275 = (bf16[256,4096]{1,0:T(8,128)(2,1)S(1)}, bf16[256,4096]{1,0:T(8,128)(2,1)}) custom-call(s32[5]{0:T(128)S(1)} %shift-right-arithmetic_and_fusion.ids, bf16[512,768]{1,0:T(8,128)(2,1)S(1)} %copy-done.45, bf16[512,768]{1,0:T(8,128)(2,1)} %collective-permute-done.19.rest_0_.refs_1_.refs_5_, bf16[384,4096]{1,0:T(8,128)(2,1)} %get-tuple-element.120.refs_4_.refs_2_, ...), custom_call_target="tpu_custom_call" | custom-call | flops 20132659200 | bytes 209715200 | tf_op jit(solution)/shard_map/pallas_call | solution.py:657
  262.0 20.1 %shard_map.276 = (bf16[3072,1024]{1,0:T(8,128)(2,1)}, f32[8,1024]{1,0:T(8,128)}) custom-call(s32[2,3]{1,0:T(2,128)} %copy-done.36, bf16[384,1024]{1,0:T(8,128)(2,1)} %copy-done.19, bf16[1024,2048]{1,0:T(8,128)(2,1)} %copy-done.51, f32[3,8,1,256]{3,2,1,0:T(1,128)} %copy-done.59, bf16[384,1024]{1,0:T(8,128)(2,1)} %copy-done.58, bf16[1024,3072]{1,0:T(8,128)(2,1)} %copy-done.1, ...), custom_call_target="tpu_custom_call" | custom-call | flops 160000000000 | bytes 125829120 | tf_op jit(solution)/shard_map/pallas_call | solution.py:214
  283.3 13.4 %shard_map.277 = (bf16[1536,1024]{1,0:T(8,128)(2,1)}, f32[8,1024]{1,0:T(8,128)S(1)}, f32[384,1024]{1,0:T(8,128)S(1)}) custom-call(s32[3]{0:T(128)S(1)} %bitcast.127, bf16[384,3072]{1,0:T(8,128)(2,1)} %copy-done.50, f32[3,8,1,256]{3,2,1,0:T(1,128)S(1)} %get-tuple-element.111.summary, f32[384,1024]{1,0:T(8,128)S(1)} %copy-done.57, ...), custom_call_target="tpu_custom_call" | custom-call | flops 60000002048 | bytes 125829120 | tf_op jit(solution)/shard_map/pallas_call | solution.py:330
  300.8 2.2 shard_map.279
  304.0 5.4 %collective-permute-done.25 = bf16[256,4096]{1,0:T(8,128)(2,1)} collective-permute-done((bf16[256,4096]{1,0:T(8,128)(2,1)}, bf16[256,4096]{1,0:T(8,128)(2,1)}, u32[]{:S(2)}, u32[]{:S(2)}) %collective-permute-start.25) | collective-permute-done | bytes 2097184 | tf_op jit(solution)/shard_map/ppermute | solution.py:680
  309.5 2.2 shard_map.280
  313.2 13.1 %shard_map.281 = (bf16[256,2048]{1,0:T(8,128)(2,1)S(1)}, bf16[256,2048]{1,0:T(8,128)(2,1)}, bf16[256,2048]{1,0:T(8,128)(2,1)}, bf16[256,2048]{1,0:T(8,128)(2,1)}) custom-call(s32[5]{0:T(128)S(1)} %copy-done.30, bf16[512,1024]{1,0:T(8,128)(2,1)} %copy-done.13, bf16[512,768]{1,0:T(8,128)(2,1)S(1)} %copy-done.18, bf16[512,768]{1,0:T(8,128)(2,1)S(1)} %copy-done.46, ...), custom_call_target="tpu_custom_call" | custom-call | flops 31317469184 | bytes 209715200 | tf_op jit(solution)/shard_map/pallas_call | solution.py:657
  326.3 7.4 %collective-permute-done.24 = bf16[4,128,1024]{2,1,0:T(8,128)(2,1)S(1)} collective-permute-done((bf16[4,128,1024]{2,1,0:T(8,128)(2,1)S(1)}, bf16[4,128,1024]{2,1,0:T(8,128)(2,1)S(1)}, u32[]{:S(2)}, u32[]{:S(2)}) %collective-permute-start.24) | collective-permute-done | bytes 1048608 | tf_op jit(solution)/shard_map/ppermute | solution.py:680
  333.7 2.3 collective-permute-done.26
  339.0 6.3 %collective-permute-start.28 = (bf16[2,32,8192]{2,1,0:T(8,128)(2,1)}, bf16[2,32,8192]{2,1,0:T(8,128)(2,1)S(1)}, u32[]{:S(2)}, u32[]{:S(2)}) collective-permute-start(bf16[2,32,8192]{2,1,0:T(8,128)(2,1)} %get-tuple-element.141), channel_id=1, source_target_pairs={{0,8},{1,9},{2,10},{3,11},{4,12},{5,13},{6,14},{7,15},{8,0},{9,1},... | collective-permute-start | bytes 3145736 | tf_op jit(solution)/shard_map/ppermute | solution.py:680
  348.3 8.5 %shard_map.283 = (bf16[256,2048]{1,0:T(8,128)(2,1)S(1)}, bf16[256,2048]{1,0:T(8,128)(2,1)}, bf16[256,2048]{1,0:T(8,128)(2,1)S(1)}, bf16[256,2048]{1,0:T(8,128)(2,1)}) custom-call(s32[5]{0:T(128)S(1)} %copy-done.30, bf16[512,384]{1,0:T(8,128)(2,1)S(1)} %copy-done.26, bf16[512,768]{1,0:T(8,128)(2,1)S(1)} %copy-done.18, ...), custom_call_target="tpu_custom_call" | custom-call | flops 20132659200 | bytes 209715200 | tf_op jit(solution)/shard_map/pallas_call | solution.py:657
  359.1 12.7 %collective-permute-done.29 = bf16[256,2048]{1,0:T(8,128)(2,1)} collective-permute-done((bf16[256,2048]{1,0:T(8,128)(2,1)}, bf16[256,2048]{1,0:T(8,128)(2,1)}, u32[]{:S(2)}, u32[]{:S(2)}) %collective-permute-start.29) | collective-permute-done | bytes 1048608 | tf_op jit(solution)/shard_map/ppermute | solution.py:680
  377.1 2.8 copy-done.37
  379.9 6.6 %shard_map.285.refs_2_ = f32[1024,1024]{1,0:T(8,128)} custom-call(bf16[3072,1024]{1,0:T(8,128)(2,1)S(1)} %copy-done.37, bf16[3072,1024]{1,0:T(8,128)(2,1)S(1)} %copy-done.37, bf16[1024,3072]{1,0:T(8,128)(2,1)S(1)} %bitcast.94, bf16[1024,3072]{1,0:T(8,128)(2,1)S(1)} %bitcast.94, bf16[4,32,2048]{2,1,0:T(8,128)(2,1)S(1)} %get-tuple-element.146.refs_4_, ...), custom_call_target="tpu_custom_call" | custom-call | flops 64424509440 | bytes 125829120 | tf_op jit(solution)/shard_map/pallas_call | solution.py:898
  386.5 2.2 copy-done.2
  391.0 6.6 %shard_map.287.refs_6_ = f32[384,1024]{1,0:T(8,128)} custom-call(bf16[1536,1024]{1,0:T(8,128)(2,1)S(1)} %copy-done.38, bf16[1536,1024]{1,0:T(8,128)(2,1)S(1)} %copy-done.38, bf16[1536,1024]{1,0:T(8,128)(2,1)S(1)} %copy-done.38, bf16[1024,5248]{1,0:T(8,128)(2,1)} %copy-done, bf16[1024,5248]{1,0:T(8,128)(2,1)} %copy-done, bf16[1024,5248]{1,0:T(8,128)(2,1)} %copy-done, ...), custom_call_target="tpu_custom_call" | custom-call | flops 36238786560 | bytes 125829120 | tf_op jit(solution)/shard_map/pallas_call | solution.py:898
  401.5 4.4 collective-permute-done.38
  407.6 5.3 %collective-permute-done.36 = bf16[4,32,2048]{2,1,0:T(8,128)(2,1)S(1)} collective-permute-done((bf16[4,32,2048]{2,1,0:T(8,128)(2,1)S(1)}, bf16[4,32,2048]{2,1,0:T(8,128)(2,1)S(1)}, u32[]{:S(2)}, u32[]{:S(2)}) %collective-permute-start.36) | collective-permute-done | bytes 524320 | tf_op jit(solution)/shard_map/ppermute | solution.py:680
  415.3 8.4 %collective-permute-done.41 = bf16[2,32,4096]{2,1,0:T(8,128)(2,1)S(1)} collective-permute-done((bf16[2,32,4096]{2,1,0:T(8,128)(2,1)S(1)}, bf16[2,32,4096]{2,1,0:T(8,128)(2,1)S(1)}, u32[]{:S(2)}, u32[]{:S(2)}) %collective-permute-start.41) | collective-permute-done | bytes 524320 | tf_op jit(solution)/shard_map/ppermute | solution.py:680
  427.9 4.9 %collective-permute-done.40 = bf16[2,32,4352]{2,1,0:T(8,128)(2,1)S(1)} collective-permute-done((bf16[2,32,4352]{2,1,0:T(8,128)(2,1)S(1)}, bf16[2,32,4352]{2,1,0:T(8,128)(2,1)S(1)}, u32[]{:S(2)}, u32[]{:S(2)}) %collective-permute-start.40) | collective-permute-done | bytes 557088 | tf_op jit(solution)/shard_map/ppermute | solution.py:680
  433.6 8.6 %collective-permute-done.43 = bf16[1,32,4096]{2,1,0:T(8,128)(2,1)S(1)} collective-permute-done((bf16[1,32,4096]{2,1,0:T(8,128)(2,1)S(1)}, bf16[1,32,4096]{2,1,0:T(8,128)(2,1)S(1)}, u32[]{:S(2)}, u32[]{:S(2)}) %collective-permute-start.43) | collective-permute-done | bytes 262176 | tf_op jit(solution)/shard_map/ppermute | solution.py:680
  443.7 2.4 collective-permute-done.42
  (281 shorter events, 87.7 us)
Async XLA Ops:
  7.2 190.6 %all-gather.3.cloned.1.call-start = ((), (), s32[]{:S(2)}) async-start(), calls=%async_computation | async-start | bytes 17301504 | tf_op jit(solution)/shard_map/all_gather | solution.py:952
  10.7 19.2 %collective-permute-start = (bf16[1,32,5248]{2,1,0:T(8,128)(2,1)S(1)}, bf16[1,32,5248]{2,1,0:T(8,128)(2,1)S(1)}, u32[]{:S(2)}, u32[]{:S(2)}) collective-permute-start(bf16[1,32,5248]{2,1,0:T(8,128)(2,1)S(1)} %maximum_bitcast_fusion.refs_0_), channel_id=1, source_target_pairs={{0,16},{1,17},{2,18},{3,19},{4,20},{5,21},{6,22},{7,23},{8,24},{9,... | collective-permute-start | bytes 1007624 | tf_op jit(solution)/shard_map/ppermute | solution.py:680
  29.9 20.5 %collective-permute-start.1 = (bf16[2,32,5248]{2,1,0:T(8,128)(2,1)S(1)}, bf16[2,32,5248]{2,1,0:T(8,128)(2,1)S(1)}, u32[]{:S(2)}, u32[]{:S(2)}) collective-permute-start(bf16[2,32,5248]{2,1,0:T(8,128)(2,1)S(1)} %shard_map.257.refs_2_.refs_0_), channel_id=1, source_target_pairs={{0,8},{1,9},{2,10},{3,11},{4,12},{5,13},{6,14},{7,15},{8,0},{9,1},... | collective-permute-start | bytes 2015240 | tf_op jit(solution)/shard_map/ppermute | solution.py:680
  30.7 18.7 %collective-permute-start.2 = (bf16[1,32,3072]{2,1,0:T(8,128)(2,1)S(1)}, bf16[1,32,3072]{2,1,0:T(8,128)(2,1)S(1)}, u32[]{:S(2)}, u32[]{:S(2)}) collective-permute-start(bf16[1,32,3072]{2,1,0:T(8,128)(2,1)S(1)} %maximum_bitcast_fusion.1.refs_0_), channel_id=1, source_target_pairs={{0,16},{1,17},{2,18},{3,19},{4,20},{5,21},{6,22},{7,23},{8,24},{9,... | collective-permute-start | bytes 589832 | tf_op jit(solution)/shard_map/ppermute | solution.py:680
  51.4 21.4 %collective-permute-start.4 = (bf16[4,32,2688]{2,1,0:T(8,128)(2,1)S(1)}, bf16[4,32,2688]{2,1,0:T(8,128)(2,1)S(1)}, u32[]{:S(2)}, u32[]{:S(2)}) collective-permute-start(bf16[4,32,2688]{2,1,0:T(8,128)(2,1)S(1)} %get-tuple-element.93.refs_2_), channel_id=1, source_target_pairs={{0,2},{1,3},{2,0},{3,1},{4,6},{5,7},{6,4},{7,5},{8,10},{9,11},{10,... | collective-permute-start | bytes 2064392 | tf_op jit(solution)/shard_map/ppermute | solution.py:680
  52.8 20.1 %collective-permute-start.3 = (bf16[4,32,2560]{2,1,0:T(8,128)(2,1)S(1)}, bf16[4,32,2560]{2,1,0:T(8,128)(2,1)S(1)}, u32[]{:S(2)}, u32[]{:S(2)}) collective-permute-start(bf16[4,32,2560]{2,1,0:T(8,128)(2,1)S(1)} %get-tuple-element.92.refs_2_.refs_0_), channel_id=1, source_target_pairs={{0,4},{1,5},{2,6},{3,7},{4,0},{5,1},{6,2},{7,3},{8,12},{9,13},{10,... | collective-permute-start | bytes 1966088 | tf_op jit(solution)/shard_map/ppermute | solution.py:680
  54.3 15.0 %collective-permute-start.5 = (bf16[2,32,3072]{2,1,0:T(8,128)(2,1)S(1)}, bf16[2,32,3072]{2,1,0:T(8,128)(2,1)S(1)}, u32[]{:S(2)}, u32[]{:S(2)}) collective-permute-start(bf16[2,32,3072]{2,1,0:T(8,128)(2,1)S(1)} %shard_map.258.refs_2_.refs_0_), channel_id=1, source_target_pairs={{0,8},{1,9},{2,10},{3,11},{4,12},{5,13},{6,14},{7,15},{8,0},{9,1},... | collective-permute-start | bytes 1179656 | tf_op jit(solution)/shard_map/ppermute | solution.py:680
  73.0 51.3 %collective-permute-start.7 = (bf16[8,32,2688]{2,1,0:T(8,128)(2,1)S(1)}, bf16[8,32,2688]{2,1,0:T(8,128)(2,1)S(1)}, u32[]{:S(2)}, u32[]{:S(2)}) collective-permute-start(bf16[8,32,2688]{2,1,0:T(8,128)(2,1)S(1)} %get-tuple-element.96.refs_2_), channel_id=1, source_target_pairs={{0,4},{1,5},{2,6},{3,7},{4,0},{5,1},{6,2},{7,3},{8,12},{9,13},{10,... | collective-permute-start | bytes 4128776 | tf_op jit(solution)/shard_map/ppermute | solution.py:680
  74.9 49.4 %collective-permute-start.6 = (bf16[8,32,2560]{2,1,0:T(8,128)(2,1)S(1)}, bf16[8,32,2560]{2,1,0:T(8,128)(2,1)S(1)}, u32[]{:S(2)}, u32[]{:S(2)}) collective-permute-start(bf16[8,32,2560]{2,1,0:T(8,128)(2,1)S(1)} %get-tuple-element.95.refs_4_.refs_0_), channel_id=1, source_target_pairs={{0,2},{1,3},{2,0},{3,1},{4,6},{5,7},{6,4},{7,5},{8,10},{9,11},{10,... | collective-permute-start | bytes 3932168 | tf_op jit(solution)/shard_map/ppermute | solution.py:680
  75.5 48.7 %collective-permute-start.8 = (bf16[4,32,1536]{2,1,0:T(8,128)(2,1)S(1)}, bf16[4,32,1536]{2,1,0:T(8,128)(2,1)S(1)}, u32[]{:S(2)}, u32[]{:S(2)}) collective-permute-start(bf16[4,32,1536]{2,1,0:T(8,128)(2,1)S(1)} %get-tuple-element.94.refs_4_.refs_0_), channel_id=1, source_target_pairs={{0,4},{1,5},{2,6},{3,7},{4,0},{5,1},{6,2},{7,3},{8,12},{9,13},{10,... | collective-permute-start | bytes 1179656 | tf_op jit(solution)/shard_map/ppermute | solution.py:680
  75.8 48.3 %collective-permute-start.9 = (bf16[4,32,1536]{2,1,0:T(8,128)(2,1)S(1)}, bf16[4,32,1536]{2,1,0:T(8,128)(2,1)S(1)}, u32[]{:S(2)}, u32[]{:S(2)}) collective-permute-start(bf16[4,32,1536]{2,1,0:T(8,128)(2,1)S(1)} %get-tuple-element.97.refs_2_), channel_id=1, source_target_pairs={{0,2},{1,3},{2,0},{3,1},{4,6},{5,7},{6,4},{7,5},{8,10},{9,11},{10,... | collective-permute-start | bytes 1179656 | tf_op jit(solution)/shard_map/ppermute | solution.py:680
  124.7 8.9 %collective-permute-start.11 = (bf16[16,32,2688]{2,1,0:T(8,128)(2,1)S(1)}, bf16[16,32,2688]{2,1,0:T(8,128)(2,1)S(1)}, u32[]{:S(2)}, u32[]{:S(2)}) collective-permute-start(bf16[16,32,2688]{2,1,0:T(8,128)(2,1)S(1)} %get-tuple-element.100.refs_2_), channel_id=1, source_target_pairs={{0,1},{1,0},{2,3},{3,2},{4,5},{5,4},{6,7},{7,6},{8,9},{9,8},{10,11... | collective-permute-start | bytes 8257544 | tf_op jit(solution)/shard_map/ppermute | solution.py:680
  124.8 8.8 %collective-permute-start.10 = (bf16[16,32,2560]{2,1,0:T(8,128)(2,1)S(1)}, bf16[16,32,2560]{2,1,0:T(8,128)(2,1)S(1)}, u32[]{:S(2)}, u32[]{:S(2)}) collective-permute-start(bf16[16,32,2560]{2,1,0:T(8,128)(2,1)S(1)} %get-tuple-element.99.refs_0_.refs_4_), channel_id=1, source_target_pairs={{0,1},{1,0},{2,3},{3,2},{4,5},{5,4},{6,7},{7,6},{8,9},{9,8},{10,11... | collective-permute-start | bytes 7864328 | tf_op jit(solution)/shard_map/ppermute | solution.py:680
  125.2 35.5 %collective-permute-start.12 = (bf16[8,32,1536]{2,1,0:T(8,128)(2,1)S(1)}, bf16[8,32,1536]{2,1,0:T(8,128)(2,1)S(1)}, u32[]{:S(2)}, u32[]{:S(2)}) collective-permute-start(bf16[8,32,1536]{2,1,0:T(8,128)(2,1)S(1)} %get-tuple-element.98.refs_4_.refs_0_), channel_id=1, source_target_pairs={{0,2},{1,3},{2,0},{3,1},{4,6},{5,7},{6,4},{7,5},{8,10},{9,11},{10,... | collective-permute-start | bytes 2359304 | tf_op jit(solution)/shard_map/ppermute | solution.py:680
  125.9 35.8 %collective-permute-start.13 = (bf16[8,32,1536]{2,1,0:T(8,128)(2,1)S(1)}, bf16[8,32,1536]{2,1,0:T(8,128)(2,1)}, u32[]{:S(2)}, u32[]{:S(2)}) collective-permute-start(bf16[8,32,1536]{2,1,0:T(8,128)(2,1)S(1)} %get-tuple-element.102.refs_2_), channel_id=1, source_target_pairs={{0,4},{1,5},{2,6},{3,7},{4,0},{5,1},{6,2},{7,3},{8,12},{9,13},{10,... | collective-permute-start | bytes 2359304 | tf_op jit(solution)/shard_map/ppermute | solution.py:680
  155.1 34.5 %copy-start.34 = (f32[1,1024]{1,0:T(1,128)}, f32[1,1024]{1,0:T(1,128)S(1)}, u32[]{:S(2)}) copy-start(f32[1,1024]{1,0:T(1,128)S(1)} %get-tuple-element.229.gain) | copy-start | bytes 12292
  165.4 4.5 collective-permute-start.14
  165.5 7.2 %collective-permute-start.15 = (bf16[16,32,1536]{2,1,0:T(8,128)(2,1)}, bf16[16,32,1536]{2,1,0:T(8,128)(2,1)}, u32[]{:S(2)}, u32[]{:S(2)}) collective-permute-start(bf16[16,32,1536]{2,1,0:T(8,128)(2,1)} %get-tuple-element.105.refs_2_), channel_id=1, source_target_pairs={{0,1},{1,0},{2,3},{3,2},{4,5},{5,4},{6,7},{7,6},{8,9},{9,8},{10,11... | collective-permute-start | bytes 4718600 | tf_op jit(solution)/shard_map/ppermute | solution.py:680
  165.9 27.2 %collective-permute-start.16 = (bf16[512,1024]{1,0:T(8,128)(2,1)}, bf16[512,1024]{1,0:T(8,128)(2,1)}, u32[]{:S(2)}, u32[]{:S(2)}) collective-permute-start(bf16[512,1024]{1,0:T(8,128)(2,1)} %get-tuple-element.107), channel_id=1, source_target_pairs={{0,1},{1,0},{2,3},{3,2},{4,5},{5,4},{6,7},{7,6},{8,9},{9,8},{10,11... | collective-permute-start | bytes 3145736 | tf_op jit(solution)/shard_map/ppermute | solution.py:680
  166.0 27.1 %collective-permute-start.17 = (bf16[512,384]{1,0:T(8,128)(2,1)}, bf16[512,384]{1,0:T(8,128)(2,1)}, u32[]{:S(2)}, u32[]{:S(2)}) collective-permute-start(bf16[512,384]{1,0:T(8,128)(2,1)} %get-tuple-element.108), channel_id=1, source_target_pairs={{0,1},{1,0},{2,3},{3,2},{4,5},{5,4},{6,7},{7,6},{8,9},{9,8},{10,11... | collective-permute-start | bytes 1179656 | tf_op jit(solution)/shard_map/ppermute | solution.py:680
  167.2 25.9 %collective-permute-start.18 = (bf16[512,768]{1,0:T(8,128)(2,1)}, bf16[512,768]{1,0:T(8,128)(2,1)S(1)}, u32[]{:S(2)}, u32[]{:S(2)}) collective-permute-start(bf16[512,768]{1,0:T(8,128)(2,1)} %copy-done.47), channel_id=1, source_target_pairs={{0,1},{1,0},{2,3},{3,2},{4,5},{5,4},{6,7},{7,6},{8,9},{9,8},{10,11... | collective-permute-start | bytes 2359304 | tf_op jit(solution)/shard_map/ppermute | solution.py:680
  192.3 25.2 %collective-permute-start.19 = (bf16[512,768]{1,0:T(8,128)(2,1)}, bf16[512,768]{1,0:T(8,128)(2,1)}, u32[]{:S(2)}, u32[]{:S(2)}) collective-permute-start(bf16[512,768]{1,0:T(8,128)(2,1)} %get-tuple-element.115), channel_id=1, source_target_pairs={{0,1},{1,0},{2,3},{3,2},{4,5},{5,4},{6,7},{7,6},{8,9},{9,8},{10,11... | collective-permute-start | bytes 2359304 | tf_op jit(solution)/shard_map/ppermute | solution.py:680
  217.2 23.1 %collective-permute-start.21 = (bf16[2048,384]{1,0:T(8,128)(2,1)}, bf16[2048,384]{1,0:T(8,128)(2,1)}, u32[]{:S(2)}, u32[]{:S(2)}) collective-permute-start(bf16[2048,384]{1,0:T(8,128)(2,1)} %get-tuple-element.122), channel_id=1, source_target_pairs={{0,1},{1,0},{2,3},{3,2},{4,5},{5,4},{6,7},{7,6},{8,9},{9,8},{10,11... | collective-permute-start | bytes 4718600 | tf_op jit(solution)/shard_map/ppermute | solution.py:680
  234.2 17.2 %collective-permute-start.20 = (bf16[384,4096]{1,0:T(8,128)(2,1)}, bf16[384,4096]{1,0:T(8,128)(2,1)}, u32[]{:S(2)}, u32[]{:S(2)}) collective-permute-start(bf16[384,4096]{1,0:T(8,128)(2,1)} %get-tuple-element.120.refs_4_.refs_2_), channel_id=1, source_target_pairs={{0,1},{1,0},{2,3},{3,2},{4,5},{5,4},{6,7},{7,6},{8,9},{9,8},{10,11... | collective-permute-start | bytes 9437192 | tf_op jit(solution)/shard_map/ppermute | solution.py:680
  234.4 5.9 %collective-permute-start.22 = (bf16[384,1024]{1,0:T(8,128)(2,1)}, bf16[384,1024]{1,0:T(8,128)(2,1)S(1)}, u32[]{:S(2)}, u32[]{:S(2)}) collective-permute-start(bf16[384,1024]{1,0:T(8,128)(2,1)} %get-tuple-element.114.out_grad.refs_2_), channel_id=1, source_target_pairs={{0,1},{1,0},{2,3},{3,2},{4,5},{5,4},{6,7},{7,6},{8,9},{9,8},{10,11... | collective-permute-start | bytes 2359304 | tf_op jit(solution)/shard_map/ppermute | solution.py:680
  249.8 51.0 %collective-permute-start.23 = (bf16[1024,1024]{1,0:T(8,128)(2,1)}, bf16[1024,1024]{1,0:T(8,128)(2,1)}, u32[]{:S(2)}, u32[]{:S(2)}) collective-permute-start(bf16[1024,1024]{1,0:T(8,128)(2,1)} %get-tuple-element.123.refs_4_), channel_id=1, source_target_pairs={{0,4},{1,5},{2,6},{3,7},{4,0},{5,1},{6,2},{7,3},{8,12},{9,13},{10,... | collective-permute-start | bytes 6291464 | tf_op jit(solution)/shard_map/ppermute | solution.py:680
  260.6 48.8 %collective-permute-start.25 = (bf16[256,4096]{1,0:T(8,128)(2,1)}, bf16[256,4096]{1,0:T(8,128)(2,1)}, u32[]{:S(2)}, u32[]{:S(2)}) collective-permute-start(bf16[256,4096]{1,0:T(8,128)(2,1)} %get-tuple-element.124.rest_0_), channel_id=1, source_target_pairs={{0,2},{1,3},{2,0},{3,1},{4,6},{5,7},{6,4},{7,5},{8,10},{9,11},{10,... | collective-permute-start | bytes 6291464 | tf_op jit(solution)/shard_map/ppermute | solution.py:680
  282.0 31.1 %collective-permute-start.27 = (bf16[3072,1024]{1,0:T(8,128)(2,1)}, bf16[3072,1024]{1,0:T(8,128)(2,1)}, u32[]{:S(2)}, u32[]{:S(2)}) collective-permute-start(bf16[3072,1024]{1,0:T(8,128)(2,1)} %get-tuple-element.125.query_delta.refs_6_.refs_8_.refs_0_.refs_1_), channel_id=1, source_target_pairs={{0,1},{1,0},{2,3},{3,2},{4,5},{5,4},{6,7},{7,6},{8,9},{9,8},{10,11... | collective-permute-start | bytes 18874376 | tf_op jit(solution)/shard_map/ppermute | solution.py:680
  297.9 1.6 collective-permute-start.32
  298.0 49.2 %collective-permute-start.31 = (bf16[1536,1024]{1,0:T(8,128)(2,1)}, bf16[1536,1024]{1,0:T(8,128)(2,1)}, u32[]{:S(2)}, u32[]{:S(2)}) collective-permute-start(bf16[1536,1024]{1,0:T(8,128)(2,1)} %get-tuple-element.126.refs_4_.refs_0_.refs_1_.refs_2_), channel_id=1, source_target_pairs={{0,1},{1,0},{2,3},{3,2},{4,5},{5,4},{6,7},{7,6},{8,9},{9,8},{10,11... | collective-permute-start | bytes 9437192 | tf_op jit(solution)/shard_map/ppermute | solution.py:680
  299.6 47.6 %collective-permute-start.33 = (bf16[2,2,2,32,256]{4,3,2,1,0:T(8,128)(2,1)S(1)}, bf16[2,2,2,32,256]{4,3,2,1,0:T(8,128)(2,1)S(1)}, u32[]{:S(2)}, u32[]{:S(2)}) collective-permute-start(bf16[2,2,2,32,256]{4,3,2,1,0:T(8,128)(2,1)S(1)} %get-tuple-element.217), channel_id=1, source_target_pairs={{0,2},{1,3},{2,0},{3,1},{4,6},{5,7},{6,4},{7,5},{8,10},{9,11},{10,... | collective-permute-start | bytes 393224 | tf_op jit(solution)/shard_map/ppermute | solution.py:680
  303.0 30.7 %collective-permute-start.24 = (bf16[4,128,1024]{2,1,0:T(8,128)(2,1)S(1)}, bf16[4,128,1024]{2,1,0:T(8,128)(2,1)S(1)}, u32[]{:S(2)}, u32[]{:S(2)}) collective-permute-start(bf16[4,128,1024]{2,1,0:T(8,128)(2,1)S(1)} %get-tuple-element.135), channel_id=1, source_target_pairs={{0,2},{1,3},{2,0},{3,1},{4,6},{5,7},{6,4},{7,5},{8,10},{9,11},{10,... | collective-permute-start | bytes 3145736 | tf_op jit(solution)/shard_map/ppermute | solution.py:680
  312.7 23.4 %collective-permute-start.26 = (bf16[4,32,4096]{2,1,0:T(8,128)(2,1)S(1)}, bf16[4,32,4096]{2,1,0:T(8,128)(2,1)S(1)}, u32[]{:S(2)}, u32[]{:S(2)}) collective-permute-start(bf16[4,32,4096]{2,1,0:T(8,128)(2,1)S(1)} %get-tuple-element.138), channel_id=1, source_target_pairs={{0,4},{1,5},{2,6},{3,7},{4,0},{5,1},{6,2},{7,3},{8,12},{9,13},{10,... | collective-permute-start | bytes 3145736 | tf_op jit(solution)/shard_map/ppermute | solution.py:680
  336.1 41.0 %slice-start = ((s8[6291456]{0:T(1024)(128)(4,1)}), s8[4194304]{0:T(1024)(128)(4,1)S(1)}, s32[]{:S(2)}) async-start(s8[6291456]{0:T(1024)(128)(4,1)} %bitcast.93), calls=%async_computation.1 | async-start | bytes 8388608
  339.0 47.4 %collective-permute-start.28 = (bf16[2,32,8192]{2,1,0:T(8,128)(2,1)}, bf16[2,32,8192]{2,1,0:T(8,128)(2,1)S(1)}, u32[]{:S(2)}, u32[]{:S(2)}) collective-permute-start(bf16[2,32,8192]{2,1,0:T(8,128)(2,1)} %get-tuple-element.141), channel_id=1, source_target_pairs={{0,8},{1,9},{2,10},{3,11},{4,12},{5,13},{6,14},{7,15},{8,0},{9,1},... | collective-permute-start | bytes 3145736 | tf_op jit(solution)/shard_map/ppermute | solution.py:680
  345.3 26.4 %collective-permute-start.29 = (bf16[256,2048]{1,0:T(8,128)(2,1)}, bf16[256,2048]{1,0:T(8,128)(2,1)}, u32[]{:S(2)}, u32[]{:S(2)}) collective-permute-start(bf16[256,2048]{1,0:T(8,128)(2,1)} %get-tuple-element.142), channel_id=1, source_target_pairs={{0,4},{1,5},{2,6},{3,7},{4,0},{5,1},{6,2},{7,3},{8,12},{9,13},{10,... | collective-permute-start | bytes 3145736 | tf_op jit(solution)/shard_map/ppermute | solution.py:680
  345.8 26.4 %collective-permute-start.30 = (bf16[256,2048]{1,0:T(8,128)(2,1)}, bf16[256,2048]{1,0:T(8,128)(2,1)}, u32[]{:S(2)}, u32[]{:S(2)}) collective-permute-start(bf16[256,2048]{1,0:T(8,128)(2,1)} %get-tuple-element.144), channel_id=1, source_target_pairs={{0,2},{1,3},{2,0},{3,1},{4,6},{5,7},{6,4},{7,5},{8,10},{9,11},{10,... | collective-permute-start | bytes 3145736 | tf_op jit(solution)/shard_map/ppermute | solution.py:680
  356.8 40.8 %collective-permute-start.34 = (bf16[256,2048]{1,0:T(8,128)(2,1)}, bf16[256,2048]{1,0:T(8,128)(2,1)S(1)}, u32[]{:S(2)}, u32[]{:S(2)}) collective-permute-start(bf16[256,2048]{1,0:T(8,128)(2,1)} %get-tuple-element.149), channel_id=1, source_target_pairs={{0,4},{1,5},{2,6},{3,7},{4,0},{5,1},{6,2},{7,3},{8,12},{9,13},{10,... | collective-permute-start | bytes 3145736 | tf_op jit(solution)/shard_map/ppermute | solution.py:680
  358.2 39.4 %collective-permute-start.35 = (bf16[256,2048]{1,0:T(8,128)(2,1)}, bf16[256,2048]{1,0:T(8,128)(2,1)S(1)}, u32[]{:S(2)}, u32[]{:S(2)}) collective-permute-start(bf16[256,2048]{1,0:T(8,128)(2,1)} %get-tuple-element.151), channel_id=1, source_target_pairs={{0,2},{1,3},{2,0},{3,1},{4,6},{5,7},{6,4},{7,5},{8,10},{9,11},{10,... | collective-permute-start | bytes 3145736 | tf_op jit(solution)/shard_map/ppermute | solution.py:680
  374.3 31.7 %collective-permute-start.38 = (bf16[4,32,2048]{2,1,0:T(8,128)(2,1)S(1)}, bf16[4,32,2048]{2,1,0:T(8,128)(2,1)}, u32[]{:S(2)}, u32[]{:S(2)}) collective-permute-start(bf16[4,32,2048]{2,1,0:T(8,128)(2,1)S(1)} %get-tuple-element.156), channel_id=1, source_target_pairs={{0,2},{1,3},{2,0},{3,1},{4,6},{5,7},{6,4},{7,5},{8,10},{9,11},{10,... | collective-permute-start | bytes 1572872 | tf_op jit(solution)/shard_map/ppermute | solution.py:680
  375.7 30.3 %collective-permute-start.39 = (bf16[4,32,2048]{2,1,0:T(8,128)(2,1)S(1)}, bf16[4,32,2048]{2,1,0:T(8,128)(2,1)}, u32[]{:S(2)}, u32[]{:S(2)}) collective-permute-start(bf16[4,32,2048]{2,1,0:T(8,128)(2,1)S(1)} %get-tuple-element.157), channel_id=1, source_target_pairs={{0,4},{1,5},{2,6},{3,7},{4,0},{5,1},{6,2},{7,3},{8,12},{9,13},{10,... | collective-permute-start | bytes 1572872 | tf_op jit(solution)/shard_map/ppermute | solution.py:680
  389.5 18.0 %collective-permute-start.44 = (bf16[1,32,8192]{2,1,0:T(8,128)(2,1)S(1)}, bf16[1,32,8192]{2,1,0:T(8,128)(2,1)S(1)}, u32[]{:S(2)}, u32[]{:S(2)}) collective-permute-start(bf16[1,32,8192]{2,1,0:T(8,128)(2,1)S(1)} %get-tuple-element.166), channel_id=1, source_target_pairs={{0,16},{1,17},{2,18},{3,19},{4,20},{5,21},{6,22},{7,23},{8,24},{9,... | collective-permute-start | bytes 1572872 | tf_op jit(solution)/shard_map/ppermute | solution.py:680
  400.1 12.8 %collective-permute-start.36 = (bf16[4,32,2048]{2,1,0:T(8,128)(2,1)S(1)}, bf16[4,32,2048]{2,1,0:T(8,128)(2,1)S(1)}, u32[]{:S(2)}, u32[]{:S(2)}) collective-permute-start(bf16[4,32,2048]{2,1,0:T(8,128)(2,1)S(1)} %get-tuple-element.153), channel_id=1, source_target_pairs={{0,2},{1,3},{2,0},{3,1},{4,6},{5,7},{6,4},{7,5},{8,10},{9,11},{10,... | collective-permute-start | bytes 1572872 | tf_op jit(solution)/shard_map/ppermute | solution.py:680
  401.0 13.1 %collective-permute-start.37 = (bf16[4,32,2304]{2,1,0:T(8,128)(2,1)S(1)}, bf16[4,32,2304]{2,1,0:T(8,128)(2,1)S(1)}, u32[]{:S(2)}, u32[]{:S(2)}) collective-permute-start(bf16[4,32,2304]{2,1,0:T(8,128)(2,1)S(1)} %get-tuple-element.155), channel_id=1, source_target_pairs={{0,4},{1,5},{2,6},{3,7},{4,0},{5,1},{6,2},{7,3},{8,12},{9,13},{10,... | collective-permute-start | bytes 1769480 | tf_op jit(solution)/shard_map/ppermute | solution.py:680
  407.4 16.3 %collective-permute-start.41 = (bf16[2,32,4096]{2,1,0:T(8,128)(2,1)S(1)}, bf16[2,32,4096]{2,1,0:T(8,128)(2,1)S(1)}, u32[]{:S(2)}, u32[]{:S(2)}) collective-permute-start(bf16[2,32,4096]{2,1,0:T(8,128)(2,1)S(1)} %get-tuple-element.161), channel_id=1, source_target_pairs={{0,8},{1,9},{2,10},{3,11},{4,12},{5,13},{6,14},{7,15},{8,0},{9,1},... | collective-permute-start | bytes 1572872 | tf_op jit(solution)/shard_map/ppermute | solution.py:680
  414.9 17.9 %collective-permute-start.40 = (bf16[2,32,4352]{2,1,0:T(8,128)(2,1)S(1)}, bf16[2,32,4352]{2,1,0:T(8,128)(2,1)S(1)}, u32[]{:S(2)}, u32[]{:S(2)}) collective-permute-start(bf16[2,32,4352]{2,1,0:T(8,128)(2,1)S(1)} %get-tuple-element.160), channel_id=1, source_target_pairs={{0,8},{1,9},{2,10},{3,11},{4,12},{5,13},{6,14},{7,15},{8,0},{9,1},... | collective-permute-start | bytes 1671176 | tf_op jit(solution)/shard_map/ppermute | solution.py:680
  424.3 17.9 %collective-permute-start.43 = (bf16[1,32,4096]{2,1,0:T(8,128)(2,1)S(1)}, bf16[1,32,4096]{2,1,0:T(8,128)(2,1)S(1)}, u32[]{:S(2)}, u32[]{:S(2)}) collective-permute-start(bf16[1,32,4096]{2,1,0:T(8,128)(2,1)S(1)} %get-tuple-element.165), channel_id=1, source_target_pairs={{0,16},{1,17},{2,18},{3,19},{4,20},{5,21},{6,22},{7,23},{8,24},{9,... | collective-permute-start | bytes 786440 | tf_op jit(solution)/shard_map/ppermute | solution.py:680
  433.5 12.6 %collective-permute-start.42 = (bf16[1,32,4352]{2,1,0:T(8,128)(2,1)S(1)}, bf16[1,32,4352]{2,1,0:T(8,128)(2,1)S(1)}, u32[]{:S(2)}, u32[]{:S(2)}) collective-permute-start(bf16[1,32,4352]{2,1,0:T(8,128)(2,1)S(1)} %get-tuple-element.164), channel_id=1, source_target_pairs={{0,16},{1,17},{2,18},{3,19},{4,20},{5,21},{6,22},{7,23},{8,24},{9,... | collective-permute-start | bytes 835592 | tf_op jit(solution)/shard_map/ppermute | solution.py:680
  (66 other events, 553.4 us)
Sparse Core Ops, SparseCore 0:
  51.5 146.2 all-gather.2

commit v5 on v4

--- a/solution.py
+++ b/solution.py
@@ -399,7 +399,7 @@
     for array in arrays:
         tokens = array.shape[0]
         columns = slice(start, start + tokens)
-        turned = array[...].astype(jnp.float32).T
+        turned = array[...].astype(jnp.float32 if rows % 16 else jnp.bfloat16).T
         deal(core[0], turned, rows, into(keep, columns), into(send, columns))
         start += tokens
 
@@ -448,10 +448,9 @@
 
     pre = dot(low[...], flat(w_in), (1, 0)) + bias[...]
     part = 0.5 + 0.5 * lax.erf(pre * 0.5**0.5)
-    active = pre * part
+    active = (pre * part).astype(jnp.bfloat16)
     everything = slice(None)
     deal(core[0], active.T, rows, into(keep, everything), into(send, everything))
-    active = active.astype(jnp.bfloat16)
     slope[...] = (part + pre * jnp.exp(-0.5 * pre * pre) * 0.3989422804014327).astype(jnp.bfloat16)
     acc[...] += dot(active, flat(w_out), (1, 0))
 
@@ -471,7 +470,7 @@
 def ffn_forward(core, second, packed, bias, cot, vectors, rows, after):
     tokens, width = second.shape
     hidden = packed.shape[0] * packed.shape[1] // 2
-    chunk = 512
+    chunk = 1024
     whole = lambda shape: pl.BlockSpec(shape, lambda j: (0, 0))
     full = whole((tokens, width))
     strip = pl.BlockSpec((tokens, chunk), lambda j: (0, j))
@@ -536,7 +535,7 @@
 def ffn_backward(packed, slope, third_grad, out_grad, unit, inverse, gain, after):
     tokens, width = third_grad.shape
     hidden = packed.shape[0] * packed.shape[1] // 2
-    chunk = 512
+    chunk = 1024
     whole = lambda shape: pl.BlockSpec(shape, lambda j: (0, 0))
     full = whole((tokens, width))
     strip = pl.BlockSpec((tokens, chunk), lambda j: (0, j))
@@ -905,7 +904,7 @@
         + [anywhere] * len(after),
         out_specs=block,
         compiler_params=kernel_params(40),
-        cost_estimate=cost(3 * rows * count * width * width, 12),
+        cost_estimate=cost(0, 0.001),
     )(*[stack] * count, *[weights] * count, *bases, *after)
 
 
@@ -1000,7 +999,7 @@
     )
     hidden_other, out_grad_other = exchange(hidden_send, 0), exchange(out_grad, 0)
     pre_grad, ffn_bias_grad, second_grad, cross_branch, second_sums = ffn_backward(
-        packed, slope, third_grad, out_grad, second_unit, second_inverse, gains[1:2], cross_turned[1:]
+        packed, slope, third_grad, out_grad, second_unit, second_inverse, gains[1:2], (cross_turned[1], out_grad_other)
     )
     pre_grad_other = exchange(pre_grad, 0)
     parts = products(
@@ -1098,7 +1097,6 @@
         after=in_chain.second(after=out_chain.second(after=(small_grad,))),
     )
     cross_chain = Chain(ids, parts, owned)
-    out_chain.join(in_chain)
     parts = products(
         ids,
         [part for i in range(2) for part in ((target_turned[i], tokens, 0), (self_turned[i], tokens, 0))],
@@ -1107,15 +1105,18 @@
         + [(tokens, 3 * tokens, tokens, 0, 3, width)],
         owned,
         1024,
-        after=(*out_chain.third(after=parts[:1]), small_other),
+        after=(parts[0], small_other),
     )
     self_chain = Chain(ids, parts, owned)
     self_chain.groups[1].append((small_keep, small_other, owned))
-    last = cross_chain.second(after=parts[:1])
+    out_chain.join(in_chain)
+    last = out_chain.third(after=parts[:1])
+    last = cross_chain.second(after=last)
     memory_grad = add_product(cross_delta, [0, mems], late, [0, 1], mems, 512, after=last)
     last = (memory_grad,)
     while out_chain.rest:
         last = out_chain.third(after=last)
+    last = self_chain.second(after=last)
     target_grad = add_product(
         self_delta,
         [0, tokens, 2 * tokens],
@@ -1126,7 +1127,7 @@
         first_grad,
         after=last,
     )
-    last = self_chain.second(after=(target_grad,))
+    last = (target_grad,)
     last = cross_chain.third(after=last)
     last = self_chain.third(after=last)
     while self_chain.rest:

time: 461 us -> 459 us (level)
  waiting for transfers between devices: 175 us -> 153 us
  starting transfers between devices: 46.6 us -> 56.4 us
  local copies, waits for them, and re-layouts: 42.1 us -> 50.5 us
    ppermute x45, waiting for transfers between devices: 171 us -> 148 us  [exchange(): return lax.ppermute(values, AXES, [(i, i ^ 1 << bit) for i in range(count)])]
    ppermute x45, starting transfers between devices: 46.6 us -> 56.3 us  [exchange(): return lax.ppermute(values, AXES, [(i, i ^ 1 << bit) for i in range(count)])]
    unnamed x141 -> x157, local copies, waits for them, and re-layouts: 33.3 us -> 42.3 us
  transfers between devices with their start and end apart: 46 -> 46, of which waited for: 24 -> 22; matrix products, arithmetic and copies ran while one was open for 6% -> 6% of each run, Pallas kernels for 34% -> 34%
where the time goes in v5:
time: 459 us; the launch traced here: 455 us
  Pallas kernels  157 us (34%)
  waiting for transfers between devices  153 us (33%)
  starting transfers between devices  56.4 us (12%)
  local copies, waits for them, and re-layouts  50.5 us (11%)
  matrix products  16.8 us (4%)
  between operations  15.2 us (3%)
  other arithmetic  6.06 us (1%)
    ppermute x45, waiting for transfers between devices, exchange(): return lax.ppermute(values, AXES, [(i, i ^ 1 << bit) for i in range(count)])  148 us
    ppermute x45, starting transfers between devices, exchange(): return lax.ppermute(values, AXES, [(i, i ^ 1 << bit) for i in range(count)])  56.3 us
    unnamed x157, local copies, waits for them, and re-layouts  42.3 us
    pallas_call x4, Pallas kernels, products(): pl.pallas_call(functools.partial(product_kernel, spans=spans, n_left=len(...  37.3 us
    pallas_call x1, Pallas kernels, cross_backward(): pl.pallas_call(functools.partial(cross_backward_kernel, extra=len(after))...  21.6 us
    dot_general x5, matrix products, matmul(): return jnp.dot(first, second, preferred_element_type=jnp.float32)  16.8 us
    pallas_call x10, Pallas kernels, advance(): pl.pallas_call(functools.partial(stage_kernel, groups=[(b, len(g)) for b,...  16.1 us
    pallas_call x1, Pallas kernels, ffn_forward(): pl.pallas_call(functools.partial(ffn_forward_kernel, rows=rows, extra=len...  14.9 us
  transfers between devices with their start and end apart: 46, of which 22 were waited for; matrix products, arithmetic and copies ran while one was open for 6% of the time, Pallas kernels for 34%

profile of v5, /device:TPU:0, one launch (start us, length us, event | category | flops | bytes accessed | tf_op | source)
XLA Modules:
  0.0 454.9 jit_solution(5937307428189487006)
XLA Ops:
  10.7 4.1 collective-permute-start
  19.0 10.9 %collective-permute-done.refs_1_ = bf16[1,32,5248]{2,1,0:T(8,128)(2,1)S(1)} collective-permute-done((bf16[1,32,5248]{2,1,0:T(8,128)(2,1)S(1)}, bf16[1,32,5248]{2,1,0:T(8,128)(2,1)S(1)}, u32[]{:S(2)}, u32[]{:S(2)}) %collective-permute-start) | collective-permute-done | bytes 335904 | tf_op jit(solution)/shard_map/ppermute | solution.py:679
  30.7 3.4 collective-permute-start.2
  34.2 15.2 %collective-permute-done.2.refs_1_ = bf16[1,32,3072]{2,1,0:T(8,128)(2,1)S(1)} collective-permute-done((bf16[1,32,3072]{2,1,0:T(8,128)(2,1)S(1)}, bf16[1,32,3072]{2,1,0:T(8,128)(2,1)S(1)}, u32[]{:S(2)}, u32[]{:S(2)}) %collective-permute-start.2) | collective-permute-done | bytes 196640 | tf_op jit(solution)/shard_map/ppermute | solution.py:679
  54.3 3.4 collective-permute-start.5
  57.7 11.6 %collective-permute-done.5.refs_1_ = bf16[2,32,3072]{2,1,0:T(8,128)(2,1)S(1)} collective-permute-done((bf16[2,32,3072]{2,1,0:T(8,128)(2,1)S(1)}, bf16[2,32,3072]{2,1,0:T(8,128)(2,1)S(1)}, u32[]{:S(2)}, u32[]{:S(2)}) %collective-permute-start.5) | collective-permute-done | bytes 393248 | tf_op jit(solution)/shard_map/ppermute | solution.py:679
  69.3 3.6 collective-permute-done.3.refs_1_
  77.1 47.0 %collective-permute-done.8.refs_1_ = bf16[4,32,1536]{2,1,0:T(8,128)(2,1)S(1)} collective-permute-done((bf16[4,32,1536]{2,1,0:T(8,128)(2,1)S(1)}, bf16[4,32,1536]{2,1,0:T(8,128)(2,1)S(1)}, u32[]{:S(2)}, u32[]{:S(2)}) %collective-permute-start.8) | collective-permute-done | bytes 393248 | tf_op jit(solution)/shard_map/ppermute | solution.py:679
  127.2 6.3 %collective-permute-done.10.refs_1_ = bf16[16,32,2560]{2,1,0:T(8,128)(2,1)S(1)} collective-permute-done((bf16[16,32,2560]{2,1,0:T(8,128)(2,1)S(1)}, bf16[16,32,2560]{2,1,0:T(8,128)(2,1)S(1)}, u32[]{:S(2)}, u32[]{:S(2)}) %collective-permute-start.10) | collective-permute-done | bytes 2621472 | tf_op jit(solution)/shard_map/ppermute | solution.py:679
  133.6 5.1 %shard_map.264.w_query.w_self.refs_3_.refs_4_.refs_5_ = bf16[1024,5248]{1,0:T(8,128)(2,1)S(1)} custom-call(bf16[16,32,2560]{2,1,0:T(8,128)(2,1)S(1)} %get-tuple-element.99.refs_0_.refs_4_, bf16[16,32,2560]{2,1,0:T(8,128)(2,1)S(1)} %collective-permute-done.10.refs_1_, bf16[16,32,2688]{2,1,0:T(8,128)(2,1)S(1)} %get-tuple-element.100.refs_2_, ...), custom_call_target="tpu_custom_call" | custom-call | bytes 214958080 | tf_op jit(solution)/shard_map/pallas_call | solution.py:775
  138.7 4.0 copy-done
  142.9 5.6 %fusion.7.qkv = bf16[384,3072]{1,0:T(8,128)(2,1)S(1)} fusion(bf16[384,1024]{1,0:T(8,128)(2,1)S(1)} %copy-done.32, bf16[1024,5248]{1,0:T(8,128)(2,1)} %copy-done, f32[3072]{0:T(1024)S(1)} %pad_maximum_fusion), kind=kOutput, calls=%fused_computation.7 | convolution fusion | flops 2418278400 | bytes 9449472 | tf_op jit(solution)/shard_map/dot_general | solution.py:33
  148.6 3.5 shard_map.265
  152.1 2.7 fusion.35
  158.0 2.6 add_convert_fusion.2.refs_4_.q
  162.8 2.5 shard_map.267
  167.4 2.3 collective-permute-done.14.refs_1_
  169.8 2.9 collective-permute-done.15.refs_3_
  172.7 3.5 shard_map.268.weight.refs_2_.refs_3_
  176.2 4.7 %fusion.4.pairs = bf16[1024,2048]{1,0:T(8,128)(2,1)S(1)} fusion(f32[2048]{0:T(1024)S(1)} %concatenate.22, bf16[1024,1024]{1,0:T(8,128)(2,1)S(1)} %copy-done.11, bf16[1024,3072]{1,0:T(8,128)(2,1)S(1)} %shard_map.268.weight.refs_2_.refs_3_), kind=kOutput, calls=%fused_computation.4 | convolution fusion | flops 4299161600 | bytes 10493952 | tf_op jit(solution)/shard_map/dot_general | solution.py:33
  181.0 7.0 %shard_map.269 = (bf16[384,1024]{1,0:T(8,128)(2,1)S(1)}, f32[3,8,1,256]{3,2,1,0:T(1,128)S(1)}) custom-call(s32[2,3]{1,0:T(2,128)S(1)} %pad_add_fusion.bound, bf16[384,1024]{1,0:T(8,128)(2,1)S(1)} %add_convert_fusion.2.refs_4_.q, bf16[1024,2048]{1,0:T(8,128)(2,1)S(1)} %fusion.4.pairs), custom_call_target="tpu_custom_call" | custom-call | flops 80000000000 | bytes 83886080 | tf_op jit(solution)/shard_map/pallas_call | solution.py:188
  193.3 4.5 all-gather.3.cloned.1.call-done
  200.1 14.9 %shard_map.271 = (bf16[2048,384]{1,0:T(8,128)(2,1)S(1)}, bf16[2048,384]{1,0:T(8,128)(2,1)}, bf16[384,4096]{1,0:T(8,128)(2,1)S(1)}, bf16[384,1024]{1,0:T(8,128)(2...) custom-call(s32[1]{0:T(128)} %bitcast.core, ...), custom_call_target="tpu_custom_call" | custom-call | flops 160000000000 | bytes 272629760 | tf_op jit(solution)/shard_map/pallas_call | solution.py:478
  218.5 12.7 %shard_map.273 = (bf16[384,4096]{1,0:T(8,128)(2,1)}, f32[1,4096]{1,0:T(1,128)S(1)}, f32[384,1024]{1,0:T(8,128)S(1)}, bf16[384,1024]{1,0:T(8,128)(2,1)S(1)}, f32[8,1024]{1,0:T(8,128)S(1)}) custom-call(bf16[32,256,1024]{2,1,0:T(8,128)(2,1)} %bitcast.145, bf16[32,256,1024]{2,1,0:T(8,128)(2,1)} %bitcast.146, bf16[384,4096]{1,0:T(8,128)(2,1)S(1)} %get-tuple-element.112.slope, ...), custom_call_target="tpu_custom_call" | custom-call | flops 140000002048 | bytes 272629760 | tf_op jit(solution)/shard_map/pallas_call | solution.py:542
  236.1 7.9 %shard_map.274 = (bf16[1024,1024]{1,0:T(8,128)(2,1)}, bf16[1024,1024]{1,0:T(8,128)(2,1)}) custom-call(s32[5]{0:T(128)S(1)} %shift-right-arithmetic_and_fusion.ids, bf16[2048,384]{1,0:T(8,128)(2,1)S(1)} %copy-done.61, bf16[2048,384]{1,0:T(8,128)(2,1)} %collective-permute-done.22.refs_1_, bf16[384,1024]{1,0:T(8,128)(2,1)S(1)} %copy-done.55, ...), custom_call_target="tpu_custom_call" | custom-call | flops 20132659200 | bytes 209715200 | tf_op jit(solution)/shard_map/pallas_call | solution.py:656
  245.6 8.0 %shard_map.275 = (bf16[256,4096]{1,0:T(8,128)(2,1)S(1)}, bf16[256,4096]{1,0:T(8,128)(2,1)}) custom-call(s32[5]{0:T(128)S(1)} %shift-right-arithmetic_and_fusion.ids, bf16[512,768]{1,0:T(8,128)(2,1)S(1)} %copy-done.51, bf16[512,768]{1,0:T(8,128)(2,1)} %collective-permute-done.19.rest_0_.refs_1_.refs_5_, bf16[384,4096]{1,0:T(8,128)(2,1)} %get-tuple-element.120.refs_4_.refs_2_, ...), custom_call_target="tpu_custom_call" | custom-call | flops 20132659200 | bytes 209715200 | tf_op jit(solution)/shard_map/pallas_call | solution.py:656
  256.3 21.6 %shard_map.276 = (bf16[3072,1024]{1,0:T(8,128)(2,1)}, f32[8,1024]{1,0:T(8,128)}) custom-call(s32[2,3]{1,0:T(2,128)} %copy-done.44, bf16[384,1024]{1,0:T(8,128)(2,1)} %copy-done.27, bf16[1024,2048]{1,0:T(8,128)(2,1)} %copy-done.59, f32[3,8,1,256]{3,2,1,0:T(1,128)} %copy-done.65, bf16[384,1024]{1,0:T(8,128)(2,1)} %copy-done.64, bf16[1024,3072]{1,0:T(8,128)(2,1)} %copy-done.1, ...), custom_call_target="tpu_custom_call" | custom-call | flops 160000000000 | bytes 125829120 | tf_op jit(solution)/shard_map/pallas_call | solution.py:214
  277.9 13.4 %shard_map.277 = (bf16[1536,1024]{1,0:T(8,128)(2,1)}, f32[8,1024]{1,0:T(8,128)S(1)}, f32[384,1024]{1,0:T(8,128)S(1)}) custom-call(s32[3]{0:T(128)S(1)} %bitcast.127, bf16[384,3072]{1,0:T(8,128)(2,1)} %copy-done.58, f32[3,8,1,256]{3,2,1,0:T(1,128)S(1)} %get-tuple-element.111.summary, f32[384,1024]{1,0:T(8,128)S(1)} %copy-done.63, ...), custom_call_target="tpu_custom_call" | custom-call | flops 60000002048 | bytes 125829120 | tf_op jit(solution)/shard_map/pallas_call | solution.py:330
  297.1 3.1 shard_map.279
  303.4 3.2 shard_map.280
  311.6 13.1 %shard_map.281 = (bf16[256,2048]{1,0:T(8,128)(2,1)S(1)}, bf16[256,2048]{1,0:T(8,128)(2,1)}, bf16[256,2048]{1,0:T(8,128)(2,1)}, bf16[256,2048]{1,0:T(8,128)(2,1)}) custom-call(s32[5]{0:T(128)S(1)} %copy-done.38, bf16[512,1024]{1,0:T(8,128)(2,1)} %copy-done.18, bf16[512,768]{1,0:T(8,128)(2,1)S(1)} %copy-done.25, bf16[512,768]{1,0:T(8,128)(2,1)S(1)} %copy-done.52, ...), custom_call_target="tpu_custom_call" | custom-call | flops 31317469184 | bytes 209715200 | tf_op jit(solution)/shard_map/pallas_call | solution.py:656
  332.8 8.2 %shard_map.282 = (bf16[256,2048]{1,0:T(8,128)(2,1)S(1)}, bf16[256,2048]{1,0:T(8,128)(2,1)S(1)}, bf16[256,2048]{1,0:T(8,128)(2,1)S(1)}, bf16[256,2048]{1,0:T(8,128)(2,1)}) custom-call(s32[5]{0:T(128)S(1)} %copy-done.38, bf16[512,384]{1,0:T(8,128)(2,1)S(1)} %copy-done.34, bf16[512,768]{1,0:T(8,128)(2,1)S(1)} %copy-done.26, ...), custom_call_target="tpu_custom_call" | custom-call | flops 20132659200 | bytes 209715200 | tf_op jit(solution)/shard_map/pallas_call | solution.py:656
  341.1 2.2 shard_map.283
  343.2 5.9 %collective-permute-start.33 = (bf16[2,32,8192]{2,1,0:T(8,128)(2,1)S(1)}, bf16[2,32,8192]{2,1,0:T(8,128)(2,1)S(1)}, u32[]{:S(2)}, u32[]{:S(2)}) collective-permute-start(bf16[2,32,8192]{2,1,0:T(8,128)(2,1)S(1)} %get-tuple-element.145), channel_id=1, source_target_pairs={{0,8},{1,9},{2,10},{3,11},{4,12},{5,13},{6,14},{7,15},{8,0},{9,1},... | collective-permute-start | bytes 3145736 | tf_op jit(solution)/shard_map/ppermute | solution.py:679
  350.9 5.4 %collective-permute-done.34 = bf16[256,2048]{1,0:T(8,128)(2,1)} collective-permute-done((bf16[256,2048]{1,0:T(8,128)(2,1)}, bf16[256,2048]{1,0:T(8,128)(2,1)}, u32[]{:S(2)}, u32[]{:S(2)}) %collective-permute-start.34) | collective-permute-done | bytes 1048608 | tf_op jit(solution)/shard_map/ppermute | solution.py:679
  356.4 2.9 shard_map.284
  360.8 2.8 copy-done.4
  363.6 6.6 %shard_map.285.refs_2_ = f32[1024,1024]{1,0:T(8,128)} custom-call(bf16[3072,1024]{1,0:T(8,128)(2,1)S(1)} %copy-done.4, bf16[3072,1024]{1,0:T(8,128)(2,1)S(1)} %copy-done.4, bf16[1024,3072]{1,0:T(8,128)(2,1)S(1)} %bitcast.94, bf16[1024,3072]{1,0:T(8,128)(2,1)S(1)} %bitcast.94, bf16[4,32,2048]{2,1,0:T(8,128)(2,1)S(1)} %get-tuple-element.149.refs_4_, ...), custom_call_target="tpu_custom_call" | custom-call | bytes 10485 | tf_op jit(solution)/shard_map/pallas_call | solution.py:897
  370.2 2.1 collective-permute-done.33
  372.3 2.2 copy-done.5
  376.4 2.4 collective-permute-done.29
  381.4 6.6 %shard_map.288.refs_4_ = f32[384,1024]{1,0:T(8,128)} custom-call(bf16[1536,1024]{1,0:T(8,128)(2,1)S(1)} %copy-done.3, bf16[1536,1024]{1,0:T(8,128)(2,1)S(1)} %copy-done.3, bf16[1536,1024]{1,0:T(8,128)(2,1)S(1)} %copy-done.3, bf16[1024,5248]{1,0:T(8,128)(2,1)} %copy-done, bf16[1024,5248]{1,0:T(8,128)(2,1)} %copy-done, bf16[1024,5248]{1,0:T(8,128)(2,1)} %copy-done, ...), custom_call_target="tpu_custom_call" | custom-call | bytes 10485 | tf_op jit(solution)/shard_map/pallas_call | solution.py:897
  392.2 6.4 %collective-permute-start.41 = (bf16[2,32,4096]{2,1,0:T(8,128)(2,1)S(1)}, bf16[2,32,4096]{2,1,0:T(8,128)(2,1)S(1)}, u32[]{:S(2)}, u32[]{:S(2)}) collective-permute-start(bf16[2,32,4096]{2,1,0:T(8,128)(2,1)S(1)} %get-tuple-element.161), channel_id=1, source_target_pairs={{0,8},{1,9},{2,10},{3,11},{4,12},{5,13},{6,14},{7,15},{8,0},{9,1},... | collective-permute-start | bytes 1572872 | tf_op jit(solution)/shard_map/ppermute | solution.py:679
  398.6 2.0 collective-permute-done.44
  402.4 6.4 %collective-permute-start.40 = (bf16[2,32,4352]{2,1,0:T(8,128)(2,1)S(1)}, bf16[2,32,4352]{2,1,0:T(8,128)(2,1)S(1)}, u32[]{:S(2)}, u32[]{:S(2)}) collective-permute-start(bf16[2,32,4352]{2,1,0:T(8,128)(2,1)S(1)} %get-tuple-element.160), channel_id=1, source_target_pairs={{0,8},{1,9},{2,10},{3,11},{4,12},{5,13},{6,14},{7,15},{8,0},{9,1},... | collective-permute-start | bytes 1671176 | tf_op jit(solution)/shard_map/ppermute | solution.py:679
  408.8 3.0 collective-permute-done.41
  414.8 14.4 %collective-permute-done.40 = bf16[2,32,4352]{2,1,0:T(8,128)(2,1)S(1)} collective-permute-done((bf16[2,32,4352]{2,1,0:T(8,128)(2,1)S(1)}, bf16[2,32,4352]{2,1,0:T(8,128)(2,1)S(1)}, u32[]{:S(2)}, u32[]{:S(2)}) %collective-permute-start.40) | collective-permute-done | bytes 557088 | tf_op jit(solution)/shard_map/ppermute | solution.py:679
  432.4 12.0 %collective-permute-done.42 = bf16[1,32,4352]{2,1,0:T(8,128)(2,1)S(1)} collective-permute-done((bf16[1,32,4352]{2,1,0:T(8,128)(2,1)S(1)}, bf16[1,32,4352]{2,1,0:T(8,128)(2,1)S(1)}, u32[]{:S(2)}, u32[]{:S(2)}) %collective-permute-start.42) | collective-permute-done | bytes 278560 | tf_op jit(solution)/shard_map/ppermute | solution.py:679
  (297 shorter events, 93.8 us)
Async XLA Ops:
  7.2 190.6 %all-gather.3.cloned.1.call-start = ((), (), s32[]{:S(2)}) async-start(), calls=%async_computation | async-start | bytes 17301504 | tf_op jit(solution)/shard_map/all_gather | solution.py:951
  10.7 19.2 %collective-permute-start = (bf16[1,32,5248]{2,1,0:T(8,128)(2,1)S(1)}, bf16[1,32,5248]{2,1,0:T(8,128)(2,1)S(1)}, u32[]{:S(2)}, u32[]{:S(2)}) collective-permute-start(bf16[1,32,5248]{2,1,0:T(8,128)(2,1)S(1)} %maximum_bitcast_fusion.refs_0_), channel_id=1, source_target_pairs={{0,16},{1,17},{2,18},{3,19},{4,20},{5,21},{6,22},{7,23},{8,24},{9,... | collective-permute-start | bytes 1007624 | tf_op jit(solution)/shard_map/ppermute | solution.py:679
  29.9 20.5 %collective-permute-start.1 = (bf16[2,32,5248]{2,1,0:T(8,128)(2,1)S(1)}, bf16[2,32,5248]{2,1,0:T(8,128)(2,1)S(1)}, u32[]{:S(2)}, u32[]{:S(2)}) collective-permute-start(bf16[2,32,5248]{2,1,0:T(8,128)(2,1)S(1)} %shard_map.257.refs_2_.refs_0_), channel_id=1, source_target_pairs={{0,8},{1,9},{2,10},{3,11},{4,12},{5,13},{6,14},{7,15},{8,0},{9,1},... | collective-permute-start | bytes 2015240 | tf_op jit(solution)/shard_map/ppermute | solution.py:679
  30.7 18.7 %collective-permute-start.2 = (bf16[1,32,3072]{2,1,0:T(8,128)(2,1)S(1)}, bf16[1,32,3072]{2,1,0:T(8,128)(2,1)S(1)}, u32[]{:S(2)}, u32[]{:S(2)}) collective-permute-start(bf16[1,32,3072]{2,1,0:T(8,128)(2,1)S(1)} %maximum_bitcast_fusion.1.refs_0_), channel_id=1, source_target_pairs={{0,16},{1,17},{2,18},{3,19},{4,20},{5,21},{6,22},{7,23},{8,24},{9,... | collective-permute-start | bytes 589832 | tf_op jit(solution)/shard_map/ppermute | solution.py:679
  51.4 21.4 %collective-permute-start.4 = (bf16[4,32,2688]{2,1,0:T(8,128)(2,1)S(1)}, bf16[4,32,2688]{2,1,0:T(8,128)(2,1)S(1)}, u32[]{:S(2)}, u32[]{:S(2)}) collective-permute-start(bf16[4,32,2688]{2,1,0:T(8,128)(2,1)S(1)} %get-tuple-element.93.refs_2_), channel_id=1, source_target_pairs={{0,2},{1,3},{2,0},{3,1},{4,6},{5,7},{6,4},{7,5},{8,10},{9,11},{10,... | collective-permute-start | bytes 2064392 | tf_op jit(solution)/shard_map/ppermute | solution.py:679
  52.8 20.1 %collective-permute-start.3 = (bf16[4,32,2560]{2,1,0:T(8,128)(2,1)S(1)}, bf16[4,32,2560]{2,1,0:T(8,128)(2,1)S(1)}, u32[]{:S(2)}, u32[]{:S(2)}) collective-permute-start(bf16[4,32,2560]{2,1,0:T(8,128)(2,1)S(1)} %get-tuple-element.92.refs_2_.refs_0_), channel_id=1, source_target_pairs={{0,4},{1,5},{2,6},{3,7},{4,0},{5,1},{6,2},{7,3},{8,12},{9,13},{10,... | collective-permute-start | bytes 1966088 | tf_op jit(solution)/shard_map/ppermute | solution.py:679
  54.3 15.0 %collective-permute-start.5 = (bf16[2,32,3072]{2,1,0:T(8,128)(2,1)S(1)}, bf16[2,32,3072]{2,1,0:T(8,128)(2,1)S(1)}, u32[]{:S(2)}, u32[]{:S(2)}) collective-permute-start(bf16[2,32,3072]{2,1,0:T(8,128)(2,1)S(1)} %shard_map.258.refs_2_.refs_0_), channel_id=1, source_target_pairs={{0,8},{1,9},{2,10},{3,11},{4,12},{5,13},{6,14},{7,15},{8,0},{9,1},... | collective-permute-start | bytes 1179656 | tf_op jit(solution)/shard_map/ppermute | solution.py:679
  73.0 51.3 %collective-permute-start.7 = (bf16[8,32,2688]{2,1,0:T(8,128)(2,1)S(1)}, bf16[8,32,2688]{2,1,0:T(8,128)(2,1)S(1)}, u32[]{:S(2)}, u32[]{:S(2)}) collective-permute-start(bf16[8,32,2688]{2,1,0:T(8,128)(2,1)S(1)} %get-tuple-element.96.refs_2_), channel_id=1, source_target_pairs={{0,4},{1,5},{2,6},{3,7},{4,0},{5,1},{6,2},{7,3},{8,12},{9,13},{10,... | collective-permute-start | bytes 4128776 | tf_op jit(solution)/shard_map/ppermute | solution.py:679
  74.9 49.4 %collective-permute-start.6 = (bf16[8,32,2560]{2,1,0:T(8,128)(2,1)S(1)}, bf16[8,32,2560]{2,1,0:T(8,128)(2,1)S(1)}, u32[]{:S(2)}, u32[]{:S(2)}) collective-permute-start(bf16[8,32,2560]{2,1,0:T(8,128)(2,1)S(1)} %get-tuple-element.95.refs_4_.refs_0_), channel_id=1, source_target_pairs={{0,2},{1,3},{2,0},{3,1},{4,6},{5,7},{6,4},{7,5},{8,10},{9,11},{10,... | collective-permute-start | bytes 3932168 | tf_op jit(solution)/shard_map/ppermute | solution.py:679
  75.5 48.7 %collective-permute-start.8 = (bf16[4,32,1536]{2,1,0:T(8,128)(2,1)S(1)}, bf16[4,32,1536]{2,1,0:T(8,128)(2,1)S(1)}, u32[]{:S(2)}, u32[]{:S(2)}) collective-permute-start(bf16[4,32,1536]{2,1,0:T(8,128)(2,1)S(1)} %get-tuple-element.94.refs_4_.refs_0_), channel_id=1, source_target_pairs={{0,4},{1,5},{2,6},{3,7},{4,0},{5,1},{6,2},{7,3},{8,12},{9,13},{10,... | collective-permute-start | bytes 1179656 | tf_op jit(solution)/shard_map/ppermute | solution.py:679
  75.8 48.3 %collective-permute-start.9 = (bf16[4,32,1536]{2,1,0:T(8,128)(2,1)S(1)}, bf16[4,32,1536]{2,1,0:T(8,128)(2,1)S(1)}, u32[]{:S(2)}, u32[]{:S(2)}) collective-permute-start(bf16[4,32,1536]{2,1,0:T(8,128)(2,1)S(1)} %get-tuple-element.97.refs_2_), channel_id=1, source_target_pairs={{0,2},{1,3},{2,0},{3,1},{4,6},{5,7},{6,4},{7,5},{8,10},{9,11},{10,... | collective-permute-start | bytes 1179656 | tf_op jit(solution)/shard_map/ppermute | solution.py:679
  124.7 8.9 %collective-permute-start.11 = (bf16[16,32,2688]{2,1,0:T(8,128)(2,1)S(1)}, bf16[16,32,2688]{2,1,0:T(8,128)(2,1)S(1)}, u32[]{:S(2)}, u32[]{:S(2)}) collective-permute-start(bf16[16,32,2688]{2,1,0:T(8,128)(2,1)S(1)} %get-tuple-element.100.refs_2_), channel_id=1, source_target_pairs={{0,1},{1,0},{2,3},{3,2},{4,5},{5,4},{6,7},{7,6},{8,9},{9,8},{10,11... | collective-permute-start | bytes 8257544 | tf_op jit(solution)/shard_map/ppermute | solution.py:679
  124.8 8.8 %collective-permute-start.10 = (bf16[16,32,2560]{2,1,0:T(8,128)(2,1)S(1)}, bf16[16,32,2560]{2,1,0:T(8,128)(2,1)S(1)}, u32[]{:S(2)}, u32[]{:S(2)}) collective-permute-start(bf16[16,32,2560]{2,1,0:T(8,128)(2,1)S(1)} %get-tuple-element.99.refs_0_.refs_4_), channel_id=1, source_target_pairs={{0,1},{1,0},{2,3},{3,2},{4,5},{5,4},{6,7},{7,6},{8,9},{9,8},{10,11... | collective-permute-start | bytes 7864328 | tf_op jit(solution)/shard_map/ppermute | solution.py:679
  125.2 35.5 %collective-permute-start.12 = (bf16[8,32,1536]{2,1,0:T(8,128)(2,1)S(1)}, bf16[8,32,1536]{2,1,0:T(8,128)(2,1)S(1)}, u32[]{:S(2)}, u32[]{:S(2)}) collective-permute-start(bf16[8,32,1536]{2,1,0:T(8,128)(2,1)S(1)} %get-tuple-element.98.refs_4_.refs_0_), channel_id=1, source_target_pairs={{0,2},{1,3},{2,0},{3,1},{4,6},{5,7},{6,4},{7,5},{8,10},{9,11},{10,... | collective-permute-start | bytes 2359304 | tf_op jit(solution)/shard_map/ppermute | solution.py:679
  125.9 35.7 %collective-permute-start.13 = (bf16[8,32,1536]{2,1,0:T(8,128)(2,1)S(1)}, bf16[8,32,1536]{2,1,0:T(8,128)(2,1)}, u32[]{:S(2)}, u32[]{:S(2)}) collective-permute-start(bf16[8,32,1536]{2,1,0:T(8,128)(2,1)S(1)} %get-tuple-element.102.refs_2_), channel_id=1, source_target_pairs={{0,4},{1,5},{2,6},{3,7},{4,0},{5,1},{6,2},{7,3},{8,12},{9,13},{10,... | collective-permute-start | bytes 2359304 | tf_op jit(solution)/shard_map/ppermute | solution.py:679
  165.3 4.5 collective-permute-start.14
  165.4 7.2 %collective-permute-start.15 = (bf16[16,32,1536]{2,1,0:T(8,128)(2,1)}, bf16[16,32,1536]{2,1,0:T(8,128)(2,1)}, u32[]{:S(2)}, u32[]{:S(2)}) collective-permute-start(bf16[16,32,1536]{2,1,0:T(8,128)(2,1)} %get-tuple-element.105.refs_2_), channel_id=1, source_target_pairs={{0,1},{1,0},{2,3},{3,2},{4,5},{5,4},{6,7},{7,6},{8,9},{9,8},{10,11... | collective-permute-start | bytes 4718600 | tf_op jit(solution)/shard_map/ppermute | solution.py:679
  165.8 26.5 %collective-permute-start.16 = (bf16[512,1024]{1,0:T(8,128)(2,1)}, bf16[512,1024]{1,0:T(8,128)(2,1)}, u32[]{:S(2)}, u32[]{:S(2)}) collective-permute-start(bf16[512,1024]{1,0:T(8,128)(2,1)} %get-tuple-element.107), channel_id=1, source_target_pairs={{0,1},{1,0},{2,3},{3,2},{4,5},{5,4},{6,7},{7,6},{8,9},{9,8},{10,11... | collective-permute-start | bytes 3145736 | tf_op jit(solution)/shard_map/ppermute | solution.py:679
  165.9 26.4 %collective-permute-start.17 = (bf16[512,384]{1,0:T(8,128)(2,1)}, bf16[512,384]{1,0:T(8,128)(2,1)}, u32[]{:S(2)}, u32[]{:S(2)}) collective-permute-start(bf16[512,384]{1,0:T(8,128)(2,1)} %get-tuple-element.108), channel_id=1, source_target_pairs={{0,1},{1,0},{2,3},{3,2},{4,5},{5,4},{6,7},{7,6},{8,9},{9,8},{10,11... | collective-permute-start | bytes 1179656 | tf_op jit(solution)/shard_map/ppermute | solution.py:679
  167.2 25.2 %collective-permute-start.18 = (bf16[512,768]{1,0:T(8,128)(2,1)}, bf16[512,768]{1,0:T(8,128)(2,1)S(1)}, u32[]{:S(2)}, u32[]{:S(2)}) collective-permute-start(bf16[512,768]{1,0:T(8,128)(2,1)} %copy-done.53), channel_id=1, source_target_pairs={{0,1},{1,0},{2,3},{3,2},{4,5},{5,4},{6,7},{7,6},{8,9},{9,8},{10,11... | collective-permute-start | bytes 2359304 | tf_op jit(solution)/shard_map/ppermute | solution.py:679
  192.3 24.5 %collective-permute-start.19 = (bf16[512,768]{1,0:T(8,128)(2,1)}, bf16[512,768]{1,0:T(8,128)(2,1)}, u32[]{:S(2)}, u32[]{:S(2)}) collective-permute-start(bf16[512,768]{1,0:T(8,128)(2,1)} %get-tuple-element.115), channel_id=1, source_target_pairs={{0,1},{1,0},{2,3},{3,2},{4,5},{5,4},{6,7},{7,6},{8,9},{9,8},{10,11... | collective-permute-start | bytes 2359304 | tf_op jit(solution)/shard_map/ppermute | solution.py:679
  216.2 2.3 collective-permute-start.20
  216.5 17.0 %collective-permute-start.22 = (bf16[2048,384]{1,0:T(8,128)(2,1)}, bf16[2048,384]{1,0:T(8,128)(2,1)}, u32[]{:S(2)}, u32[]{:S(2)}) collective-permute-start(bf16[2048,384]{1,0:T(8,128)(2,1)} %get-tuple-element.122), channel_id=1, source_target_pairs={{0,1},{1,0},{2,3},{3,2},{4,5},{5,4},{6,7},{7,6},{8,9},{9,8},{10,11... | collective-permute-start | bytes 4718600 | tf_op jit(solution)/shard_map/ppermute | solution.py:679
  233.1 12.5 %collective-permute-start.21 = (bf16[384,4096]{1,0:T(8,128)(2,1)}, bf16[384,4096]{1,0:T(8,128)(2,1)}, u32[]{:S(2)}, u32[]{:S(2)}) collective-permute-start(bf16[384,4096]{1,0:T(8,128)(2,1)} %get-tuple-element.120.refs_4_.refs_2_), channel_id=1, source_target_pairs={{0,1},{1,0},{2,3},{3,2},{4,5},{5,4},{6,7},{7,6},{8,9},{9,8},{10,11... | collective-permute-start | bytes 9437192 | tf_op jit(solution)/shard_map/ppermute | solution.py:679
  244.0 50.5 %collective-permute-start.26 = (bf16[1024,1024]{1,0:T(8,128)(2,1)}, bf16[1024,1024]{1,0:T(8,128)(2,1)}, u32[]{:S(2)}, u32[]{:S(2)}) collective-permute-start(bf16[1024,1024]{1,0:T(8,128)(2,1)} %get-tuple-element.123.refs_4_), channel_id=1, source_target_pairs={{0,4},{1,5},{2,6},{3,7},{4,0},{5,1},{6,2},{7,3},{8,12},{9,13},{10,... | collective-permute-start | bytes 6291464 | tf_op jit(solution)/shard_map/ppermute | solution.py:679
  254.9 48.5 %collective-permute-start.25 = (bf16[256,4096]{1,0:T(8,128)(2,1)}, bf16[256,4096]{1,0:T(8,128)(2,1)}, u32[]{:S(2)}, u32[]{:S(2)}) collective-permute-start(bf16[256,4096]{1,0:T(8,128)(2,1)} %get-tuple-element.124.rest_0_), channel_id=1, source_target_pairs={{0,2},{1,3},{2,0},{3,1},{4,6},{5,7},{6,4},{7,5},{8,10},{9,11},{10,... | collective-permute-start | bytes 6291464 | tf_op jit(solution)/shard_map/ppermute | solution.py:679
  277.9 30.3 %collective-permute-start.24 = (bf16[3072,1024]{1,0:T(8,128)(2,1)}, bf16[3072,1024]{1,0:T(8,128)(2,1)}, u32[]{:S(2)}, u32[]{:S(2)}) collective-permute-start(bf16[3072,1024]{1,0:T(8,128)(2,1)} %get-tuple-element.125.query_delta.refs_6_.refs_8_.refs_0_.refs_1_), channel_id=1, source_target_pairs={{0,1},{1,0},{2,3},{3,2},{4,5},{5,4},{6,7},{7,6},{8,9},{9,8},{10,11... | collective-permute-start | bytes 18874376 | tf_op jit(solution)/shard_map/ppermute | solution.py:679
  294.0 7.0 %collective-permute-start.27 = (bf16[2,2,2,2,32,256]{5,4,2,1,0,3:T(8,128)(2,1)}, bf16[2,2,2,2,32,256]{5,4,2,1,0,3:T(8,128)(2,1)}, u32[]{:S(2)}, u32[]{:S(2)}) collective-permute-start(bf16[2,2,2,2,32,256]{5,4,2,1,0,3:T(8,128)(2,1)} %bitcast.92), channel_id=1, source_target_pairs={{0,1},{1,0},{2,3},{3,2},{4,5},{5,4},{6,7},{7,6},{8,9},{9,8},{10,11... | collective-permute-start | bytes 786440 | tf_op jit(solution)/shard_map/ppermute | solution.py:679
  294.4 35.1 %collective-permute-start.23 = (bf16[1536,1024]{1,0:T(8,128)(2,1)S(1)}, bf16[1536,1024]{1,0:T(8,128)(2,1)}, u32[]{:S(2)}, u32[]{:S(2)}) collective-permute-start(bf16[1536,1024]{1,0:T(8,128)(2,1)S(1)} %copy-done.2), channel_id=1, source_target_pairs={{0,1},{1,0},{2,3},{3,2},{4,5},{5,4},{6,7},{7,6},{8,9},{9,8},{10,11... | collective-permute-start | bytes 9437192 | tf_op jit(solution)/shard_map/ppermute | solution.py:679
  300.2 40.8 %collective-permute-start.31 = (bf16[4,128,1024]{2,1,0:T(8,128)(2,1)}, bf16[4,128,1024]{2,1,0:T(8,128)(2,1)}, u32[]{:S(2)}, u32[]{:S(2)}) collective-permute-start(bf16[4,128,1024]{2,1,0:T(8,128)(2,1)} %get-tuple-element.142), channel_id=1, source_target_pairs={{0,2},{1,3},{2,0},{3,1},{4,6},{5,7},{6,4},{7,5},{8,10},{9,11},{10,... | collective-permute-start | bytes 3145736 | tf_op jit(solution)/shard_map/ppermute | solution.py:679
  302.0 26.8 %collective-permute-start.28 = (bf16[2,2,2,32,256]{4,3,2,1,0:T(8,128)(2,1)S(1)}, bf16[2,2,2,32,256]{4,3,2,1,0:T(8,128)(2,1)S(1)}, u32[]{:S(2)}, u32[]{:S(2)}) collective-permute-start(bf16[2,2,2,32,256]{4,3,2,1,0:T(8,128)(2,1)S(1)} %get-tuple-element.217), channel_id=1, source_target_pairs={{0,2},{1,3},{2,0},{3,1},{4,6},{5,7},{6,4},{7,5},{8,10},{9,11},{10,... | collective-permute-start | bytes 393224 | tf_op jit(solution)/shard_map/ppermute | solution.py:679
  303.4 57.4 %slice-start = ((s8[6291456]{0:T(1024)(128)(4,1)}), s8[4194304]{0:T(1024)(128)(4,1)S(1)}, s32[]{:S(2)}) async-start(s8[6291456]{0:T(1024)(128)(4,1)} %bitcast.93), calls=%async_computation.1 | async-start | bytes 8388608
  307.6 33.5 %collective-permute-start.32 = (bf16[4,32,4096]{2,1,0:T(8,128)(2,1)}, bf16[4,32,4096]{2,1,0:T(8,128)(2,1)}, u32[]{:S(2)}, u32[]{:S(2)}) collective-permute-start(bf16[4,32,4096]{2,1,0:T(8,128)(2,1)} %get-tuple-element.143), channel_id=1, source_target_pairs={{0,4},{1,5},{2,6},{3,7},{4,0},{5,1},{6,2},{7,3},{8,12},{9,13},{10,... | collective-permute-start | bytes 3145736 | tf_op jit(solution)/shard_map/ppermute | solution.py:679
  311.6 49.2 %slice-start.1 = ((s8[6291456]{0:T(1024)(128)(4,1)}), s8[2097152]{0:T(1024)(128)(4,1)S(1)}, s32[]{:S(2)}) async-start(s8[6291456]{0:T(1024)(128)(4,1)} %bitcast.93), calls=%async_computation.2 | async-start | bytes 4194304
  325.7 30.6 %collective-permute-start.34 = (bf16[256,2048]{1,0:T(8,128)(2,1)}, bf16[256,2048]{1,0:T(8,128)(2,1)}, u32[]{:S(2)}, u32[]{:S(2)}) collective-permute-start(bf16[256,2048]{1,0:T(8,128)(2,1)} %get-tuple-element.146), channel_id=1, source_target_pairs={{0,4},{1,5},{2,6},{3,7},{4,0},{5,1},{6,2},{7,3},{8,12},{9,13},{10,... | collective-permute-start | bytes 3145736 | tf_op jit(solution)/shard_map/ppermute | solution.py:679
  328.8 27.6 %collective-permute-start.35 = (bf16[256,2048]{1,0:T(8,128)(2,1)}, bf16[256,2048]{1,0:T(8,128)(2,1)}, u32[]{:S(2)}, u32[]{:S(2)}) collective-permute-start(bf16[256,2048]{1,0:T(8,128)(2,1)} %get-tuple-element.148), channel_id=1, source_target_pairs={{0,2},{1,3},{2,0},{3,1},{4,6},{5,7},{6,4},{7,5},{8,10},{9,11},{10,... | collective-permute-start | bytes 3145736 | tf_op jit(solution)/shard_map/ppermute | solution.py:679
  343.2 29.0 %collective-permute-start.33 = (bf16[2,32,8192]{2,1,0:T(8,128)(2,1)S(1)}, bf16[2,32,8192]{2,1,0:T(8,128)(2,1)S(1)}, u32[]{:S(2)}, u32[]{:S(2)}) collective-permute-start(bf16[2,32,8192]{2,1,0:T(8,128)(2,1)S(1)} %get-tuple-element.145), channel_id=1, source_target_pairs={{0,8},{1,9},{2,10},{3,11},{4,12},{5,13},{6,14},{7,15},{8,0},{9,1},... | collective-permute-start | bytes 3145736 | tf_op jit(solution)/shard_map/ppermute | solution.py:679
  349.2 29.6 %collective-permute-start.29 = (bf16[256,2048]{1,0:T(8,128)(2,1)S(1)}, bf16[256,2048]{1,0:T(8,128)(2,1)S(1)}, u32[]{:S(2)}, u32[]{:S(2)}) collective-permute-start(bf16[256,2048]{1,0:T(8,128)(2,1)S(1)} %get-tuple-element.139), channel_id=1, source_target_pairs={{0,4},{1,5},{2,6},{3,7},{4,0},{5,1},{6,2},{7,3},{8,12},{9,13},{10,... | collective-permute-start | bytes 3145736 | tf_op jit(solution)/shard_map/ppermute | solution.py:679
  349.6 29.1 %collective-permute-start.30 = (bf16[256,2048]{1,0:T(8,128)(2,1)}, bf16[256,2048]{1,0:T(8,128)(2,1)S(1)}, u32[]{:S(2)}, u32[]{:S(2)}) collective-permute-start(bf16[256,2048]{1,0:T(8,128)(2,1)} %get-tuple-element.141), channel_id=1, source_target_pairs={{0,2},{1,3},{2,0},{3,1},{4,6},{5,7},{6,4},{7,5},{8,10},{9,11},{10,... | collective-permute-start | bytes 3145736 | tf_op jit(solution)/shard_map/ppermute | solution.py:679
  359.3 29.5 %collective-permute-start.38 = (bf16[4,32,2048]{2,1,0:T(8,128)(2,1)}, bf16[4,32,2048]{2,1,0:T(8,128)(2,1)S(1)}, u32[]{:S(2)}, u32[]{:S(2)}) collective-permute-start(bf16[4,32,2048]{2,1,0:T(8,128)(2,1)} %get-tuple-element.156), channel_id=1, source_target_pairs={{0,2},{1,3},{2,0},{3,1},{4,6},{5,7},{6,4},{7,5},{8,10},{9,11},{10,... | collective-permute-start | bytes 1572872 | tf_op jit(solution)/shard_map/ppermute | solution.py:679
  360.0 29.9 %collective-permute-start.39 = (bf16[4,32,2048]{2,1,0:T(8,128)(2,1)}, bf16[4,32,2048]{2,1,0:T(8,128)(2,1)S(1)}, u32[]{:S(2)}, u32[]{:S(2)}) collective-permute-start(bf16[4,32,2048]{2,1,0:T(8,128)(2,1)} %get-tuple-element.157), channel_id=1, source_target_pairs={{0,4},{1,5},{2,6},{3,7},{4,0},{5,1},{6,2},{7,3},{8,12},{9,13},{10,... | collective-permute-start | bytes 1572872 | tf_op jit(solution)/shard_map/ppermute | solution.py:679
  375.2 25.3 %collective-permute-start.44 = (bf16[1,32,8192]{2,1,0:T(8,128)(2,1)S(1)}, bf16[1,32,8192]{2,1,0:T(8,128)(2,1)S(1)}, u32[]{:S(2)}, u32[]{:S(2)}) collective-permute-start(bf16[1,32,8192]{2,1,0:T(8,128)(2,1)S(1)} %get-tuple-element.166), channel_id=1, source_target_pairs={{0,16},{1,17},{2,18},{3,19},{4,20},{5,21},{6,22},{7,23},{8,24},{9,... | collective-permute-start | bytes 1572872 | tf_op jit(solution)/shard_map/ppermute | solution.py:679
  379.8 20.8 %collective-permute-start.36 = (bf16[4,32,2048]{2,1,0:T(8,128)(2,1)S(1)}, bf16[4,32,2048]{2,1,0:T(8,128)(2,1)S(1)}, u32[]{:S(2)}, u32[]{:S(2)}) collective-permute-start(bf16[4,32,2048]{2,1,0:T(8,128)(2,1)S(1)} %get-tuple-element.154), channel_id=1, source_target_pairs={{0,2},{1,3},{2,0},{3,1},{4,6},{5,7},{6,4},{7,5},{8,10},{9,11},{10,... | collective-permute-start | bytes 1572872 | tf_op jit(solution)/shard_map/ppermute | solution.py:679
  380.6 21.0 %collective-permute-start.37 = (bf16[4,32,2304]{2,1,0:T(8,128)(2,1)S(1)}, bf16[4,32,2304]{2,1,0:T(8,128)(2,1)S(1)}, u32[]{:S(2)}, u32[]{:S(2)}) collective-permute-start(bf16[4,32,2304]{2,1,0:T(8,128)(2,1)S(1)} %get-tuple-element.155), channel_id=1, source_target_pairs={{0,4},{1,5},{2,6},{3,7},{4,0},{5,1},{6,2},{7,3},{8,12},{9,13},{10,... | collective-permute-start | bytes 1769480 | tf_op jit(solution)/shard_map/ppermute | solution.py:679
  392.2 19.6 %collective-permute-start.41 = (bf16[2,32,4096]{2,1,0:T(8,128)(2,1)S(1)}, bf16[2,32,4096]{2,1,0:T(8,128)(2,1)S(1)}, u32[]{:S(2)}, u32[]{:S(2)}) collective-permute-start(bf16[2,32,4096]{2,1,0:T(8,128)(2,1)S(1)} %get-tuple-element.161), channel_id=1, source_target_pairs={{0,8},{1,9},{2,10},{3,11},{4,12},{5,13},{6,14},{7,15},{8,0},{9,1},... | collective-permute-start | bytes 1572872 | tf_op jit(solution)/shard_map/ppermute | solution.py:679
  402.4 26.8 %collective-permute-start.40 = (bf16[2,32,4352]{2,1,0:T(8,128)(2,1)S(1)}, bf16[2,32,4352]{2,1,0:T(8,128)(2,1)S(1)}, u32[]{:S(2)}, u32[]{:S(2)}) collective-permute-start(bf16[2,32,4352]{2,1,0:T(8,128)(2,1)S(1)} %get-tuple-element.160), channel_id=1, source_target_pairs={{0,8},{1,9},{2,10},{3,11},{4,12},{5,13},{6,14},{7,15},{8,0},{9,1},... | collective-permute-start | bytes 1671176 | tf_op jit(solution)/shard_map/ppermute | solution.py:679
  412.4 17.6 %collective-permute-start.43 = (bf16[1,32,4096]{2,1,0:T(8,128)(2,1)S(1)}, bf16[1,32,4096]{2,1,0:T(8,128)(2,1)}, u32[]{:S(2)}, u32[]{:S(2)}) collective-permute-start(bf16[1,32,4096]{2,1,0:T(8,128)(2,1)S(1)} %get-tuple-element.165), channel_id=1, source_target_pairs={{0,16},{1,17},{2,18},{3,19},{4,20},{5,21},{6,22},{7,23},{8,24},{9,... | collective-permute-start | bytes 786440 | tf_op jit(solution)/shard_map/ppermute | solution.py:679
  429.9 14.5 %collective-permute-start.42 = (bf16[1,32,4352]{2,1,0:T(8,128)(2,1)S(1)}, bf16[1,32,4352]{2,1,0:T(8,128)(2,1)S(1)}, u32[]{:S(2)}, u32[]{:S(2)}) collective-permute-start(bf16[1,32,4352]{2,1,0:T(8,128)(2,1)S(1)} %get-tuple-element.164), channel_id=1, source_target_pairs={{0,16},{1,17},{2,18},{3,19},{4,20},{5,21},{6,22},{7,23},{8,24},{9,... | collective-permute-start | bytes 835592 | tf_op jit(solution)/shard_map/ppermute | solution.py:679
  (74 other events, 557.1 us)
Sparse Core Ops, SparseCore 0:
  51.5 146.2 all-gather.2

commit v6 on v5

--- a/solution.py
+++ b/solution.py
@@ -995,7 +995,7 @@
         cotangent,
         vectors,
         ffn_out.shape[0],
-        after=(memory_turned[1], target_turned[1], self_turned[1]),
+        after=(memory_turned[1], target_turned[1]),
     )
     hidden_other, out_grad_other = exchange(hidden_send, 0), exchange(out_grad, 0)
     pre_grad, ffn_bias_grad, second_grad, cross_branch, second_sums = ffn_backward(

time: 459 us -> 454 us (0.989)
  local copies, waits for them, and re-layouts: 50.5 us -> 45.6 us
    unnamed x157 -> x147, local copies, waits for them, and re-layouts: 42.3 us -> 37.3 us
where the time goes in v6:
time: 454 us; the launch traced here: 449 us
  Pallas kernels  154 us (34%)
  waiting for transfers between devices  154 us (34%)
  starting transfers between devices  57 us (13%)
  local copies, waits for them, and re-layouts  45.6 us (10%)
  matrix products  17 us (4%)
  between operations  15.2 us (3%)
  other arithmetic  6.06 us (1%)
    ppermute x45, waiting for transfers between devices, exchange(): return lax.ppermute(values, AXES, [(i, i ^ 1 << bit) for i in range(count)])  148 us
    ppermute x45, starting transfers between devices, exchange(): return lax.ppermute(values, AXES, [(i, i ^ 1 << bit) for i in range(count)])  57 us
    pallas_call x4, Pallas kernels, products(): pl.pallas_call(functools.partial(product_kernel, spans=spans, n_left=len(...  37.5 us
    unnamed x147, local copies, waits for them, and re-layouts  37.3 us
    pallas_call x1, Pallas kernels, cross_backward(): pl.pallas_call(functools.partial(cross_backward_kernel, extra=len(after))...  18.6 us
    dot_general x5, matrix products, matmul(): return jnp.dot(first, second, preferred_element_type=jnp.float32)  17 us
    pallas_call x10, Pallas kernels, advance(): pl.pallas_call(functools.partial(stage_kernel, groups=[(b, len(g)) for b,...  16.1 us
    pallas_call x1, Pallas kernels, ffn_forward(): pl.pallas_call(functools.partial(ffn_forward_kernel, rows=rows, extra=len...  14.9 us
  transfers between devices with their start and end apart: 46, of which 22 were waited for; matrix products, arithmetic and copies ran while one was open for 6% of the time, Pallas kernels for 34%

profile of v6, /device:TPU:0, one launch (start us, length us, event | category | flops | bytes accessed | tf_op | source)
XLA Modules:
  0.0 448.5 jit_solution(5437830833536230251)
XLA Ops:
  10.7 4.1 collective-permute-start
  19.0 10.9 %collective-permute-done.refs_1_ = bf16[1,32,5248]{2,1,0:T(8,128)(2,1)S(1)} collective-permute-done((bf16[1,32,5248]{2,1,0:T(8,128)(2,1)S(1)}, bf16[1,32,5248]{2,1,0:T(8,128)(2,1)S(1)}, u32[]{:S(2)}, u32[]{:S(2)}) %collective-permute-start) | collective-permute-done | bytes 335904 | tf_op jit(solution)/shard_map/ppermute | solution.py:679
  30.7 3.4 collective-permute-start.2
  34.2 15.2 %collective-permute-done.2.refs_1_ = bf16[1,32,3072]{2,1,0:T(8,128)(2,1)S(1)} collective-permute-done((bf16[1,32,3072]{2,1,0:T(8,128)(2,1)S(1)}, bf16[1,32,3072]{2,1,0:T(8,128)(2,1)S(1)}, u32[]{:S(2)}, u32[]{:S(2)}) %collective-permute-start.2) | collective-permute-done | bytes 196640 | tf_op jit(solution)/shard_map/ppermute | solution.py:679
  54.3 3.4 collective-permute-start.5
  57.7 11.6 %collective-permute-done.5.refs_1_ = bf16[2,32,3072]{2,1,0:T(8,128)(2,1)S(1)} collective-permute-done((bf16[2,32,3072]{2,1,0:T(8,128)(2,1)S(1)}, bf16[2,32,3072]{2,1,0:T(8,128)(2,1)S(1)}, u32[]{:S(2)}, u32[]{:S(2)}) %collective-permute-start.5) | collective-permute-done | bytes 393248 | tf_op jit(solution)/shard_map/ppermute | solution.py:679
  69.3 3.6 collective-permute-done.3.refs_1_
  77.1 47.0 %collective-permute-done.8.refs_1_ = bf16[4,32,1536]{2,1,0:T(8,128)(2,1)S(1)} collective-permute-done((bf16[4,32,1536]{2,1,0:T(8,128)(2,1)S(1)}, bf16[4,32,1536]{2,1,0:T(8,128)(2,1)S(1)}, u32[]{:S(2)}, u32[]{:S(2)}) %collective-permute-start.8) | collective-permute-done | bytes 393248 | tf_op jit(solution)/shard_map/ppermute | solution.py:679
  127.2 6.3 %collective-permute-done.10.refs_1_ = bf16[16,32,2560]{2,1,0:T(8,128)(2,1)S(1)} collective-permute-done((bf16[16,32,2560]{2,1,0:T(8,128)(2,1)S(1)}, bf16[16,32,2560]{2,1,0:T(8,128)(2,1)S(1)}, u32[]{:S(2)}, u32[]{:S(2)}) %collective-permute-start.10) | collective-permute-done | bytes 2621472 | tf_op jit(solution)/shard_map/ppermute | solution.py:679
  133.6 5.1 %shard_map.264.w_query.w_self.refs_3_.refs_4_.refs_5_ = bf16[1024,5248]{1,0:T(8,128)(2,1)S(1)} custom-call(bf16[16,32,2560]{2,1,0:T(8,128)(2,1)S(1)} %get-tuple-element.99.refs_0_.refs_4_, bf16[16,32,2560]{2,1,0:T(8,128)(2,1)S(1)} %collective-permute-done.10.refs_1_, bf16[16,32,2688]{2,1,0:T(8,128)(2,1)S(1)} %get-tuple-element.100.refs_2_, ...), custom_call_target="tpu_custom_call" | custom-call | bytes 214958080 | tf_op jit(solution)/shard_map/pallas_call | solution.py:775
  138.7 4.0 copy-done
  142.9 5.6 %fusion.7.qkv = bf16[384,3072]{1,0:T(8,128)(2,1)S(1)} fusion(bf16[384,1024]{1,0:T(8,128)(2,1)S(1)} %copy-done.32, bf16[1024,5248]{1,0:T(8,128)(2,1)} %copy-done, f32[3072]{0:T(1024)S(1)} %pad_maximum_fusion), kind=kOutput, calls=%fused_computation.7 | convolution fusion | flops 2418278400 | bytes 9449472 | tf_op jit(solution)/shard_map/dot_general | solution.py:33
  148.6 3.5 shard_map.265
  152.1 2.7 fusion.35
  158.0 2.9 add_convert_fusion.2.refs_4_.q
  163.0 2.5 shard_map.267
  167.5 2.4 collective-permute-done.14.refs_1_
  171.8 3.5 shard_map.268.weight.refs_2_.refs_3_
  175.3 4.7 %fusion.4.pairs = bf16[1024,2048]{1,0:T(8,128)(2,1)S(1)} fusion(f32[2048]{0:T(1024)S(1)} %concatenate.22, bf16[1024,1024]{1,0:T(8,128)(2,1)S(1)} %copy-done.11, bf16[1024,3072]{1,0:T(8,128)(2,1)S(1)} %shard_map.268.weight.refs_2_.refs_3_), kind=kOutput, calls=%fused_computation.4 | convolution fusion | flops 4299161600 | bytes 10493952 | tf_op jit(solution)/shard_map/dot_general | solution.py:33
  180.1 5.7 %shard_map.269 = (bf16[384,1024]{1,0:T(8,128)(2,1)S(1)}, f32[3,8,1,256]{3,2,1,0:T(1,128)S(1)}) custom-call(s32[2,3]{1,0:T(2,128)S(1)} %pad_add_fusion.bound, bf16[384,1024]{1,0:T(8,128)(2,1)S(1)} %add_convert_fusion.2.refs_4_.q, bf16[1024,2048]{1,0:T(8,128)(2,1)S(1)} %fusion.4.pairs), custom_call_target="tpu_custom_call" | custom-call | flops 80000000000 | bytes 83886080 | tf_op jit(solution)/shard_map/pallas_call | solution.py:188
  190.1 2.2 collective-permute-start.18
  192.3 5.5 %all-gather.3.cloned.1.call-done = bf16[8192,1024]{1,0:T(8,128)(2,1)} async-done(((bf16[256,1024]{1,0:T(8,128)(2,1)}), bf16[8192,1024]{1,0:T(8,128)(2,1)}) %all-gather.3.cloned.1.call-update) | async-done | bytes 16777232 | tf_op jit(solution)/shard_map/all_gather | solution.py:951
  199.0 14.9 %shard_map.271 = (bf16[2048,384]{1,0:T(8,128)(2,1)S(1)}, bf16[2048,384]{1,0:T(8,128)(2,1)}, bf16[384,4096]{1,0:T(8,128)(2,1)S(1)}, bf16[384,1024]{1,0:T(8,128)(2...) custom-call(s32[1]{0:T(128)} %bitcast.core, ...), custom_call_target="tpu_custom_call" | custom-call | flops 160000000000 | bytes 272629760 | tf_op jit(solution)/shard_map/pallas_call | solution.py:478
  217.3 12.7 %shard_map.273 = (bf16[384,4096]{1,0:T(8,128)(2,1)}, f32[1,4096]{1,0:T(1,128)S(1)}, f32[384,1024]{1,0:T(8,128)S(1)}, bf16[384,1024]{1,0:T(8,128)(2,1)S(1)}, f32[8,1024]{1,0:T(8,128)S(1)}) custom-call(bf16[32,256,1024]{2,1,0:T(8,128)(2,1)} %bitcast.145, bf16[32,256,1024]{2,1,0:T(8,128)(2,1)} %bitcast.146, bf16[384,4096]{1,0:T(8,128)(2,1)S(1)} %get-tuple-element.111.slope, ...), custom_call_target="tpu_custom_call" | custom-call | flops 140000002048 | bytes 272629760 | tf_op jit(solution)/shard_map/pallas_call | solution.py:542
  235.3 7.9 %shard_map.274 = (bf16[1024,1024]{1,0:T(8,128)(2,1)}, bf16[1024,1024]{1,0:T(8,128)(2,1)}) custom-call(s32[5]{0:T(128)S(1)} %shift-right-arithmetic_and_fusion.ids, bf16[2048,384]{1,0:T(8,128)(2,1)S(1)} %copy-done.56, bf16[2048,384]{1,0:T(8,128)(2,1)} %collective-permute-done.21.refs_1_, bf16[384,1024]{1,0:T(8,128)(2,1)S(1)} %copy-done.50, ...), custom_call_target="tpu_custom_call" | custom-call | flops 20132659200 | bytes 209715200 | tf_op jit(solution)/shard_map/pallas_call | solution.py:656
  244.8 8.0 %shard_map.275 = (bf16[256,4096]{1,0:T(8,128)(2,1)S(1)}, bf16[256,4096]{1,0:T(8,128)(2,1)}) custom-call(s32[5]{0:T(128)S(1)} %shift-right-arithmetic_and_fusion.ids, bf16[512,768]{1,0:T(8,128)(2,1)S(1)} %copy-done.47, bf16[512,768]{1,0:T(8,128)(2,1)} %collective-permute-done.18.rest_0_.refs_1_.refs_5_, bf16[384,4096]{1,0:T(8,128)(2,1)} %get-tuple-element.119.refs_4_.refs_2_, ...), custom_call_target="tpu_custom_call" | custom-call | flops 20132659200 | bytes 209715200 | tf_op jit(solution)/shard_map/pallas_call | solution.py:656
  255.4 18.6 %shard_map.276 = (bf16[3072,1024]{1,0:T(8,128)(2,1)}, f32[8,1024]{1,0:T(8,128)}) custom-call(s32[2,3]{1,0:T(2,128)} %copy-done.44, bf16[384,1024]{1,0:T(8,128)(2,1)} %copy-done.27, bf16[1024,2048]{1,0:T(8,128)(2,1)} %copy-done.54, f32[3,8,1,256]{3,2,1,0:T(1,128)} %copy-done.60, bf16[384,1024]{1,0:T(8,128)(2,1)} %copy-done.59, bf16[1024,3072]{1,0:T(8,128)(2,1)} %copy-done.1, ...), custom_call_target="tpu_custom_call" | custom-call | flops 160000000000 | bytes 125829120 | tf_op jit(solution)/shard_map/pallas_call | solution.py:214
  274.0 4.1 collective-permute-start.24
  278.1 13.4 %shard_map.277 = (bf16[1536,1024]{1,0:T(8,128)(2,1)}, f32[8,1024]{1,0:T(8,128)S(1)}, f32[384,1024]{1,0:T(8,128)S(1)}) custom-call(s32[3]{0:T(128)S(1)} %bitcast.127, bf16[384,3072]{1,0:T(8,128)(2,1)} %copy-done.53, f32[3,8,1,256]{3,2,1,0:T(1,128)S(1)} %get-tuple-element.110.summary, f32[384,1024]{1,0:T(8,128)S(1)} %copy-done.58, ...), custom_call_target="tpu_custom_call" | custom-call | flops 60000002048 | bytes 125829120 | tf_op jit(solution)/shard_map/pallas_call | solution.py:330
  297.3 3.1 shard_map.279
  303.6 3.1 shard_map.280
  310.6 13.3 %shard_map.281 = (bf16[256,2048]{1,0:T(8,128)(2,1)S(1)}, bf16[256,2048]{1,0:T(8,128)(2,1)}, bf16[256,2048]{1,0:T(8,128)(2,1)}, bf16[256,2048]{1,0:T(8,128)(2,1)}) custom-call(s32[5]{0:T(128)S(1)} %copy-done.38, bf16[512,1024]{1,0:T(8,128)(2,1)} %copy-done.18, bf16[512,768]{1,0:T(8,128)(2,1)S(1)} %copy-done.25, bf16[512,768]{1,0:T(8,128)(2,1)S(1)} %copy-done.48, ...), custom_call_target="tpu_custom_call" | custom-call | flops 31317469184 | bytes 209715200 | tf_op jit(solution)/shard_map/pallas_call | solution.py:656
  331.0 8.3 %shard_map.282 = (bf16[256,2048]{1,0:T(8,128)(2,1)S(1)}, bf16[256,2048]{1,0:T(8,128)(2,1)S(1)}, bf16[256,2048]{1,0:T(8,128)(2,1)S(1)}, bf16[256,2048]{1,0:T(8,128)(2,1)}) custom-call(s32[5]{0:T(128)S(1)} %copy-done.38, bf16[512,384]{1,0:T(8,128)(2,1)S(1)} %copy-done.34, bf16[512,768]{1,0:T(8,128)(2,1)S(1)} %copy-done.26, ...), custom_call_target="tpu_custom_call" | custom-call | flops 20132659200 | bytes 209715200 | tf_op jit(solution)/shard_map/pallas_call | solution.py:656
  341.6 3.4 collective-permute-start.33
  346.2 10.5 %collective-permute-done.34 = bf16[256,2048]{1,0:T(8,128)(2,1)} collective-permute-done((bf16[256,2048]{1,0:T(8,128)(2,1)}, bf16[256,2048]{1,0:T(8,128)(2,1)}, u32[]{:S(2)}, u32[]{:S(2)}) %collective-permute-start.34) | collective-permute-done | bytes 1048608 | tf_op jit(solution)/shard_map/ppermute | solution.py:679
  356.7 2.9 shard_map.284
  360.6 2.8 copy-done.4
  363.4 6.6 %shard_map.285.refs_2_ = f32[1024,1024]{1,0:T(8,128)} custom-call(bf16[3072,1024]{1,0:T(8,128)(2,1)S(1)} %copy-done.4, bf16[3072,1024]{1,0:T(8,128)(2,1)S(1)} %copy-done.4, bf16[1024,3072]{1,0:T(8,128)(2,1)S(1)} %bitcast.94, bf16[1024,3072]{1,0:T(8,128)(2,1)S(1)} %bitcast.94, bf16[4,32,2048]{2,1,0:T(8,128)(2,1)S(1)} %get-tuple-element.149.refs_4_, ...), custom_call_target="tpu_custom_call" | custom-call | bytes 10485 | tf_op jit(solution)/shard_map/pallas_call | solution.py:897
  372.9 2.9 collective-permute-start.44
  375.9 3.2 collective-permute-done.29
  381.4 6.6 %shard_map.288.refs_4_ = f32[384,1024]{1,0:T(8,128)} custom-call(bf16[1536,1024]{1,0:T(8,128)(2,1)S(1)} %copy-done.3, bf16[1536,1024]{1,0:T(8,128)(2,1)S(1)} %copy-done.3, bf16[1536,1024]{1,0:T(8,128)(2,1)S(1)} %copy-done.3, bf16[1024,5248]{1,0:T(8,128)(2,1)} %copy-done, bf16[1024,5248]{1,0:T(8,128)(2,1)} %copy-done, bf16[1024,5248]{1,0:T(8,128)(2,1)} %copy-done, ...), custom_call_target="tpu_custom_call" | custom-call | bytes 10485 | tf_op jit(solution)/shard_map/pallas_call | solution.py:897
  392.5 4.4 collective-permute-start.41
  398.2 3.2 collective-permute-done.37
  402.2 2.7 collective-permute-start.40
  404.9 7.1 %collective-permute-done.41 = bf16[2,32,4096]{2,1,0:T(8,128)(2,1)S(1)} collective-permute-done((bf16[2,32,4096]{2,1,0:T(8,128)(2,1)S(1)}, bf16[2,32,4096]{2,1,0:T(8,128)(2,1)S(1)}, u32[]{:S(2)}, u32[]{:S(2)}) %collective-permute-start.41) | collective-permute-done | bytes 524320 | tf_op jit(solution)/shard_map/ppermute | solution.py:679
  415.1 7.1 %collective-permute-done.40 = bf16[2,32,4352]{2,1,0:T(8,128)(2,1)S(1)} collective-permute-done((bf16[2,32,4352]{2,1,0:T(8,128)(2,1)S(1)}, bf16[2,32,4352]{2,1,0:T(8,128)(2,1)S(1)}, u32[]{:S(2)}, u32[]{:S(2)}) %collective-permute-start.40) | collective-permute-done | bytes 557088 | tf_op jit(solution)/shard_map/ppermute | solution.py:679
  422.8 3.1 collective-permute-start.42
  428.4 9.6 %collective-permute-done.42 = bf16[1,32,4352]{2,1,0:T(8,128)(2,1)S(1)} collective-permute-done((bf16[1,32,4352]{2,1,0:T(8,128)(2,1)S(1)}, bf16[1,32,4352]{2,1,0:T(8,128)(2,1)S(1)}, u32[]{:S(2)}, u32[]{:S(2)}) %collective-permute-start.42) | collective-permute-done | bytes 278560 | tf_op jit(solution)/shard_map/ppermute | solution.py:679
  (287 shorter events, 93.9 us)
Async XLA Ops:
  7.2 190.6 %all-gather.3.cloned.1.call-start = ((), (), s32[]{:S(2)}) async-start(), calls=%async_computation | async-start | bytes 17301504 | tf_op jit(solution)/shard_map/all_gather | solution.py:951
  10.7 19.2 %collective-permute-start = (bf16[1,32,5248]{2,1,0:T(8,128)(2,1)S(1)}, bf16[1,32,5248]{2,1,0:T(8,128)(2,1)S(1)}, u32[]{:S(2)}, u32[]{:S(2)}) collective-permute-start(bf16[1,32,5248]{2,1,0:T(8,128)(2,1)S(1)} %maximum_bitcast_fusion.refs_0_), channel_id=1, source_target_pairs={{0,16},{1,17},{2,18},{3,19},{4,20},{5,21},{6,22},{7,23},{8,24},{9,... | collective-permute-start | bytes 1007624 | tf_op jit(solution)/shard_map/ppermute | solution.py:679
  29.9 20.5 %collective-permute-start.1 = (bf16[2,32,5248]{2,1,0:T(8,128)(2,1)S(1)}, bf16[2,32,5248]{2,1,0:T(8,128)(2,1)S(1)}, u32[]{:S(2)}, u32[]{:S(2)}) collective-permute-start(bf16[2,32,5248]{2,1,0:T(8,128)(2,1)S(1)} %shard_map.257.refs_2_.refs_0_), channel_id=1, source_target_pairs={{0,8},{1,9},{2,10},{3,11},{4,12},{5,13},{6,14},{7,15},{8,0},{9,1},... | collective-permute-start | bytes 2015240 | tf_op jit(solution)/shard_map/ppermute | solution.py:679
  30.7 18.7 %collective-permute-start.2 = (bf16[1,32,3072]{2,1,0:T(8,128)(2,1)S(1)}, bf16[1,32,3072]{2,1,0:T(8,128)(2,1)S(1)}, u32[]{:S(2)}, u32[]{:S(2)}) collective-permute-start(bf16[1,32,3072]{2,1,0:T(8,128)(2,1)S(1)} %maximum_bitcast_fusion.1.refs_0_), channel_id=1, source_target_pairs={{0,16},{1,17},{2,18},{3,19},{4,20},{5,21},{6,22},{7,23},{8,24},{9,... | collective-permute-start | bytes 589832 | tf_op jit(solution)/shard_map/ppermute | solution.py:679
  51.4 21.4 %collective-permute-start.4 = (bf16[4,32,2688]{2,1,0:T(8,128)(2,1)S(1)}, bf16[4,32,2688]{2,1,0:T(8,128)(2,1)S(1)}, u32[]{:S(2)}, u32[]{:S(2)}) collective-permute-start(bf16[4,32,2688]{2,1,0:T(8,128)(2,1)S(1)} %get-tuple-element.93.refs_2_), channel_id=1, source_target_pairs={{0,2},{1,3},{2,0},{3,1},{4,6},{5,7},{6,4},{7,5},{8,10},{9,11},{10,... | collective-permute-start | bytes 2064392 | tf_op jit(solution)/shard_map/ppermute | solution.py:679
  52.8 20.1 %collective-permute-start.3 = (bf16[4,32,2560]{2,1,0:T(8,128)(2,1)S(1)}, bf16[4,32,2560]{2,1,0:T(8,128)(2,1)S(1)}, u32[]{:S(2)}, u32[]{:S(2)}) collective-permute-start(bf16[4,32,2560]{2,1,0:T(8,128)(2,1)S(1)} %get-tuple-element.92.refs_2_.refs_0_), channel_id=1, source_target_pairs={{0,4},{1,5},{2,6},{3,7},{4,0},{5,1},{6,2},{7,3},{8,12},{9,13},{10,... | collective-permute-start | bytes 1966088 | tf_op jit(solution)/shard_map/ppermute | solution.py:679
  54.3 15.0 %collective-permute-start.5 = (bf16[2,32,3072]{2,1,0:T(8,128)(2,1)S(1)}, bf16[2,32,3072]{2,1,0:T(8,128)(2,1)S(1)}, u32[]{:S(2)}, u32[]{:S(2)}) collective-permute-start(bf16[2,32,3072]{2,1,0:T(8,128)(2,1)S(1)} %shard_map.258.refs_2_.refs_0_), channel_id=1, source_target_pairs={{0,8},{1,9},{2,10},{3,11},{4,12},{5,13},{6,14},{7,15},{8,0},{9,1},... | collective-permute-start | bytes 1179656 | tf_op jit(solution)/shard_map/ppermute | solution.py:679
  73.0 51.3 %collective-permute-start.7 = (bf16[8,32,2688]{2,1,0:T(8,128)(2,1)S(1)}, bf16[8,32,2688]{2,1,0:T(8,128)(2,1)S(1)}, u32[]{:S(2)}, u32[]{:S(2)}) collective-permute-start(bf16[8,32,2688]{2,1,0:T(8,128)(2,1)S(1)} %get-tuple-element.96.refs_2_), channel_id=1, source_target_pairs={{0,4},{1,5},{2,6},{3,7},{4,0},{5,1},{6,2},{7,3},{8,12},{9,13},{10,... | collective-permute-start | bytes 4128776 | tf_op jit(solution)/shard_map/ppermute | solution.py:679
  74.9 49.4 %collective-permute-start.6 = (bf16[8,32,2560]{2,1,0:T(8,128)(2,1)S(1)}, bf16[8,32,2560]{2,1,0:T(8,128)(2,1)S(1)}, u32[]{:S(2)}, u32[]{:S(2)}) collective-permute-start(bf16[8,32,2560]{2,1,0:T(8,128)(2,1)S(1)} %get-tuple-element.95.refs_4_.refs_0_), channel_id=1, source_target_pairs={{0,2},{1,3},{2,0},{3,1},{4,6},{5,7},{6,4},{7,5},{8,10},{9,11},{10,... | collective-permute-start | bytes 3932168 | tf_op jit(solution)/shard_map/ppermute | solution.py:679
  75.5 48.7 %collective-permute-start.8 = (bf16[4,32,1536]{2,1,0:T(8,128)(2,1)S(1)}, bf16[4,32,1536]{2,1,0:T(8,128)(2,1)S(1)}, u32[]{:S(2)}, u32[]{:S(2)}) collective-permute-start(bf16[4,32,1536]{2,1,0:T(8,128)(2,1)S(1)} %get-tuple-element.94.refs_4_.refs_0_), channel_id=1, source_target_pairs={{0,4},{1,5},{2,6},{3,7},{4,0},{5,1},{6,2},{7,3},{8,12},{9,13},{10,... | collective-permute-start | bytes 1179656 | tf_op jit(solution)/shard_map/ppermute | solution.py:679
  75.8 48.3 %collective-permute-start.9 = (bf16[4,32,1536]{2,1,0:T(8,128)(2,1)S(1)}, bf16[4,32,1536]{2,1,0:T(8,128)(2,1)S(1)}, u32[]{:S(2)}, u32[]{:S(2)}) collective-permute-start(bf16[4,32,1536]{2,1,0:T(8,128)(2,1)S(1)} %get-tuple-element.97.refs_2_), channel_id=1, source_target_pairs={{0,2},{1,3},{2,0},{3,1},{4,6},{5,7},{6,4},{7,5},{8,10},{9,11},{10,... | collective-permute-start | bytes 1179656 | tf_op jit(solution)/shard_map/ppermute | solution.py:679
  124.7 8.9 %collective-permute-start.11 = (bf16[16,32,2688]{2,1,0:T(8,128)(2,1)S(1)}, bf16[16,32,2688]{2,1,0:T(8,128)(2,1)S(1)}, u32[]{:S(2)}, u32[]{:S(2)}) collective-permute-start(bf16[16,32,2688]{2,1,0:T(8,128)(2,1)S(1)} %get-tuple-element.100.refs_2_), channel_id=1, source_target_pairs={{0,1},{1,0},{2,3},{3,2},{4,5},{5,4},{6,7},{7,6},{8,9},{9,8},{10,11... | collective-permute-start | bytes 8257544 | tf_op jit(solution)/shard_map/ppermute | solution.py:679
  124.8 8.8 %collective-permute-start.10 = (bf16[16,32,2560]{2,1,0:T(8,128)(2,1)S(1)}, bf16[16,32,2560]{2,1,0:T(8,128)(2,1)S(1)}, u32[]{:S(2)}, u32[]{:S(2)}) collective-permute-start(bf16[16,32,2560]{2,1,0:T(8,128)(2,1)S(1)} %get-tuple-element.99.refs_0_.refs_4_), channel_id=1, source_target_pairs={{0,1},{1,0},{2,3},{3,2},{4,5},{5,4},{6,7},{7,6},{8,9},{9,8},{10,11... | collective-permute-start | bytes 7864328 | tf_op jit(solution)/shard_map/ppermute | solution.py:679
  125.2 35.7 %collective-permute-start.12 = (bf16[8,32,1536]{2,1,0:T(8,128)(2,1)S(1)}, bf16[8,32,1536]{2,1,0:T(8,128)(2,1)S(1)}, u32[]{:S(2)}, u32[]{:S(2)}) collective-permute-start(bf16[8,32,1536]{2,1,0:T(8,128)(2,1)S(1)} %get-tuple-element.98.refs_4_.refs_0_), channel_id=1, source_target_pairs={{0,2},{1,3},{2,0},{3,1},{4,6},{5,7},{6,4},{7,5},{8,10},{9,11},{10,... | collective-permute-start | bytes 2359304 | tf_op jit(solution)/shard_map/ppermute | solution.py:679
  125.9 36.0 %collective-permute-start.13 = (bf16[8,32,1536]{2,1,0:T(8,128)(2,1)S(1)}, bf16[8,32,1536]{2,1,0:T(8,128)(2,1)}, u32[]{:S(2)}, u32[]{:S(2)}) collective-permute-start(bf16[8,32,1536]{2,1,0:T(8,128)(2,1)S(1)} %get-tuple-element.102.refs_2_), channel_id=1, source_target_pairs={{0,4},{1,5},{2,6},{3,7},{4,0},{5,1},{6,2},{7,3},{8,12},{9,13},{10,... | collective-permute-start | bytes 2359304 | tf_op jit(solution)/shard_map/ppermute | solution.py:679
  165.5 4.4 collective-permute-start.14
  165.7 6.1 %collective-permute-start.15 = (bf16[16,32,1536]{2,1,0:T(8,128)(2,1)}, bf16[16,32,1536]{2,1,0:T(8,128)(2,1)}, u32[]{:S(2)}, u32[]{:S(2)}) collective-permute-start(bf16[16,32,1536]{2,1,0:T(8,128)(2,1)} %get-tuple-element.105.refs_2_), channel_id=1, source_target_pairs={{0,1},{1,0},{2,3},{3,2},{4,5},{5,4},{6,7},{7,6},{8,9},{9,8},{10,11... | collective-permute-start | bytes 4718600 | tf_op jit(solution)/shard_map/ppermute | solution.py:679
  166.0 26.2 %collective-permute-start.16 = (bf16[512,1024]{1,0:T(8,128)(2,1)}, bf16[512,1024]{1,0:T(8,128)(2,1)}, u32[]{:S(2)}, u32[]{:S(2)}) collective-permute-start(bf16[512,1024]{1,0:T(8,128)(2,1)} %get-tuple-element.107), channel_id=1, source_target_pairs={{0,1},{1,0},{2,3},{3,2},{4,5},{5,4},{6,7},{7,6},{8,9},{9,8},{10,11... | collective-permute-start | bytes 3145736 | tf_op jit(solution)/shard_map/ppermute | solution.py:679
  166.2 26.1 %collective-permute-start.17 = (bf16[512,384]{1,0:T(8,128)(2,1)}, bf16[512,384]{1,0:T(8,128)(2,1)}, u32[]{:S(2)}, u32[]{:S(2)}) collective-permute-start(bf16[512,384]{1,0:T(8,128)(2,1)} %get-tuple-element.108), channel_id=1, source_target_pairs={{0,1},{1,0},{2,3},{3,2},{4,5},{5,4},{6,7},{7,6},{8,9},{9,8},{10,11... | collective-permute-start | bytes 1179656 | tf_op jit(solution)/shard_map/ppermute | solution.py:679
  190.1 25.6 %collective-permute-start.18 = (bf16[512,768]{1,0:T(8,128)(2,1)}, bf16[512,768]{1,0:T(8,128)(2,1)}, u32[]{:S(2)}, u32[]{:S(2)}) collective-permute-start(bf16[512,768]{1,0:T(8,128)(2,1)} %get-tuple-element.114), channel_id=1, source_target_pairs={{0,1},{1,0},{2,3},{3,2},{4,5},{5,4},{6,7},{7,6},{8,9},{9,8},{10,11... | collective-permute-start | bytes 2359304 | tf_op jit(solution)/shard_map/ppermute | solution.py:679
  215.0 2.3 collective-permute-start.19
  215.4 17.4 %collective-permute-start.21 = (bf16[2048,384]{1,0:T(8,128)(2,1)}, bf16[2048,384]{1,0:T(8,128)(2,1)}, u32[]{:S(2)}, u32[]{:S(2)}) collective-permute-start(bf16[2048,384]{1,0:T(8,128)(2,1)} %get-tuple-element.121), channel_id=1, source_target_pairs={{0,1},{1,0},{2,3},{3,2},{4,5},{5,4},{6,7},{7,6},{8,9},{9,8},{10,11... | collective-permute-start | bytes 4718600 | tf_op jit(solution)/shard_map/ppermute | solution.py:679
  232.1 12.7 %collective-permute-start.20 = (bf16[384,4096]{1,0:T(8,128)(2,1)}, bf16[384,4096]{1,0:T(8,128)(2,1)}, u32[]{:S(2)}, u32[]{:S(2)}) collective-permute-start(bf16[384,4096]{1,0:T(8,128)(2,1)} %get-tuple-element.119.refs_4_.refs_2_), channel_id=1, source_target_pairs={{0,1},{1,0},{2,3},{3,2},{4,5},{5,4},{6,7},{7,6},{8,9},{9,8},{10,11... | collective-permute-start | bytes 9437192 | tf_op jit(solution)/shard_map/ppermute | solution.py:679
  232.5 75.3 %collective-permute-start.22 = (bf16[512,768]{1,0:T(8,128)(2,1)}, bf16[512,768]{1,0:T(8,128)(2,1)}, u32[]{:S(2)}, u32[]{:S(2)}) collective-permute-start(bf16[512,768]{1,0:T(8,128)(2,1)} %get-tuple-element.127), channel_id=1, source_target_pairs={{0,1},{1,0},{2,3},{3,2},{4,5},{5,4},{6,7},{7,6},{8,9},{9,8},{10,11... | collective-permute-start | bytes 2359304 | tf_op jit(solution)/shard_map/ppermute | solution.py:679
  243.2 51.0 %collective-permute-start.26 = (bf16[1024,1024]{1,0:T(8,128)(2,1)}, bf16[1024,1024]{1,0:T(8,128)(2,1)}, u32[]{:S(2)}, u32[]{:S(2)}) collective-permute-start(bf16[1024,1024]{1,0:T(8,128)(2,1)} %get-tuple-element.122.refs_4_), channel_id=1, source_target_pairs={{0,4},{1,5},{2,6},{3,7},{4,0},{5,1},{6,2},{7,3},{8,12},{9,13},{10,... | collective-permute-start | bytes 6291464 | tf_op jit(solution)/shard_map/ppermute | solution.py:679
  254.1 47.8 %collective-permute-start.25 = (bf16[256,4096]{1,0:T(8,128)(2,1)}, bf16[256,4096]{1,0:T(8,128)(2,1)}, u32[]{:S(2)}, u32[]{:S(2)}) collective-permute-start(bf16[256,4096]{1,0:T(8,128)(2,1)} %get-tuple-element.123.rest_0_), channel_id=1, source_target_pairs={{0,2},{1,3},{2,0},{3,1},{4,6},{5,7},{6,4},{7,5},{8,10},{9,11},{10,... | collective-permute-start | bytes 6291464 | tf_op jit(solution)/shard_map/ppermute | solution.py:679
  274.0 34.4 %collective-permute-start.24 = (bf16[3072,1024]{1,0:T(8,128)(2,1)}, bf16[3072,1024]{1,0:T(8,128)(2,1)}, u32[]{:S(2)}, u32[]{:S(2)}) collective-permute-start(bf16[3072,1024]{1,0:T(8,128)(2,1)} %get-tuple-element.124.query_delta.refs_6_.refs_8_.refs_0_.refs_1_), channel_id=1, source_target_pairs={{0,1},{1,0},{2,3},{3,2},{4,5},{5,4},{6,7},{7,6},{8,9},{9,8},{10,11... | collective-permute-start | bytes 18874376 | tf_op jit(solution)/shard_map/ppermute | solution.py:679
  294.2 6.3 %collective-permute-start.27 = (bf16[2,2,2,2,32,256]{5,4,2,1,0,3:T(8,128)(2,1)}, bf16[2,2,2,2,32,256]{5,4,2,1,0,3:T(8,128)(2,1)}, u32[]{:S(2)}, u32[]{:S(2)}) collective-permute-start(bf16[2,2,2,2,32,256]{5,4,2,1,0,3:T(8,128)(2,1)} %bitcast.92), channel_id=1, source_target_pairs={{0,1},{1,0},{2,3},{3,2},{4,5},{5,4},{6,7},{7,6},{8,9},{9,8},{10,11... | collective-permute-start | bytes 786440 | tf_op jit(solution)/shard_map/ppermute | solution.py:679
  294.2 34.7 %collective-permute-start.23 = (bf16[1536,1024]{1,0:T(8,128)(2,1)S(1)}, bf16[1536,1024]{1,0:T(8,128)(2,1)}, u32[]{:S(2)}, u32[]{:S(2)}) collective-permute-start(bf16[1536,1024]{1,0:T(8,128)(2,1)S(1)} %copy-done.2), channel_id=1, source_target_pairs={{0,1},{1,0},{2,3},{3,2},{4,5},{5,4},{6,7},{7,6},{8,9},{9,8},{10,11... | collective-permute-start | bytes 9437192 | tf_op jit(solution)/shard_map/ppermute | solution.py:679
  300.5 38.9 %collective-permute-start.31 = (bf16[4,128,1024]{2,1,0:T(8,128)(2,1)}, bf16[4,128,1024]{2,1,0:T(8,128)(2,1)}, u32[]{:S(2)}, u32[]{:S(2)}) collective-permute-start(bf16[4,128,1024]{2,1,0:T(8,128)(2,1)} %get-tuple-element.142), channel_id=1, source_target_pairs={{0,2},{1,3},{2,0},{3,1},{4,6},{5,7},{6,4},{7,5},{8,10},{9,11},{10,... | collective-permute-start | bytes 3145736 | tf_op jit(solution)/shard_map/ppermute | solution.py:679
  301.9 26.7 %collective-permute-start.28 = (bf16[2,2,2,32,256]{4,3,2,1,0:T(8,128)(2,1)S(1)}, bf16[2,2,2,32,256]{4,3,2,1,0:T(8,128)(2,1)S(1)}, u32[]{:S(2)}, u32[]{:S(2)}) collective-permute-start(bf16[2,2,2,32,256]{4,3,2,1,0:T(8,128)(2,1)S(1)} %get-tuple-element.217), channel_id=1, source_target_pairs={{0,2},{1,3},{2,0},{3,1},{4,6},{5,7},{6,4},{7,5},{8,10},{9,11},{10,... | collective-permute-start | bytes 393224 | tf_op jit(solution)/shard_map/ppermute | solution.py:679
  303.6 56.9 %slice-start = ((s8[6291456]{0:T(1024)(128)(4,1)}), s8[4194304]{0:T(1024)(128)(4,1)S(1)}, s32[]{:S(2)}) async-start(s8[6291456]{0:T(1024)(128)(4,1)} %bitcast.93), calls=%async_computation.1 | async-start | bytes 8388608
  307.8 31.5 %collective-permute-start.32 = (bf16[4,32,4096]{2,1,0:T(8,128)(2,1)}, bf16[4,32,4096]{2,1,0:T(8,128)(2,1)}, u32[]{:S(2)}, u32[]{:S(2)}) collective-permute-start(bf16[4,32,4096]{2,1,0:T(8,128)(2,1)} %get-tuple-element.143), channel_id=1, source_target_pairs={{0,4},{1,5},{2,6},{3,7},{4,0},{5,1},{6,2},{7,3},{8,12},{9,13},{10,... | collective-permute-start | bytes 3145736 | tf_op jit(solution)/shard_map/ppermute | solution.py:679
  310.6 49.9 %slice-start.1 = ((s8[6291456]{0:T(1024)(128)(4,1)}), s8[2097152]{0:T(1024)(128)(4,1)S(1)}, s32[]{:S(2)}) async-start(s8[6291456]{0:T(1024)(128)(4,1)} %bitcast.93), calls=%async_computation.2 | async-start | bytes 4194304
  325.0 31.7 %collective-permute-start.34 = (bf16[256,2048]{1,0:T(8,128)(2,1)}, bf16[256,2048]{1,0:T(8,128)(2,1)}, u32[]{:S(2)}, u32[]{:S(2)}) collective-permute-start(bf16[256,2048]{1,0:T(8,128)(2,1)} %get-tuple-element.146), channel_id=1, source_target_pairs={{0,4},{1,5},{2,6},{3,7},{4,0},{5,1},{6,2},{7,3},{8,12},{9,13},{10,... | collective-permute-start | bytes 3145736 | tf_op jit(solution)/shard_map/ppermute | solution.py:679
  328.6 28.1 %collective-permute-start.35 = (bf16[256,2048]{1,0:T(8,128)(2,1)}, bf16[256,2048]{1,0:T(8,128)(2,1)}, u32[]{:S(2)}, u32[]{:S(2)}) collective-permute-start(bf16[256,2048]{1,0:T(8,128)(2,1)} %get-tuple-element.148), channel_id=1, source_target_pairs={{0,2},{1,3},{2,0},{3,1},{4,6},{5,7},{6,4},{7,5},{8,10},{9,11},{10,... | collective-permute-start | bytes 3145736 | tf_op jit(solution)/shard_map/ppermute | solution.py:679
  341.6 28.4 %collective-permute-start.33 = (bf16[2,32,8192]{2,1,0:T(8,128)(2,1)S(1)}, bf16[2,32,8192]{2,1,0:T(8,128)(2,1)S(1)}, u32[]{:S(2)}, u32[]{:S(2)}) collective-permute-start(bf16[2,32,8192]{2,1,0:T(8,128)(2,1)S(1)} %get-tuple-element.145), channel_id=1, source_target_pairs={{0,8},{1,9},{2,10},{3,11},{4,12},{5,13},{6,14},{7,15},{8,0},{9,1},... | collective-permute-start | bytes 3145736 | tf_op jit(solution)/shard_map/ppermute | solution.py:679
  345.0 34.1 %collective-permute-start.29 = (bf16[256,2048]{1,0:T(8,128)(2,1)S(1)}, bf16[256,2048]{1,0:T(8,128)(2,1)S(1)}, u32[]{:S(2)}, u32[]{:S(2)}) collective-permute-start(bf16[256,2048]{1,0:T(8,128)(2,1)S(1)} %get-tuple-element.139), channel_id=1, source_target_pairs={{0,4},{1,5},{2,6},{3,7},{4,0},{5,1},{6,2},{7,3},{8,12},{9,13},{10,... | collective-permute-start | bytes 3145736 | tf_op jit(solution)/shard_map/ppermute | solution.py:679
  345.9 33.1 %collective-permute-start.30 = (bf16[256,2048]{1,0:T(8,128)(2,1)}, bf16[256,2048]{1,0:T(8,128)(2,1)S(1)}, u32[]{:S(2)}, u32[]{:S(2)}) collective-permute-start(bf16[256,2048]{1,0:T(8,128)(2,1)} %get-tuple-element.141), channel_id=1, source_target_pairs={{0,2},{1,3},{2,0},{3,1},{4,6},{5,7},{6,4},{7,5},{8,10},{9,11},{10,... | collective-permute-start | bytes 3145736 | tf_op jit(solution)/shard_map/ppermute | solution.py:679
  359.6 29.0 %collective-permute-start.38 = (bf16[4,32,2048]{2,1,0:T(8,128)(2,1)}, bf16[4,32,2048]{2,1,0:T(8,128)(2,1)S(1)}, u32[]{:S(2)}, u32[]{:S(2)}) collective-permute-start(bf16[4,32,2048]{2,1,0:T(8,128)(2,1)} %get-tuple-element.156), channel_id=1, source_target_pairs={{0,2},{1,3},{2,0},{3,1},{4,6},{5,7},{6,4},{7,5},{8,10},{9,11},{10,... | collective-permute-start | bytes 1572872 | tf_op jit(solution)/shard_map/ppermute | solution.py:679
  359.9 30.4 %collective-permute-start.39 = (bf16[4,32,2048]{2,1,0:T(8,128)(2,1)}, bf16[4,32,2048]{2,1,0:T(8,128)(2,1)S(1)}, u32[]{:S(2)}, u32[]{:S(2)}) collective-permute-start(bf16[4,32,2048]{2,1,0:T(8,128)(2,1)} %get-tuple-element.157), channel_id=1, source_target_pairs={{0,4},{1,5},{2,6},{3,7},{4,0},{5,1},{6,2},{7,3},{8,12},{9,13},{10,... | collective-permute-start | bytes 1572872 | tf_op jit(solution)/shard_map/ppermute | solution.py:679
  372.9 23.9 %collective-permute-start.44 = (bf16[1,32,8192]{2,1,0:T(8,128)(2,1)S(1)}, bf16[1,32,8192]{2,1,0:T(8,128)(2,1)S(1)}, u32[]{:S(2)}, u32[]{:S(2)}) collective-permute-start(bf16[1,32,8192]{2,1,0:T(8,128)(2,1)S(1)} %get-tuple-element.166), channel_id=1, source_target_pairs={{0,16},{1,17},{2,18},{3,19},{4,20},{5,21},{6,22},{7,23},{8,24},{9,... | collective-permute-start | bytes 1572872 | tf_op jit(solution)/shard_map/ppermute | solution.py:679
  380.1 18.1 %collective-permute-start.36 = (bf16[4,32,2048]{2,1,0:T(8,128)(2,1)S(1)}, bf16[4,32,2048]{2,1,0:T(8,128)(2,1)S(1)}, u32[]{:S(2)}, u32[]{:S(2)}) collective-permute-start(bf16[4,32,2048]{2,1,0:T(8,128)(2,1)S(1)} %get-tuple-element.154), channel_id=1, source_target_pairs={{0,2},{1,3},{2,0},{3,1},{4,6},{5,7},{6,4},{7,5},{8,10},{9,11},{10,... | collective-permute-start | bytes 1572872 | tf_op jit(solution)/shard_map/ppermute | solution.py:679
  380.5 20.9 %collective-permute-start.37 = (bf16[4,32,2304]{2,1,0:T(8,128)(2,1)S(1)}, bf16[4,32,2304]{2,1,0:T(8,128)(2,1)S(1)}, u32[]{:S(2)}, u32[]{:S(2)}) collective-permute-start(bf16[4,32,2304]{2,1,0:T(8,128)(2,1)S(1)} %get-tuple-element.155), channel_id=1, source_target_pairs={{0,4},{1,5},{2,6},{3,7},{4,0},{5,1},{6,2},{7,3},{8,12},{9,13},{10,... | collective-permute-start | bytes 1769480 | tf_op jit(solution)/shard_map/ppermute | solution.py:679
  392.5 19.5 %collective-permute-start.41 = (bf16[2,32,4096]{2,1,0:T(8,128)(2,1)S(1)}, bf16[2,32,4096]{2,1,0:T(8,128)(2,1)S(1)}, u32[]{:S(2)}, u32[]{:S(2)}) collective-permute-start(bf16[2,32,4096]{2,1,0:T(8,128)(2,1)S(1)} %get-tuple-element.161), channel_id=1, source_target_pairs={{0,8},{1,9},{2,10},{3,11},{4,12},{5,13},{6,14},{7,15},{8,0},{9,1},... | collective-permute-start | bytes 1572872 | tf_op jit(solution)/shard_map/ppermute | solution.py:679
  402.2 19.9 %collective-permute-start.40 = (bf16[2,32,4352]{2,1,0:T(8,128)(2,1)S(1)}, bf16[2,32,4352]{2,1,0:T(8,128)(2,1)S(1)}, u32[]{:S(2)}, u32[]{:S(2)}) collective-permute-start(bf16[2,32,4352]{2,1,0:T(8,128)(2,1)S(1)} %get-tuple-element.160), channel_id=1, source_target_pairs={{0,8},{1,9},{2,10},{3,11},{4,12},{5,13},{6,14},{7,15},{8,0},{9,1},... | collective-permute-start | bytes 1671176 | tf_op jit(solution)/shard_map/ppermute | solution.py:679
  412.7 13.3 %collective-permute-start.43 = (bf16[1,32,4096]{2,1,0:T(8,128)(2,1)S(1)}, bf16[1,32,4096]{2,1,0:T(8,128)(2,1)}, u32[]{:S(2)}, u32[]{:S(2)}) collective-permute-start(bf16[1,32,4096]{2,1,0:T(8,128)(2,1)S(1)} %get-tuple-element.165), channel_id=1, source_target_pairs={{0,16},{1,17},{2,18},{3,19},{4,20},{5,21},{6,22},{7,23},{8,24},{9,... | collective-permute-start | bytes 786440 | tf_op jit(solution)/shard_map/ppermute | solution.py:679
  422.8 15.2 %collective-permute-start.42 = (bf16[1,32,4352]{2,1,0:T(8,128)(2,1)S(1)}, bf16[1,32,4352]{2,1,0:T(8,128)(2,1)S(1)}, u32[]{:S(2)}, u32[]{:S(2)}) collective-permute-start(bf16[1,32,4352]{2,1,0:T(8,128)(2,1)S(1)} %get-tuple-element.164), channel_id=1, source_target_pairs={{0,16},{1,17},{2,18},{3,19},{4,20},{5,21},{6,22},{7,23},{8,24},{9,... | collective-permute-start | bytes 835592 | tf_op jit(solution)/shard_map/ppermute | solution.py:679
  (69 other events, 547.3 us)
Sparse Core Ops, SparseCore 0:
  51.5 146.2 all-gather.2
